TPU v7x, 32 devices: a whole 2x2x4 slice. The times are simulated.
32 devices in a mesh: dp: 8 (over y, x, core), expert: 4 (over z).
Axes of the slice: x: 2, y: 2, z: 4, core: 2. Of those that a mesh axis runs over, the one named last changes fastest.
Arguments:
- image_tokens: bfloat16 [6304, 768], P(('dp', 'expert')), may hold values from -6 to 6
- norm_gains: float32 [2, 2, 768], P(None, None, 'dp'), may hold values from 0.5 to 1.5
- biases: float32 [2, 5, 768], P(None, None, 'dp'), may hold values from -2 to 2
- w_qkv: bfloat16 [2, 768, 2304], P(None, 'dp'), may hold values from -0.21875 to 0.21875
- w_out: bfloat16 [2, 768, 768], P(None, 'dp'), may hold values from -1.25 to 1.25
- w_router: float32 [2, 768, 4], P(None, 'dp'), may hold values from -0.15625 to 0.15625
- router_noise: float32 [2, 6304, 4], P(None, ('dp', 'expert')), may hold values from -3 to 3
- w_in: bfloat16 [2, 4, 768, 3072], P(None, 'expert', 'dp'), may hold values from -0.21875 to 0.21875
- b_in: float32 [2, 4, 3072], P(None, 'expert', 'dp'), may hold values from -2 to 2
- w_outexp: bfloat16 [2, 4, 3072, 768], P(None, 'expert', 'dp'), may hold values from -0.625 to 0.625
- b_expout: float32 [2, 4, 768], P(None, 'expert', 'dp'), may hold values from -3.2 to 3.2
- routes: int32 [2, 6304, 2], P(None, ('dp', 'expert')), may hold values from 0 to 3, all different within a row
- seat_order: int32 [2, 32, 394], P(None, ('dp', 'expert')), may hold values from 0 to 393, each once within a row
- cotangent: bfloat16 [6304, 768], P(('dp', 'expert')), may hold values from -6 to 6
Outputs:
- mixed: float32 [6304, 768], P(('dp', 'expert'))
- grad_tokens: float32 [6304, 768], P(('dp', 'expert'))
- grad_gains: float32 [2, 2, 768], P(None, None, 'dp')
- grad_biases: float32 [2, 5, 768], P(None, None, 'dp')
- grad_qkv: float32 [2, 768, 2304], P(None, 'dp')
- grad_out: float32 [2, 768, 768], P(None, 'dp')
- grad_router: float32 [2, 768, 4], P(None, 'dp')
- grad_in: float32 [2, 4, 768, 3072], P(None, 'expert', 'dp')
- grad_in_bias: float32 [2, 4, 3072], P(None, 'expert', 'dp')
- grad_outexp: float32 [2, 4, 3072, 768], P(None, 'expert', 'dp')
- grad_expout_bias: float32 [2, 4, 768], P(None, 'expert', 'dp')
Inputs may be any that keep to these rules, and one draw needn't show every extreme that they name: `routes`: the two experts of a token differ, and every expert is named by some token. `seat_order`: each device's row of 394 numbers holds each number once.
All inputs are finite; a program needn't handle non-finite values.
Results may differ from a plain program's by a relative error of at most 0.035.
Values may be sent and summed in bfloat16 or wider, within the bound.
No kernel may reach another device: no remote copies, remote signals or barrier semaphores. Data moves between devices by JAX's collectives and lax.ppermute only.
A program may use at most 192 MiB of HBM per device.

v0:
```python
import jax
import jax.numpy as jnp
from jax import lax
from jax.sharding import PartitionSpec as P

D = 768
HEADS = 12
HEAD_DIM = 64
SEQ = 197


EPS = 1e-06
HIGH = lax.Precision.HIGHEST


def norm_rows(x):
    centered = x - jnp.mean(x, -1, keepdims=True)
    rstd = lax.rsqrt(jnp.mean(centered * centered, -1, keepdims=True) + EPS)
    return (centered * rstd, rstd)


def norm_back(grad_hat, normed, rstd):
    return rstd * (
        grad_hat
        - jnp.mean(grad_hat, -1, keepdims=True)
        - normed * jnp.mean(grad_hat * normed, -1, keepdims=True)
    )


def contract_rows(left, right, precision=None):
    return lax.dot_general(
        left,
        right,
        (((0,), (0,)), ((), ())),
        preferred_element_type=jnp.float32,
        precision=precision,
    )


def times_transposed(left, right, precision=None):
    return lax.dot_general(
        left,
        right,
        (((1,), (1,)), ((), ())),
        preferred_element_type=jnp.float32,
        precision=precision,
    )


def seat_pairs(pair_expert, seat_rows, experts, capacity):
    count = pair_expert.shape[0]
    inverse = jnp.zeros((count,), jnp.int32).at[seat_rows].set(jnp.arange(count, dtype=jnp.int32))
    sorted_expert = pair_expert[inverse]
    onehot = (sorted_expert[:, None] == jnp.arange(experts, dtype=jnp.int32)[None, :]).astype(
        jnp.int32
    )
    before = jnp.cumsum(onehot, 0) - onehot
    rank = jnp.sum(before * onehot, 1)[seat_rows]
    valid = rank < capacity
    raw_slot = jnp.where(valid, pair_expert * capacity + rank, experts * capacity)
    pair_token = jnp.arange(count, dtype=jnp.int32) // 2
    slot_token = (
        jnp.zeros((experts * capacity,), jnp.int32).at[raw_slot].set(pair_token, mode="drop")
    )
    slot_used = jnp.zeros((experts * capacity,), jnp.float32).at[raw_slot].set(1.0, mode="drop")
    return (raw_slot, valid, slot_token, slot_used)


def fetch_attention(gains, shifts, wide_qkv, wide_out, router):
    return (
        lax.all_gather(wide_qkv, "dp", axis=0, tiled=True),
        lax.all_gather(wide_out, "dp", axis=0, tiled=True),
        lax.all_gather(router.astype(jnp.bfloat16), "dp", axis=0, tiled=True).astype(router.dtype),
        lax.all_gather(gains.astype(jnp.bfloat16), "dp", axis=1, tiled=True).astype(gains.dtype),
        lax.all_gather(shifts.astype(jnp.bfloat16), "dp", axis=1, tiled=True).astype(shifts.dtype),
    )


def fetch_attention_again(gains, shifts, wide_qkv, wide_out, router):
    return (
        lax.all_gather(wide_qkv, "dp", axis=0, tiled=True),
        lax.all_gather(wide_out, "dp", axis=0, tiled=True),
        lax.all_gather(router.astype(jnp.bfloat16), "dp", axis=0, tiled=True).astype(router.dtype),
        lax.all_gather(gains.astype(jnp.bfloat16), "dp", axis=1, tiled=True).astype(gains.dtype),
        lax.all_gather(shifts.astype(jnp.bfloat16), "dp", axis=1, tiled=True).astype(shifts.dtype),
    )


def fetch_experts(wide_in, bias_in, wide_oe, bias_oe):
    return (
        lax.all_gather(wide_in, "dp", axis=1, tiled=True),
        lax.all_gather(wide_oe, "dp", axis=1, tiled=True),
        lax.all_gather(bias_in.astype(jnp.bfloat16), "dp", axis=1, tiled=True).astype(
            bias_in.dtype
        ),
        lax.all_gather(bias_oe.astype(jnp.bfloat16), "dp", axis=1, tiled=True).astype(
            bias_oe.dtype
        ),
    )


def fetch_experts_again(wide_in, bias_in, wide_oe, bias_oe):
    return (
        lax.all_gather(wide_in, "dp", axis=1, tiled=True),
        lax.all_gather(wide_oe, "dp", axis=1, tiled=True),
        lax.all_gather(bias_in.astype(jnp.bfloat16), "dp", axis=1, tiled=True).astype(
            bias_in.dtype
        ),
        lax.all_gather(bias_oe.astype(jnp.bfloat16), "dp", axis=1, tiled=True).astype(
            bias_oe.dtype
        ),
    )


def forward_layer(x, attn, expert, noise, route_rows, seat_rows):
    wide_qkv, wide_out, wide_router, gains, shifts = attn
    wide_in, wide_oe, bias_in, bias_oe = expert
    tokens_here = x.shape[0]
    images = tokens_here // SEQ
    scale = HEAD_DIM ** (-0.5)
    normed1, rstd1 = norm_rows(x)
    a_low = (normed1 * gains[0] + shifts[0]).astype(jnp.bfloat16)
    qkv = jnp.dot(a_low, wide_qkv, preferred_element_type=jnp.float32)
    qkv = qkv + jnp.concatenate([shifts[2], jnp.zeros_like(shifts[2]), shifts[3]])
    qkv_low = qkv.astype(jnp.bfloat16).reshape(images, SEQ, 3, HEADS, HEAD_DIM)
    query, keys, values = (qkv_low[:, :, 0], qkv_low[:, :, 1], qkv_low[:, :, 2])
    scores = jnp.einsum("bqhd,bkhd->bhqk", query, keys, preferred_element_type=jnp.float32) * scale
    top = jnp.max(scores, -1, keepdims=True)
    lse = top + jnp.log(jnp.sum(jnp.exp(scores - top), -1, keepdims=True))
    probs = jnp.exp(scores - lse).astype(jnp.bfloat16)
    attended = jnp.einsum("bhqk,bkhd->bqhd", probs, values, preferred_element_type=jnp.float32)
    mixed_low = attended.reshape(tokens_here, D).astype(jnp.bfloat16)
    x1 = x + jnp.dot(mixed_low, wide_out, preferred_element_type=jnp.float32) + shifts[4]
    normed2, rstd2 = norm_rows(x1)
    moe_in = normed2 * gains[1] + shifts[1]
    gates = jax.nn.softmax(jnp.dot(moe_in, wide_router, precision=HIGH) + noise, -1)
    pair_gate = jnp.take_along_axis(gates, route_rows, 1)
    experts = gates.shape[1]
    capacity = 2 * tokens_here // experts
    raw_slot, valid, slot_token, slot_used = seat_pairs(
        route_rows.reshape(-1), seat_rows, experts, capacity
    )
    slot = jnp.minimum(raw_slot, experts * capacity - 1)
    slot_gate = (
        jnp.zeros((experts * capacity,), jnp.float32)
        .at[raw_slot]
        .set(pair_gate.reshape(-1), mode="drop")
    )
    rows_low = moe_in.astype(jnp.bfloat16)
    sending = jnp.where(slot_used[:, None] > 0, rows_low[slot_token], jnp.zeros((), jnp.bfloat16))
    owners = lax.axis_size("expert")
    sending = sending.reshape(owners, experts // owners, capacity, D)
    arrived = lax.all_to_all(sending, "expert", split_axis=0, concat_axis=0, tiled=True)
    pre = (
        jnp.einsum("sicd,idf->sicf", arrived, wide_in, preferred_element_type=jnp.float32)
        + bias_in[None, :, None, :]
    )
    hidden = jax.nn.gelu(pre).astype(jnp.bfloat16)
    produced = (
        jnp.einsum("sicf,ifd->sicd", hidden, wide_oe, preferred_element_type=jnp.float32)
        + bias_oe[None, :, None, :]
    )
    returned = lax.all_to_all(
        produced.astype(jnp.bfloat16), "expert", split_axis=0, concat_axis=0, tiled=True
    ).reshape(experts * capacity, D)
    weight = jnp.where(valid, pair_gate.reshape(-1), 0.0).reshape(tokens_here, 2)
    pieces = returned[slot].astype(jnp.float32).reshape(tokens_here, 2, D)
    x2 = x1 + weight[:, 0:1] * pieces[:, 0] + weight[:, 1:2] * pieces[:, 1]
    kept = (
        normed1,
        rstd1,
        a_low,
        qkv_low,
        lse,
        mixed_low,
        normed2,
        rstd2,
        moe_in,
        gates,
        valid,
        slot,
        slot_token,
        slot_gate,
        arrived,
        pre,
        hidden,
        returned,
    )
    return (x2, kept)


def backward_layer(grad, kept, attn, expert, route_rows):
    wide_qkv, wide_out, wide_router, gains, shifts = attn
    wide_in, wide_oe, bias_in, bias_oe = expert
    (
        normed1,
        rstd1,
        a_low,
        qkv_low,
        lse,
        mixed_low,
        normed2,
        rstd2,
        moe_in,
        gates,
        valid,
        slot,
        slot_token,
        slot_gate,
        arrived,
        pre,
        hidden,
        returned,
    ) = kept
    tokens_here = grad.shape[0]
    images = tokens_here // SEQ
    scale = HEAD_DIM ** (-0.5)
    valid_pairs = valid.reshape(tokens_here, 2)
    pieces = returned[slot].astype(jnp.float32).reshape(tokens_here, 2, D)
    d_pair = jnp.where(valid_pairs, jnp.sum(grad[:, None, :] * pieces, -1), 0.0)
    d_rows = (grad[slot_token] * slot_gate[:, None]).astype(jnp.bfloat16).reshape(arrived.shape)
    d_produced = lax.all_to_all(d_rows, "expert", split_axis=0, concat_axis=0, tiled=True)
    d_bias_oe = jnp.sum(d_produced.astype(jnp.float32), (0, 2))
    d_wide_oe = jnp.einsum("sicf,sicd->ifd", hidden, d_produced, preferred_element_type=jnp.float32)
    d_hidden = jnp.einsum("sicd,ifd->sicf", d_produced, wide_oe, preferred_element_type=jnp.float32)
    unused, gelu_pull = jax.vjp(jax.nn.gelu, pre)
    d_pre = gelu_pull(d_hidden)[0].astype(jnp.bfloat16)
    d_bias_in = jnp.sum(d_pre.astype(jnp.float32), (0, 2))
    d_wide_in = jnp.einsum("sicd,sicf->idf", arrived, d_pre, preferred_element_type=jnp.float32)
    d_sent = jnp.einsum(
        "sicf,idf->sicd", d_pre, wide_in, preferred_element_type=jnp.float32
    ).astype(jnp.bfloat16)
    d_back = lax.all_to_all(d_sent, "expert", split_axis=0, concat_axis=0, tiled=True).reshape(
        -1, D
    )
    d_parts = d_back[slot].astype(jnp.float32).reshape(tokens_here, 2, D)
    d_moe = jnp.sum(jnp.where(valid_pairs[:, :, None], d_parts, 0.0), 1)
    experts = gates.shape[1]
    choose = (route_rows[:, :, None] == jnp.arange(experts, dtype=jnp.int32)[None, None, :]).astype(
        jnp.float32
    )
    d_gates = jnp.sum(d_pair[:, :, None] * choose, 1)
    d_logits = gates * (d_gates - jnp.sum(d_gates * gates, -1, keepdims=True))
    d_router = contract_rows(moe_in, d_logits, HIGH)
    d_moe = d_moe + times_transposed(d_logits, wide_router, HIGH)
    d_gain2 = jnp.sum(d_moe * normed2, 0)
    d_shift2 = jnp.sum(d_moe, 0)
    d_x1 = grad + norm_back(d_moe * gains[1], normed2, rstd2)
    d_branch = d_x1.astype(jnp.bfloat16)
    d_shift_out = jnp.sum(d_branch.astype(jnp.float32), 0)
    d_wide_out = contract_rows(mixed_low, d_branch)
    d_mixed = (
        times_transposed(d_branch, wide_out)
        .astype(jnp.bfloat16)
        .reshape(images, SEQ, HEADS, HEAD_DIM)
    )
    query, keys, values = (qkv_low[:, :, 0], qkv_low[:, :, 1], qkv_low[:, :, 2])
    scores = jnp.einsum("bqhd,bkhd->bhqk", query, keys, preferred_element_type=jnp.float32) * scale
    probs = jnp.exp(scores - lse)
    d_probs = jnp.einsum("bqhd,bkhd->bhqk", d_mixed, values, preferred_element_type=jnp.float32)
    d_values = jnp.einsum(
        "bhqk,bqhd->bkhd", probs.astype(jnp.bfloat16), d_mixed, preferred_element_type=jnp.float32
    )
    d_scores = (probs * (d_probs - jnp.sum(d_probs * probs, -1, keepdims=True))).astype(
        jnp.bfloat16
    )
    d_query = (
        jnp.einsum("bhqk,bkhd->bqhd", d_scores, keys, preferred_element_type=jnp.float32) * scale
    )
    d_keys = (
        jnp.einsum("bhqk,bqhd->bkhd", d_scores, query, preferred_element_type=jnp.float32) * scale
    )
    d_qkv = (
        jnp.stack([d_query, d_keys, d_values], 2).reshape(tokens_here, 3 * D).astype(jnp.bfloat16)
    )
    column_sums = jnp.sum(d_qkv.astype(jnp.float32), 0)
    d_wide_qkv = contract_rows(a_low, d_qkv)
    d_normed = times_transposed(d_qkv, wide_qkv)
    d_gain1 = jnp.sum(d_normed * normed1, 0)
    d_shift1 = jnp.sum(d_normed, 0)
    d_x = d_x1 + norm_back(d_normed * gains[0], normed1, rstd1)
    d_gains = jnp.stack([d_gain1, d_gain2])
    d_shifts = jnp.stack([d_shift1, d_shift2, column_sums[:D], column_sums[2 * D :], d_shift_out])
    return (
        d_x,
        (d_wide_qkv, d_wide_out, d_router, d_gains, d_shifts),
        (d_wide_in, d_wide_oe, d_bias_in, d_bias_oe),
    )


def per_device(
    image_tokens,
    norm_gains,
    biases,
    w_qkv,
    w_out,
    w_router,
    router_noise,
    w_in,
    b_in,
    w_outexp,
    b_expout,
    routes,
    seat_order,
    cotangent,
):
    layers = w_qkv.shape[0]
    state = image_tokens.astype(jnp.float32)
    saved = []
    for layer in range(layers):
        attn = fetch_attention(
            norm_gains[layer], biases[layer], w_qkv[layer], w_out[layer], w_router[layer]
        )
        expert = fetch_experts(w_in[layer], b_in[layer], w_outexp[layer], b_expout[layer])
        state, kept = forward_layer(
            state, attn, expert, router_noise[layer], routes[layer], seat_order[layer, 0]
        )
        saved.append((None, None, kept))
    grad = cotangent.astype(jnp.float32)
    attn_grads = [None] * layers
    expert_grads = [None] * layers
    for layer in reversed(range(layers)):
        attn, expert, kept = saved[layer]
        attn = fetch_attention_again(
            norm_gains[layer], biases[layer], w_qkv[layer], w_out[layer], w_router[layer]
        )
        expert = fetch_experts_again(w_in[layer], b_in[layer], w_outexp[layer], b_expout[layer])
        grad, local_attn, local_expert = backward_layer(grad, kept, attn, expert, routes[layer])
        shares = (
            lax.psum_scatter(
                local_attn[0].astype(jnp.bfloat16), "dp", scatter_dimension=0, tiled=True
            ).astype(jnp.float32),
            lax.psum_scatter(
                local_attn[1].astype(jnp.bfloat16), "dp", scatter_dimension=0, tiled=True
            ).astype(jnp.float32),
            lax.psum_scatter(
                local_attn[2].astype(jnp.bfloat16), "dp", scatter_dimension=0, tiled=True
            ).astype(jnp.float32),
            lax.psum_scatter(
                local_attn[3].astype(jnp.bfloat16), "dp", scatter_dimension=1, tiled=True
            ).astype(jnp.float32),
            lax.psum_scatter(
                local_attn[4].astype(jnp.bfloat16), "dp", scatter_dimension=1, tiled=True
            ).astype(jnp.float32),
        )
        attn_grads[layer] = (
            lax.psum(shares[0].astype(jnp.bfloat16), "expert").astype(jnp.float32),
            lax.psum(shares[1].astype(jnp.bfloat16), "expert").astype(jnp.float32),
            lax.psum(shares[2].astype(jnp.bfloat16), "expert").astype(jnp.float32),
            lax.psum(shares[3].astype(jnp.bfloat16), "expert").astype(jnp.float32),
            lax.psum(shares[4].astype(jnp.bfloat16), "expert").astype(jnp.float32),
        )
        expert_grads[layer] = (
            lax.psum_scatter(
                local_expert[0].astype(jnp.bfloat16), "dp", scatter_dimension=1, tiled=True
            ).astype(jnp.float32),
            lax.psum_scatter(
                local_expert[1].astype(jnp.bfloat16), "dp", scatter_dimension=1, tiled=True
            ).astype(jnp.float32),
            lax.psum_scatter(
                local_expert[2].astype(jnp.bfloat16), "dp", scatter_dimension=1, tiled=True
            ).astype(jnp.float32),
            lax.psum_scatter(
                local_expert[3].astype(jnp.bfloat16), "dp", scatter_dimension=1, tiled=True
            ).astype(jnp.float32),
        )
    grad_qkv = jnp.stack([item[0] for item in attn_grads])
    grad_out = jnp.stack([item[1] for item in attn_grads])
    grad_router = jnp.stack([item[2] for item in attn_grads])
    grad_gains = jnp.stack([item[3] for item in attn_grads])
    grad_biases = jnp.stack([item[4] for item in attn_grads])
    grad_in = jnp.stack([item[0] for item in expert_grads])
    grad_outexp = jnp.stack([item[1] for item in expert_grads])
    grad_in_bias = jnp.stack([item[2] for item in expert_grads])
    grad_expout_bias = jnp.stack([item[3] for item in expert_grads])
    return (
        state,
        grad,
        grad_gains,
        grad_biases,
        grad_qkv,
        grad_out,
        grad_router,
        grad_in,
        grad_in_bias,
        grad_outexp,
        grad_expout_bias,
    )


def solution(mesh):
    return jax.shard_map(
        per_device,
        mesh=mesh,
        in_specs=(
            P(("dp", "expert"), None),
            P(None, None, "dp"),
            P(None, None, "dp"),
            P(None, "dp", None),
            P(None, "dp", None),
            P(None, "dp", None),
            P(None, ("dp", "expert"), None),
            P(None, "expert", "dp", None),
            P(None, "expert", "dp"),
            P(None, "expert", "dp", None),
            P(None, "expert", "dp"),
            P(None, ("dp", "expert"), None),
            P(None, ("dp", "expert"), None),
            P(("dp", "expert"), None),
        ),
        out_specs=(
            P(("dp", "expert"), None),
            P(("dp", "expert"), None),
            P(None, None, "dp"),
            P(None, None, "dp"),
            P(None, "dp", None),
            P(None, "dp", None),
            P(None, "dp", None),
            P(None, "expert", "dp", None),
            P(None, "expert", "dp"),
            P(None, "expert", "dp", None),
            P(None, "expert", "dp"),
        ),
        check_vma=False,
    )
```

profile of v0, /device:TPU:0, one launch (start us, length us, event | category | flops | bytes accessed | tf_op | source)
XLA Modules:
  0.0 1259.7 jit_solution(5275462718790450586)
XLA Ops:
  50.5 12.1 all-gather
  67.6 9.9 all-gather.1
  78.0 11.8 slice_reduce_fusion.9
  89.8 9.2 all-gather.10
  99.4 12.4 slice_reduce_fusion.2
  133.2 13.8 %all-reduce.4 = (bf16[768]{0:T(1024)(128)(2,1)S(1)}, bf16[768]{0:T(1024)(128)(2,1)}) all-reduce(bf16[768]{0:T(1024)(128)(2,1)S(1)} %dynamic-update-slice, bf16[768]{0:T(1024)(128)(2,1)S(1)} %dynamic-update-slice.1), channel_id=10, replica_groups=mesh['dp'=8,'expert'=4] {'dp'}, use_global_device_ids=true, to_apply=%add.2 | all-reduce | flops 1536 | bytes 6144
  147.0 9.0 all-gather.6
  157.2 8.9 all-gather.9
  167.1 10.8 all-gather.4
  211.0 9.9 all-to-all-done.1
  272.1 32.0 %all-gather.41.cloned.1.call-done = bf16[1,1,3072,768]{3,2,1,0:T(8,128)(2,1)} async-done(((bf16[1,1,384,768]{3,2,1,0:T(8,128)(2,1)}), bf16[1,1,3072,768]{3,2,1,0:T(8,128)(2,1)}) %all-gather.41.cloned.1.call-update) | async-done | bytes 4718608 | tf_op jit(solution)/shard_map/all_gather | solution.py:92
  318.0 9.8 all-gather.13
  370.7 13.2 %all-to-all-done.4 = bf16[4,1,98,768]{3,2,1,0:T(8,128)(2,1)} async-done(((bf16[4,1,98,768]{3,2,1,0:T(8,128)(2,1)}), bf16[4,1,98,768]{3,2,1,0:T(8,128)(2,1)}, u32[]{:S(2)}, u32[]{:S(2)}) %all-to-all-start.4) | async-done | bytes 602144 | tf_op jit(solution)/shard_map/all_to_all | solution.py:222
  459.5 12.2 all-to-all-done.6
  471.8 8.5 fusion.266
  495.6 12.4 all-to-all-done.7
  573.5 15.4 %reduce-scatter.63.cloned.1.call-done = bf16[96,4]{1,0:T(8,128)(2,1)} async-done(((bf16[768,4]{1,0:T(8,128)(2,1)}), bf16[96,4]{1,0:T(8,128)(2,1)}) %reduce-scatter.63.cloned.1.call-update) | async-done | bytes 784
  589.7 35.6 %reduce-scatter.61.cloned.1.call-done = bf16[96,5]{1,0:T(8,128)(2,1)} async-done(((bf16[768,5]{1,0:T(8,128)(2,1)}), bf16[96,5]{1,0:T(8,128)(2,1)}) %reduce-scatter.61.cloned.1.call-update) | async-done | bytes 976
  626.1 35.9 %reduce-scatter.71.cloned.1.call-done = bf16[96,1]{1,0:T(8,128)(2,1)} async-done(((bf16[768,1]{1,0:T(8,128)(2,1)}), bf16[96,1]{1,0:T(8,128)(2,1)}) %reduce-scatter.71.cloned.1.call-update) | async-done | bytes 208
  663.5 37.2 %reduce-scatter.67.cloned.1.call-done = bf16[384,1]{1,0:T(8,128)(2,1)} async-done(((bf16[3072,1]{1,0:T(8,128)(2,1)}), bf16[384,1]{1,0:T(8,128)(2,1)}) %reduce-scatter.67.cloned.1.call-update) | async-done | bytes 784
  702.3 38.9 %reduce-scatter.45.cloned.1.call-done = bf16[96,768]{1,0:T(8,128)(2,1)} async-done(((bf16[768,768]{1,0:T(8,128)(2,1)}), bf16[96,768]{1,0:T(8,128)(2,1)}) %reduce-scatter.45.cloned.1.call-update) | async-done | bytes 147472 | tf_op jit(solution)/shard_map/reduce_scatter | solution.py:333
  741.2 40.8 %reduce-scatter.43.cloned.1.call-done = bf16[96,768]{1,0:T(8,128)(2,1)} async-done(((bf16[768,768]{1,0:T(8,128)(2,1)}), bf16[96,768]{1,0:T(8,128)(2,1)}) %reduce-scatter.43.cloned.1.call-update) | async-done | bytes 147472 | tf_op jit(solution)/shard_map/reduce_scatter | solution.py:333
  782.0 51.6 %reduce-scatter.41.cloned.1.call-done = bf16[96,2304]{1,0:T(8,128)(2,1)} async-done(((bf16[768,2304]{1,0:T(8,128)(2,1)}), bf16[96,2304]{1,0:T(8,128)(2,1)}) %reduce-scatter.41.cloned.1.call-update) | async-done | bytes 442384 | tf_op jit(solution)/shard_map/reduce_scatter | solution.py:330
  833.6 51.4 %reduce-scatter.39.cloned.1.call-done = bf16[96,2304]{1,0:T(8,128)(2,1)} async-done(((bf16[768,2304]{1,0:T(8,128)(2,1)}), bf16[96,2304]{1,0:T(8,128)(2,1)}) %reduce-scatter.39.cloned.1.call-update) | async-done | bytes 442384 | tf_op jit(solution)/shard_map/reduce_scatter | solution.py:330
  886.1 36.0 %reduce-scatter.55.cloned.1.call-done = bf16[96,2]{1,0:T(8,128)(2,1)} async-done(((bf16[768,2]{1,0:T(8,128)(2,1)}), bf16[96,2]{1,0:T(8,128)(2,1)}) %reduce-scatter.55.cloned.1.call-update) | async-done | bytes 400
  922.9 36.0 %reduce-scatter.59.cloned.1.call-done = bf16[96,5]{1,0:T(8,128)(2,1)} async-done(((bf16[768,5]{1,0:T(8,128)(2,1)}), bf16[96,5]{1,0:T(8,128)(2,1)}) %reduce-scatter.59.cloned.1.call-update) | async-done | bytes 976
  959.8 11.8 all-reduce.5
  973.4 42.9 %reduce-scatter.53.cloned.1.call-done = bf16[1,384,768]{2,1,0:T(8,128)(2,1)} async-done(((bf16[1,3072,768]{2,1,0:T(8,128)(2,1)}), bf16[1,384,768]{2,1,0:T(8,128)(2,1)}) %reduce-scatter.53.cloned.1.call-update) | async-done | bytes 589840 | tf_op jit(solution)/shard_map/reduce_scatter | solution.py:357
  1016.3 57.6 %reduce-scatter.51.cloned.1.call-done = bf16[1,384,768]{2,1,0:T(8,128)(2,1)} async-done(((bf16[1,3072,768]{2,1,0:T(8,128)(2,1)}), bf16[1,384,768]{2,1,0:T(8,128)(2,1)}) %reduce-scatter.51.cloned.1.call-update) | async-done | bytes 589840 | tf_op jit(solution)/shard_map/reduce_scatter | solution.py:357
  1076.7 54.6 %reduce-scatter.49.cloned.1.call-done = bf16[1,96,3072]{2,1,0:T(8,128)(2,1)} async-done(((bf16[1,768,3072]{2,1,0:T(8,128)(2,1)}), bf16[1,96,3072]{2,1,0:T(8,128)(2,1)}) %reduce-scatter.49.cloned.1.call-update) | async-done | bytes 589840 | tf_op jit(solution)/shard_map/reduce_scatter | solution.py:354
  1131.3 57.6 %reduce-scatter.47.cloned.1.call-done = bf16[1,96,3072]{2,1,0:T(8,128)(2,1)} async-done(((bf16[1,768,3072]{2,1,0:T(8,128)(2,1)}), bf16[1,96,3072]{2,1,0:T(8,128)(2,1)}) %reduce-scatter.47.cloned.1.call-update) | async-done | bytes 589840 | tf_op jit(solution)/shard_map/reduce_scatter | solution.py:354
  1191.7 56.7 %all-reduce.9.cloned.1.call-done = (bf16[1,96,2304]{2,1,0:T(8,128)(2,1)}, bf16[1,96,2304]{2,1,0:T(8,128)(2,1)}, bf16[1,96,768]{2,1,0:T(8,128)(2,1)}, bf16[1,96,768]{2,1,0:T(8,128)(2,1)}) async-done(((bf16[1,96,2304]{2,1,0:T(8,128)(2,1)}, bf16[1,96,2304]{2,1,0:T(8,128)(2,1)}, bf16[1,96,768]{2,1,0:T(8,128)(2,1)}, bf16[1,96,768]{2,1,0:T(8,128)(2,1)}), (bf16[1,96,2304]{2,1,0:T(8,128)(2,1)}, ...) | async-done | bytes 1179664 | tf_op jit(solution)/shard_map/psum | solution.py:347
  (615 shorter events, 386.0 us)
Async XLA Ops:
  7.2 104.6 %all-gather.27.cloned.1.call-start = ((), (), s32[]{:S(2)}) async-start(), calls=%async_computation.34 | async-start | bytes 3981312 | tf_op jit(solution)/shard_map/all_gather | solution.py:71
  9.5 108.7 %all-gather.29.cloned.1.call-start = ((), (), s32[]{:S(2)}) async-start(), calls=%async_computation.35 | async-start | bytes 1327104 | tf_op jit(solution)/shard_map/all_gather | solution.py:72
  11.3 172.1 %all-gather.31.cloned.1.call-start = ((), (), s32[]{:S(2)}) async-start(), calls=%async_computation.36 | async-start | bytes 5308416 | tf_op jit(solution)/shard_map/all_gather | solution.py:91
  12.6 177.9 %all-gather.33.cloned.1.call-start = ((), (), s32[]{:S(2)}) async-start(), calls=%async_computation.37 | async-start | bytes 5308416 | tf_op jit(solution)/shard_map/all_gather | solution.py:92
  13.7 211.8 %all-gather.35.cloned.1.call-start = ((), (), s32[]{:S(2)}) async-start(), calls=%async_computation.38 | async-start | bytes 3981312 | tf_op jit(solution)/shard_map/all_gather | solution.py:71
  14.3 220.3 %all-gather.37.cloned.1.call-start = ((), (), s32[]{:S(2)}) async-start(), calls=%async_computation.39 | async-start | bytes 1327104 | tf_op jit(solution)/shard_map/all_gather | solution.py:72
  14.9 247.8 %all-gather.39.cloned.1.call-start = ((), (), s32[]{:S(2)}) async-start(), calls=%async_computation.40 | async-start | bytes 5308416 | tf_op jit(solution)/shard_map/all_gather | solution.py:91
  15.6 288.5 %all-gather.41.cloned.1.call-start = ((), (), s32[]{:S(2)}) async-start(), calls=%async_computation.41 | async-start | bytes 5308416 | tf_op jit(solution)/shard_map/all_gather | solution.py:92
  123.9 59.5 %all-to-all-start = ((bf16[4,1,98,768]{3,2,1,0:T(8,128)(2,1)}), bf16[4,1,98,768]{3,2,1,0:T(8,128)(2,1)S(1)}, u32[]{:S(2)}, u32[]{:S(2)}) async-start(bf16[4,1,98,768]{3,2,1,0:T(8,128)(2,1)} %select_bitcast_fusion.1), calls=%async_computation | async-start | bytes 1277952 | tf_op jit(solution)/shard_map/all_to_all | solution.py:153
  198.6 22.4 %all-to-all-start.1 = ((bf16[4,1,98,768]{3,2,1,0:T(8,128)(2,1)}), bf16[4,1,98,768]{3,2,1,0:T(8,128)(2,1)S(1)}, u32[]{:S(2)}, u32[]{:S(2)}) async-start(bf16[4,1,98,768]{3,2,1,0:T(8,128)(2,1)} %fusion.118), calls=%async_computation.1 | async-start | bytes 1277952 | tf_op jit(solution)/shard_map/all_to_all | solution.py:163
  312.3 24.1 %all-to-all-start.3 = ((bf16[4,1,98,768]{3,2,1,0:T(8,128)(2,1)}), bf16[4,1,98,768]{3,2,1,0:T(8,128)(2,1)}, u32[]{:S(2)}, u32[]{:S(2)}) async-start(bf16[4,1,98,768]{3,2,1,0:T(8,128)(2,1)} %fusion.123), calls=%async_computation.3 | async-start | bytes 1277952 | tf_op jit(solution)/shard_map/all_to_all | solution.py:163
  361.2 22.7 %all-to-all-start.4 = ((bf16[4,1,98,768]{3,2,1,0:T(8,128)(2,1)}), bf16[4,1,98,768]{3,2,1,0:T(8,128)(2,1)}, u32[]{:S(2)}, u32[]{:S(2)}) async-start(bf16[4,1,98,768]{3,2,1,0:T(8,128)(2,1)} %fusion.140), calls=%async_computation.4 | async-start | bytes 1277952 | tf_op jit(solution)/shard_map/all_to_all | solution.py:222
  398.5 20.9 %all-to-all-start.5 = ((bf16[4,1,98,768]{3,2,1,0:T(8,128)(2,1)}), bf16[4,1,98,768]{3,2,1,0:T(8,128)(2,1)}, u32[]{:S(2)}, u32[]{:S(2)}) async-start(bf16[4,1,98,768]{3,2,1,0:T(8,128)(2,1)} %fusion.113), calls=%async_computation.5 | async-start | bytes 1277952 | tf_op jit(solution)/shard_map/all_to_all | solution.py:233
  402.7 167.4 %reduce-scatter.65.cloned.1.call-start = ((), (), s32[]{:S(2)}) async-start(), calls=%async_computation.47 | async-start | bytes 221184
  404.2 166.6 %reduce-scatter.73.cloned.1.call-start = ((), (), s32[]{:S(2)}) async-start(), calls=%async_computation.51 | async-start | bytes 221184
  410.4 161.3 %reduce-scatter.69.cloned.1.call-start = ((), (), s32[]{:S(2)}) async-start(), calls=%async_computation.49 | async-start | bytes 884736
  455.4 117.3 %reduce-scatter.57.cloned.1.call-start = ((), (), s32[]{:S(2)}) async-start(), calls=%async_computation.43 | async-start | bytes 221184
  456.4 132.4 %reduce-scatter.63.cloned.1.call-start = ((), (), s32[]{:S(2)}) async-start(), calls=%async_computation.46 | async-start | bytes 221184
  458.3 167.0 %reduce-scatter.61.cloned.1.call-start = ((), (), s32[]{:S(2)}) async-start(), calls=%async_computation.45 | async-start | bytes 221184
  491.5 170.6 %reduce-scatter.71.cloned.1.call-start = ((), (), s32[]{:S(2)}) async-start(), calls=%async_computation.50 | async-start | bytes 221184
  492.5 208.1 %reduce-scatter.67.cloned.1.call-start = ((), (), s32[]{:S(2)}) async-start(), calls=%async_computation.48 | async-start | bytes 884736
  494.0 247.2 %reduce-scatter.45.cloned.1.call-start = ((), (), s32[]{:S(2)}) async-start(), calls=%async_computation.29 | async-start | bytes 1327104 | tf_op jit(solution)/shard_map/reduce_scatter | solution.py:333
  495.5 286.4 %reduce-scatter.43.cloned.1.call-start = ((), (), s32[]{:S(2)}) async-start(), calls=%async_computation.28 | async-start | bytes 1327104 | tf_op jit(solution)/shard_map/reduce_scatter | solution.py:333
  518.2 315.4 %reduce-scatter.41.cloned.1.call-start = ((), (), s32[]{:S(2)}) async-start(), calls=%async_computation.27 | async-start | bytes 3981312 | tf_op jit(solution)/shard_map/reduce_scatter | solution.py:330
  521.8 363.2 %reduce-scatter.39.cloned.1.call-start = ((), (), s32[]{:S(2)}) async-start(), calls=%async_computation.26 | async-start | bytes 3981312 | tf_op jit(solution)/shard_map/reduce_scatter | solution.py:330
  533.2 388.9 %reduce-scatter.55.cloned.1.call-start = ((), (), s32[]{:S(2)}) async-start(), calls=%async_computation.42 | async-start | bytes 221184
  537.6 421.3 %reduce-scatter.59.cloned.1.call-start = ((), (), s32[]{:S(2)}) async-start(), calls=%async_computation.44 | async-start | bytes 221184
  538.8 477.5 %reduce-scatter.53.cloned.1.call-start = ((), (), s32[]{:S(2)}) async-start(), calls=%async_computation.33 | async-start | bytes 5308416 | tf_op jit(solution)/shard_map/reduce_scatter | solution.py:357
  547.0 526.9 %reduce-scatter.51.cloned.1.call-start = ((), (), s32[]{:S(2)}) async-start(), calls=%async_computation.32 | async-start | bytes 5308416 | tf_op jit(solution)/shard_map/reduce_scatter | solution.py:357
  556.1 575.2 %reduce-scatter.49.cloned.1.call-start = ((), (), s32[]{:S(2)}) async-start(), calls=%async_computation.31 | async-start | bytes 5308416 | tf_op jit(solution)/shard_map/reduce_scatter | solution.py:354
  562.9 626.0 %reduce-scatter.47.cloned.1.call-start = ((), (), s32[]{:S(2)}) async-start(), calls=%async_computation.30 | async-start | bytes 5308416 | tf_op jit(solution)/shard_map/reduce_scatter | solution.py:354
  570.0 678.4 %all-reduce.9.cloned.1.call-start = ((), (), s32[]{:S(2)}) async-start(), calls=%async_computation.52 | async-start | bytes 2359296 | tf_op jit(solution)/shard_map/psum | solution.py:347
  (125 other events, 1843.1 us)
Sparse Core Ops, SparseCore 0:
  10.5 36.6 all-gather.26
  49.6 25.0 all-gather.28
  77.2 39.4 all-gather.30
  119.0 39.0 all-gather.32
  160.4 35.5 all-gather.34
  197.8 24.0 all-gather.36
  223.8 38.9 all-gather.38
  265.2 38.9 all-gather.40
  406.5 33.9 reduce-scatter.64
  443.7 33.5 reduce-scatter.72
  480.5 34.9 reduce-scatter.68
  518.4 33.5 reduce-scatter.56
  555.3 33.5 reduce-scatter.62
  591.8 33.5 reduce-scatter.60
  628.5 33.5 reduce-scatter.70
  665.7 34.9 reduce-scatter.66
  704.3 36.7 reduce-scatter.44
  745.2 36.7 reduce-scatter.42
  785.5 48.0 reduce-scatter.40
  836.9 48.0 reduce-scatter.38
  888.6 33.4 reduce-scatter.54
  925.4 33.4 reduce-scatter.58
  962.4 53.8 reduce-scatter.52
  1020.0 53.8 reduce-scatter.50
  1077.3 53.8 reduce-scatter.48
  1135.0 53.8 reduce-scatter.46
  1191.4 56.9 all-reduce.8
where the time goes:
time: 1270 us; the launch traced here: 1260 us
  waiting for transfers between devices  746 us (59%)
  local copies, waits for them, and re-layouts  178 us (14%)
  matrix products  131 us (10%)
  blocking collectives  104 us (8%)
  other arithmetic  45.7 us (4%)
  starting transfers between devices  37.6 us (3%)
  between operations  17.7 us (1%)
    unnamed x37, waiting for transfers between devices  199 us
    reduce_scatter x2, waiting for transfers between devices, per_device(): lax.psum_scatter(local_expert[0].astype(jnp.bfloat16), 'dp', scatter_dime...  112 us
    reduce_scatter x2, waiting for transfers between devices, per_device(): lax.psum_scatter(local_attn[0].astype(jnp.bfloat16), 'dp', scatter_dimens...  103 us
    reduce_scatter x2, waiting for transfers between devices, per_device(): lax.psum_scatter(local_expert[1].astype(jnp.bfloat16), 'dp', scatter_dime...  101 us
    reduce_scatter x2, waiting for transfers between devices, per_device(): lax.psum_scatter(local_attn[1].astype(jnp.bfloat16), 'dp', scatter_dimens...  79.7 us
    psum x1, waiting for transfers between devices, per_device(): lax.psum(shares[0].astype(jnp.bfloat16), 'expert').astype(jnp.float32)  56.7 us
    unnamed x278, local copies, waits for them, and re-layouts  32.7 us
    all_gather x2, waiting for transfers between devices, fetch_experts(): lax.all_gather(wide_oe, 'dp', axis=1, tiled=True)  32 us
  transfers between devices with their start and end apart: 35, of which 23 were waited for; matrix products, arithmetic and copies ran while one was open for 23% of the time, Pallas kernels for 0%

commit v1 on v0

v1 whole, which is shorter than its diff:
```python
import functools

import jax
import jax.numpy as jnp
from jax import lax
from jax.experimental import pallas as pl
from jax.experimental.pallas import tpu as pltpu
from jax.sharding import PartitionSpec as P

HEADS = 12
HEAD_DIM = 64
SEQ = 197
EPS = 1e-06
BF = jnp.bfloat16
F32 = jnp.float32
LANES = 128
NEG = -1e30
VMEM_LIMIT = 60 * 1024 * 1024


def up(value, step):
    return -(-value // step) * step


def dot(left, right):
    return lax.dot_general(left, right, (((1,), (0,)), ((), ())), preferred_element_type=F32)


def dot_nt(left, right):
    return lax.dot_general(left, right, (((1,), (1,)), ((), ())), preferred_element_type=F32)


def dot_tn(left, right):
    return lax.dot_general(left, right, (((0,), (0,)), ((), ())), preferred_element_type=F32)


def norm_rows(x):
    centered = x - jnp.mean(x, -1, keepdims=True)
    rstd = lax.rsqrt(jnp.mean(centered * centered, -1, keepdims=True) + EPS)
    return centered * rstd, rstd


def norm_back(grad_hat, normed, rstd):
    return rstd * (
        grad_hat
        - jnp.mean(grad_hat, -1, keepdims=True)
        - normed * jnp.mean(grad_hat * normed, -1, keepdims=True)
    )


def split(value):
    high = value.astype(BF)
    return high, (value - high.astype(F32)).astype(BF)


def join(refs):
    return jnp.concatenate([ref[...].astype(F32) for ref in refs], 0).astype(BF)


def part(value, refs):
    rows = refs[0].shape[0]
    for number, ref in enumerate(refs):
        ref[...] = value[number * rows : (number + 1) * rows].astype(ref.dtype)


def seat_mask(cols_ref, pair, seats):
    column = cols_ref[:, pair : pair + 1]
    return lax.broadcasted_iota(jnp.int32, (column.shape[0], seats), 1) == column


def token_mask(rows_ref, pair, seats):
    row = rows_ref[pair : pair + 1, :]
    return lax.broadcasted_iota(jnp.int32, (seats, row.shape[1]), 0) == row


def one(mask):
    return jnp.where(mask, 1.0, 0.0).astype(BF)


def pair_gate(gates, cols_ref, pair):
    route = cols_ref[:, 2 + pair : 3 + pair]
    lanes = lax.broadcasted_iota(jnp.int32, gates.shape, 1)
    return jnp.sum(jnp.where(lanes == route, gates, 0.0), -1, keepdims=True)


def combine(x1, gates, cols_ref, returned):
    total = x1
    for pair in range(2):
        piece = dot(one(seat_mask(cols_ref, pair, returned.shape[0])), returned)
        total = total + pair_gate(gates, cols_ref, pair) * piece
    return total


def seat_grads(grad, gates, cols_ref, rows_ref, seats):
    total = None
    for pair in range(2):
        scaled = (pair_gate(gates, cols_ref, pair) * grad).astype(BF)
        piece = dot(one(token_mask(rows_ref, pair, seats)), scaled)
        total = piece if total is None else total + piece
    return total


def head_masks():
    lanes = lax.broadcasted_iota(jnp.int32, (1, 2 * HEAD_DIM), 1)
    return (lanes < HEAD_DIM, lanes >= HEAD_DIM)


def head_probs(query, keys, mask, tokens):
    query = jnp.where(mask, query, 0).astype(F32) * HEAD_DIM ** (-0.5)
    scores = dot_nt(query.astype(BF), keys)
    lanes = lax.broadcasted_iota(jnp.int32, scores.shape, 1)
    scores = jnp.where(lanes < tokens, scores, NEG)
    raised = jnp.exp(scores - jnp.max(scores, -1, keepdims=True))
    return raised * (1.0 / jnp.sum(raised, -1, keepdims=True))


class Blocks:
    def __init__(self, arrays, offsets):
        self.arrays, self.offsets = arrays, offsets


def fetch_plan(refs, offsets, me, targets, sems, first):
    copies = []
    number = first
    for ref, offs in zip(refs, offsets):
        rows = ref.shape[1]
        for k, off in enumerate(offs):
            place = 0 if off is None else pl.multiple_of((me ^ off) * rows, rows)
            for scratch, start, width, into in targets:
                copies.append(
                    pltpu.make_async_copy(
                        ref.at[k, :, pl.ds(start, width)],
                        scratch.at[pl.ds(place, rows), pl.ds(into, width)],
                        sems.at[number],
                    )
                )
                number += 1
    return copies


def spread_plan(scratch, outs, offsets, me, sems, first, columns):
    copies = []
    number = first
    start, width = columns
    for out, offs in zip(outs, offsets):
        rows = out.shape[1]
        for k, off in enumerate(offs):
            place = 0 if off is None else pl.multiple_of((me ^ off) * rows, rows)
            copies.append(
                pltpu.make_async_copy(
                    scratch.at[pl.ds(place, rows), pl.ds(start, width)],
                    out.at[k],
                    sems.at[number],
                )
            )
            number += 1
    return copies


def count(offsets):
    return sum(len(offs) for offs in offsets)


VM = pl.BlockSpec(memory_space=pltpu.VMEM)
ANY = pl.BlockSpec(memory_space=pl.ANY)
SM = pl.BlockSpec(memory_space=pltpu.SMEM)


def call(kernel, name, args, specs, outs, out_specs, scratch, flops, moved):
    return pl.pallas_call(
        kernel,
        name=name,
        in_specs=specs,
        out_specs=out_specs,
        out_shape=outs,
        scratch_shapes=scratch,
        compiler_params=pltpu.CompilerParams(vmem_limit_bytes=VMEM_LIMIT),
        cost_estimate=pl.CostEstimate(flops=flops, bytes_accessed=moved, transcendentals=0),
    )(*args)


def sds(shape, dtype):
    return jax.ShapeDtypeStruct(shape, dtype)


def attn_fwd(me, first, x_args, a_blocks, b_blocks, vecs, router, noise, cols, rows, tokens, cap_pad):
    padded, width = noise.shape[0], vecs.shape[1]
    owners = len(x_args[3]) if not first else None
    experts = noise_experts = cap_pad[1]
    cap = cap_pad[0]
    seats = experts * cap
    na, nb = len(a_blocks.arrays), len(b_blocks.arrays)
    half = 2 * width
    total = count(a_blocks.offsets) + 2 * count(b_blocks.offsets)

    def kernel(*refs):
        refs = list(refs)
        me_ref = refs.pop(0)
        if first:
            tok_ref = refs.pop(0)
        else:
            below_x1, below_gates, below_cols = refs.pop(0), refs.pop(0), refs.pop(0)
            below_blocks = [refs.pop(0) for _ in range(owners)]
        a_refs = [refs.pop(0) for _ in range(na)]
        b_refs = [refs.pop(0) for _ in range(nb)]
        vec_ref, router_ref, noise_ref, cols_ref, rows_ref = (refs.pop(0) for _ in range(5))
        x_out, x1_out, a_out, qkv_out, o_out, gates_out, m_out = (refs.pop(0) for _ in range(7))
        seat_outs = [refs.pop(0) for _ in range(experts)]
        wqkv, wout, sems = refs
        index = me_ref[0]
        copies_a = fetch_plan(a_refs, a_blocks.offsets, index, [(wqkv, 0, half, 0)], sems, 0)
        copies_b = fetch_plan(
            b_refs,
            b_blocks.offsets,
            index,
            [(wqkv, 0, width, half), (wout, width, width, 0)],
            sems,
            len(copies_a),
        )
        for copy in copies_a + copies_b:
            copy.start()
        vec = lambda k: vec_ref[k : k + 1, :]
        if first:
            x_out[...] = jnp.zeros_like(x_out)
            x_out[0:tokens, :] = tok_ref[...].astype(F32)
            x = x_out[...]
        else:
            x = combine(below_x1[...], below_gates[...], below_cols, join(below_blocks))
            x_out[...] = x
        normed, rstd = norm_rows(x)
        a_low = (normed * vec(0) + vec(2)).astype(BF)
        a_out[...] = a_low
        for copy in copies_a + copies_b:
            copy.wait()
        for k in range(3):
            piece = dot(a_low, wqkv[:, k * width : (k + 1) * width])
            if k == 0:
                piece = piece + vec(4)
            if k == 2:
                piece = piece + vec(5)
            qkv_out[:, k * width : (k + 1) * width] = piece.astype(BF)
        masks = head_masks()
        for two in range(HEADS // 2):
            at = two * 2 * HEAD_DIM
            query = qkv_out[:, at : at + 2 * HEAD_DIM]
            keys = qkv_out[:, width + at : width + at + 2 * HEAD_DIM]
            values = qkv_out[:, 2 * width + at : 2 * width + at + 2 * HEAD_DIM]
            mixed = None
            for mask in masks:
                probs = head_probs(query, keys, mask, tokens).astype(BF)
                piece = dot(probs, jnp.where(mask, values, 0).astype(BF))
                mixed = piece if mixed is None else mixed + piece
            o_out[:, at : at + 2 * HEAD_DIM] = mixed.astype(BF)
        x1 = x + dot(o_out[...], wout[...]) + vec(6)
        x1_out[...] = x1
        normed2, rstd2 = norm_rows(x1)
        moe = normed2 * vec(1) + vec(3)
        high, low = split(moe)
        logits = dot(high, router_ref[...]) + dot(low, router_ref[...]) + noise_ref[...]
        lanes = lax.broadcasted_iota(jnp.int32, logits.shape, 1)
        logits = jnp.where(lanes < experts, logits, NEG)
        raised = jnp.exp(logits - jnp.max(logits, -1, keepdims=True))
        gates_out[...] = raised / jnp.sum(raised, -1, keepdims=True)
        m_out[...] = high
        chosen = jnp.logical_or(token_mask(rows_ref, 0, seats), token_mask(rows_ref, 1, seats))
        part(dot(one(chosen), high), seat_outs)

    args = [me]
    specs = [SM]
    if first:
        args += [x_args[0]]
        specs += [VM]
    else:
        args += [x_args[0], x_args[1], x_args[2], *x_args[3]]
        specs += [VM] * (3 + owners)
    args += [*a_blocks.arrays, *b_blocks.arrays, vecs, router, noise, cols, rows]
    specs += [ANY] * (na + nb) + [VM] * 5
    outs = [
        sds((padded, width), F32),
        sds((padded, width), F32),
        sds((padded, width), BF),
        sds((padded, 3 * width), BF),
        sds((padded, width), BF),
        sds((padded, LANES), F32),
        sds((padded, width), BF),
    ] + [sds((cap, width), BF)] * experts
    result = call(
        kernel,
        "attn_fwd",
        args,
        specs,
        outs,
        [VM] * len(outs),
        [
            pltpu.VMEM((width, 3 * width), BF),
            pltpu.VMEM((width, width), BF),
            pltpu.SemaphoreType.DMA((total,)),
        ],
        flops=4 * 2 * padded * width * width * 4,
        moved=20 << 20,
    )
    return result[:7], result[7:]


def expert_fwd(me, seat_blocks, in_blocks, oe_blocks, bias_in, bias_oe):
    owners = len(seat_blocks)
    cap, width = seat_blocks[0].shape
    seats = owners * cap
    hidden = bias_in.shape[1]
    ni, no = len(in_blocks.arrays), len(oe_blocks.arrays)
    total = count(in_blocks.offsets) + count(oe_blocks.offsets)
    step = width

    def kernel(*refs):
        refs = list(refs)
        me_ref = refs.pop(0)
        seat_refs = [refs.pop(0) for _ in range(owners)]
        in_refs = [refs.pop(0) for _ in range(ni)]
        oe_refs = [refs.pop(0) for _ in range(no)]
        bin_ref, boe_ref = refs.pop(0), refs.pop(0)
        rows_out, h_out, slope_out = refs.pop(0), refs.pop(0), refs.pop(0)
        outs = [refs.pop(0) for _ in range(owners)]
        win, woe, sems = refs
        index = me_ref[0]
        copies_in = fetch_plan(in_refs, in_blocks.offsets, index, [(win, 0, hidden, 0)], sems, 0)
        copies_oe = fetch_plan(
            oe_refs, oe_blocks.offsets, index, [(woe, 0, width, 0)], sems, len(copies_in)
        )
        for copy in copies_in + copies_oe:
            copy.start()
        rows = join(seat_refs)
        rows_out[...] = rows
        for copy in copies_in:
            copy.wait()
        total_out = None
        for at in range(0, hidden, step):
            pre = dot(rows, win[:, at : at + step]) + bin_ref[:, at : at + step]
            square = pre * pre
            bend = jnp.tanh(0.7978845608028654 * (pre + 0.044715 * square * pre))
            h = (0.5 * pre * (1.0 + bend)).astype(BF)
            slope = 0.5 * (1.0 + bend) + 0.5 * pre * (1.0 - bend * bend) * (
                0.7978845608028654 * (1.0 + 0.134145 * square)
            )
            h_out[:, at : at + step] = h
            slope_out[:, at : at + step] = slope.astype(BF)
            if at == 0:
                for copy in copies_oe:
                    copy.wait()
            piece = dot(h, woe[at : at + step, :])
            total_out = piece if total_out is None else total_out + piece
        part(total_out + boe_ref[...], outs)

    shapes = [
        sds((seats, width), BF),
        sds((seats, hidden), BF),
        sds((seats, hidden), BF),
    ] + [sds((cap, width), BF)] * owners
    result = call(
        kernel,
        "expert_fwd",
        [me, *seat_blocks, *in_blocks.arrays, *oe_blocks.arrays, bias_in, bias_oe],
        [SM] + [VM] * owners + [ANY] * (ni + no) + [VM] * 2,
        shapes,
        [VM] * len(shapes),
        [
            pltpu.VMEM((width, hidden), BF),
            pltpu.VMEM((hidden, width), BF),
            pltpu.SemaphoreType.DMA((total,)),
        ],
        flops=8 * seats * width * hidden,
        moved=20 << 20,
    )
    return result[:3], result[3:]


def top_seats(cotangent, gates, cols, rows, seats, tokens, experts):
    padded, width = cols.shape[0], cotangent.shape[1]

    def kernel(cot_ref, gates_ref, cols_ref, rows_ref, grad_out, *outs):
        grad_out[...] = jnp.zeros_like(grad_out)
        grad_out[0:tokens, :] = cot_ref[...].astype(F32)
        part(seat_grads(grad_out[...], gates_ref[...], cols_ref, rows_ref, seats), outs)

    shapes = [sds((padded, width), F32)] + [sds((seats // experts, width), BF)] * experts
    result = call(
        kernel,
        "top_seats",
        [cotangent, gates, cols, rows],
        [VM] * 4,
        shapes,
        [VM] * len(shapes),
        [],
        flops=4 * seats * padded * width,
        moved=4 << 20,
    )
    return result[0], result[1:]


def gate_back(grad, x1, gates, cols, router, returned, tokens, last):
    padded, width = grad.shape
    owners = len(returned)

    def kernel(*refs):
        refs = list(refs)
        grad_ref = refs.pop(0)
        x1_ref = refs.pop(0) if last else None
        gates_ref, cols_ref, router_ref = (refs.pop(0) for _ in range(3))
        blocks = [refs.pop(0) for _ in range(owners)]
        dz_out, moe_out = refs.pop(0), refs.pop(0)
        back = join(blocks)
        grad_here = grad_ref[...]
        gates_here = gates_ref[...]
        lanes = lax.broadcasted_iota(jnp.int32, gates_here.shape, 1)
        d_gates = jnp.zeros_like(gates_here)
        mixed = x1_ref[...] if last else None
        for pair in range(2):
            piece = dot(one(seat_mask(cols_ref, pair, back.shape[0])), back)
            if last:
                mixed = mixed + pair_gate(gates_here, cols_ref, pair) * piece
            d_pair = jnp.sum(grad_here * piece, -1, keepdims=True)
            d_gates = d_gates + jnp.where(lanes == cols_ref[:, 2 + pair : 3 + pair], d_pair, 0.0)
        dz = gates_here * (d_gates - jnp.sum(d_gates * gates_here, -1, keepdims=True))
        dz_out[...] = dz
        high, low = split(dz)
        moe_out[...] = dot_nt(high, router_ref[...]) + dot_nt(low, router_ref[...])
        if last:
            refs.pop(0)[...] = mixed[0:tokens, :]

    shapes = [sds((padded, LANES), F32), sds((padded, width), F32)]
    if last:
        shapes.append(sds((tokens, width), F32))
    return call(
        kernel,
        "gate_back",
        [grad] + ([x1] if last else []) + [gates, cols, router, *returned],
        [VM] * (4 + owners + int(last)),
        shapes,
        [VM] * len(shapes),
        [],
        flops=6 * padded * width * 512,
        moved=5 << 20,
    )


def expert_back(me, grad_blocks, slope, in_blocks, oe_blocks):
    owners = len(grad_blocks)
    cap, width = grad_blocks[0].shape
    seats, hidden = slope.shape
    ni, no = len(in_blocks.arrays), len(oe_blocks.arrays)
    total = count(in_blocks.offsets) + count(oe_blocks.offsets)
    step = width

    def kernel(*refs):
        refs = list(refs)
        me_ref = refs.pop(0)
        seat_refs = [refs.pop(0) for _ in range(owners)]
        slope_ref = refs.pop(0)
        in_refs = [refs.pop(0) for _ in range(ni)]
        oe_refs = [refs.pop(0) for _ in range(no)]
        grad_out, pre_out = refs.pop(0), refs.pop(0)
        outs = [refs.pop(0) for _ in range(owners)]
        win, woe, sems = refs
        index = me_ref[0]
        copies_oe = fetch_plan(oe_refs, oe_blocks.offsets, index, [(woe, 0, width, 0)], sems, 0)
        copies_in = fetch_plan(
            in_refs, in_blocks.offsets, index, [(win, 0, hidden, 0)], sems, len(copies_oe)
        )
        for copy in copies_oe + copies_in:
            copy.start()
        grad = join(seat_refs)
        grad_out[...] = grad
        for copy in copies_oe:
            copy.wait()
        total_out = None
        for at in range(0, hidden, step):
            d_hidden = dot_nt(grad, woe[at : at + step, :])
            d_pre = (d_hidden * slope_ref[:, at : at + step].astype(F32)).astype(BF)
            pre_out[:, at : at + step] = d_pre
            if at == 0:
                for copy in copies_in:
                    copy.wait()
            piece = dot_nt(d_pre, win[:, at : at + step])
            total_out = piece if total_out is None else total_out + piece
        part(total_out, outs)

    shapes = [sds((seats, width), BF), sds((seats, hidden), BF)]
    shapes += [sds((cap, width), BF)] * owners
    result = call(
        kernel,
        "expert_back",
        [me, *grad_blocks, slope, *in_blocks.arrays, *oe_blocks.arrays],
        [SM] + [VM] * (owners + 1) + [ANY] * (ni + no),
        shapes,
        [VM] * len(shapes),
        [
            pltpu.VMEM((width, hidden), BF),
            pltpu.VMEM((hidden, width), BF),
            pltpu.SemaphoreType.DMA((total,)),
        ],
        flops=8 * seats * width * hidden,
        moved=20 << 20,
    )
    return result[0], result[1], result[2:]


def expert_grads(me, rows, h, grad, d_pre, plan_in, plan_oe):
    seats, width = rows.shape
    hidden = h.shape[1]
    total = count([offs for _, offs in plan_in]) + count([offs for _, offs in plan_oe])

    def kernel(me_ref, rows_ref, h_ref, grad_ref, pre_ref, *refs):
        refs = list(refs)
        in_outs = [refs.pop(0) for _ in plan_in]
        oe_outs = [refs.pop(0) for _ in plan_oe]
        bin_out, boe_out = refs.pop(0), refs.pop(0)
        win, woe, sems = refs
        index = me_ref[0]
        step = width
        for at in range(0, hidden, step):
            woe[at : at + step, :] = dot_tn(h_ref[:, at : at + step], grad_ref[...]).astype(BF)
        copies_oe = spread_plan(
            woe, oe_outs, [offs for _, offs in plan_oe], index, sems, 0, (0, width)
        )
        for copy in copies_oe:
            copy.start()
        for at in range(0, hidden, step):
            win[:, at : at + step] = dot_tn(rows_ref[...], pre_ref[:, at : at + step]).astype(BF)
        copies_in = spread_plan(
            win, in_outs, [offs for _, offs in plan_in], index, sems, len(copies_oe), (0, hidden)
        )
        for copy in copies_in:
            copy.start()
        bin_out[...] = jnp.sum(pre_ref[...].astype(F32), 0, keepdims=True)
        boe_out[...] = jnp.sum(grad_ref[...].astype(F32), 0, keepdims=True)
        for copy in copies_oe + copies_in:
            copy.wait()

    shapes = [sds(shape, BF) for shape, _ in plan_in] + [sds(shape, BF) for shape, _ in plan_oe]
    shapes += [sds((1, hidden), F32), sds((1, width), F32)]
    result = call(
        kernel,
        "expert_grads",
        [me, rows, h, grad, d_pre],
        [SM] + [VM] * 4,
        shapes,
        [ANY] * (len(plan_in) + len(plan_oe)) + [VM] * 2,
        [
            pltpu.VMEM((width, hidden), BF),
            pltpu.VMEM((hidden, width), BF),
            pltpu.SemaphoreType.DMA((total,)),
        ],
        flops=8 * seats * width * hidden,
        moved=20 << 20,
    )
    cut = len(plan_in)
    more = cut + len(plan_oe)
    return result[:cut], result[cut:more], result[more], result[more + 1]


def attn_back(me, back_blocks, moe_part, grad, x, x1, qkv, cols, vecs, a_blocks, b_blocks, below, tokens):
    padded, width = grad.shape
    owners = len(back_blocks)
    cap = back_blocks[0].shape[0]
    seats = owners * cap
    na, nb = len(a_blocks.arrays), len(b_blocks.arrays)
    half = 2 * width
    total = count(a_blocks.offsets) + 2 * count(b_blocks.offsets)

    def kernel(*refs):
        refs = list(refs)
        me_ref = refs.pop(0)
        back_refs = [refs.pop(0) for _ in range(owners)]
        part_ref, grad_ref, x_ref, x1_ref, qkv_ref, cols_ref, vec_ref = (
            refs.pop(0) for _ in range(7)
        )
        a_refs = [refs.pop(0) for _ in range(na)]
        b_refs = [refs.pop(0) for _ in range(nb)]
        if below is not None:
            gates_ref, below_cols, below_rows = (refs.pop(0) for _ in range(3))
        dx_out, dy_out, dqkv_out, small_out = (refs.pop(0) for _ in range(4))
        seat_outs = [refs.pop(0) for _ in range(owners)] if below is not None else None
        wqkv, wout, sems = refs
        index = me_ref[0]
        copies_b = fetch_plan(
            b_refs,
            b_blocks.offsets,
            index,
            [(wqkv, 0, width, half), (wout, width, width, 0)],
            sems,
            0,
        )
        copies_a = fetch_plan(
            a_refs, a_blocks.offsets, index, [(wqkv, 0, half, 0)], sems, len(copies_b)
        )
        for copy in copies_b + copies_a:
            copy.start()
        vec = lambda k: vec_ref[k : k + 1, :]
        chosen = jnp.logical_or(seat_mask(cols_ref, 0, seats), seat_mask(cols_ref, 1, seats))
        d_moe = dot(one(chosen), join(back_refs)) + part_ref[...]
        normed2, rstd2 = norm_rows(x1_ref[...])
        small_out[...] = jnp.zeros_like(small_out)
        small_out[1:2, :] = jnp.sum(d_moe * normed2, 0, keepdims=True)
        small_out[3:4, :] = jnp.sum(d_moe, 0, keepdims=True)
        d_x1 = grad_ref[...] + norm_back(d_moe * vec(1), normed2, rstd2)
        dy = d_x1.astype(BF)
        dy_out[...] = dy
        small_out[6:7, :] = jnp.sum(dy.astype(F32), 0, keepdims=True)
        for copy in copies_b + copies_a:
            copy.wait()
        d_mixed = dot_nt(dy, wout[...]).astype(BF)
        masks = head_masks()
        scale = HEAD_DIM ** (-0.5)
        for two in range(HEADS // 2):
            at = two * 2 * HEAD_DIM
            query = qkv_ref[:, at : at + 2 * HEAD_DIM]
            keys = qkv_ref[:, width + at : width + at + 2 * HEAD_DIM]
            values = qkv_ref[:, 2 * width + at : 2 * width + at + 2 * HEAD_DIM]
            d_o = d_mixed[:, at : at + 2 * HEAD_DIM]
            sums = None
            for mask in masks:
                probs = head_probs(query, keys, mask, tokens)
                d_here = jnp.where(mask, d_o, 0).astype(BF)
                d_probs = dot_nt(d_here, values)
                d_values = dot_tn(probs.astype(BF), d_here)
                d_scores = probs * (d_probs - jnp.sum(d_probs * probs, -1, keepdims=True))
                d_scores = d_scores.astype(BF)
                d_query = dot(d_scores, jnp.where(mask, keys, 0).astype(BF))
                d_keys = dot_tn(d_scores, jnp.where(mask, query, 0).astype(BF))
                here = (d_query, d_keys, d_values)
                sums = here if sums is None else tuple(s + h for s, h in zip(sums, here))
            dqkv_out[:, at : at + 2 * HEAD_DIM] = (sums[0] * scale).astype(BF)
            dqkv_out[:, width + at : width + at + 2 * HEAD_DIM] = (sums[1] * scale).astype(BF)
            dqkv_out[:, 2 * width + at : 2 * width + at + 2 * HEAD_DIM] = sums[2].astype(BF)
        d_normed = None
        for k in range(3):
            here = dqkv_out[:, k * width : (k + 1) * width]
            if k != 1:
                row = 4 if k == 0 else 5
                small_out[row : row + 1, :] = jnp.sum(here.astype(F32), 0, keepdims=True)
            piece = dot_nt(here, wqkv[:, k * width : (k + 1) * width])
            d_normed = piece if d_normed is None else d_normed + piece
        normed1, rstd1 = norm_rows(x_ref[...])
        small_out[0:1, :] = jnp.sum(d_normed * normed1, 0, keepdims=True)
        small_out[2:3, :] = jnp.sum(d_normed, 0, keepdims=True)
        d_x = d_x1 + norm_back(d_normed * vec(0), normed1, rstd1)
        dx_out[...] = d_x[0 : dx_out.shape[0], :]
        if below is not None:
            part(seat_grads(d_x, gates_ref[...], below_cols, below_rows, seats), seat_outs)

    shapes = [
        sds((padded if below is not None else tokens, width), F32),
        sds((padded, width), BF),
        sds((padded, 3 * width), BF),
        sds((16, width), F32),
    ]
    args = [me, *back_blocks, moe_part, grad, x, x1, qkv, cols, vecs]
    args += [*a_blocks.arrays, *b_blocks.arrays]
    specs = [SM] + [VM] * (owners + 7) + [ANY] * (na + nb)
    if below is not None:
        shapes += [sds((cap, width), BF)] * owners
        args += list(below)
        specs += [VM] * 3
    result = call(
        kernel,
        "attn_back",
        args,
        specs,
        shapes,
        [VM] * len(shapes),
        [
            pltpu.VMEM((width, 3 * width), BF),
            pltpu.VMEM((width, width), BF),
            pltpu.SemaphoreType.DMA((total,)),
        ],
        flops=4 * 2 * padded * width * width * 8,
        moved=25 << 20,
    )
    return result[:4], result[4:]


def attn_grads(me, a_low, o_low, moe_low, dqkv, dy, dz, small, plan_a, plan_b):
    padded, width = a_low.shape
    half = 2 * width
    total = count([offs for _, offs in plan_a]) + count([offs for _, offs in plan_b])

    def kernel(me_ref, a_ref, o_ref, moe_ref, dqkv_ref, dy_ref, dz_ref, small_ref, *refs):
        refs = list(refs)
        a_outs = [refs.pop(0) for _ in plan_a]
        b_outs = [refs.pop(0) for _ in plan_b]
        wide, sems = refs
        index = me_ref[0]
        for k in range(2):
            wide[:, k * width : (k + 1) * width] = dot_tn(
                a_ref[...], dqkv_ref[:, k * width : (k + 1) * width]
            ).astype(BF)
        copies_a = spread_plan(
            wide, a_outs, [offs for _, offs in plan_a], index, sems, 0, (0, half)
        )
        for copy in copies_a:
            copy.start()
        wide[:, half : half + width] = dot_tn(a_ref[...], dqkv_ref[:, half : half + width]).astype(
            BF
        )
        wide[:, half + width : 2 * half] = dot_tn(o_ref[...], dy_ref[...]).astype(BF)
        high, low = split(dz_ref[...])
        d_router = dot_tn(moe_ref[...], high) + dot_tn(moe_ref[...], low)
        rows = jnp.concatenate(
            [jnp.zeros((16, width), F32), small_ref[...], jnp.zeros((LANES - 32, width), F32)], 0
        )
        wide[:, 2 * half : 2 * half + LANES] = (d_router + rows.T).astype(BF)
        copies_b = spread_plan(
            wide,
            b_outs,
            [offs for _, offs in plan_b],
            index,
            sems,
            len(copies_a),
            (half, half + LANES),
        )
        for copy in copies_b:
            copy.start()
        for copy in copies_a + copies_b:
            copy.wait()

    shapes = [sds(shape, BF) for shape, _ in plan_a + plan_b]
    result = call(
        kernel,
        "attn_grads",
        [me, a_low, o_low, moe_low, dqkv, dy, dz, small],
        [SM] + [VM] * 7,
        shapes,
        [ANY] * len(shapes),
        [pltpu.VMEM((width, 2 * half + LANES), BF), pltpu.SemaphoreType.DMA((total,))],
        flops=2 * padded * width * width * 8,
        moved=12 << 20,
    )
    return result[: len(plan_a)], result[len(plan_a) :]


def swap(value, axis, bit):
    size = lax.axis_size(axis)
    return lax.ppermute(value, axis, [(i, i ^ bit) for i in range(size)])


def chip_bits():
    bits = []
    bit = 2
    while bit < lax.axis_size("dp"):
        bits.append(bit)
        bit *= 2
    return bits


def gather(shard, bits):
    held, offsets = shard[None], [0]
    pieces = []
    for number, bit in enumerate(bits):
        other = swap(held, "dp", bit)
        theirs = [off ^ bit for off in offsets]
        if number + 1 < len(bits):
            held = jnp.concatenate([held, other], 0)
            offsets = offsets + theirs
        else:
            pieces += [(held, offsets), (other, theirs)]
    if not bits:
        pieces.append((held, offsets))
    pieces += [(swap(value, "dp", 1), [off ^ 1 for off in offs]) for value, offs in pieces]
    return pieces


def as_blocks(pieces, me):
    rows, width = pieces[0][0].shape[1:]
    if rows % 16 == 0:
        return Blocks([value for value, _ in pieces], [offs for _, offs in pieces])
    full = jnp.zeros((lax.axis_size("dp") * rows, width), BF)
    for value, offs in pieces:
        for k, off in enumerate(offs):
            full = lax.dynamic_update_slice(full, value[k], ((me ^ off) * rows, 0))
    return Blocks([full[None]], [[None]])


def halving_order(bits):
    order = [0]
    for bit in reversed(bits):
        order = order + [off ^ bit for off in order]
    return order


def send_plan(rows, width, bits):
    order = halving_order(bits)
    if rows % 16 == 0:
        mine = [((len(order), rows, width), order)]
        return mine + [((len(order), rows, width), [off ^ 1 for off in order])]
    size = 2 * len(order)
    return [((1, size * rows, width), [None])]


def reduce_shards(arrays, rows, bits, me):
    order = halving_order(bits)
    if len(arrays) == 1:
        whole = arrays[0].reshape((-1, rows) + arrays[0].shape[2:])
        mine = whole[me ^ jnp.array(order, jnp.int32)]
        theirs = whole[me ^ 1 ^ jnp.array(order, jnp.int32)]
    else:
        mine, theirs = arrays
    held = mine.astype(F32) + swap(theirs, "dp", 1).astype(F32)
    for bit in bits:
        low = held.astype(BF)
        half = low.shape[0] // 2
        held = low[:half].astype(F32) + swap(low[half:], "dp", bit).astype(F32)
    return held[0]


def sum_over_experts(value):
    bit = 1
    while bit < lax.axis_size("expert"):
        low = value.astype(BF)
        value = low.astype(F32) + swap(low, "expert", bit).astype(F32)
        bit *= 2
    return value


def exchange(blocks):
    return [blocks[0]] + [swap(blocks[k], "expert", k) for k in range(1, len(blocks))]


def place_pairs(routes, seat_rows, padded, cap, cap_pad):
    layers, tokens, _ = routes.shape
    expert = routes.reshape(layers, 2 * tokens)
    same = expert[:, :, None] == expert[:, None, :]
    ahead = seat_rows[:, :, None] > seat_rows[:, None, :]
    rank = jnp.sum(jnp.logical_and(same, ahead).astype(jnp.int32), 2)
    near = expert ^ lax.axis_index("expert")
    seat = jnp.where(rank < cap, near * cap_pad + rank, -1).reshape(layers, tokens, 2)
    cols = jnp.concatenate([seat, routes], 2)
    cols = jnp.pad(cols, ((0, 0), (0, padded - tokens), (0, 0)), constant_values=-1)
    rows = jnp.transpose(cols, (0, 2, 1))
    return cols, jnp.pad(rows, ((0, 0), (0, 4), (0, 0)), constant_values=-1)


def per_device(
    image_tokens,
    norm_gains,
    biases,
    w_qkv,
    w_out,
    w_router,
    router_noise,
    w_in,
    b_in,
    w_outexp,
    b_expout,
    routes,
    seat_order,
    cotangent,
):
    layers = w_qkv.shape[0]
    tokens, width = image_tokens.shape
    experts = w_router.shape[2]
    dp = lax.axis_size("dp")
    assert tokens == SEQ and experts == lax.axis_size("expert")
    assert width == HEADS * HEAD_DIM
    padded = up(tokens, 16)
    cap = 2 * tokens // experts
    cap_pad = up(cap, 8)
    seats = experts * cap_pad
    shard = w_qkv.shape[1]
    hidden_shard = w_outexp.shape[2]
    index = lax.axis_index("dp")
    me = index.astype(jnp.int32).reshape(1)
    bits = chip_bits()
    back_bits = bits[::-1]

    per = hidden_shard // shard
    small = jnp.concatenate(
        [
            norm_gains,
            biases,
            jnp.transpose(w_router, (0, 2, 1)),
            b_in.reshape(layers, per, shard),
            b_expout.reshape(layers, 1, shard),
        ],
        1,
    )
    small = lax.all_gather(small, "dp", axis=0)
    wide = jnp.transpose(small, (1, 2, 0, 3))
    vecs = wide[:, :7].reshape(layers, 7, width)
    vecs = jnp.pad(vecs, ((0, 0), (0, 1), (0, 0)))
    router = jnp.transpose(wide[:, 7 : 7 + experts].reshape(layers, experts, width), (0, 2, 1))
    router = jnp.pad(router, ((0, 0), (0, 0), (0, LANES - experts))).astype(BF)
    at = 7 + experts
    bias_in = jnp.transpose(wide[:, at : at + per], (0, 2, 1, 3)).reshape(layers, 1, -1)
    bias_oe = wide[:, at + per].reshape(layers, 1, width)

    noise = jnp.pad(
        router_noise, ((0, 0), (0, padded - tokens), (0, LANES - experts))
    )
    cols, rows = place_pairs(routes, seat_order[:, 0], padded, cap, cap_pad)

    attn_blocks, expert_blocks = [], []
    for layer in range(layers):
        left = w_qkv[layer][:, : 2 * width]
        right = jnp.concatenate([w_qkv[layer][:, 2 * width :], w_out[layer]], 1)
        attn_blocks.append(
            (
                as_blocks(gather(left, bits), index),
                as_blocks(gather(right, back_bits), index),
            )
        )
        expert_blocks.append(
            (
                as_blocks(gather(w_in[layer, 0], bits), index),
                as_blocks(gather(w_outexp[layer, 0], back_bits), index),
            )
        )

    saved = []
    x_args = (image_tokens,)
    for layer in range(layers):
        kept, sent = attn_fwd(
            me,
            layer == 0,
            x_args,
            *attn_blocks[layer],
            vecs[layer],
            router[layer],
            noise[layer],
            cols[layer],
            rows[layer],
            tokens,
            (cap_pad, experts),
        )
        held, made = expert_fwd(
            me, exchange(sent), *expert_blocks[layer], bias_in[layer], bias_oe[layer]
        )
        returned = exchange(made)
        saved.append((kept, held, returned))
        x_args = (kept[1], kept[5], cols[layer], returned)

    last = layers - 1
    grad, grad_seats = top_seats(
        cotangent, saved[last][0][5], cols[last], rows[last], seats, tokens, experts
    )
    mixed = None
    grads = [None] * layers
    for layer in reversed(range(layers)):
        (x, x1, a_low, qkv, o_low, gates, moe_low), (seat_rows, h, slope), returned = saved[layer]
        parts = gate_back(
            grad, x1, gates, cols[layer], router[layer], returned, tokens, layer == last
        )
        dz, moe_part = parts[0], parts[1]
        if layer == last:
            mixed = parts[2]
        d_out, d_pre, d_rows = expert_back(
            me, exchange(grad_seats), slope, *expert_blocks[layer]
        )
        d_back = exchange(d_rows)
        below = None
        if layer > 0:
            below = (saved[layer - 1][0][5], cols[layer - 1], rows[layer - 1])
        (grad, dy, dqkv, small_grads), grad_seats = attn_back(
            me,
            d_back,
            moe_part,
            grad,
            x,
            x1,
            qkv,
            cols[layer],
            vecs[layer],
            *attn_blocks[layer],
            below,
            tokens,
        )
        g_in, g_oe, g_bin, g_boe = expert_grads(
            me,
            seat_rows,
            h,
            d_out,
            d_pre,
            send_plan(shard, w_in.shape[3], bits),
            send_plan(hidden_shard, width, back_bits),
        )
        g_left, g_right = attn_grads(
            me,
            a_low,
            o_low,
            moe_low,
            dqkv,
            dy,
            dz,
            small_grads,
            send_plan(shard, 2 * width, bits),
            send_plan(shard, 2 * width + LANES, back_bits),
        )
        sum_in = reduce_shards(g_in, shard, bits, index)
        sum_oe = reduce_shards(g_oe, hidden_shard, back_bits, index)
        sum_left = sum_over_experts(reduce_shards(g_left, shard, bits, index))
        sum_right = sum_over_experts(reduce_shards(g_right, shard, back_bits, index))
        biases_here = jnp.concatenate([g_bin.reshape(dp, -1), g_boe.reshape(dp, -1)], 1)
        grads[layer] = (sum_left, sum_right, sum_in, sum_oe, biases_here)

    expert_small = lax.psum_scatter(
        jnp.stack([item[4] for item in grads], 1), "dp", scatter_dimension=0, tiled=False
    )
    left = jnp.stack([item[0] for item in grads])
    right = jnp.stack([item[1] for item in grads])
    tail = jnp.transpose(right[:, :, 2 * width :], (0, 2, 1))
    return (
        mixed,
        grad,
        tail[:, 16:18],
        tail[:, 18:23],
        jnp.concatenate([left, right[:, :, :width]], 2),
        right[:, :, width : 2 * width],
        jnp.transpose(tail[:, :experts], (0, 2, 1)),
        jnp.stack([item[2] for item in grads])[:, None],
        expert_small[:, None, :hidden_shard],
        jnp.stack([item[3] for item in grads])[:, None],
        expert_small[:, None, hidden_shard:],
    )


def solution(mesh):
    return jax.shard_map(
        per_device,
        mesh=mesh,
        in_specs=(
            P(("dp", "expert"), None),
            P(None, None, "dp"),
            P(None, None, "dp"),
            P(None, "dp", None),
            P(None, "dp", None),
            P(None, "dp", None),
            P(None, ("dp", "expert"), None),
            P(None, "expert", "dp", None),
            P(None, "expert", "dp"),
            P(None, "expert", "dp", None),
            P(None, "expert", "dp"),
            P(None, ("dp", "expert"), None),
            P(None, ("dp", "expert"), None),
            P(("dp", "expert"), None),
        ),
        out_specs=(
            P(("dp", "expert"), None),
            P(("dp", "expert"), None),
            P(None, None, "dp"),
            P(None, None, "dp"),
            P(None, "dp", None),
            P(None, "dp", None),
            P(None, "dp", None),
            P(None, "expert", "dp", None),
            P(None, "expert", "dp"),
            P(None, "expert", "dp", None),
            P(None, "expert", "dp"),
        ),
        check_vma=False,
    )
```

time: 1270 us -> 554 us (0.44)
  waiting for transfers between devices: 746 us -> 201 us
  local copies, waits for them, and re-layouts: 178 us -> 35.9 us
  matrix products: 131 us -> 0 us
  Pallas kernels: 0 us -> 131 us
  blocking collectives: 104 us -> 36.6 us
  starting transfers between devices: 37.6 us -> 95 us
  between operations: 17.7 us -> 2.25 us
    reduce_scatter x8 -> x0, waiting for transfers between devices: 395 us -> none  [the longest x2 112 us: per_device(): lax.psum_scatter(local_expert[0].astype(jnp.bfloat16), 'dp', scatter_dime...]
    ppermute x0 -> x88, waiting for transfers between devices: none -> 201 us  [swap(): return lax.ppermute(value, axis, [(i, i ^ bit) for i in range(size)])]
    unnamed x37 -> x0, waiting for transfers between devices: 199 us -> none
    dot_general x42 -> x0, matrix products: 131 us -> none  [the longest x2 16.2 us: forward_layer(): jnp.einsum('sicf,ifd->sicd', hidden, wide_oe, preferred_element_type=jnp....]
    pallas_call x0 -> x15, Pallas kernels: none -> 131 us  [call(): pl.pallas_call(kernel, name=name, in_specs=specs, out_specs=out_specs, ou...]
    ppermute x0 -> x88, starting transfers between devices: none -> 95 us  [swap(): return lax.ppermute(value, axis, [(i, i ^ bit) for i in range(size)])]
    all_gather x8 -> x1, blocking collectives: 77.9 us -> 13.6 us  [per_device(): small = lax.all_gather(small, 'dp', axis=0)]
    all_to_all x8 -> x0, waiting for transfers between devices: 57.5 us -> none  [the longest x2 25.5 us: backward_layer(): lax.all_to_all(d_rows, 'expert', split_axis=0, concat_axis=0, tiled=True)]
  transfers between devices with their start and end apart: 35 -> 88, of which waited for: 23 -> 30; matrix products, arithmetic and copies ran while one was open for 23% -> 13% of each run, Pallas kernels for 0% -> 24%
where the time goes in v1:
time: 554 us; the launch traced here: 549 us
  waiting for transfers between devices  201 us (36%)
  Pallas kernels  131 us (24%)
  starting transfers between devices  95 us (17%)
  other arithmetic  47.7 us (9%)
  blocking collectives  36.6 us (7%)
  local copies, waits for them, and re-layouts  35.9 us (6%)
    ppermute x88, waiting for transfers between devices, swap(): return lax.ppermute(value, axis, [(i, i ^ bit) for i in range(size)])  201 us
    pallas_call x15, Pallas kernels, call(): pl.pallas_call(kernel, name=name, in_specs=specs, out_specs=out_specs, ou...  131 us
    ppermute x88, starting transfers between devices, swap(): return lax.ppermute(value, axis, [(i, i ^ bit) for i in range(size)])  95 us
    unnamed x1, blocking collectives  22.9 us
    convert_element_type x16, other arithmetic, reduce_shards(): low = held.astype(BF)  16.4 us
    all_gather x1, blocking collectives, per_device(): small = lax.all_gather(small, 'dp', axis=0)  13.6 us
    unnamed x169, local copies, waits for them, and re-layouts  12.6 us
  transfers between devices with their start and end apart: 88, of which 30 were waited for; matrix products, arithmetic and copies ran while one was open for 13% of the time, Pallas kernels for 24%

profile of v1, /device:TPU:0, one launch (start us, length us, event | category | flops | bytes accessed | tf_op | source)
XLA Modules:
  0.0 549.2 jit_solution(9382064460079375534)
XLA Ops:
  12.9 9.2 %fusion.1 = s32[2,394]{0,1:T(8,128)S(1)} fusion(s32[2,394]{1,0:T(2,128)S(1)} %bitcast.115, s32[2,394]{0,1:T(8,128)} %copy.96, s32[2,394]{1,0:T(2,128)S(1)} %eq.15, s32[2,394]{0,1:T(8,128)} %copy.95), kind=kLoop, calls=%fused_computation.17 | loop fusion | flops 1551572 | bytes 15760 | tf_op jit(solution)/shard_map/reduce_sum | solution.py:832
  22.9 13.6 %all-gather = f32[16,16,96]{2,1,0:T(8,128)S(1)} all-gather(f32[2,16,96]{2,1,0:T(8,128)S(1)} %concatenate.48), channel_id=2, replica_groups=mesh['dp'=8,'expert'=4] {'dp'}, dimensions={0}, use_global_device_ids=true | all-gather | bytes 110592 | tf_op jit(solution)/shard_map/all_gather | solution.py:885
  53.2 10.5 %collective-permute-done.33 = bf16[1,96,3072]{2,1,0:T(8,128)(2,1)S(1)} collective-permute-done((bf16[1,96,3072]{2,1,0:T(8,128)(2,1)S(1)}, bf16[1,96,3072]{2,1,0:T(8,128)(2,1)S(1)}, u32[]{:S(2)}, u32[]{:S(2)}) %collective-permute-start.33) | collective-permute-done | bytes 589856 | tf_op jit(solution)/shard_map/ppermute | solution.py:742
  67.4 8.9 %collective-permute-done.5.refs_7_.refs_17_ = bf16[2,96,1536]{2,1,0:T(8,128)(2,1)S(1)} collective-permute-done((bf16[2,96,1536]{2,1,0:T(8,128)(2,1)S(1)}, bf16[2,96,1536]{2,1,0:T(8,128)(2,1)S(1)}, u32[]{:S(2)}, u32[]{:S(2)}) %collective-permute-start.5) | collective-permute-done | bytes 589856 | tf_op jit(solution)/shard_map/ppermute | solution.py:742
  82.6 5.8 %collective-permute-done.27.refs_13_.refs_17_ = bf16[2,96,1536]{2,1,0:T(8,128)(2,1)S(1)} collective-permute-done((bf16[2,96,1536]{2,1,0:T(8,128)(2,1)S(1)}, bf16[2,96,1536]{2,1,0:T(8,128)(2,1)S(1)}, u32[]{:S(2)}, u32[]{:S(2)}) %collective-permute-start.27) | collective-permute-done | bytes 589856 | tf_op jit(solution)/shard_map/ppermute | solution.py:742
  97.5 8.1 %attn_fwd.2 = (f32[208,768]{1,0:T(8,128)}, f32[208,768]{1,0:T(8,128)}, bf16[208,768]{1,0:T(8,128)(2,1)}, bf16[208,2304]{1,0:T(8,128)(2,1)}, bf16[208,768]{1,0:T(...) custom-call(s32[1]{0:T(128)} %bitcast.refs_0_.me_ref, ...), custom_call_target="tpu_custom_call" | custom-call | flops 3925868544 | bytes 20971520 | tf_op jit(solution)/shard_map/attn_fwd/pallas_call | solution.py:170
  109.3 5.5 collective-permute-done.10.refs_4_
  120.7 5.2 collective-permute-done.9.refs_3_
  131.3 21.7 %collective-permute-done.34.refs_6_.refs_7_ = bf16[2,96,3072]{2,1,0:T(8,128)(2,1)} collective-permute-done((bf16[2,96,3072]{2,1,0:T(8,128)(2,1)}, bf16[2,96,3072]{2,1,0:T(8,128)(2,1)}, u32[]{:S(2)}, u32[]{:S(2)}) %collective-permute-start.34) | collective-permute-done | bytes 1179680 | tf_op jit(solution)/shard_map/ppermute | solution.py:742
  154.9 12.5 %expert_fwd.2 = (bf16[416,768]{1,0:T(8,128)(2,1)}, bf16[416,3072]{1,0:T(8,128)(2,1)}, bf16[416,3072]{1,0:T(8,128)(2,1)}, bf16[104,768]{1,0:T(8,128)(2,1)}, bf16[...) custom-call(s32[1]{0:T(128)} %bitcast.refs_0_.me_ref, ...), custom_call_target="tpu_custom_call" | custom-call | flops 7851737088 | bytes 20971520 | tf_op jit(solution)/shard_map/expert_fwd/pallas_call | solution.py:170
  167.5 6.4 %collective-permute-done.19.refs_5_ = bf16[104,768]{1,0:T(8,128)(2,1)S(1)} collective-permute-done((bf16[104,768]{1,0:T(8,128)(2,1)}, bf16[104,768]{1,0:T(8,128)(2,1)S(1)}, u32[]{:S(2)}, u32[]{:S(2)}) %collective-permute-start.19) | collective-permute-done | bytes 159776 | tf_op jit(solution)/shard_map/ppermute | solution.py:742
  174.3 9.5 %collective-permute-done.20.refs_6_ = bf16[104,768]{1,0:T(8,128)(2,1)S(1)} collective-permute-done((bf16[104,768]{1,0:T(8,128)(2,1)}, bf16[104,768]{1,0:T(8,128)(2,1)S(1)}, u32[]{:S(2)}, u32[]{:S(2)}) %collective-permute-start.20) | collective-permute-done | bytes 159776 | tf_op jit(solution)/shard_map/ppermute | solution.py:742
  186.1 5.7 %collective-permute-done.21.refs_7_ = bf16[104,768]{1,0:T(8,128)(2,1)S(1)} collective-permute-done((bf16[104,768]{1,0:T(8,128)(2,1)}, bf16[104,768]{1,0:T(8,128)(2,1)S(1)}, u32[]{:S(2)}, u32[]{:S(2)}) %collective-permute-start.21) | collective-permute-done | bytes 159776 | tf_op jit(solution)/shard_map/ppermute | solution.py:742
  192.5 8.4 %attn_fwd.3 = (f32[208,768]{1,0:T(8,128)}, f32[208,768]{1,0:T(8,128)}, bf16[208,768]{1,0:T(8,128)(2,1)}, bf16[208,2304]{1,0:T(8,128)(2,1)}, bf16[208,768]{1,0:T(...) custom-call(s32[1]{0:T(128)} %bitcast.refs_0_.me_ref, ...), custom_call_target="tpu_custom_call" | custom-call | flops 3925868544 | bytes 20971520 | tf_op jit(solution)/shard_map/attn_fwd/pallas_call | solution.py:170
  216.9 12.2 %expert_fwd.3 = (bf16[416,768]{1,0:T(8,128)(2,1)}, bf16[416,3072]{1,0:T(8,128)(2,1)}, bf16[416,3072]{1,0:T(8,128)(2,1)}, bf16[104,768]{1,0:T(8,128)(2,1)}, bf16[...) custom-call(s32[1]{0:T(128)} %bitcast.refs_0_.me_ref, ...), custom_call_target="tpu_custom_call" | custom-call | flops 7851737088 | bytes 20971520 | tf_op jit(solution)/shard_map/expert_fwd/pallas_call | solution.py:170
  229.0 10.2 %collective-permute-start.41 = (bf16[104,768]{1,0:T(8,128)(2,1)}, bf16[104,768]{1,0:T(8,128)(2,1)S(1)}, u32[]{:S(2)}, u32[]{:S(2)}) collective-permute-start(bf16[104,768]{1,0:T(8,128)(2,1)} %get-tuple-element.119), channel_id=1, source_target_pairs={{0,1},{1,0},{2,3},{3,2},{4,5},{5,4},{6,7},{7,6},{8,9},{9,8},{10,11... | collective-permute-start | bytes 479240 | tf_op jit(solution)/shard_map/ppermute | solution.py:742
  240.0 10.7 %expert_back.2 = (bf16[416,768]{1,0:T(8,128)(2,1)}, bf16[416,3072]{1,0:T(8,128)(2,1)}, bf16[104,768]{1,0:T(8,128)(2,1)}, bf16[104,768]{1,0:T(8,128)(2,1)}, bf16[...) custom-call(s32[1]{0:T(128)} %bitcast.refs_0_.me_ref, bf16[104,768]{1,0:T(8,128)(2,1)} %get-tuple-element.123.refs_1_, ...), custom_call_target="tpu_custom_call" | custom-call | flops 7851737088 | bytes 20971520 | tf_op jit(solution)/shard_map/expert_back/pallas_call | solution.py:170
  257.8 11.5 %expert_grads.3 = (bf16[4,96,3072]{2,1,0:T(8,128)(2,1)}, bf16[4,96,3072]{2,1,0:T(8,128)(2,1)}, bf16[4,384,768]{2,1,0:T(8,128)(2,1)}, bf16[4,384,768]{2,1,0:T(8,1...) custom-call(s32[1]{0:T(128)} %bitcast.refs_0_.me_ref, bf16[416,768]{1,0:T(8,128)(2,1)} %get-tuple-element.177.rows_ref, ...), custom_call_target="tpu_custom_call" | custom-call | flops 7851737088 | bytes 20971520 | tf_op jit(solution)/shard_map/expert_grads/pallas_call | solution.py:170
  277.5 13.1 %attn_back.2 = (f32[208,768]{1,0:T(8,128)}, bf16[208,768]{1,0:T(8,128)(2,1)}, bf16[208,2304]{1,0:T(8,128)(2,1)}, f32[16,768]{1,0:T(8,128)}, bf16[104,768]{1,0:T(...) custom-call(s32[1]{0:T(128)} %bitcast.refs_0_.me_ref, ...), custom_call_target="tpu_custom_call" | custom-call | flops 7851737088 | bytes 26214400 | tf_op jit(solution)/shard_map/attn_back/pallas_call | solution.py:170
  308.2 10.9 %expert_back.3 = (bf16[416,768]{1,0:T(8,128)(2,1)}, bf16[416,3072]{1,0:T(8,128)(2,1)}, bf16[104,768]{1,0:T(8,128)(2,1)}, bf16[104,768]{1,0:T(8,128)(2,1)}, bf16[...) custom-call(s32[1]{0:T(128)} %bitcast.refs_0_.me_ref, bf16[104,768]{1,0:T(8,128)(2,1)} %get-tuple-element.135.refs_1_, ...), custom_call_target="tpu_custom_call" | custom-call | flops 7851737088 | bytes 20971520 | tf_op jit(solution)/shard_map/expert_back/pallas_call | solution.py:170
  319.1 11.5 %expert_grads.2 = (bf16[4,96,3072]{2,1,0:T(8,128)(2,1)}, bf16[4,96,3072]{2,1,0:T(8,128)(2,1)}, bf16[4,384,768]{2,1,0:T(8,128)(2,1)}, bf16[4,384,768]{2,1,0:T(8,1...) custom-call(s32[1]{0:T(128)} %bitcast.refs_0_.me_ref, bf16[416,768]{1,0:T(8,128)(2,1)} %get-tuple-element.171.rows_ref, ...), custom_call_target="tpu_custom_call" | custom-call | flops 7851737088 | bytes 20971520 | tf_op jit(solution)/shard_map/expert_grads/pallas_call | solution.py:170
  337.6 22.9 %all-reduce.5 = f32[8,2,480]{2,1,0:T(2,128)S(1)} all-reduce(f32[8,2,480]{2,1,0:T(2,128)S(1)} %pad_maximum_fusion.10), channel_id=3, replica_groups=mesh['dp'=8,'expert'=4] {'dp'}, use_global_device_ids=true, to_apply=%region_1.2.clone | all-reduce | flops 7680 | bytes 61440
  362.4 12.4 %attn_back.3 = (f32[197,768]{1,0:T(8,128)}, bf16[208,768]{1,0:T(8,128)(2,1)}, bf16[208,2304]{1,0:T(8,128)(2,1)}, f32[16,768]{1,0:T(8,128)}) custom-call(s32[1]{0:T(128)} %bitcast.refs_0_.me_ref, bf16[104,768]{1,0:T(8,128)(2,1)} %get-tuple-element.140.refs_1_, bf16[104,768]{1,0:T(8,128)(2,1)} %copy-done.75, bf16[104,768]{1,0:T(8,128)(2,1)} %copy-done.77, ...), custom_call_target="tpu_custom_call" | custom-call | flops 7851737088 | bytes 26214400 | tf_op jit(solution)/shard_map/attn_back/pallas_call | solution.py:170
  388.8 12.4 %collective-permute-done.72 = bf16[2,96,1536]{2,1,0:T(8,128)(2,1)S(1)} collective-permute-done((bf16[2,96,1536]{2,1,0:T(8,128)(2,1)S(1)}, bf16[2,96,1536]{2,1,0:T(8,128)(2,1)S(1)}, u32[]{:S(2)}, u32[]{:S(2)}) %collective-permute-start.72) | collective-permute-done | bytes 589856 | tf_op jit(solution)/shard_map/ppermute | solution.py:742
  405.1 7.0 %collective-permute-done.73 = bf16[1,96,1536]{2,1,0:T(8,128)(2,1)S(1)} collective-permute-done((bf16[1,96,1536]{2,1,0:T(8,128)(2,1)S(1)}, bf16[1,96,1536]{2,1,0:T(8,128)(2,1)S(1)}, u32[]{:S(2)}, u32[]{:S(2)}) %collective-permute-start.73) | collective-permute-done | bytes 294944 | tf_op jit(solution)/shard_map/ppermute | solution.py:742
  424.4 6.0 %collective-permute-done.57 = bf16[2,96,1664]{2,1,0:T(8,128)(2,1)S(1)} collective-permute-done((bf16[2,96,1664]{2,1,0:T(8,128)(2,1)S(1)}, bf16[2,96,1664]{2,1,0:T(8,128)(2,1)S(1)}, u32[]{:S(2)}, u32[]{:S(2)}) %collective-permute-start.57) | collective-permute-done | bytes 639008 | tf_op jit(solution)/shard_map/ppermute | solution.py:742
  433.9 6.5 %collective-permute-done.68 = bf16[1,96,1536]{2,1,0:T(8,128)(2,1)S(1)} collective-permute-done((bf16[1,96,1536]{2,1,0:T(8,128)(2,1)S(1)}, bf16[1,96,1536]{2,1,0:T(8,128)(2,1)S(1)}, u32[]{:S(2)}, u32[]{:S(2)}) %collective-permute-start.68) | collective-permute-done | bytes 294944 | tf_op jit(solution)/shard_map/ppermute | solution.py:742
  448.3 16.4 %collective-permute-done.58 = bf16[1,96,1664]{2,1,0:T(8,128)(2,1)S(1)} collective-permute-done((bf16[1,96,1664]{2,1,0:T(8,128)(2,1)S(1)}, bf16[1,96,1664]{2,1,0:T(8,128)(2,1)S(1)}, u32[]{:S(2)}, u32[]{:S(2)}) %collective-permute-start.58) | collective-permute-done | bytes 319520 | tf_op jit(solution)/shard_map/ppermute | solution.py:742
  475.7 8.8 %collective-permute-done.65 = bf16[96,1664]{1,0:T(8,128)(2,1)S(1)} collective-permute-done((bf16[96,1664]{1,0:T(8,128)(2,1)S(1)}, bf16[96,1664]{1,0:T(8,128)(2,1)S(1)}, u32[]{:S(2)}, u32[]{:S(2)}) %collective-permute-start.65) | collective-permute-done | bytes 319520 | tf_op jit(solution)/shard_map/ppermute | solution.py:742
  484.6 8.8 %collective-permute-done.59 = bf16[96,1664]{1,0:T(8,128)(2,1)S(1)} collective-permute-done((bf16[96,1664]{1,0:T(8,128)(2,1)S(1)}, bf16[96,1664]{1,0:T(8,128)(2,1)S(1)}, u32[]{:S(2)}, u32[]{:S(2)}) %collective-permute-start.59) | collective-permute-done | bytes 319520 | tf_op jit(solution)/shard_map/ppermute | solution.py:742
  496.4 14.2 %collective-permute-done.70 = bf16[96,1536]{1,0:T(8,128)(2,1)S(1)} collective-permute-done((bf16[96,1536]{1,0:T(8,128)(2,1)S(1)}, bf16[96,1536]{1,0:T(8,128)(2,1)S(1)}, u32[]{:S(2)}, u32[]{:S(2)}) %collective-permute-start.70) | collective-permute-done | bytes 294944 | tf_op jit(solution)/shard_map/ppermute | solution.py:742
  510.7 10.5 %collective-permute-done.60 = bf16[96,1664]{1,0:T(8,128)(2,1)S(1)} collective-permute-done((bf16[96,1664]{1,0:T(8,128)(2,1)S(1)}, bf16[96,1664]{1,0:T(8,128)(2,1)S(1)}, u32[]{:S(2)}, u32[]{:S(2)}) %collective-permute-start.60) | collective-permute-done | bytes 319520 | tf_op jit(solution)/shard_map/ppermute | solution.py:742
  (455 shorter events, 210.0 us)
Async XLA Ops:
  2.7 38.5 %collective-permute-start.4 = (bf16[1,96,1536]{2,1,0:T(8,128)(2,1)}, bf16[1,96,1536]{2,1,0:T(8,128)(2,1)}, u32[]{:S(2)}, u32[]{:S(2)}) collective-permute-start(bf16[1,96,1536]{2,1,0:T(8,128)(2,1)} %maximum_bitcast_fusion.2), channel_id=1, source_target_pairs={{0,16},{4,20},{8,24},{12,28},{16,0},{20,4},{24,8},{28,12},{1,17},{... | collective-permute-start | bytes 884744 | tf_op jit(solution)/shard_map/ppermute | solution.py:742
  6.4 36.3 %collective-permute-start = (bf16[1,96,1536]{2,1,0:T(8,128)(2,1)}, bf16[1,96,1536]{2,1,0:T(8,128)(2,1)}, u32[]{:S(2)}, u32[]{:S(2)}) collective-permute-start(bf16[1,96,1536]{2,1,0:T(8,128)(2,1)} %slice_bitcast_fusion.7), channel_id=1, source_target_pairs={{0,8},{4,12},{8,0},{12,4},{16,24},{20,28},{24,16},{28,20},{1,9},{5... | collective-permute-start | bytes 884744 | tf_op jit(solution)/shard_map/ppermute | solution.py:742
  8.0 44.6 %collective-permute-start.11 = (bf16[1,96,3072]{2,1,0:T(8,128)(2,1)S(1)}, bf16[1,96,3072]{2,1,0:T(8,128)(2,1)}, u32[]{:S(2)}, u32[]{:S(2)}) collective-permute-start(bf16[1,96,3072]{2,1,0:T(8,128)(2,1)S(1)} %get-tuple-element.238), channel_id=1, source_target_pairs={{0,8},{4,12},{8,0},{12,4},{16,24},{20,28},{24,16},{28,20},{1,9},{5... | collective-permute-start | bytes 1769480 | tf_op jit(solution)/shard_map/ppermute | solution.py:742
  8.7 43.9 %collective-permute-start.15 = (bf16[1,384,768]{2,1,0:T(8,128)(2,1)S(1)}, bf16[1,384,768]{2,1,0:T(8,128)(2,1)}, u32[]{:S(2)}, u32[]{:S(2)}) collective-permute-start(bf16[1,384,768]{2,1,0:T(8,128)(2,1)S(1)} %get-tuple-element.236), channel_id=1, source_target_pairs={{0,16},{4,20},{8,24},{12,28},{16,0},{20,4},{24,8},{28,12},{1,17},{... | collective-permute-start | bytes 1769480 | tf_op jit(solution)/shard_map/ppermute | solution.py:742
  8.8 36.9 %collective-permute-start.26 = (bf16[1,96,1536]{2,1,0:T(8,128)(2,1)S(1)}, bf16[1,96,1536]{2,1,0:T(8,128)(2,1)}, u32[]{:S(2)}, u32[]{:S(2)}) collective-permute-start(bf16[1,96,1536]{2,1,0:T(8,128)(2,1)S(1)} %maximum_bitcast_fusion.3), channel_id=1, source_target_pairs={{0,16},{4,20},{8,24},{12,28},{16,0},{20,4},{24,8},{28,12},{1,17},{... | collective-permute-start | bytes 884744 | tf_op jit(solution)/shard_map/ppermute | solution.py:742
  88.4 38.0 %collective-permute-start.12 = (bf16[2,96,3072]{2,1,0:T(8,128)(2,1)S(1)}, bf16[2,96,3072]{2,1,0:T(8,128)(2,1)}, u32[]{:S(2)}, u32[]{:S(2)}) collective-permute-start(bf16[2,96,3072]{2,1,0:T(8,128)(2,1)S(1)} %pad_maximum_fusion.1.refs_5_.refs_6_), channel_id=1, source_target_pairs={{0,16},{4,20},{8,24},{12,28},{16,0},{20,4},{24,8},{28,12},{1,17},{... | collective-permute-start | bytes 3538952 | tf_op jit(solution)/shard_map/ppermute | solution.py:742
  92.8 35.2 %collective-permute-start.13 = (bf16[2,96,3072]{2,1,0:T(8,128)(2,1)S(1)}, bf16[2,96,3072]{2,1,0:T(8,128)(2,1)}, u32[]{:S(2)}, u32[]{:S(2)}) collective-permute-start(bf16[2,96,3072]{2,1,0:T(8,128)(2,1)S(1)} %pad_maximum_fusion.1.refs_5_.refs_6_), channel_id=1, source_target_pairs={{0,4},{4,0},{8,12},{12,8},{16,20},{20,16},{24,28},{28,24},{1,5},{5... | collective-permute-start | bytes 3538952 | tf_op jit(solution)/shard_map/ppermute | solution.py:742
  92.8 35.1 %collective-permute-start.16 = (bf16[2,384,768]{2,1,0:T(8,128)(2,1)}, bf16[2,384,768]{2,1,0:T(8,128)(2,1)}, u32[]{:S(2)}, u32[]{:S(2)}) collective-permute-start(bf16[2,384,768]{2,1,0:T(8,128)(2,1)} %pad_maximum_fusion.2.refs_9_.refs_10_), channel_id=1, source_target_pairs={{0,8},{4,12},{8,0},{12,4},{16,24},{20,28},{24,16},{28,20},{1,9},{5... | collective-permute-start | bytes 3538952 | tf_op jit(solution)/shard_map/ppermute | solution.py:742
  125.9 27.1 %collective-permute-start.34 = (bf16[2,96,3072]{2,1,0:T(8,128)(2,1)}, bf16[2,96,3072]{2,1,0:T(8,128)(2,1)}, u32[]{:S(2)}, u32[]{:S(2)}) collective-permute-start(bf16[2,96,3072]{2,1,0:T(8,128)(2,1)} %pad_maximum_fusion.3.refs_5_.refs_6_), channel_id=1, source_target_pairs={{0,16},{4,20},{8,24},{12,28},{16,0},{20,4},{24,8},{28,12},{1,17},{... | collective-permute-start | bytes 3538952 | tf_op jit(solution)/shard_map/ppermute | solution.py:742
  126.4 26.9 %collective-permute-start.38 = (bf16[2,384,768]{2,1,0:T(8,128)(2,1)}, bf16[2,384,768]{2,1,0:T(8,128)(2,1)}, u32[]{:S(2)}, u32[]{:S(2)}) collective-permute-start(bf16[2,384,768]{2,1,0:T(8,128)(2,1)} %pad_maximum_fusion.4.refs_9_.refs_10_), channel_id=1, source_target_pairs={{0,8},{4,12},{8,0},{12,4},{16,24},{20,28},{24,16},{28,20},{1,9},{5... | collective-permute-start | bytes 3538952 | tf_op jit(solution)/shard_map/ppermute | solution.py:742
  127.9 25.9 %collective-permute-start.18 = (bf16[2,384,768]{2,1,0:T(8,128)(2,1)}, bf16[2,384,768]{2,1,0:T(8,128)(2,1)S(1)}, u32[]{:S(2)}, u32[]{:S(2)}) collective-permute-start(bf16[2,384,768]{2,1,0:T(8,128)(2,1)} %collective-permute-done.16.refs_10_.refs_11_), channel_id=1, source_target_pairs={{0,4},{4,0},{8,12},{12,8},{16,20},{20,16},{24,28},{28,24},{1,5},{5... | collective-permute-start | bytes 3538952 | tf_op jit(solution)/shard_map/ppermute | solution.py:742
  131.3 69.7 %collective-permute-start.35 = (bf16[2,96,3072]{2,1,0:T(8,128)(2,1)}, bf16[2,96,3072]{2,1,0:T(8,128)(2,1)}, u32[]{:S(2)}, u32[]{:S(2)}) collective-permute-start(bf16[2,96,3072]{2,1,0:T(8,128)(2,1)} %pad_maximum_fusion.3.refs_5_.refs_6_), channel_id=1, source_target_pairs={{0,4},{4,0},{8,12},{12,8},{16,20},{20,16},{24,28},{28,24},{1,5},{5... | collective-permute-start | bytes 3538952 | tf_op jit(solution)/shard_map/ppermute | solution.py:742
  153.0 50.3 %collective-permute-start.39 = (bf16[2,384,768]{2,1,0:T(8,128)(2,1)}, bf16[2,384,768]{2,1,0:T(8,128)(2,1)}, u32[]{:S(2)}, u32[]{:S(2)}) collective-permute-start(bf16[2,384,768]{2,1,0:T(8,128)(2,1)} %pad_maximum_fusion.4.refs_9_.refs_10_), channel_id=1, source_target_pairs={{0,4},{4,0},{8,12},{12,8},{16,20},{20,16},{24,28},{28,24},{1,5},{5... | collective-permute-start | bytes 3538952 | tf_op jit(solution)/shard_map/ppermute | solution.py:742
  153.5 56.3 %collective-permute-start.36 = (bf16[2,96,3072]{2,1,0:T(8,128)(2,1)}, bf16[2,96,3072]{2,1,0:T(8,128)(2,1)}, u32[]{:S(2)}, u32[]{:S(2)}) collective-permute-start(bf16[2,96,3072]{2,1,0:T(8,128)(2,1)} %collective-permute-done.34.refs_6_.refs_7_), channel_id=1, source_target_pairs={{0,4},{4,0},{8,12},{12,8},{16,20},{20,16},{24,28},{28,24},{1,5},{5... | collective-permute-start | bytes 3538952 | tf_op jit(solution)/shard_map/ppermute | solution.py:742
  153.8 56.0 %collective-permute-start.40 = (bf16[2,384,768]{2,1,0:T(8,128)(2,1)}, bf16[2,384,768]{2,1,0:T(8,128)(2,1)}, u32[]{:S(2)}, u32[]{:S(2)}) collective-permute-start(bf16[2,384,768]{2,1,0:T(8,128)(2,1)} %collective-permute-done.38.refs_10_.refs_11_), channel_id=1, source_target_pairs={{0,4},{4,0},{8,12},{12,8},{16,20},{20,16},{24,28},{28,24},{1,5},{5... | collective-permute-start | bytes 3538952 | tf_op jit(solution)/shard_map/ppermute | solution.py:742
  209.8 29.4 %collective-permute-start.44 = (bf16[104,768]{1,0:T(8,128)(2,1)}, bf16[104,768]{1,0:T(8,128)(2,1)S(1)}, u32[]{:S(2)}, u32[]{:S(2)}) collective-permute-start(bf16[104,768]{1,0:T(8,128)(2,1)} %get-tuple-element.124), channel_id=1, source_target_pairs={{0,1},{1,0},{2,3},{3,2},{4,5},{5,4},{6,7},{7,6},{8,9},{9,8},{10,11... | collective-permute-start | bytes 479240 | tf_op jit(solution)/shard_map/ppermute | solution.py:742
  209.8 29.4 %collective-permute-start.45 = (bf16[104,768]{1,0:T(8,128)(2,1)}, bf16[104,768]{1,0:T(8,128)(2,1)S(1)}, u32[]{:S(2)}, u32[]{:S(2)}) collective-permute-start(bf16[104,768]{1,0:T(8,128)(2,1)} %get-tuple-element.125), channel_id=1, source_target_pairs={{0,2},{1,3},{2,0},{3,1},{4,6},{5,7},{6,4},{7,5},{8,10},{9,11},{10,... | collective-permute-start | bytes 479240 | tf_op jit(solution)/shard_map/ppermute | solution.py:742
  212.1 27.1 %collective-permute-start.46 = (bf16[104,768]{1,0:T(8,128)(2,1)}, bf16[104,768]{1,0:T(8,128)(2,1)S(1)}, u32[]{:S(2)}, u32[]{:S(2)}) collective-permute-start(bf16[104,768]{1,0:T(8,128)(2,1)} %get-tuple-element.126), channel_id=1, source_target_pairs={{0,3},{1,2},{2,1},{3,0},{4,7},{5,6},{6,5},{7,4},{8,11},{9,10},{10,... | collective-permute-start | bytes 479240 | tf_op jit(solution)/shard_map/ppermute | solution.py:742
  229.0 26.3 %collective-permute-start.41 = (bf16[104,768]{1,0:T(8,128)(2,1)}, bf16[104,768]{1,0:T(8,128)(2,1)S(1)}, u32[]{:S(2)}, u32[]{:S(2)}) collective-permute-start(bf16[104,768]{1,0:T(8,128)(2,1)} %get-tuple-element.119), channel_id=1, source_target_pairs={{0,1},{1,0},{2,3},{3,2},{4,5},{5,4},{6,7},{7,6},{8,9},{9,8},{10,11... | collective-permute-start | bytes 479240 | tf_op jit(solution)/shard_map/ppermute | solution.py:742
  250.8 25.9 %collective-permute-start.47 = (bf16[104,768]{1,0:T(8,128)(2,1)}, bf16[104,768]{1,0:T(8,128)(2,1)S(1)}, u32[]{:S(2)}, u32[]{:S(2)}) collective-permute-start(bf16[104,768]{1,0:T(8,128)(2,1)} %get-tuple-element.129), channel_id=1, source_target_pairs={{0,1},{1,0},{2,3},{3,2},{4,5},{5,4},{6,7},{7,6},{8,9},{9,8},{10,11... | collective-permute-start | bytes 479240 | tf_op jit(solution)/shard_map/ppermute | solution.py:742
  250.9 25.9 %collective-permute-start.48 = (bf16[104,768]{1,0:T(8,128)(2,1)}, bf16[104,768]{1,0:T(8,128)(2,1)S(1)}, u32[]{:S(2)}, u32[]{:S(2)}) collective-permute-start(bf16[104,768]{1,0:T(8,128)(2,1)} %get-tuple-element.130), channel_id=1, source_target_pairs={{0,2},{1,3},{2,0},{3,1},{4,6},{5,7},{6,4},{7,5},{8,10},{9,11},{10,... | collective-permute-start | bytes 479240 | tf_op jit(solution)/shard_map/ppermute | solution.py:742
  272.2 148.2 %collective-permute-start.85 = (bf16[4,384,768]{2,1,0:T(8,128)(2,1)}, bf16[4,384,768]{2,1,0:T(8,128)(2,1)S(1)}, u32[]{:S(2)}, u32[]{:S(2)}) collective-permute-start(bf16[4,384,768]{2,1,0:T(8,128)(2,1)} %get-tuple-element.190), channel_id=1, source_target_pairs={{0,4},{4,0},{8,12},{12,8},{16,20},{20,16},{24,28},{28,24},{1,5},{5... | collective-permute-start | bytes 7077896 | tf_op jit(solution)/shard_map/ppermute | solution.py:742
  300.1 81.0 %collective-permute-start.71 = (bf16[4,96,1536]{2,1,0:T(8,128)(2,1)}, bf16[4,96,1536]{2,1,0:T(8,128)(2,1)}, u32[]{:S(2)}, u32[]{:S(2)}) collective-permute-start(bf16[4,96,1536]{2,1,0:T(8,128)(2,1)} %get-tuple-element.170), channel_id=1, source_target_pairs={{0,4},{4,0},{8,12},{12,8},{16,20},{20,16},{24,28},{28,24},{1,5},{5... | collective-permute-start | bytes 3538952 | tf_op jit(solution)/shard_map/ppermute | solution.py:742
  332.8 28.4 %collective-permute-start.53 = (bf16[104,768]{1,0:T(8,128)(2,1)S(1)}, bf16[104,768]{1,0:T(8,128)(2,1)S(1)}, u32[]{:S(2)}, u32[]{:S(2)}) collective-permute-start(bf16[104,768]{1,0:T(8,128)(2,1)S(1)} %copy-done.71), channel_id=1, source_target_pairs={{0,1},{1,0},{2,3},{3,2},{4,5},{5,4},{6,7},{7,6},{8,9},{9,8},{10,11... | collective-permute-start | bytes 479240 | tf_op jit(solution)/shard_map/ppermute | solution.py:742
  335.1 26.2 %collective-permute-start.54 = (bf16[104,768]{1,0:T(8,128)(2,1)S(1)}, bf16[104,768]{1,0:T(8,128)(2,1)S(1)}, u32[]{:S(2)}, u32[]{:S(2)}) collective-permute-start(bf16[104,768]{1,0:T(8,128)(2,1)S(1)} %copy-done.67), channel_id=1, source_target_pairs={{0,2},{1,3},{2,0},{3,1},{4,6},{5,7},{6,4},{7,5},{8,10},{9,11},{10,... | collective-permute-start | bytes 479240 | tf_op jit(solution)/shard_map/ppermute | solution.py:742
  361.2 55.8 %collective-permute-start.79 = (bf16[4,96,3072]{2,1,0:T(8,128)(2,1)}, bf16[4,96,3072]{2,1,0:T(8,128)(2,1)}, u32[]{:S(2)}, u32[]{:S(2)}) collective-permute-start(bf16[4,96,3072]{2,1,0:T(8,128)(2,1)} %get-tuple-element.182), channel_id=1, source_target_pairs={{0,4},{4,0},{8,12},{12,8},{16,20},{20,16},{24,28},{28,24},{1,5},{5... | collective-permute-start | bytes 7077896 | tf_op jit(solution)/shard_map/ppermute | solution.py:742
  383.6 59.5 %collective-permute-start.82 = (bf16[4,384,768]{2,1,0:T(8,128)(2,1)S(1)}, bf16[4,384,768]{2,1,0:T(8,128)(2,1)S(1)}, u32[]{:S(2)}, u32[]{:S(2)}) collective-permute-start(bf16[4,384,768]{2,1,0:T(8,128)(2,1)S(1)} %copy-done.41), channel_id=1, source_target_pairs={{0,4},{4,0},{8,12},{12,8},{16,20},{20,16},{24,28},{28,24},{1,5},{5... | collective-permute-start | bytes 7077896 | tf_op jit(solution)/shard_map/ppermute | solution.py:742
  412.0 29.4 %collective-permute-start.76 = (bf16[4,96,3072]{2,1,0:T(8,128)(2,1)S(1)}, bf16[4,96,3072]{2,1,0:T(8,128)(2,1)S(1)}, u32[]{:S(2)}, u32[]{:S(2)}) collective-permute-start(bf16[4,96,3072]{2,1,0:T(8,128)(2,1)S(1)} %copy-done.42), channel_id=1, source_target_pairs={{0,4},{4,0},{8,12},{12,8},{16,20},{20,16},{24,28},{28,24},{1,5},{5... | collective-permute-start | bytes 7077896 | tf_op jit(solution)/shard_map/ppermute | solution.py:742
  431.7 94.0 %collective-permute-start.86 = (bf16[2,384,768]{2,1,0:T(8,128)(2,1)}, bf16[2,384,768]{2,1,0:T(8,128)(2,1)}, u32[]{:S(2)}, u32[]{:S(2)}) collective-permute-start(bf16[2,384,768]{2,1,0:T(8,128)(2,1)} %slice.343), channel_id=1, source_target_pairs={{0,16},{4,20},{8,24},{12,28},{16,0},{20,4},{24,8},{28,12},{1,17},{... | collective-permute-start | bytes 3538952 | tf_op jit(solution)/shard_map/ppermute | solution.py:742
  432.8 95.5 %collective-permute-start.80 = (bf16[2,96,3072]{2,1,0:T(8,128)(2,1)}, bf16[2,96,3072]{2,1,0:T(8,128)(2,1)}, u32[]{:S(2)}, u32[]{:S(2)}) collective-permute-start(bf16[2,96,3072]{2,1,0:T(8,128)(2,1)} %slice.334), channel_id=1, source_target_pairs={{0,8},{4,12},{8,0},{12,4},{16,24},{20,28},{24,16},{28,20},{1,9},{5... | collective-permute-start | bytes 3538952 | tf_op jit(solution)/shard_map/ppermute | solution.py:742
  465.6 66.0 %collective-permute-start.83 = (bf16[2,384,768]{2,1,0:T(8,128)(2,1)}, bf16[2,384,768]{2,1,0:T(8,128)(2,1)}, u32[]{:S(2)}, u32[]{:S(2)}) collective-permute-start(bf16[2,384,768]{2,1,0:T(8,128)(2,1)} %slice.339), channel_id=1, source_target_pairs={{0,16},{4,20},{8,24},{12,28},{16,0},{20,4},{24,8},{28,12},{1,17},{... | collective-permute-start | bytes 3538952 | tf_op jit(solution)/shard_map/ppermute | solution.py:742
  466.9 67.8 %collective-permute-start.77 = (bf16[2,96,3072]{2,1,0:T(8,128)(2,1)}, bf16[2,96,3072]{2,1,0:T(8,128)(2,1)}, u32[]{:S(2)}, u32[]{:S(2)}) collective-permute-start(bf16[2,96,3072]{2,1,0:T(8,128)(2,1)} %slice.330), channel_id=1, source_target_pairs={{0,8},{4,12},{8,0},{12,4},{16,24},{20,28},{24,16},{28,20},{1,9},{5... | collective-permute-start | bytes 3538952 | tf_op jit(solution)/shard_map/ppermute | solution.py:742
  (136 other events, 1445.4 us)

commit v2 on v1

v2 whole, which is shorter than its diff:
```python
import functools

import jax
import jax.numpy as jnp
from jax import lax
from jax.experimental import pallas as pl
from jax.experimental.pallas import tpu as pltpu
from jax.sharding import PartitionSpec as P

HEADS = 12
HEAD_DIM = 64
SEQ = 197
EPS = 1e-06
BF = jnp.bfloat16
F32 = jnp.float32
LANES = 128
NEG = -1e30
VMEM_LIMIT = 60 * 1024 * 1024


def up(value, step):
    return -(-value // step) * step


def dot(left, right):
    return lax.dot_general(left, right, (((1,), (0,)), ((), ())), preferred_element_type=F32)


def dot_nt(left, right):
    return lax.dot_general(left, right, (((1,), (1,)), ((), ())), preferred_element_type=F32)


def dot_tn(left, right):
    return lax.dot_general(left, right, (((0,), (0,)), ((), ())), preferred_element_type=F32)


def norm_rows(x):
    centered = x - jnp.mean(x, -1, keepdims=True)
    rstd = lax.rsqrt(jnp.mean(centered * centered, -1, keepdims=True) + EPS)
    return centered * rstd, rstd


def norm_back(grad_hat, normed, rstd):
    return rstd * (
        grad_hat
        - jnp.mean(grad_hat, -1, keepdims=True)
        - normed * jnp.mean(grad_hat * normed, -1, keepdims=True)
    )


def split(value):
    high = value.astype(BF)
    return high, (value - high.astype(F32)).astype(BF)


def join(refs):
    return jnp.concatenate([ref[...].astype(F32) for ref in refs], 0).astype(BF)


def part(value, refs):
    rows = refs[0].shape[0]
    for number, ref in enumerate(refs):
        ref[...] = value[number * rows : (number + 1) * rows].astype(ref.dtype)


def seat_mask(cols_ref, pair, seats):
    column = cols_ref[:, pair : pair + 1]
    return lax.broadcasted_iota(jnp.int32, (column.shape[0], seats), 1) == column


def token_mask(rows_ref, pair, seats):
    row = rows_ref[pair : pair + 1, :]
    return lax.broadcasted_iota(jnp.int32, (seats, row.shape[1]), 0) == row


def one(mask):
    return jnp.where(mask, 1.0, 0.0).astype(BF)


def pair_gate(gates, cols_ref, pair):
    route = cols_ref[:, 2 + pair : 3 + pair]
    lanes = lax.broadcasted_iota(jnp.int32, gates.shape, 1)
    return jnp.sum(jnp.where(lanes == route, gates, 0.0), -1, keepdims=True)


def combine(x1, gates, cols_ref, returned):
    total = x1
    for pair in range(2):
        piece = dot(one(seat_mask(cols_ref, pair, returned.shape[0])), returned)
        total = total + pair_gate(gates, cols_ref, pair) * piece
    return total


def seat_grads(grad, gates, cols_ref, rows_ref, seats):
    total = None
    for pair in range(2):
        scaled = (pair_gate(gates, cols_ref, pair) * grad).astype(BF)
        piece = dot(one(token_mask(rows_ref, pair, seats)), scaled)
        total = piece if total is None else total + piece
    return total


def head_masks():
    lanes = lax.broadcasted_iota(jnp.int32, (1, 2 * HEAD_DIM), 1)
    return (lanes < HEAD_DIM, lanes >= HEAD_DIM)


def head_probs(query, keys, mask, tokens):
    query = jnp.where(mask, query, 0).astype(F32) * HEAD_DIM ** (-0.5)
    scores = dot_nt(query.astype(BF), keys)
    lanes = lax.broadcasted_iota(jnp.int32, scores.shape, 1)
    scores = jnp.where(lanes < tokens, scores, NEG)
    raised = jnp.exp(scores - jnp.max(scores, -1, keepdims=True))
    return raised * (1.0 / jnp.sum(raised, -1, keepdims=True))


VM = pl.BlockSpec(memory_space=pltpu.VMEM)
ANY = pl.BlockSpec(memory_space=pl.ANY)
SM = pl.BlockSpec(memory_space=pltpu.SMEM)


def sds(shape, dtype):
    return jax.ShapeDtypeStruct(tuple(shape), dtype)


class Order:
    token = None


def call(kernel, name, args, specs, outs, out_specs, scratch, aliases=None):
    after = []
    if Order.token is not None and not any(Order.token is arg for arg in args):
        after = [Order.token]
    given = len(args)

    def body(*refs):
        return kernel(*refs[:given], *refs[given + len(after) :])

    result = pl.pallas_call(
        body,
        name=name,
        in_specs=list(specs) + [ANY] * len(after),
        out_specs=out_specs,
        out_shape=outs,
        scratch_shapes=scratch,
        input_output_aliases=aliases or {},
        compiler_params=pltpu.CompilerParams(vmem_limit_bytes=VMEM_LIMIT),
    )(*args, *after)
    Order.token = result[0] if isinstance(result, (tuple, list)) else result
    return result


def hold(values, after):
    def kernel(*refs):
        pass

    return call(
        kernel,
        "hold",
        [*values, *after],
        [ANY] * (len(values) + len(after)),
        [sds(value.shape, value.dtype) for value in values],
        [ANY] * len(values),
        [],
        {i: i for i in range(len(values))},
    )


def move(name, args, copies, outs):
    total = len(copies)

    def kernel(*refs):
        ins, rest = refs[: len(args)], refs[len(args) :]
        results, held = rest[: len(outs)], rest[len(outs) : len(outs) + total]
        in_sems, out_sems = rest[-2:]
        loads = [
            pltpu.make_async_copy(ins[i].at[where], held[n], in_sems.at[n])
            for n, (i, where, _, _, _) in enumerate(copies)
        ]
        stores = [
            pltpu.make_async_copy(held[n], results[o].at[into], out_sems.at[n])
            for n, (_, _, o, into, _) in enumerate(copies)
        ]
        start(loads)
        for load, store in zip(loads, stores):
            load.wait()
            store.start()
        wait(stores)

    return call(
        kernel,
        name,
        args,
        [ANY] * len(args),
        outs,
        [ANY] * len(outs),
        [pltpu.VMEM(shape, BF) for *_, shape in copies]
        + [pltpu.SemaphoreType.DMA((total,)), pltpu.SemaphoreType.DMA((total,))],
    )


def fold(name, args, block, tasks, outs, aliases=None):
    terms = [(t, term) for t, (listed, _, _) in enumerate(tasks) for term in listed]
    writes = [(t, write) for t, (_, _, listed) in enumerate(tasks) for write in listed]
    wide = [t for t, task in enumerate(tasks) if task[1] == F32]
    slim = [t for t, task in enumerate(tasks) if task[1] != F32]

    def kernel(*refs):
        ins, rest = refs[: len(args)], refs[len(args) :]
        results = rest[: len(outs)]
        loaded, wide_ref, slim_ref, in_sems, out_sems = rest[len(outs) :]
        loads = [
            pltpu.make_async_copy(ins[i].at[where], loaded.at[n], in_sems.at[n])
            for n, (_, (i, where)) in enumerate(terms)
        ]
        for copy in loads:
            copy.start()
        stores = []
        for t, (_, kind, _) in enumerate(tasks):
            total = None
            for n, (task, _) in enumerate(terms):
                if task == t:
                    loads[n].wait()
                    piece = loaded[n].astype(F32)
                    total = piece if total is None else total + piece
            holder = wide_ref.at[wide.index(t)] if kind == F32 else slim_ref.at[slim.index(t)]
            holder[...] = total.astype(kind)
            for n, (task, (o, into, within)) in enumerate(writes):
                if task == t:
                    copy = pltpu.make_async_copy(
                        holder.at[within], results[o].at[into], out_sems.at[n]
                    )
                    copy.start()
                    stores.append(copy)
        for copy in stores:
            copy.wait()

    return call(
        kernel,
        name,
        args,
        [ANY] * len(args),
        outs,
        [ANY] * len(outs),
        [
            pltpu.VMEM((len(terms), *block), BF),
            pltpu.VMEM((max(len(wide), 1), *(block if wide else (16, LANES))), F32),
            pltpu.VMEM((max(len(slim), 1), *(block if slim else (16, LANES))), BF),
            pltpu.SemaphoreType.DMA((len(terms),)),
            pltpu.SemaphoreType.DMA((len(writes),)),
        ],
        aliases=aliases,
    )


ALL = slice(None)


class Weights:
    def __init__(self, arrays, places):
        self.arrays, self.places = list(arrays), places


OWNERS = -1


def attn_targets(width, rows, wqkv, wout):
    return {
        0: [(wqkv, 0, 2 * width, 0, rows, 0)],
        1: [(wqkv, 0, width, 2 * width, rows, 0), (wout, width, width, 0, rows, 0)],
    }


def expert_targets(width, hidden, rows, whole, win, woe):
    if whole:
        return {0: [(win, 0, hidden, 0, rows, 0)], 1: [(woe, 0, width, 0, rows, 0)]}
    per = hidden // width
    return {
        0: [(win, 0, hidden, 0, rows, 0)],
        1: [(woe, q * width, width, 0, per * rows, q * rows) for q in range(per)],
    }


def copies_in(weights):
    return 4 * sum(
        len(parts) if array.ndim == 3 else array.shape[0]
        for array, (off, parts) in zip(weights.arrays, weights.places)
    )


def fetch(refs, weights, me, targets, part_number, sems):
    copies = []
    for ref, (off, parts) in zip(refs, weights.places):
        rows = ref.shape[-2]
        if off == OWNERS:
            sources = [(d, (d, part_number)) for d in range(ref.shape[0])]
        elif isinstance(off, tuple):
            sources = [(me ^ o, (k, part_number)) for k, o in enumerate(off)]
        elif part_number in parts:
            at = None if off is None else me ^ off
            sources = [(at, (parts.index(part_number),))]
        else:
            sources = []
        for at, where in sources:
            for scratch, first, size, into, times, plus in targets[part_number]:
                place = 0 if at is None else at * times + plus
                if off not in (None, OWNERS):
                    place = pl.multiple_of(place, 16)
                copies.append(
                    pltpu.make_async_copy(
                        ref.at[(*where, ALL, pl.ds(first, size))],
                        scratch.at[pl.ds(place, rows), pl.ds(into, size)],
                        sems.at[len(copies)],
                    )
                )
    return copies


def start(copies):
    for copy in copies:
        copy.start()


def wait(copies):
    for copy in copies:
        copy.wait()


def small_rows(per, experts):
    return up(7 + experts + per + 1, 8)


def pack_small(norm_gains, biases, w_router, b_in, b_expout):
    layers, shard, experts = w_router.shape
    per = b_in.shape[2] // shard
    height = small_rows(per, experts)

    def kernel(gain_ref, bias_ref, router_ref, in_ref, oe_ref, out, square):
        out[...] = jnp.zeros_like(out)
        for layer in range(layers):
            at = layer * height
            out[at : at + 2, 0:shard] = gain_ref[layer]
            out[at + 2 : at + 7, 0:shard] = bias_ref[layer]
            square[...] = jnp.zeros_like(square)
            square[0:shard, 0:experts] = router_ref[layer]
            turned = square[...].T
            out[at + 7 : at + 7 + experts, :] = turned[0:experts, :]
            at = at + 7 + experts
            for q in range(per):
                out[at + q : at + q + 1, 0:shard] = in_ref[layer, :, q * shard : (q + 1) * shard]
            out[at + per : at + per + 1, 0:shard] = oe_ref[layer]

    return call(
        kernel,
        "pack_small",
        [norm_gains, biases, w_router, b_in, b_expout],
        [VM] * 5,
        sds((layers * height, LANES), F32),
        VM,
        [pltpu.VMEM((LANES, LANES), F32)],
    )


def unpack_small(gathered, layers, shard, per, experts):
    shards = gathered.shape[0]
    width = shards * shard
    height = small_rows(per, experts)

    def kernel(ref, *refs):
        tall = refs[-1]
        for layer in range(layers):
            vec, router, bias_in, bias_oe = refs[4 * layer : 4 * layer + 4]
            at = layer * height
            vec[...] = jnp.zeros_like(vec)
            tall[...] = jnp.zeros_like(tall)
            for d in range(shards):
                here = slice(d * shard, (d + 1) * shard)
                vec[0:7, here] = ref[d, at : at + 7, 0:shard]
                tall[0:experts, here] = ref[d, at + 7 : at + 7 + experts, 0:shard]
                row = at + 7 + experts
                for q in range(per):
                    first = (d * per + q) * shard
                    bias_in[:, first : first + shard] = ref[d, row + q : row + q + 1, 0:shard]
                bias_oe[:, here] = ref[d, row + per : row + per + 1, 0:shard]
            router[...] = tall[...].T.astype(BF)

    shapes = []
    for _ in range(layers):
        shapes += [
            sds((8, width), F32),
            sds((width, LANES), BF),
            sds((1, width * per), F32),
            sds((1, width), F32),
        ]
    outs = call(
        kernel,
        "unpack_small",
        [gathered],
        [VM],
        shapes,
        [VM] * len(shapes),
        [pltpu.VMEM((LANES, width), F32)],
    )
    return [outs[4 * layer : 4 * layer + 4] for layer in range(layers)]


def place_pairs(routes, seat_order, padded, cap, cap_pad, z):
    layers, tokens, _ = routes.shape
    tall = up(padded, LANES)

    def kernel(z_ref, route_ref, order_ref, *refs):
        outs, wide = refs[:-1], refs[-1]
        lanes = lax.broadcasted_iota(jnp.int32, (tokens, LANES), 1)
        lanes_tall = lax.broadcasted_iota(jnp.int32, (tall, LANES), 1)
        for layer in range(layers):
            given = jnp.full((tokens, LANES), -1.0, F32)
            for k in range(2):
                given = jnp.where(lanes == k, route_ref[layer, :, k : k + 1].astype(F32), given)
                given = jnp.where(lanes == 2 + k, order_ref[layer, :, k : k + 1].astype(F32), given)
            wide[...] = jnp.full((tall, LANES), -1.0, F32)
            wide[0:tokens, :] = given
            table = wide[...]
            turned = table.T
            seats = []
            for k in range(2):
                expert, order = table[:, k : k + 1], table[:, 2 + k : 3 + k]
                rank = jnp.zeros((tall, 1), F32)
                for j in range(2):
                    ahead = jnp.logical_and(
                        turned[j : j + 1, :] == expert, turned[2 + j : 3 + j, :] < order
                    )
                    rank = rank + jnp.sum(jnp.where(ahead, 1.0, 0.0), -1, keepdims=True)
                expert, rank = expert.astype(jnp.int32), rank.astype(jnp.int32)
                near = jnp.bitwise_xor(expert, z_ref[0])
                good = jnp.logical_and(expert >= 0, rank < cap)
                seats.append(jnp.where(good, near * cap_pad + rank, -1).astype(F32))
            table = jnp.where(lanes_tall == 2, table[:, 0:1], table)
            table = jnp.where(lanes_tall == 3, wide[:, 1:2], table)
            table = jnp.where(lanes_tall == 0, seats[0], table)
            table = jnp.where(lanes_tall == 1, seats[1], table)
            cols, rows = outs[2 * layer], outs[2 * layer + 1]
            cols[...] = table[0:padded, :].astype(jnp.int32)
            rows[...] = table.T[0:8, 0:padded].astype(jnp.int32)

    shapes = []
    for _ in range(layers):
        shapes += [sds((padded, LANES), jnp.int32), sds((8, padded), jnp.int32)]
    outs = call(
        kernel,
        "place_pairs",
        [z, routes, seat_order],
        [SM, VM, VM],
        shapes,
        [VM] * len(shapes),
        [pltpu.VMEM((tall, LANES), F32)],
    )
    return outs[0::2], outs[1::2]


def attn_fwd(me, layer, x_args, weights, vecs, router, noise, cols, rows, cap):
    first = len(x_args) == 1
    padded, width = cols.shape[0], vecs.shape[1]
    tokens, experts = noise.shape[1:]
    seats = experts * cap
    owners = 0 if first else len(x_args[3])
    count = len(weights.arrays)
    shard = weights.arrays[0].shape[-2]

    def kernel(*refs):
        refs = list(refs)
        me_ref = refs.pop(0)
        if first:
            tok_ref = refs.pop(0)
        else:
            below_x1, below_gates, below_cols = refs.pop(0), refs.pop(0), refs.pop(0)
            below_blocks = [refs.pop(0) for _ in range(owners)]
        w_refs = [refs.pop(0) for _ in range(count)]
        vec_ref, router_ref, noise_ref, cols_ref, rows_ref = (refs.pop(0) for _ in range(5))
        x_out, x1_out, a_out, qkv_out, o_out, gates_out, m_out = (refs.pop(0) for _ in range(7))
        seat_outs = [refs.pop(0) for _ in range(experts)]
        wqkv, wout, sems, more_sems = refs
        targets = attn_targets(width, shard, wqkv, wout)
        left = fetch(w_refs, weights, me_ref[0], targets, 0, sems)
        right = fetch(w_refs, weights, me_ref[0], targets, 1, more_sems)
        start(left + right)
        vec = lambda k: vec_ref[k : k + 1, :]
        if first:
            x_out[...] = jnp.zeros_like(x_out)
            x_out[0:tokens, :] = tok_ref[...].astype(F32)
            x = x_out[...]
        else:
            x = combine(below_x1[...], below_gates[...], below_cols, join(below_blocks))
            x_out[...] = x
        normed, rstd = norm_rows(x)
        a_low = (normed * vec(0) + vec(2)).astype(BF)
        a_out[...] = a_low
        gates_out[...] = jnp.zeros_like(gates_out)
        gates_out[0:tokens, 0:experts] = noise_ref[layer]
        noise_here = gates_out[...]
        wait(left)
        for k in range(3):
            if k == 2:
                wait(right)
            piece = dot(a_low, wqkv[:, k * width : (k + 1) * width])
            if k == 0:
                piece = piece + vec(4)
            if k == 2:
                piece = piece + vec(5)
            qkv_out[:, k * width : (k + 1) * width] = piece.astype(BF)
        masks = head_masks()
        for two in range(HEADS // 2):
            at = two * 2 * HEAD_DIM
            query = qkv_out[:, at : at + 2 * HEAD_DIM]
            keys = qkv_out[:, width + at : width + at + 2 * HEAD_DIM]
            values = qkv_out[:, 2 * width + at : 2 * width + at + 2 * HEAD_DIM]
            mixed = None
            for mask in masks:
                probs = head_probs(query, keys, mask, tokens).astype(BF)
                piece = dot(probs, jnp.where(mask, values, 0).astype(BF))
                mixed = piece if mixed is None else mixed + piece
            o_out[:, at : at + 2 * HEAD_DIM] = mixed.astype(BF)
        x1 = x + dot(o_out[...], wout[...]) + vec(6)
        x1_out[...] = x1
        normed2, rstd2 = norm_rows(x1)
        moe = normed2 * vec(1) + vec(3)
        high, low = split(moe)
        logits = dot(high, router_ref[...]) + dot(low, router_ref[...]) + noise_here
        lanes = lax.broadcasted_iota(jnp.int32, logits.shape, 1)
        logits = jnp.where(lanes < experts, logits, NEG)
        raised = jnp.exp(logits - jnp.max(logits, -1, keepdims=True))
        gates_out[...] = raised / jnp.sum(raised, -1, keepdims=True)
        m_out[...] = high
        chosen = jnp.logical_or(token_mask(rows_ref, 0, seats), token_mask(rows_ref, 1, seats))
        part(dot(one(chosen), high), seat_outs)

    args = [me]
    specs = [SM]
    if first:
        args += [x_args[0]]
        specs += [VM]
    else:
        args += [x_args[0], x_args[1], x_args[2], *x_args[3]]
        specs += [VM] * (3 + owners)
    args += [*weights.arrays, vecs, router, noise, cols, rows]
    specs += [ANY] * count + [VM] * 5
    outs = [
        sds((padded, width), F32),
        sds((padded, width), F32),
        sds((padded, width), BF),
        sds((padded, 3 * width), BF),
        sds((padded, width), BF),
        sds((padded, LANES), F32),
        sds((padded, width), BF),
    ] + [sds((cap, width), BF)] * experts
    result = call(
        kernel,
        "attn_fwd",
        args,
        specs,
        outs,
        [VM] * len(outs),
        [
            pltpu.VMEM((width, 3 * width), BF),
            pltpu.VMEM((width, width), BF),
            pltpu.SemaphoreType.DMA((copies_in(weights),)),
            pltpu.SemaphoreType.DMA((copies_in(weights),)),
        ],
    )
    return result[:7], result[7:]


def expert_fwd(me, seat_blocks, weights, bias_in, bias_oe):
    owners = len(seat_blocks)
    cap, width = seat_blocks[0].shape
    seats = owners * cap
    hidden = bias_in.shape[1]
    count = len(weights.arrays)
    shard = weights.arrays[0].shape[-2]
    whole = weights.places[0][0] is None
    step = width

    def kernel(*refs):
        refs = list(refs)
        me_ref = refs.pop(0)
        seat_refs = [refs.pop(0) for _ in range(owners)]
        w_refs = [refs.pop(0) for _ in range(count)]
        bin_ref, boe_ref = refs.pop(0), refs.pop(0)
        rows_out, h_out, slope_out = refs.pop(0), refs.pop(0), refs.pop(0)
        outs = [refs.pop(0) for _ in range(owners)]
        win, woe, sems, more_sems = refs
        targets = expert_targets(width, hidden, shard, whole, win, woe)
        left = fetch(w_refs, weights, me_ref[0], targets, 0, sems)
        right = fetch(w_refs, weights, me_ref[0], targets, 1, more_sems)
        start(left + right)
        rows = join(seat_refs)
        rows_out[...] = rows
        wait(left)
        total_out = None
        for at in range(0, hidden, step):
            pre = dot(rows, win[:, at : at + step]) + bin_ref[:, at : at + step]
            square = pre * pre
            bend = jnp.tanh(0.7978845608028654 * (pre + 0.044715 * square * pre))
            h = (0.5 * pre * (1.0 + bend)).astype(BF)
            slope = 0.5 * (1.0 + bend) + 0.5 * pre * (1.0 - bend * bend) * (
                0.7978845608028654 * (1.0 + 0.134145 * square)
            )
            h_out[:, at : at + step] = h
            slope_out[:, at : at + step] = slope.astype(BF)
            if at == 0:
                wait(right)
            piece = dot(h, woe[at : at + step, :])
            total_out = piece if total_out is None else total_out + piece
        part(total_out + boe_ref[...], outs)

    shapes = [
        sds((seats, width), BF),
        sds((seats, hidden), BF),
        sds((seats, hidden), BF),
    ] + [sds((cap, width), BF)] * owners
    result = call(
        kernel,
        "expert_fwd",
        [me, *seat_blocks, *weights.arrays, bias_in, bias_oe],
        [SM] + [VM] * owners + [ANY] * count + [VM] * 2,
        shapes,
        [VM] * len(shapes),
        [
            pltpu.VMEM((width, hidden), BF),
            pltpu.VMEM((hidden, width), BF),
            pltpu.SemaphoreType.DMA((copies_in(weights),)),
            pltpu.SemaphoreType.DMA((copies_in(weights),)),
        ],
    )
    return result[:3], result[3:]


def top_seats(cotangent, gates, cols, rows, cap, experts):
    tokens, width = cotangent.shape
    padded = cols.shape[0]

    def kernel(cot_ref, gates_ref, cols_ref, rows_ref, *refs):
        grad_out, *outs = refs
        grad_out[...] = jnp.zeros_like(grad_out)
        grad_out[0:tokens, :] = cot_ref[...].astype(F32)
        part(seat_grads(grad_out[...], gates_ref[...], cols_ref, rows_ref, cap * experts), outs)

    shapes = [sds((padded, width), F32)] + [sds((cap, width), BF)] * experts
    result = call(
        kernel,
        "top_seats",
        [cotangent, gates, cols, rows],
        [VM] * 4,
        shapes,
        [VM] * len(shapes),
        [],
    )
    return result[0], result[1:]


def gate_back(grad, x1, gates, cols, router, returned, tokens, last):
    padded, width = grad.shape
    owners = len(returned)

    def kernel(*refs):
        refs = list(refs)
        grad_ref = refs.pop(0)
        x1_ref = refs.pop(0) if last else None
        gates_ref, cols_ref, router_ref = (refs.pop(0) for _ in range(3))
        blocks = [refs.pop(0) for _ in range(owners)]
        dz_out, moe_out = refs.pop(0), refs.pop(0)
        back = join(blocks)
        grad_here = grad_ref[...]
        gates_here = gates_ref[...]
        lanes = lax.broadcasted_iota(jnp.int32, gates_here.shape, 1)
        d_gates = jnp.zeros_like(gates_here)
        mixed = x1_ref[...] if last else None
        for pair in range(2):
            piece = dot(one(seat_mask(cols_ref, pair, back.shape[0])), back)
            if last:
                mixed = mixed + pair_gate(gates_here, cols_ref, pair) * piece
            d_pair = jnp.sum(grad_here * piece, -1, keepdims=True)
            d_gates = d_gates + jnp.where(lanes == cols_ref[:, 2 + pair : 3 + pair], d_pair, 0.0)
        dz = gates_here * (d_gates - jnp.sum(d_gates * gates_here, -1, keepdims=True))
        dz_out[...] = dz
        high, low = split(dz)
        moe_out[...] = dot_nt(high, router_ref[...]) + dot_nt(low, router_ref[...])
        if last:
            refs.pop(0)[...] = mixed[0:tokens, :]

    shapes = [sds((padded, LANES), F32), sds((padded, width), F32)]
    if last:
        shapes.append(sds((tokens, width), F32))
    return call(
        kernel,
        "gate_back",
        [grad] + ([x1] if last else []) + [gates, cols, router, *returned],
        [VM] * (4 + owners + int(last)),
        shapes,
        [VM] * len(shapes),
        [],
    )


def expert_back(me, grad_blocks, slope, weights):
    owners = len(grad_blocks)
    cap, width = grad_blocks[0].shape
    seats, hidden = slope.shape
    count = len(weights.arrays)
    shard = weights.arrays[0].shape[-2]
    whole = weights.places[0][0] is None
    step = width

    def kernel(*refs):
        refs = list(refs)
        me_ref = refs.pop(0)
        seat_refs = [refs.pop(0) for _ in range(owners)]
        slope_ref = refs.pop(0)
        w_refs = [refs.pop(0) for _ in range(count)]
        grad_out, pre_out = refs.pop(0), refs.pop(0)
        outs = [refs.pop(0) for _ in range(owners)]
        win, woe, sems, more_sems = refs
        targets = expert_targets(width, hidden, shard, whole, win, woe)
        right = fetch(w_refs, weights, me_ref[0], targets, 1, sems)
        left = fetch(w_refs, weights, me_ref[0], targets, 0, more_sems)
        start(right + left)
        grad = join(seat_refs)
        grad_out[...] = grad
        wait(right)
        total_out = None
        for at in range(0, hidden, step):
            d_hidden = dot_nt(grad, woe[at : at + step, :])
            d_pre = (d_hidden * slope_ref[:, at : at + step].astype(F32)).astype(BF)
            pre_out[:, at : at + step] = d_pre
            if at == 0:
                wait(left)
            piece = dot_nt(d_pre, win[:, at : at + step])
            total_out = piece if total_out is None else total_out + piece
        part(total_out, outs)

    shapes = [sds((seats, width), BF), sds((seats, hidden), BF)]
    shapes += [sds((cap, width), BF)] * owners
    result = call(
        kernel,
        "expert_back",
        [me, *grad_blocks, slope, *weights.arrays],
        [SM] + [VM] * (owners + 1) + [ANY] * count,
        shapes,
        [VM] * len(shapes),
        [
            pltpu.VMEM((width, hidden), BF),
            pltpu.VMEM((hidden, width), BF),
            pltpu.SemaphoreType.DMA((copies_in(weights),)),
            pltpu.SemaphoreType.DMA((copies_in(weights),)),
        ],
    )
    return result[0], result[1], result[2:]


def spread(wide, index, outs, orders, rows, pieces, sems):
    copies = []
    for out, order in zip(outs, orders):
        for k, off in enumerate(order):
            for times, plus, first, size, into in pieces:
                place = pl.multiple_of((index ^ off) * times + plus, 16)
                copies.append(
                    pltpu.make_async_copy(
                        wide.at[pl.ds(place, rows), pl.ds(first, size)],
                        out.at[(k, *into)],
                        sems.at[len(copies)],
                    )
                )
    return copies


def column_sums(value):
    return dot(jnp.ones((8, value.shape[0]), BF), value)[0:1, :]


def expert_grads(rows_in, h, d_out, d_pre, shards, blocks):
    seats, width = rows_in.shape
    hidden = h.shape[1]
    per, shard = hidden // width, width // shards
    total = shards * (1 + per) if blocks else 2

    def kernel(rows_ref, h_ref, out_ref, pre_ref, *refs):
        refs = list(refs)
        outs = [refs.pop(0) for _ in range(1 if blocks else 2)]
        bias_ref, win, woe, sems = refs
        copies = []

        def send(source, target):
            copy = pltpu.make_async_copy(source, target, sems.at[len(copies)])
            copy.start()
            copies.append(copy)

        for k in range(per):
            here = slice(k * width, (k + 1) * width)
            woe[here, :] = dot_tn(h_ref[:, here], out_ref[...]).astype(BF)
            if blocks:
                for d in range(k * shards // per, (k + 1) * shards // per):
                    for q in range(per):
                        send(
                            woe.at[pl.ds((d * per + q) * shard, shard)],
                            outs[0].at[d, 1, :, pl.ds(q * width, width)],
                        )
        for k in range(per):
            here = slice(k * width, (k + 1) * width)
            win[:, here] = dot_tn(rows_ref[...], pre_ref[:, here]).astype(BF)
        if blocks:
            for d in range(shards):
                send(win.at[pl.ds(d * shard, shard)], outs[0].at[d, 0])
        else:
            send(win, outs[0])
            send(woe, outs[1])
        bias_ref[...] = jnp.zeros_like(bias_ref)
        sums = column_sums(pre_ref[...])
        for d in range(shards):
            for q in range(per):
                first = (d * per + q) * shard
                bias_ref[q : q + 1, d * shard : (d + 1) * shard] = sums[:, first : first + shard]
        bias_ref[per : per + 1, :] = column_sums(out_ref[...])
        wait(copies)

    if blocks:
        shapes = [sds((shards, 2, shard, hidden), BF)]
    else:
        shapes = [sds((width, hidden), BF), sds((hidden, width), BF)]
    result = call(
        kernel,
        "expert_grads",
        [rows_in, h, d_out, d_pre],
        [VM] * 4,
        shapes + [sds((8, width), F32)],
        [ANY] * len(shapes) + [VM],
        [
            pltpu.VMEM((width, hidden), BF),
            pltpu.VMEM((hidden, width), BF),
            pltpu.SemaphoreType.DMA((total,)),
        ],
    )
    return result[:-1], result[-1]


def attn_back(me, back_blocks, moe_part, grad, x, x1, qkv, cols, vecs, weights, below, tokens):
    padded, width = grad.shape
    owners = len(back_blocks)
    cap = back_blocks[0].shape[0]
    seats = owners * cap
    count = len(weights.arrays)
    shard = weights.arrays[0].shape[-2]

    def kernel(*refs):
        refs = list(refs)
        me_ref = refs.pop(0)
        back_refs = [refs.pop(0) for _ in range(owners)]
        part_ref, grad_ref, x_ref, x1_ref, qkv_ref, cols_ref, vec_ref = (
            refs.pop(0) for _ in range(7)
        )
        w_refs = [refs.pop(0) for _ in range(count)]
        if below is not None:
            gates_ref, below_cols, below_rows = (refs.pop(0) for _ in range(3))
        dx_out, dy_out, dqkv_out, small_out = (refs.pop(0) for _ in range(4))
        seat_outs = [refs.pop(0) for _ in range(owners)] if below is not None else None
        wqkv, wout, sems, more_sems = refs
        targets = attn_targets(width, shard, wqkv, wout)
        right = fetch(w_refs, weights, me_ref[0], targets, 1, sems)
        left = fetch(w_refs, weights, me_ref[0], targets, 0, more_sems)
        start(right + left)
        vec = lambda k: vec_ref[k : k + 1, :]
        chosen = jnp.logical_or(seat_mask(cols_ref, 0, seats), seat_mask(cols_ref, 1, seats))
        d_moe = dot(one(chosen), join(back_refs)) + part_ref[...]
        normed2, rstd2 = norm_rows(x1_ref[...])
        small_out[...] = jnp.zeros_like(small_out)
        small_out[1:2, :] = jnp.sum(d_moe * normed2, 0, keepdims=True)
        small_out[3:4, :] = jnp.sum(d_moe, 0, keepdims=True)
        d_x1 = grad_ref[...] + norm_back(d_moe * vec(1), normed2, rstd2)
        dy = d_x1.astype(BF)
        dy_out[...] = dy
        small_out[6:7, :] = jnp.sum(dy.astype(F32), 0, keepdims=True)
        wait(right)
        d_mixed = dot_nt(dy, wout[...]).astype(BF)
        masks = head_masks()
        scale = HEAD_DIM ** (-0.5)
        for two in range(HEADS // 2):
            at = two * 2 * HEAD_DIM
            query = qkv_ref[:, at : at + 2 * HEAD_DIM]
            keys = qkv_ref[:, width + at : width + at + 2 * HEAD_DIM]
            values = qkv_ref[:, 2 * width + at : 2 * width + at + 2 * HEAD_DIM]
            d_o = d_mixed[:, at : at + 2 * HEAD_DIM]
            sums = None
            for mask in masks:
                probs = head_probs(query, keys, mask, tokens)
                d_here = jnp.where(mask, d_o, 0).astype(BF)
                d_probs = dot_nt(d_here, values)
                d_values = dot_tn(probs.astype(BF), d_here)
                d_scores = probs * (d_probs - jnp.sum(d_probs * probs, -1, keepdims=True))
                d_scores = d_scores.astype(BF)
                d_query = dot(d_scores, jnp.where(mask, keys, 0).astype(BF))
                d_keys = dot_tn(d_scores, jnp.where(mask, query, 0).astype(BF))
                here = (d_query, d_keys, d_values)
                sums = here if sums is None else tuple(s + h for s, h in zip(sums, here))
            dqkv_out[:, at : at + 2 * HEAD_DIM] = (sums[0] * scale).astype(BF)
            dqkv_out[:, width + at : width + at + 2 * HEAD_DIM] = (sums[1] * scale).astype(BF)
            dqkv_out[:, 2 * width + at : 2 * width + at + 2 * HEAD_DIM] = sums[2].astype(BF)
        wait(left)
        d_normed = None
        for k in range(3):
            here = dqkv_out[:, k * width : (k + 1) * width]
            if k != 1:
                row = 4 if k == 0 else 5
                small_out[row : row + 1, :] = jnp.sum(here.astype(F32), 0, keepdims=True)
            piece = dot_nt(here, wqkv[:, k * width : (k + 1) * width])
            d_normed = piece if d_normed is None else d_normed + piece
        normed1, rstd1 = norm_rows(x_ref[...])
        small_out[0:1, :] = jnp.sum(d_normed * normed1, 0, keepdims=True)
        small_out[2:3, :] = jnp.sum(d_normed, 0, keepdims=True)
        d_x = d_x1 + norm_back(d_normed * vec(0), normed1, rstd1)
        dx_out[...] = d_x[0 : dx_out.shape[0], :]
        if below is not None:
            part(seat_grads(d_x, gates_ref[...], below_cols, below_rows, seats), seat_outs)

    shapes = [
        sds((padded if below is not None else tokens, width), F32),
        sds((padded, width), BF),
        sds((padded, 3 * width), BF),
        sds((16, width), F32),
    ]
    args = [me, *back_blocks, moe_part, grad, x, x1, qkv, cols, vecs, *weights.arrays]
    specs = [SM] + [VM] * (owners + 7) + [ANY] * count
    if below is not None:
        shapes += [sds((cap, width), BF)] * owners
        args += list(below)
        specs += [VM] * 3
    result = call(
        kernel,
        "attn_back",
        args,
        specs,
        shapes,
        [VM] * len(shapes),
        [
            pltpu.VMEM((width, 3 * width), BF),
            pltpu.VMEM((width, width), BF),
            pltpu.SemaphoreType.DMA((copies_in(weights),)),
            pltpu.SemaphoreType.DMA((copies_in(weights),)),
        ],
    )
    return result[:4], result[4:]


def attn_grads(me, z, a_low, o_low, moe_low, dqkv, dy, dz, small, biases, rows, order):
    padded, width = a_low.shape
    half = 2 * width + LANES
    total = 4 * len(order) if order else 2

    def kernel(
        me_ref, z_ref, a_ref, o_ref, moe_ref, dqkv_ref, dy_ref, dz_ref, small_ref, bias_ref, *refs
    ):
        refs = list(refs)
        outs = [refs.pop(0) for _ in range(2)]
        wide, tall, sems = refs
        for k in range(3):
            at = k * width + (LANES if k == 2 else 0)
            wide[:, at : at + width] = dot_tn(
                a_ref[...], dqkv_ref[:, k * width : (k + 1) * width]
            ).astype(BF)
        wide[:, 2 * width : half] = jnp.zeros((width, LANES), BF)
        wide[:, half + width : half + 2 * width] = dot_tn(o_ref[...], dy_ref[...]).astype(BF)
        high, low = split(dz_ref[...])
        d_router = dot_tn(moe_ref[...], high) + dot_tn(moe_ref[...], low)
        tall[...] = jnp.zeros_like(tall)
        tall[16:32, :] = small_ref[...]
        tall[pl.ds(pl.multiple_of(32 + 8 * z_ref[0], 8), 8), :] = bias_ref[...]
        wide[:, half + 2 * width : 2 * half] = (d_router + tall[...].T).astype(BF)
        if order:
            pieces = [(rows, 0, p * half, half, (p, ALL, ALL)) for p in range(2)]
            copies = spread(wide, me_ref[0], outs, (order, [o ^ 1 for o in order]), rows, pieces, sems)
        else:
            copies = [
                pltpu.make_async_copy(wide.at[:, pl.ds(p * half, half)], outs[p], sems.at[p])
                for p in range(2)
            ]
        start(copies)
        wait(copies)

    if order:
        shapes = [sds((len(order), 2, rows, half), BF)] * 2
    else:
        shapes = [sds((width, half), BF)] * 2
    return call(
        kernel,
        "attn_grads",
        [me, z, a_low, o_low, moe_low, dqkv, dy, dz, small, biases],
        [SM, SM] + [VM] * 8,
        shapes,
        [ANY] * 2,
        [
            pltpu.VMEM((width, 2 * half), BF),
            pltpu.VMEM((LANES, width), F32),
            pltpu.SemaphoreType.DMA((total,)),
        ],
    )


def small_out(smalls, z, experts, per):
    layers = len(smalls)
    shard = smalls[0].shape[0]

    def kernel(z_ref, *refs):
        ins = refs[:layers]
        gains, biases, router, bias_in, bias_oe, square = refs[layers:]
        for layer in range(layers):
            square[...] = jnp.zeros_like(square)
            square[0:shard, :] = ins[layer][...]
            square[...] = square[...].T
            router[layer] = square[0:experts, 0:shard]
            gains[layer] = square[16:18, 0:shard]
            for k in range(5):
                biases[k, layer : layer + 1, :] = square[18 + k : 19 + k, 0:shard]
            own = square[pl.ds(pl.multiple_of(32 + 8 * z_ref[0], 8), 8), :]
            for q in range(per):
                bias_in[layer, :, q * shard : (q + 1) * shard] = own[q : q + 1, 0:shard]
            bias_oe[layer] = own[per : per + 1, 0:shard]

    shapes = [
        sds((layers, 2, shard), F32),
        sds((5, layers, shard), F32),
        sds((layers, experts, shard), F32),
        sds((layers, 1, per * shard), F32),
        sds((layers, 1, shard), F32),
    ]
    return call(
        kernel,
        "small_out",
        [z, *smalls],
        [SM] + [VM] * layers,
        shapes,
        [VM] * 5,
        [pltpu.VMEM((LANES, LANES), F32)],
    )


def swap(value, axis, bit):
    size = lax.axis_size(axis)
    return lax.ppermute(value, axis, [(i, i ^ bit) for i in range(size)])


def exchange(blocks):
    order = sorted(range(1, len(blocks)), key=lambda k: -(k & 2))
    got = {k: swap(blocks[k], "expert", k) for k in order}
    return [blocks[0]] + [got[k] for k in range(1, len(blocks))]


def axis_bits(axis, bit):
    bits = []
    while bit < lax.axis_size(axis):
        bits.append(bit)
        bit *= 2
    return bits


def sum_experts(value):
    for bit in axis_bits("expert", 1):
        low = value.astype(BF)
        value = low.astype(F32) + swap(low, "expert", bit).astype(F32)
    return value


def gather_rows(shard):
    return lax.all_gather(shard, "dp", axis=0, tiled=True)


def scatter_rows(whole):
    return lax.psum_scatter(whole, "dp", scatter_dimension=0, tiled=True)


ORDER = [0, 2, 4, 6]


class Gather:
    def __init__(self, shard):
        self.shard = shard
        self.x, self.y = swap(shard, "dp", 2), swap(shard, "dp", 4)

    def turn(self):
        two, rows, width = self.shard.shape
        block = (two, rows, width)
        half = (1, rows, width)
        self.cut = move(
            "cut",
            [self.x, self.y, self.shard],
            [
                (0, (pl.ds(0, 1),), 0, (ALL,), half),
                (1, (pl.ds(1, 1),), 1, (ALL,), half),
                (0, (ALL,), 2, (1,), block),
                (1, (ALL,), 2, (2,), block),
                (2, (ALL,), 2, (0,), block),
            ],
            [sds(half, BF)] * 2 + [sds((3, *block), BF)],
        )

    def send(self, after=()):
        if after:
            self.cut = hold(self.cut, after)
        self.xy = swap(self.cut[0], "dp", 4), swap(self.cut[1], "dp", 2)
        self.other = swap(self.cut[2], "dp", 1)

    def cross(self, after=()):
        if after:
            self.xy = hold(self.xy, after)
        self.across = [swap(value, "dp", 1) for value in self.xy]

    def weights(self):
        pieces = [
            (self.shard, 0, (0, 1)),
            (self.x, 2, (0, 1)),
            (self.y, 4, (0, 1)),
            (self.xy[0], 6, (0,)),
            (self.xy[1], 6, (1,)),
            (self.across[0], 7, (0,)),
            (self.across[1], 7, (1,)),
            (self.other, (1, 3, 5), (0, 1)),
        ]
        return Weights([p[0] for p in pieces], [p[1:] for p in pieces])


def full(rows):
    return (pl.ds(0, rows), ALL)


class AttnSum:
    def __init__(self, grads, after=()):
        self.mine, theirs = grads
        if after:
            theirs = hold([theirs], after)[0]
        self.came = swap(theirs, "dp", 1)
        self.rows, self.width = self.mine.shape[2:]

    def fold0(self):
        shape = (self.rows, self.width)
        flat = full(self.rows)
        places = [(3, 0, 0, flat), (3, 1, 1, flat)]
        places += [(k, p, o, (p,)) for k, o in ((1, 2), (2, 3), (0, 4)) for p in range(2)]
        out = fold(
            "fold0",
            [self.mine, self.came],
            shape,
            [([(0, (k, p)), (1, (k, p))], BF, [(o, into, flat)]) for k, p, o, into in places],
            [sds(shape, BF)] * 2 + [sds((2, *shape), BF)] * 3,
        )
        self.across = out[:2]
        self.x, self.y, self.own = out[2:]

    def send_across(self):
        self.across = swap(self.across[0], "dp", 4), swap(self.across[1], "dp", 2)

    def fold1(self):
        self.x, self.y = fold1(self.x, self.y, self.across)
        self.came = swap(self.x, "dp", 2), swap(self.y, "dp", 4)

    def fold2(self):
        shape = (self.rows, self.width)
        flat = full(self.rows)
        self.parts = fold(
            "fold2",
            [self.own, *self.came],
            shape,
            [([(i, (p,)) for i in range(3)], BF, [(p, flat, flat)]) for p in range(2)],
            [sds(shape, BF)] * 2,
        )
        self.bits = axis_bits("expert", 1)
        self.send()

    def send(self):
        n = len(self.bits)
        up_bit = self.bits[self.done] if hasattr(self, "done") else self.bits[0]
        self.done = getattr(self, "done", 0)
        down_bit = self.bits[n - 1 - self.done]
        self.came = swap(self.parts[0], "expert", up_bit), swap(self.parts[1], "expert", down_bit)

    def fold3(self, layer, layers, given):
        shape = (self.rows, self.width)
        flat = full(self.rows)
        self.done += 1
        terms = [[(0, flat), (2, flat)], [(1, flat), (3, flat)]]
        args = [*self.parts, *self.came]
        if self.done < len(self.bits):
            self.parts = fold(
                "fold3",
                args,
                shape,
                [(terms[p], BF, [(p, flat, flat)]) for p in range(2)],
                [sds(shape, BF)] * 2,
                )
            self.send()
            return None
        wide = (self.width - LANES) // 2
        cut = lambda first, size: (ALL, pl.ds(first, size))
        tasks = [
            (terms[0], F32, [(0, (layer, ALL, pl.ds(0, 2 * wide)), cut(0, 2 * wide))]),
            (
                terms[1],
                F32,
                [
                    (0, (layer, ALL, pl.ds(2 * wide, wide)), cut(0, wide)),
                    (1, (layer,), cut(wide, wide)),
                    (2, flat, cut(2 * wide, LANES)),
                ],
            ),
        ]
        outs = [
            sds((layers, self.rows, 3 * wide), F32),
            sds((layers, self.rows, wide), F32),
            sds((self.rows, LANES), F32),
        ]
        aliases = {4: 0, 5: 1} if given else None
        return fold("attn_out", args + list(given), shape, tasks, outs, aliases)


def fold1(x, y, across):
    shape = x.shape[1:]
    flat = full(shape[0])
    return fold(
        "fold1",
        [x, y, *across],
        shape,
        [
            ([(0, (0,)), (2, flat)], BF, [(0, (0,), flat)]),
            ([(1, (1,)), (3, flat)], BF, [(1, (1,), flat)]),
        ],
        [sds(x.shape, BF)] * 2,
        {0: 0, 1: 1},
    )


def expert_out(total, layer, layers, given, width):
    rows, broad = total.shape[1:]
    per = broad // width
    second = [
        (1, (layer, 0, pl.ds(q * rows, rows)), (ALL, pl.ds(q * width, width))) for q in range(per)
    ]
    outs = [sds((layers, 1, rows, broad), F32), sds((layers, 1, per * rows, width), F32)]
    return fold(
        "expert_out",
        [total, *given],
        (rows, broad),
        [
            ([(0, (0,))], F32, [(0, (layer, 0), full(rows))]),
            ([(0, (1,))], F32, second),
        ],
        outs,
        {1: 0, 2: 1} if given else None,
    )


def per_device(
    image_tokens,
    norm_gains,
    biases,
    w_qkv,
    w_out,
    w_router,
    router_noise,
    w_in,
    b_in,
    w_outexp,
    b_expout,
    routes,
    seat_order,
    cotangent,
):
    layers = w_qkv.shape[0]
    tokens, width = image_tokens.shape
    experts = w_router.shape[2]
    shards = lax.axis_size("dp")
    assert tokens == SEQ and experts == lax.axis_size("expert")
    assert width == HEADS * HEAD_DIM
    padded = up(tokens, 16)
    cap = 2 * tokens // experts
    cap_pad = up(cap, 8)
    shard = w_qkv.shape[1]
    hidden_shard = w_outexp.shape[2]
    hidden = w_in.shape[3]
    per = hidden_shard // shard
    index = lax.axis_index("dp").astype(jnp.int32)
    me = index.reshape(1)
    z = lax.axis_index("expert").astype(jnp.int32).reshape(1)
    bits = axis_bits("dp", 2)
    four = bits == [2, 4] and shard % 16 == 0 and axis_bits("expert", 1) == [1, 2]
    order = ORDER if four else None

    Order.token = None

    def pack_attn(layer):
        return move(
            "pack_attn",
            [w_qkv, w_out],
            [
                (0, (layer, ALL, pl.ds(0, 2 * width)), 0, (0,), (shard, 2 * width)),
                (
                    0,
                    (layer, ALL, pl.ds(2 * width, width)),
                    0,
                    (1, ALL, pl.ds(0, width)),
                    (shard, width),
                ),
                (1, (layer,), 0, (1, ALL, pl.ds(width, width)), (shard, width)),
            ],
            [sds((2, shard, 2 * width), BF)],
        )[0]

    def pack_expert(layer):
        return move(
            "pack_expert",
            [w_in, w_outexp],
            [(0, (layer, 0), 0, (0,), (shard, hidden))]
            + [
                (
                    1,
                    (layer, 0, pl.ds(q * shard, shard)),
                    0,
                    (1, ALL, pl.ds(q * width, width)),
                    (shard, width),
                )
                for q in range(per)
            ],
            [sds((2, shard, hidden), BF)],
        )[0]

    aligned = shard % 16 == 0
    whole = [(None, (0,)), (None, (1,))]

    def fetch_attn(layer):
        if four:
            return Gather(pack_attn(layer))
        right = jnp.concatenate([w_qkv[layer][:, 2 * width :], w_out[layer]], 1)
        attn = [gather_rows(v)[None] for v in (w_qkv[layer][:, : 2 * width], right)]
        return Weights(attn, whole)

    def fetch_expert(layer):
        if aligned:
            both = lax.all_gather(pack_expert(layer), "dp", axis=0)
            return Weights([both], [(OWNERS, (0, 1))])
        both = [gather_rows(w_in[layer, 0])[None], gather_rows(w_outexp[layer, 0])[None]]
        return Weights(both, whole)

    def attn_weights(gathered):
        return gathered.weights() if four else gathered

    last = layers - 1
    attn_w = [fetch_attn(0)]
    expert_w = [fetch_expert(layer) for layer in range(layers)]
    cols, rows = place_pairs(
        routes, seat_order.reshape(layers, tokens, 2), padded, cap, cap_pad, z
    )
    small = pack_small(norm_gains, biases, w_router, b_in, b_expout)
    if four:
        attn_w[0].turn()
        attn_w[0].send()
    small = lax.all_gather(small, "dp", axis=0)
    params = unpack_small(small, layers, shard, per, experts)
    if last > 0:
        attn_w.append(fetch_attn(1))

    saved = []
    x_args = (image_tokens,)
    if four:
        attn_w[0].cross()
    for layer in range(layers):
        vecs, router, bias_in, bias_oe = params[layer]
        attn_w[layer] = attn_weights(attn_w[layer])
        kept, sent = attn_fwd(
            me,
            layer,
            x_args,
            attn_w[layer],
            vecs,
            router,
            router_noise,
            cols[layer],
            rows[layer],
            cap_pad,
        )
        sent = exchange(sent)
        if layer < last:
            if four:
                attn_w[layer + 1].turn()
                attn_w[layer + 1].send(sent[1:])
            if layer + 1 < last:
                attn_w.append(fetch_attn(layer + 2))
        else:
            grad, grad_seats = top_seats(
                cotangent, kept[5], cols[last], rows[last], cap_pad, experts
            )
            grad_seats = exchange(hold(grad_seats, sent[1:]))
        held, made = expert_fwd(me, sent, expert_w[layer], bias_in, bias_oe)
        if four and layer < last:
            attn_w[layer + 1].cross(made[:1])
        returned = exchange(made)
        saved.append((kept, held, returned))
        x_args = (kept[1], kept[5], cols[layer], returned)

    mixed = None
    attn_sums, expert_sums = [None] * layers, [None] * layers
    for layer in reversed(range(layers)):
        (x, x1, a_low, qkv, o_low, gates, moe_low), (seat_rows, h, slope), returned = saved[layer]
        vecs, router = params[layer][:2]

        def gate_part():
            return gate_back(
                grad, x1, gates, cols[layer], router, returned, tokens, layer == last
            )

        if layer < last:
            dz, moe_part = gate_part()
            if four:
                attn_sums[layer + 1] = AttnSum(g_attn, grad_seats[1:])
        d_out, d_pre, d_rows = expert_back(me, grad_seats, slope, expert_w[layer])
        d_back = exchange(d_rows)
        if layer == last:
            dz, moe_part, mixed = gate_part()
        g_expert, g_bias = expert_grads(seat_rows, h, d_out, d_pre, shards, aligned)
        held = list(g_expert)
        above = attn_sums[layer + 1] if four and layer < last else None
        if above:
            above.fold0()
            held += above.across
        held = hold(held, d_back[1:])
        g_expert = held[: len(g_expert)]
        if above:
            above.across = held[len(g_expert) :]
            above.send_across()
        if aligned:
            expert_sums[layer] = lax.psum_scatter(g_expert[0], "dp", scatter_dimension=0)
        else:
            expert_sums[layer] = [scatter_rows(v) for v in g_expert]
        below = None
        if layer > 0:
            below = (saved[layer - 1][0][5], cols[layer - 1], rows[layer - 1])
        (grad, dy, dqkv, small_grads), grad_seats = attn_back(
            me,
            d_back,
            moe_part,
            grad,
            x,
            x1,
            qkv,
            cols[layer],
            vecs,
            attn_w[layer],
            below,
            tokens,
        )
        grad_seats = exchange(grad_seats) if layer > 0 else None
        if above:
            above.fold1()
        g_attn = attn_grads(
            me, z, a_low, o_low, moe_low, dqkv, dy, dz, small_grads, g_bias, shard, order
        )
        if not four:
            attn_sums[layer] = [sum_experts(scatter_rows(v)) for v in g_attn]

    if four:
        done_attn, smalls = (), [None] * layers
        attn_sums[0] = AttnSum(g_attn)
        attn_sums[0].fold0()
        attn_sums[0].send_across()
        for layer in reversed(range(1, layers)):
            attn_sums[layer].fold2()
        attn_sums[0].fold1()
        for layer in reversed(range(1, layers)):
            attn_sums[layer].fold3(layer, layers, done_attn)
        attn_sums[0].fold2()
        for layer in reversed(range(1, layers)):
            out = attn_sums[layer].fold3(layer, layers, done_attn)
            done_attn, smalls[layer] = out[:2], out[2]
    if aligned:
        done_expert = ()
        for layer in reversed(range(layers)):
            done_expert = expert_out(expert_sums[layer], layer, layers, done_expert, width)
            if four and layer == 1:
                attn_sums[0].fold3(0, layers, done_attn)
        grad_in, grad_oe = done_expert
    else:
        grad_in = jnp.stack([item[0] for item in expert_sums])[:, None].astype(F32)
        grad_oe = jnp.stack([item[1] for item in expert_sums])[:, None].astype(F32)
    if four:
        out = attn_sums[0].fold3(0, layers, done_attn)
        (grad_qkv, grad_out), smalls[0] = out[:2], out[2]
    else:
        left = jnp.stack([item[0] for item in attn_sums])
        right = jnp.stack([item[1] for item in attn_sums])
        grad_qkv = jnp.concatenate([left[:, :, : 2 * width], right[:, :, :width]], 2)
        grad_out = right[:, :, width : 2 * width]
        smalls = [right[layer, :, 2 * width :] for layer in range(layers)]
    gains, shifts, grad_router, grad_bin, grad_boe = small_out(smalls, z, experts, per)
    return (
        mixed,
        grad,
        gains,
        jnp.transpose(shifts, (1, 0, 2)),
        grad_qkv,
        grad_out,
        jnp.transpose(grad_router, (0, 2, 1)),
        grad_in,
        grad_bin,
        grad_oe,
        grad_boe,
    )


def solution(mesh):
    return jax.shard_map(
        per_device,
        mesh=mesh,
        in_specs=(
            P(("dp", "expert"), None),
            P(None, None, "dp"),
            P(None, None, "dp"),
            P(None, "dp", None),
            P(None, "dp", None),
            P(None, "dp", None),
            P(None, ("dp", "expert"), None),
            P(None, "expert", "dp", None),
            P(None, "expert", "dp"),
            P(None, "expert", "dp", None),
            P(None, "expert", "dp"),
            P(None, ("dp", "expert"), None),
            P(None, ("dp", "expert"), None),
            P(("dp", "expert"), None),
        ),
        out_specs=(
            P(("dp", "expert"), None),
            P(("dp", "expert"), None),
            P(None, None, "dp"),
            P(None, None, "dp"),
            P(None, "dp", None),
            P(None, "dp", None),
            P(None, "dp", None),
            P(None, "expert", "dp", None),
            P(None, "expert", "dp"),
            P(None, "expert", "dp", None),
            P(None, "expert", "dp"),
        ),
        check_vma=False,
    )
```

time: 554 us -> 427 us (0.77)
  waiting for transfers between devices: 201 us -> 96.6 us
  Pallas kernels: 131 us -> 198 us
  other arithmetic: 47.7 us -> 0.02 us
  starting transfers between devices: 95 us -> 73.3 us
  blocking collectives: 36.6 us -> 17.2 us
  between operations: 2.25 us -> 15 us
  local copies, waits for them, and re-layouts: 35.9 us -> 23.7 us
    ppermute x88 -> x56, waiting for transfers between devices: 201 us -> 95.3 us  [swap(): return lax.ppermute(value, axis, [(i, i ^ bit) for i in range(size)])]
    pallas_call x15 -> x43, Pallas kernels: 131 us -> 198 us  [call(): pl.pallas_call(body, name=name, in_specs=list(specs) + [ANY] * len(after)...]
    unnamed x1 -> x0, blocking collectives: 22.9 us -> none
    ppermute x88 -> x56, starting transfers between devices: 95 us -> 72.9 us  [swap(): return lax.ppermute(value, axis, [(i, i ^ bit) for i in range(size)])]
    convert_element_type x24 -> x0, other arithmetic: 17 us -> none  [the longest x16 16.4 us: reduce_shards(): low = held.astype(BF)]
    concatenate x12 -> x0, other arithmetic: 11.7 us -> none  [the longest x8 10.2 us: gather(): held = jnp.concatenate([held, other], 0)]
    unnamed x169 -> x128, local copies, waits for them, and re-layouts: 12.6 us -> 22.9 us
    reduce_sum x1 -> x0, other arithmetic: 9.23 us -> none  [place_pairs(): rank = jnp.sum(jnp.logical_and(same, ahead).astype(jnp.int32), 2)]
  transfers between devices with their start and end apart: 88 -> 60, of which waited for: 30 -> 23; matrix products, arithmetic and copies ran while one was open for 13% -> 1% of each run, Pallas kernels for 24% -> 45%
where the time goes in v2:
time: 427 us; the launch traced here: 424 us
  Pallas kernels  198 us (46%)
  waiting for transfers between devices  96.6 us (23%)
  starting transfers between devices  73.3 us (17%)
  local copies, waits for them, and re-layouts  23.7 us (6%)
  blocking collectives  17.2 us (4%)
  between operations  15 us (4%)
    pallas_call x43, Pallas kernels, call(): pl.pallas_call(body, name=name, in_specs=list(specs) + [ANY] * len(after)...  198 us
    ppermute x56, waiting for transfers between devices, swap(): return lax.ppermute(value, axis, [(i, i ^ bit) for i in range(size)])  95.3 us
    ppermute x56, starting transfers between devices, swap(): return lax.ppermute(value, axis, [(i, i ^ bit) for i in range(size)])  72.9 us
    unnamed x128, local copies, waits for them, and re-layouts  22.9 us
    all_gather x1, blocking collectives, per_device(): small = lax.all_gather(small, 'dp', axis=0)  17.2 us
  transfers between devices with their start and end apart: 60, of which 23 were waited for; matrix products, arithmetic and copies ran while one was open for 1% of the time, Pallas kernels for 45%

profile of v2, /device:TPU:0, one launch (start us, length us, event | category | flops | bytes accessed | tf_op | source)
XLA Modules:
  0.0 423.6 jit_solution(13421370669942780856)
XLA Ops:
  21.3 3.4 place_pairs.1
  26.4 10.2 %collective-permute-done.1.refs_1_.refs_4_.refs_14_ = bf16[2,96,1536]{2,1,0:T(8,128)(2,1)S(1)} collective-permute-done((bf16[2,96,1536]{2,1,0:T(8,128)(2,1)S(1)}, bf16[2,96,1536]{2,1,0:T(8,128)(2,1)S(1)}, u32[]{:S(2)}, u32[]{:S(2)}) %collective-permute-start.1) | collective-permute-done | bytes 589856 | tf_op jit(solution)/shard_map/ppermute | solution.py:1045
  36.5 3.3 collective-permute-done.refs_0_.refs_3_.refs_13_
  46.2 17.2 %all-gather = f32[256,128]{1,0:T(8,128)} all-gather(f32[32,128]{1,0:T(8,128)} %pack_small.1.refs_3_), channel_id=2, replica_groups=mesh['dp'=8,'expert'=4] {'dp'}, dimensions={0}, use_global_device_ids=true | all-gather | bytes 147456 | tf_op jit(solution)/shard_map/all_gather | solution.py:1360
  72.8 8.3 %attn_fwd.2 = (f32[208,768]{1,0:T(8,128)}, f32[208,768]{1,0:T(8,128)}, bf16[208,768]{1,0:T(8,128)(2,1)}, bf16[208,2304]{1,0:T(8,128)(2,1)}, bf16[208,768]{1,0:T(...) custom-call(s32[1]{0:T(128)} %bitcast.refs_0_, ...), custom_call_target="tpu_custom_call" | custom-call | tf_op jit(solution)/shard_map/attn_fwd/pallas_call | solution.py:139
  82.5 3.2 collective-permute-start.8
  85.7 8.2 %collective-permute-done.11.refs_1_.refs_10_.refs_14_ = bf16[2,96,1536]{2,1,0:T(8,128)(2,1)S(1)} collective-permute-done((bf16[2,96,1536]{2,1,0:T(8,128)(2,1)}, bf16[2,96,1536]{2,1,0:T(8,128)(2,1)S(1)}, u32[]{:S(2)}, u32[]{:S(2)}) %collective-permute-start.11) | collective-permute-done | bytes 589856 | tf_op jit(solution)/shard_map/ppermute | solution.py:1045
  100.8 14.6 %expert_fwd.2 = (bf16[416,768]{1,0:T(8,128)(2,1)}, bf16[416,3072]{1,0:T(8,128)(2,1)}, bf16[416,3072]{1,0:T(8,128)(2,1)}, bf16[104,768]{1,0:T(8,128)(2,1)}, bf16[...) custom-call(s32[1]{0:T(128)} %bitcast.refs_0_, ...), custom_call_target="tpu_custom_call" | custom-call | tf_op jit(solution)/shard_map/expert_fwd/pallas_call | solution.py:139
  116.7 4.0 collective-permute-start.12
  123.2 4.5 %collective-permute-done.12.refs_5_ = bf16[104,768]{1,0:T(8,128)(2,1)S(1)} collective-permute-done((bf16[104,768]{1,0:T(8,128)(2,1)}, bf16[104,768]{1,0:T(8,128)(2,1)S(1)}, u32[]{:S(2)}, u32[]{:S(2)}) %collective-permute-start.12) | collective-permute-done | bytes 159776 | tf_op jit(solution)/shard_map/ppermute | solution.py:1045
  127.7 8.0 %collective-permute-done.13.refs_6_ = bf16[104,768]{1,0:T(8,128)(2,1)S(1)} collective-permute-done((bf16[104,768]{1,0:T(8,128)(2,1)}, bf16[104,768]{1,0:T(8,128)(2,1)S(1)}, u32[]{:S(2)}, u32[]{:S(2)}) %collective-permute-start.13) | collective-permute-done | bytes 159776 | tf_op jit(solution)/shard_map/ppermute | solution.py:1045
  136.8 8.7 %attn_fwd.3 = (f32[208,768]{1,0:T(8,128)}, f32[208,768]{1,0:T(8,128)}, bf16[208,768]{1,0:T(8,128)(2,1)}, bf16[208,2304]{1,0:T(8,128)(2,1)}, bf16[208,768]{1,0:T(...) custom-call(s32[1]{0:T(128)} %bitcast.refs_0_, ...), custom_call_target="tpu_custom_call" | custom-call | tf_op jit(solution)/shard_map/attn_fwd/pallas_call | solution.py:139
  153.7 9.1 %collective-permute-done.21.refs_5_.refs_3_ = bf16[104,768]{1,0:T(8,128)(2,1)S(1)} collective-permute-done((bf16[104,768]{1,0:T(8,128)(2,1)}, bf16[104,768]{1,0:T(8,128)(2,1)S(1)}, u32[]{:S(2)}, u32[]{:S(2)}) %collective-permute-start.21) | collective-permute-done | bytes 159776 | tf_op jit(solution)/shard_map/ppermute | solution.py:1045
  168.2 13.8 %expert_fwd.3 = (bf16[416,768]{1,0:T(8,128)(2,1)}, bf16[416,3072]{1,0:T(8,128)(2,1)}, bf16[416,3072]{1,0:T(8,128)(2,1)}, bf16[104,768]{1,0:T(8,128)(2,1)}, bf16[...) custom-call(s32[1]{0:T(128)} %bitcast.refs_0_, ...), custom_call_target="tpu_custom_call" | custom-call | tf_op jit(solution)/shard_map/expert_fwd/pallas_call | solution.py:139
  187.3 12.5 %expert_back.2 = (bf16[416,768]{1,0:T(8,128)(2,1)}, bf16[416,3072]{1,0:T(8,128)(2,1)}, bf16[104,768]{1,0:T(8,128)(2,1)}, bf16[104,768]{1,0:T(8,128)(2,1)}, bf16[...) custom-call(s32[1]{0:T(128)} %bitcast.refs_0_, bf16[104,768]{1,0:T(8,128)(2,1)} %get-tuple-element.203.refs_8_.refs_1_, ...), custom_call_target="tpu_custom_call" | custom-call | tf_op jit(solution)/shard_map/expert_back/pallas_call | solution.py:139
  205.0 3.8 gate_back.2
  208.7 11.7 %expert_grads.2 = (bf16[8,2,96,3072]{3,2,1,0:T(8,128)(2,1)}, f32[8,768]{1,0:T(8,128)}) custom-call(bf16[416,768]{1,0:T(8,128)(2,1)} %get-tuple-element.212.refs_7_.refs_0_, bf16[416,3072]{1,0:T(8,128)(2,1)} %get-tuple-element.221.refs_1_, bf16[416,768]{1,0:T(8,128)(2,1)} %get-tuple-element.213.refs_9_.refs_2_, bf16[416,3072]{1,0:T(8,128)(2,1)} %get-tuple-element.222.refs_3_, ...), custom_call_target="tpu_custom_call" | custom-call | tf_op jit(solution)/shard_map/expert_grads/pallas_call | solution.py:139
  221.5 14.4 %attn_back.2 = (f32[208,768]{1,0:T(8,128)}, bf16[208,768]{1,0:T(8,128)(2,1)}, bf16[208,2304]{1,0:T(8,128)(2,1)}, f32[16,768]{1,0:T(8,128)}, bf16[104,768]{1,0:T(...) custom-call(s32[1]{0:T(128)} %bitcast.refs_0_, ...), custom_call_target="tpu_custom_call" | custom-call | tf_op jit(solution)/shard_map/attn_back/pallas_call | solution.py:139
  240.4 5.7 %attn_grads.2 = (bf16[4,2,96,1664]{3,2,1,0:T(8,128)(2,1)}, bf16[4,2,96,1664]{3,2,1,0:T(8,128)(2,1)}) custom-call(s32[1]{0:T(128)} %bitcast.refs_0_, s32[1]{0:T(128)} %bitcast.1.refs_0_.refs_1_, bf16[208,768]{1,0:T(8,128)(2,1)} %get-tuple-element.230.refs_2_, bf16[208,768]{1,0:T(8,128)(2,1)} %get-tuple-element.231.refs_3_, ...), custom_call_target="tpu_custom_call" | custom-call | tf_op jit(solution)/shard_map/attn_grads/pallas_call | solution.py:139
  246.2 3.7 gate_back.3
  250.6 12.6 %expert_back.3 = (bf16[416,768]{1,0:T(8,128)(2,1)}, bf16[416,3072]{1,0:T(8,128)(2,1)}, bf16[104,768]{1,0:T(8,128)(2,1)}, bf16[104,768]{1,0:T(8,128)(2,1)}, bf16[...) custom-call(s32[1]{0:T(128)} %bitcast.refs_0_, bf16[104,768]{1,0:T(8,128)(2,1)} %get-tuple-element.225.refs_1_, ...), custom_call_target="tpu_custom_call" | custom-call | tf_op jit(solution)/shard_map/expert_back/pallas_call | solution.py:139
  267.6 11.8 %expert_grads.3 = (bf16[8,2,96,3072]{3,2,1,0:T(8,128)(2,1)}, f32[8,768]{1,0:T(8,128)}) custom-call(bf16[416,768]{1,0:T(8,128)(2,1)} %get-tuple-element.181.refs_3_.refs_0_, bf16[416,3072]{1,0:T(8,128)(2,1)} %get-tuple-element.247.refs_1_, bf16[416,768]{1,0:T(8,128)(2,1)} %get-tuple-element.248.refs_2_, bf16[416,3072]{1,0:T(8,128)(2,1)} %get-tuple-element.249.refs_3_), custom_call_target="tpu_custom_call" | custom-call | tf_op jit(solution)/shard_map/expert_grads/pallas_call | solution.py:139
  280.9 4.1 fold0.2
  288.5 13.6 %attn_back.3 = (f32[197,768]{1,0:T(8,128)}, bf16[208,768]{1,0:T(8,128)(2,1)}, bf16[208,2304]{1,0:T(8,128)(2,1)}, f32[16,768]{1,0:T(8,128)}) custom-call(s32[1]{0:T(128)} %bitcast.refs_0_, bf16[104,768]{1,0:T(8,128)(2,1)} %get-tuple-element.241.refs_1_, bf16[104,768]{1,0:T(8,128)(2,1)} %copy-done.28, bf16[104,768]{1,0:T(8,128)(2,1)} %copy-done.29, ...), custom_call_target="tpu_custom_call" | custom-call | tf_op jit(solution)/shard_map/attn_back/pallas_call | solution.py:139
  305.1 5.8 %attn_grads.3 = (bf16[4,2,96,1664]{3,2,1,0:T(8,128)(2,1)}, bf16[4,2,96,1664]{3,2,1,0:T(8,128)(2,1)}) custom-call(s32[1]{0:T(128)} %bitcast.refs_0_, s32[1]{0:T(128)} %bitcast.1.refs_0_.refs_1_, bf16[208,768]{1,0:T(8,128)(2,1)} %get-tuple-element.255.refs_2_, bf16[208,768]{1,0:T(8,128)(2,1)} %get-tuple-element.256.refs_3_, ...), custom_call_target="tpu_custom_call" | custom-call | tf_op jit(solution)/shard_map/attn_grads/pallas_call | solution.py:139
  317.6 5.1 %fold0.3 = (bf16[96,1664]{1,0:T(8,128)(2,1)}, bf16[96,1664]{1,0:T(8,128)(2,1)}, bf16[2,96,1664]{2,1,0:T(8,128)(2,1)}, bf16[2,96,1664]{2,1,0:T(8,128)(2,1)}, bf16[2,96,1664]{2,1,0:T(8,128)(2,1)}) custom-call(bf16[4,2,96,1664]{3,2,1,0:T(8,128)(2,1)} %get-tuple-element.267.refs_0_, bf16[4,2,96,1664]{3,2,1,0:T(8,128)(2,1)} %copy-done.11), custom_call_target="tpu_custom_call" | custom-call | tf_op jit(solution)/shard_map/fold0/pallas_call | solution.py:139
  325.0 3.4 collective-permute-done.45.refs_2_
  332.1 3.7 collective-permute-done.43.refs_3_
  344.2 12.9 %collective-permute-done.49.refs_3_ = bf16[96,1664]{1,0:T(8,128)(2,1)S(1)} collective-permute-done((bf16[96,1664]{1,0:T(8,128)(2,1)}, bf16[96,1664]{1,0:T(8,128)(2,1)S(1)}, u32[]{:S(2)}, u32[]{:S(2)}) %collective-permute-start.49) | collective-permute-done | bytes 319520 | tf_op jit(solution)/shard_map/ppermute | solution.py:1045
  363.6 5.8 %collective-permute-done.47.refs_2_ = bf16[2,96,1664]{2,1,0:T(8,128)(2,1)S(1)} collective-permute-done((bf16[2,96,1664]{2,1,0:T(8,128)(2,1)}, bf16[2,96,1664]{2,1,0:T(8,128)(2,1)S(1)}, u32[]{:S(2)}, u32[]{:S(2)}) %collective-permute-start.47) | collective-permute-done | bytes 639008 | tf_op jit(solution)/shard_map/ppermute | solution.py:1045
  377.2 8.4 %collective-permute-done.52.refs_2_ = bf16[96,1664]{1,0:T(8,128)(2,1)S(1)} collective-permute-done((bf16[96,1664]{1,0:T(8,128)(2,1)}, bf16[96,1664]{1,0:T(8,128)(2,1)S(1)}, u32[]{:S(2)}, u32[]{:S(2)}) %collective-permute-start.52) | collective-permute-done | bytes 319520 | tf_op jit(solution)/shard_map/ppermute | solution.py:1045
  401.8 8.5 %collective-permute-done.55.refs_3_ = bf16[96,1664]{1,0:T(8,128)(2,1)S(1)} collective-permute-done((bf16[96,1664]{1,0:T(8,128)(2,1)}, bf16[96,1664]{1,0:T(8,128)(2,1)S(1)}, u32[]{:S(2)}, u32[]{:S(2)}) %collective-permute-start.55) | collective-permute-done | bytes 319520 | tf_op jit(solution)/shard_map/ppermute | solution.py:1045
  (266 shorter events, 144.7 us)
Async XLA Ops:
  7.2 93.6 %all-gather.6.cloned.1.call-start = ((), (), s32[]{:S(2)}) async-start(), calls=%async_computation.4 | async-start | bytes 10616832 | tf_op jit(solution)/shard_map/all_gather | solution.py:1342
  11.3 156.9 %all-gather.8.cloned.1.call-start = ((), (), s32[]{:S(2)}) async-start(), calls=%async_computation.5 | async-start | bytes 10616832 | tf_op jit(solution)/shard_map/all_gather | solution.py:1342
  13.6 374.9 %reduce-scatter.3.cloned.1.call-start = ((), (), s32[]{:S(2)}) async-start(), calls=%async_computation.2 | async-start | bytes 10616832 | tf_op jit(solution)/shard_map/reduce_scatter | solution.py:1434
  13.7 22.8 %collective-permute-start.1 = (bf16[2,96,1536]{2,1,0:T(8,128)(2,1)S(1)}, bf16[2,96,1536]{2,1,0:T(8,128)(2,1)S(1)}, u32[]{:S(2)}, u32[]{:S(2)}) collective-permute-start(bf16[2,96,1536]{2,1,0:T(8,128)(2,1)S(1)} %copy-done), channel_id=1, source_target_pairs={{0,16},{4,20},{8,24},{12,28},{16,0},{20,4},{24,8},{28,12},{1,17},{... | collective-permute-start | bytes 1769480 | tf_op jit(solution)/shard_map/ppermute | solution.py:1045
  16.7 23.1 %collective-permute-start = (bf16[2,96,1536]{2,1,0:T(8,128)(2,1)S(1)}, bf16[2,96,1536]{2,1,0:T(8,128)(2,1)S(1)}, u32[]{:S(2)}, u32[]{:S(2)}) collective-permute-start(bf16[2,96,1536]{2,1,0:T(8,128)(2,1)S(1)} %copy-done), channel_id=1, source_target_pairs={{0,8},{4,12},{8,0},{12,4},{16,24},{20,28},{24,16},{28,20},{1,9},{5... | collective-permute-start | bytes 1769480 | tf_op jit(solution)/shard_map/ppermute | solution.py:1045
  43.5 28.0 %collective-permute-start.6 = (bf16[3,2,96,1536]{3,2,1,0:T(8,128)(2,1)}, bf16[3,2,96,1536]{3,2,1,0:T(8,128)(2,1)S(1)}, u32[]{:S(2)}, u32[]{:S(2)}) collective-permute-start(bf16[3,2,96,1536]{3,2,1,0:T(8,128)(2,1)} %get-tuple-element.159), channel_id=1, source_target_pairs={{0,4},{4,0},{8,12},{12,8},{16,20},{20,16},{24,28},{28,24},{1,5},{5... | collective-permute-start | bytes 5308424 | tf_op jit(solution)/shard_map/ppermute | solution.py:1045
  43.6 25.8 %collective-permute-start.3 = (bf16[1,96,1536]{2,1,0:T(8,128)(2,1)}, bf16[1,96,1536]{2,1,0:T(8,128)(2,1)S(1)}, u32[]{:S(2)}, u32[]{:S(2)}) collective-permute-start(bf16[1,96,1536]{2,1,0:T(8,128)(2,1)} %get-tuple-element.158), channel_id=1, source_target_pairs={{0,8},{4,12},{8,0},{12,4},{16,24},{20,28},{24,16},{28,20},{1,9},{5... | collective-permute-start | bytes 884744 | tf_op jit(solution)/shard_map/ppermute | solution.py:1045
  46.2 23.3 %collective-permute-start.2 = (bf16[1,96,1536]{2,1,0:T(8,128)(2,1)}, bf16[1,96,1536]{2,1,0:T(8,128)(2,1)S(1)}, u32[]{:S(2)}, u32[]{:S(2)}) collective-permute-start(bf16[1,96,1536]{2,1,0:T(8,128)(2,1)} %get-tuple-element.157.refs_1_), channel_id=1, source_target_pairs={{0,16},{4,20},{8,24},{12,28},{16,0},{20,4},{24,8},{28,12},{1,17},{... | collective-permute-start | bytes 884744 | tf_op jit(solution)/shard_map/ppermute | solution.py:1045
  67.1 26.8 %collective-permute-start.11 = (bf16[2,96,1536]{2,1,0:T(8,128)(2,1)}, bf16[2,96,1536]{2,1,0:T(8,128)(2,1)S(1)}, u32[]{:S(2)}, u32[]{:S(2)}) collective-permute-start(bf16[2,96,1536]{2,1,0:T(8,128)(2,1)} %pack_attn.3.refs_15_.refs_2_.refs_8_.refs_12_), channel_id=1, source_target_pairs={{0,16},{4,20},{8,24},{12,28},{16,0},{20,4},{24,8},{28,12},{1,17},{... | collective-permute-start | bytes 1769480 | tf_op jit(solution)/shard_map/ppermute | solution.py:1045
  69.3 24.6 %collective-permute-start.10 = (bf16[2,96,1536]{2,1,0:T(8,128)(2,1)}, bf16[2,96,1536]{2,1,0:T(8,128)(2,1)S(1)}, u32[]{:S(2)}, u32[]{:S(2)}) collective-permute-start(bf16[2,96,1536]{2,1,0:T(8,128)(2,1)} %pack_attn.3.refs_15_.refs_2_.refs_8_.refs_12_), channel_id=1, source_target_pairs={{0,8},{4,12},{8,0},{12,4},{16,24},{20,28},{24,16},{28,20},{1,9},{5... | collective-permute-start | bytes 1769480 | tf_op jit(solution)/shard_map/ppermute | solution.py:1045
  98.6 23.1 %collective-permute-start.19 = (bf16[3,2,96,1536]{3,2,1,0:T(8,128)(2,1)}, bf16[3,2,96,1536]{3,2,1,0:T(8,128)(2,1)S(1)}, u32[]{:S(2)}, u32[]{:S(2)}) collective-permute-start(bf16[3,2,96,1536]{3,2,1,0:T(8,128)(2,1)} %get-tuple-element.184), channel_id=1, source_target_pairs={{0,4},{4,0},{8,12},{12,8},{16,20},{20,16},{24,28},{28,24},{1,5},{5... | collective-permute-start | bytes 5308424 | tf_op jit(solution)/shard_map/ppermute | solution.py:1045
  116.2 19.5 %collective-permute-start.17 = (bf16[1,96,1536]{2,1,0:T(8,128)(2,1)}, bf16[1,96,1536]{2,1,0:T(8,128)(2,1)S(1)}, u32[]{:S(2)}, u32[]{:S(2)}) collective-permute-start(bf16[1,96,1536]{2,1,0:T(8,128)(2,1)} %get-tuple-element.182.refs_11_.refs_15_), channel_id=1, source_target_pairs={{0,4},{4,0},{8,12},{12,8},{16,20},{20,16},{24,28},{28,24},{1,5},{5... | collective-permute-start | bytes 884744 | tf_op jit(solution)/shard_map/ppermute | solution.py:1045
  116.5 19.3 %collective-permute-start.18 = (bf16[1,96,1536]{2,1,0:T(8,128)(2,1)}, bf16[1,96,1536]{2,1,0:T(8,128)(2,1)S(1)}, u32[]{:S(2)}, u32[]{:S(2)}) collective-permute-start(bf16[1,96,1536]{2,1,0:T(8,128)(2,1)} %get-tuple-element.183.refs_12_.refs_16_), channel_id=1, source_target_pairs={{0,4},{4,0},{8,12},{12,8},{16,20},{20,16},{24,28},{28,24},{1,5},{5... | collective-permute-start | bytes 884744 | tf_op jit(solution)/shard_map/ppermute | solution.py:1045
  163.6 21.5 %collective-permute-start.26 = (bf16[104,768]{1,0:T(8,128)(2,1)}, bf16[104,768]{1,0:T(8,128)(2,1)S(1)}, u32[]{:S(2)}, u32[]{:S(2)}) collective-permute-start(bf16[104,768]{1,0:T(8,128)(2,1)} %get-tuple-element.208), channel_id=1, source_target_pairs={{0,1},{1,0},{2,3},{3,2},{4,5},{5,4},{6,7},{7,6},{8,9},{9,8},{10,11... | collective-permute-start | bytes 479240 | tf_op jit(solution)/shard_map/ppermute | solution.py:1045
  165.8 20.7 %collective-permute-start.27 = (bf16[104,768]{1,0:T(8,128)(2,1)}, bf16[104,768]{1,0:T(8,128)(2,1)S(1)}, u32[]{:S(2)}, u32[]{:S(2)}) collective-permute-start(bf16[104,768]{1,0:T(8,128)(2,1)} %get-tuple-element.209), channel_id=1, source_target_pairs={{0,2},{1,3},{2,0},{3,1},{4,6},{5,7},{6,4},{7,5},{8,10},{9,11},{10,... | collective-permute-start | bytes 479240 | tf_op jit(solution)/shard_map/ppermute | solution.py:1045
  166.8 19.8 %collective-permute-start.28 = (bf16[104,768]{1,0:T(8,128)(2,1)}, bf16[104,768]{1,0:T(8,128)(2,1)S(1)}, u32[]{:S(2)}, u32[]{:S(2)}) collective-permute-start(bf16[104,768]{1,0:T(8,128)(2,1)} %get-tuple-element.210), channel_id=1, source_target_pairs={{0,3},{1,2},{2,1},{3,0},{4,7},{5,6},{6,5},{7,4},{8,11},{9,10},{10,... | collective-permute-start | bytes 479240 | tf_op jit(solution)/shard_map/ppermute | solution.py:1045
  182.1 20.7 %collective-permute-start.23 = (bf16[104,768]{1,0:T(8,128)(2,1)}, bf16[104,768]{1,0:T(8,128)(2,1)S(1)}, u32[]{:S(2)}, u32[]{:S(2)}) collective-permute-start(bf16[104,768]{1,0:T(8,128)(2,1)} %get-tuple-element.205), channel_id=1, source_target_pairs={{0,1},{1,0},{2,3},{3,2},{4,5},{5,4},{6,7},{7,6},{8,9},{9,8},{10,11... | collective-permute-start | bytes 479240 | tf_op jit(solution)/shard_map/ppermute | solution.py:1045
  183.2 21.0 %collective-permute-start.24 = (bf16[104,768]{1,0:T(8,128)(2,1)}, bf16[104,768]{1,0:T(8,128)(2,1)S(1)}, u32[]{:S(2)}, u32[]{:S(2)}) collective-permute-start(bf16[104,768]{1,0:T(8,128)(2,1)} %get-tuple-element.206), channel_id=1, source_target_pairs={{0,2},{1,3},{2,0},{3,1},{4,6},{5,7},{6,4},{7,5},{8,10},{9,11},{10,... | collective-permute-start | bytes 479240 | tf_op jit(solution)/shard_map/ppermute | solution.py:1045
  185.1 19.2 %collective-permute-start.25 = (bf16[104,768]{1,0:T(8,128)(2,1)}, bf16[104,768]{1,0:T(8,128)(2,1)S(1)}, u32[]{:S(2)}, u32[]{:S(2)}) collective-permute-start(bf16[104,768]{1,0:T(8,128)(2,1)} %get-tuple-element.207), channel_id=1, source_target_pairs={{0,3},{1,2},{2,1},{3,0},{4,7},{5,6},{6,5},{7,4},{8,11},{9,10},{10,... | collective-permute-start | bytes 479240 | tf_op jit(solution)/shard_map/ppermute | solution.py:1045
  199.8 20.7 %collective-permute-start.29 = (bf16[104,768]{1,0:T(8,128)(2,1)}, bf16[104,768]{1,0:T(8,128)(2,1)S(1)}, u32[]{:S(2)}, u32[]{:S(2)}) collective-permute-start(bf16[104,768]{1,0:T(8,128)(2,1)} %get-tuple-element.216), channel_id=1, source_target_pairs={{0,1},{1,0},{2,3},{3,2},{4,5},{5,4},{6,7},{7,6},{8,9},{9,8},{10,11... | collective-permute-start | bytes 479240 | tf_op jit(solution)/shard_map/ppermute | solution.py:1045
  200.0 20.5 %collective-permute-start.30 = (bf16[104,768]{1,0:T(8,128)(2,1)}, bf16[104,768]{1,0:T(8,128)(2,1)S(1)}, u32[]{:S(2)}, u32[]{:S(2)}) collective-permute-start(bf16[104,768]{1,0:T(8,128)(2,1)} %get-tuple-element.217), channel_id=1, source_target_pairs={{0,2},{1,3},{2,0},{3,1},{4,6},{5,7},{6,4},{7,5},{8,10},{9,11},{10,... | collective-permute-start | bytes 479240 | tf_op jit(solution)/shard_map/ppermute | solution.py:1045
  202.8 17.7 %collective-permute-start.31 = (bf16[104,768]{1,0:T(8,128)(2,1)}, bf16[104,768]{1,0:T(8,128)(2,1)S(1)}, u32[]{:S(2)}, u32[]{:S(2)}) collective-permute-start(bf16[104,768]{1,0:T(8,128)(2,1)} %get-tuple-element.218), channel_id=1, source_target_pairs={{0,3},{1,2},{2,1},{3,0},{4,7},{5,6},{6,5},{7,4},{8,11},{9,10},{10,... | collective-permute-start | bytes 479240 | tf_op jit(solution)/shard_map/ppermute | solution.py:1045
  221.3 177.9 %reduce-scatter.5.cloned.1.call-start = ((), (), s32[]{:S(2)}) async-start(), calls=%async_computation.3 | async-start | bytes 10616832 | tf_op jit(solution)/shard_map/reduce_scatter | solution.py:1434
  250.6 28.8 %collective-permute-start.38 = (bf16[4,2,96,1664]{3,2,1,0:T(8,128)(2,1)}, bf16[4,2,96,1664]{3,2,1,0:T(8,128)(2,1)S(1)}, u32[]{:S(2)}, u32[]{:S(2)}) collective-permute-start(bf16[4,2,96,1664]{3,2,1,0:T(8,128)(2,1)} %hold.10.refs_7_), channel_id=1, source_target_pairs={{0,4},{4,0},{8,12},{12,8},{16,20},{20,16},{24,28},{28,24},{1,5},{5... | collective-permute-start | bytes 7667720 | tf_op jit(solution)/shard_map/ppermute | solution.py:1045
  263.2 21.9 %collective-permute-start.35 = (bf16[104,768]{1,0:T(8,128)(2,1)}, bf16[104,768]{1,0:T(8,128)(2,1)S(1)}, u32[]{:S(2)}, u32[]{:S(2)}) collective-permute-start(bf16[104,768]{1,0:T(8,128)(2,1)} %get-tuple-element.242), channel_id=1, source_target_pairs={{0,1},{1,0},{2,3},{3,2},{4,5},{5,4},{6,7},{7,6},{8,9},{9,8},{10,11... | collective-permute-start | bytes 479240 | tf_op jit(solution)/shard_map/ppermute | solution.py:1045
  263.7 21.4 %collective-permute-start.36 = (bf16[104,768]{1,0:T(8,128)(2,1)}, bf16[104,768]{1,0:T(8,128)(2,1)S(1)}, u32[]{:S(2)}, u32[]{:S(2)}) collective-permute-start(bf16[104,768]{1,0:T(8,128)(2,1)} %get-tuple-element.243), channel_id=1, source_target_pairs={{0,2},{1,3},{2,0},{3,1},{4,6},{5,7},{6,4},{7,5},{8,10},{9,11},{10,... | collective-permute-start | bytes 479240 | tf_op jit(solution)/shard_map/ppermute | solution.py:1045
  265.5 19.6 %collective-permute-start.37 = (bf16[104,768]{1,0:T(8,128)(2,1)}, bf16[104,768]{1,0:T(8,128)(2,1)S(1)}, u32[]{:S(2)}, u32[]{:S(2)}) collective-permute-start(bf16[104,768]{1,0:T(8,128)(2,1)} %get-tuple-element.244), channel_id=1, source_target_pairs={{0,3},{1,2},{2,1},{3,0},{4,7},{5,6},{6,5},{7,4},{8,11},{9,10},{10,... | collective-permute-start | bytes 479240 | tf_op jit(solution)/shard_map/ppermute | solution.py:1045
  311.1 17.4 %collective-permute-start.45 = (bf16[2,96,1664]{2,1,0:T(8,128)(2,1)S(1)}, bf16[2,96,1664]{2,1,0:T(8,128)(2,1)}, u32[]{:S(2)}, u32[]{:S(2)}) collective-permute-start(bf16[2,96,1664]{2,1,0:T(8,128)(2,1)S(1)} %copy-done.19), channel_id=1, source_target_pairs={{0,16},{4,20},{8,24},{12,28},{16,0},{20,4},{24,8},{28,12},{1,17},{... | collective-permute-start | bytes 1916936 | tf_op jit(solution)/shard_map/ppermute | solution.py:1045
  338.7 30.6 %collective-permute-start.47 = (bf16[2,96,1664]{2,1,0:T(8,128)(2,1)}, bf16[2,96,1664]{2,1,0:T(8,128)(2,1)S(1)}, u32[]{:S(2)}, u32[]{:S(2)}) collective-permute-start(bf16[2,96,1664]{2,1,0:T(8,128)(2,1)} %get-tuple-element.278), channel_id=1, source_target_pairs={{0,16},{4,20},{8,24},{12,28},{16,0},{20,4},{24,8},{28,12},{1,17},{... | collective-permute-start | bytes 1916936 | tf_op jit(solution)/shard_map/ppermute | solution.py:1045
  339.5 30.6 %collective-permute-start.46 = (bf16[2,96,1664]{2,1,0:T(8,128)(2,1)}, bf16[2,96,1664]{2,1,0:T(8,128)(2,1)S(1)}, u32[]{:S(2)}, u32[]{:S(2)}) collective-permute-start(bf16[2,96,1664]{2,1,0:T(8,128)(2,1)} %get-tuple-element.277.refs_4_), channel_id=1, source_target_pairs={{0,8},{4,12},{8,0},{12,4},{16,24},{20,28},{24,16},{28,20},{1,9},{5... | collective-permute-start | bytes 1916936 | tf_op jit(solution)/shard_map/ppermute | solution.py:1045
  360.8 24.7 %collective-permute-start.52 = (bf16[96,1664]{1,0:T(8,128)(2,1)}, bf16[96,1664]{1,0:T(8,128)(2,1)S(1)}, u32[]{:S(2)}, u32[]{:S(2)}) collective-permute-start(bf16[96,1664]{1,0:T(8,128)(2,1)} %get-tuple-element.280.refs_3_.refs_0_), channel_id=1, source_target_pairs={{0,2},{1,3},{2,0},{3,1},{4,6},{5,7},{6,4},{7,5},{8,10},{9,11},{10,... | collective-permute-start | bytes 958472 | tf_op jit(solution)/shard_map/ppermute | solution.py:1045
  373.2 18.8 %collective-permute-start.51 = (bf16[96,1664]{1,0:T(8,128)(2,1)}, bf16[96,1664]{1,0:T(8,128)(2,1)S(1)}, u32[]{:S(2)}, u32[]{:S(2)}) collective-permute-start(bf16[96,1664]{1,0:T(8,128)(2,1)} %get-tuple-element.282.refs_1_), channel_id=1, source_target_pairs={{0,2},{1,3},{2,0},{3,1},{4,6},{5,7},{6,4},{7,5},{8,10},{9,11},{10,... | collective-permute-start | bytes 958472 | tf_op jit(solution)/shard_map/ppermute | solution.py:1045
  (90 other events, 549.3 us)
Sparse Core Ops, SparseCore 0:
  11.4 82.3 all-gather.5
  95.6 62.7 all-gather.7
  221.4 81.3 reduce-scatter.2
  306.1 92.9 reduce-scatter.4

commit v3 on v2

--- a/solution.py
+++ b/solution.py
@@ -91,13 +91,44 @@
     return total
 
 
-def seat_grads(grad, gates, cols_ref, rows_ref, seats):
-    total = None
-    for pair in range(2):
-        scaled = (pair_gate(gates, cols_ref, pair) * grad).astype(BF)
-        piece = dot(one(token_mask(rows_ref, pair, seats)), scaled)
-        total = piece if total is None else total + piece
-    return total
+def rows_to_seats(rows_ref, seats, values):
+    chosen = jnp.logical_or(token_mask(rows_ref, 0, seats), token_mask(rows_ref, 1, seats))
+    return dot(one(chosen), values)
+
+
+def with_note(block, cap, note):
+    base = cap // 8 * 8
+    tail = block[base:]
+    left = tail[:, 0:LANES]
+    row = lax.broadcasted_iota(jnp.int32, left.shape, 0)
+    high = note.astype(BF).astype(F32)
+    left = jnp.where(row == cap - base, high, left)
+    left = jnp.where(row == cap - base + 1, note - high, left)
+    return jnp.concatenate([block[:base], jnp.concatenate([left, tail[:, LANES:]], 1)], 0)
+
+
+def note_of(block, cap):
+    return block[cap : cap + 1, 0:LANES] + block[cap + 1 : cap + 2, 0:LANES]
+
+
+def as_column(note, rows):
+    shape = (rows, LANES)
+    same = lax.broadcasted_iota(jnp.int32, shape, 0) == lax.broadcasted_iota(jnp.int32, shape, 1)
+    return jnp.sum(jnp.where(same, note, 0.0), -1, keepdims=True)
+
+
+def lane_sums(value):
+    rows, width = value.shape
+    value = jnp.concatenate([value, jnp.zeros((LANES - rows, width), F32)], 0)
+    ones = jnp.ones((8, width), BF)
+    high, low = split(value)
+    return (dot_nt(ones, high) + dot_nt(ones, low))[0:1, :]
+
+
+def near_lanes(cols_ref, pair, block, cap_pad):
+    column = cols_ref[:, pair : pair + 1] - block * cap_pad
+    lanes = lax.broadcasted_iota(jnp.int32, (column.shape[0], LANES), 1)
+    return jnp.logical_and(lanes == column, lanes < cap_pad)
 
 
 def head_masks():
@@ -127,22 +158,97 @@
     token = None
 
 
+LOAD = "load"
+STORE = "store"
+
+
+class Load:
+    def __init__(self, source, held, sem):
+        self.copy, self.held, self.came = pltpu.make_async_copy(source, held, sem), held, False
+        self.shape = held.shape
+        self.copy.start()
+
+    def wait(self):
+        if not self.came:
+            self.copy.wait()
+            self.came = True
+
+    def __getitem__(self, index):
+        self.wait()
+        return self.held[index]
+
+
+class Store:
+    def __init__(self, target, held, sems):
+        self.target, self.held, self.sems, self.copies = target, held, sems, []
+        self.shape, self.dtype = held.shape, held.dtype
+
+    def __getitem__(self, index):
+        return self.held[index]
+
+    def __setitem__(self, index, value):
+        self.held[index] = value
+
+    def send(self, *index):
+        number = len(self.copies)
+        copy = pltpu.make_async_copy(
+            self.held.at[index], self.target.at[index], self.sems.at[number]
+        )
+        copy.start()
+        self.copies.append(copy)
+
+    def finish(self):
+        if not self.copies:
+            self.send(*[slice(None)] * len(self.shape))
+
+
+PARTS = 8
+
+
 def call(kernel, name, args, specs, outs, out_specs, scratch, aliases=None):
     after = []
     if Order.token is not None and not any(Order.token is arg for arg in args):
         after = [Order.token]
     given = len(args)
+    single = not isinstance(outs, (tuple, list))
+    results = [outs] if single else list(outs)
+    out_kinds = [out_specs] if single else list(out_specs)
+    loads = [i for i, spec in enumerate(specs) if spec is LOAD]
+    stores = [i for i, spec in enumerate(out_kinds) if spec is STORE]
+    extra = [pltpu.VMEM(args[i].shape, args[i].dtype) for i in loads]
+    extra += [pltpu.VMEM(results[i].shape, results[i].dtype) for i in stores]
+    extra += [pltpu.SemaphoreType.DMA((max(len(loads), 1),))]
+    extra += [pltpu.SemaphoreType.DMA((max(PARTS * len(stores), 1),))]
 
     def body(*refs):
-        return kernel(*refs[:given], *refs[given + len(after) :])
+        ins = list(refs[:given])
+        rest = list(refs[given + len(after) :])
+        made, own = rest[: len(results)], rest[len(results) : len(rest) - len(extra)]
+        held = rest[len(rest) - len(extra) :]
+        load_sems, store_sems = held[-2:]
+        for n, i in enumerate(loads):
+            ins[i] = Load(ins[i], held[n], load_sems.at[n])
+        for n, i in enumerate(stores):
+            sems = store_sems.at[pl.ds(PARTS * n, PARTS)]
+            made[i] = Store(made[i], held[len(loads) + n], sems)
+        kernel(*ins, *made, *own)
+        for i in loads:
+            ins[i].wait()
+        for i in stores:
+            made[i].finish()
+        for i in stores:
+            for copy in made[i].copies:
+                copy.wait()
 
     result = pl.pallas_call(
         body,
         name=name,
-        in_specs=list(specs) + [ANY] * len(after),
-        out_specs=out_specs,
+        in_specs=[ANY if spec is LOAD else spec for spec in specs] + [ANY] * len(after),
+        out_specs=ANY if single and out_specs is STORE else (
+            out_specs if single else [ANY if spec is STORE else spec for spec in out_kinds]
+        ),
         out_shape=outs,
-        scratch_shapes=scratch,
+        scratch_shapes=list(scratch) + extra,
         input_output_aliases=aliases or {},
         compiler_params=pltpu.CompilerParams(vmem_limit_bytes=VMEM_LIMIT),
     )(*args, *after)
@@ -279,6 +385,48 @@
         0: [(win, 0, hidden, 0, rows, 0)],
         1: [(woe, q * width, width, 0, per * rows, q * rows) for q in range(per)],
     }
+
+
+class Chunks:
+    def __init__(self, refs, weights, width, hidden, rows, whole, win, woe, sems, more=()):
+        per = hidden // width
+        self.parts = []
+        if whole:
+            copies = fetch(refs, weights, None, expert_targets(width, hidden, rows, True, win, woe), 0, sems)
+            copies += fetch(
+                refs, weights, None, expert_targets(width, hidden, rows, True, win, woe), 1, sems
+            )
+            self.parts = [copies] + [[] for _ in range(per - 1)]
+        else:
+            ref = refs[0]
+            shards = ref.shape[0]
+            for c in range(per):
+                here = pl.ds(c * width, width)
+                copies = [
+                    pltpu.make_async_copy(
+                        ref.at[d, 0, :, here], win.at[pl.ds(d * rows, rows), here], sems.at[d]
+                    )
+                    for d in range(shards)
+                ]
+                first = c * shards // per
+                for n in range(shards):
+                    d, q = first + n // per, n % per
+                    copies.append(
+                        pltpu.make_async_copy(
+                            ref.at[d, 1, :, pl.ds(q * width, width)],
+                            woe.at[pl.ds((d * per + q) * rows, rows)],
+                            sems.at[shards + n],
+                        )
+                    )
+                self.parts.append(copies)
+        for copies, extra in zip(self.parts, more):
+            copies.append(extra)
+        start(self.parts[0])
+
+    def take(self, c):
+        wait(self.parts[c])
+        if c + 1 < len(self.parts):
+            start(self.parts[c + 1])
 
 
 def copies_in(weights):
@@ -457,7 +605,7 @@
     return outs[0::2], outs[1::2]
 
 
-def attn_fwd(me, layer, x_args, weights, vecs, router, noise, cols, rows, cap):
+def attn_fwd(me, layer, x_args, weights, vecs, router, noise, cols, rows, cap, used):
     first = len(x_args) == 1
     padded, width = cols.shape[0], vecs.shape[1]
     tokens, experts = noise.shape[1:]
@@ -476,7 +624,7 @@
             below_blocks = [refs.pop(0) for _ in range(owners)]
         w_refs = [refs.pop(0) for _ in range(count)]
         vec_ref, router_ref, noise_ref, cols_ref, rows_ref = (refs.pop(0) for _ in range(5))
-        x_out, x1_out, a_out, qkv_out, o_out, gates_out, m_out = (refs.pop(0) for _ in range(7))
+        x_out, x1_out, qkv_out, gates_out, ao_out = (refs.pop(0) for _ in range(5))
         seat_outs = [refs.pop(0) for _ in range(experts)]
         wqkv, wout, sems, more_sems = refs
         targets = attn_targets(width, shard, wqkv, wout)
@@ -493,7 +641,7 @@
             x_out[...] = x
         normed, rstd = norm_rows(x)
         a_low = (normed * vec(0) + vec(2)).astype(BF)
-        a_out[...] = a_low
+        ao_out[:, 0:width] = a_low
         gates_out[...] = jnp.zeros_like(gates_out)
         gates_out[0:tokens, 0:experts] = noise_ref[layer]
         noise_here = gates_out[...]
@@ -518,8 +666,8 @@
                 probs = head_probs(query, keys, mask, tokens).astype(BF)
                 piece = dot(probs, jnp.where(mask, values, 0).astype(BF))
                 mixed = piece if mixed is None else mixed + piece
-            o_out[:, at : at + 2 * HEAD_DIM] = mixed.astype(BF)
-        x1 = x + dot(o_out[...], wout[...]) + vec(6)
+            ao_out[:, width + at : width + at + 2 * HEAD_DIM] = mixed.astype(BF)
+        x1 = x + dot(ao_out[:, width : 2 * width], wout[...]) + vec(6)
         x1_out[...] = x1
         normed2, rstd2 = norm_rows(x1)
         moe = normed2 * vec(1) + vec(3)
@@ -528,10 +676,18 @@
         lanes = lax.broadcasted_iota(jnp.int32, logits.shape, 1)
         logits = jnp.where(lanes < experts, logits, NEG)
         raised = jnp.exp(logits - jnp.max(logits, -1, keepdims=True))
-        gates_out[...] = raised / jnp.sum(raised, -1, keepdims=True)
-        m_out[...] = high
-        chosen = jnp.logical_or(token_mask(rows_ref, 0, seats), token_mask(rows_ref, 1, seats))
-        part(dot(one(chosen), high), seat_outs)
+        gates = raised / jnp.sum(raised, -1, keepdims=True)
+        gates_out[...] = gates
+        ao_out[:, 2 * width : 3 * width] = high
+        sent = rows_to_seats(rows_ref, seats, high)
+        chosen = [pair_gate(gates, cols_ref, pair) for pair in range(2)]
+        for block, ref in enumerate(seat_outs):
+            note = jnp.zeros((1, LANES), F32)
+            for pair in range(2):
+                here = near_lanes(cols_ref, pair, block, cap)
+                note = note + jnp.sum(jnp.where(here, chosen[pair], 0.0), 0, keepdims=True)
+            piece = sent[block * cap : (block + 1) * cap]
+            ref[...] = with_note(piece, used, note).astype(BF)
 
     args = [me]
     specs = [SM]
@@ -546,11 +702,9 @@
     outs = [
         sds((padded, width), F32),
         sds((padded, width), F32),
-        sds((padded, width), BF),
         sds((padded, 3 * width), BF),
-        sds((padded, width), BF),
         sds((padded, LANES), F32),
-        sds((padded, width), BF),
+        sds((padded, 3 * width), BF),
     ] + [sds((cap, width), BF)] * experts
     result = call(
         kernel,
@@ -566,10 +720,10 @@
             pltpu.SemaphoreType.DMA((copies_in(weights),)),
         ],
     )
-    return result[:7], result[7:]
-
-
-def expert_fwd(me, seat_blocks, weights, bias_in, bias_oe):
+    return result[:5], result[5:]
+
+
+def expert_fwd(me, seat_blocks, weights, bias_in, bias_oe, used):
     owners = len(seat_blocks)
     cap, width = seat_blocks[0].shape
     seats = owners * cap
@@ -585,18 +739,19 @@
         seat_refs = [refs.pop(0) for _ in range(owners)]
         w_refs = [refs.pop(0) for _ in range(count)]
         bin_ref, boe_ref = refs.pop(0), refs.pop(0)
-        rows_out, h_out, slope_out = refs.pop(0), refs.pop(0), refs.pop(0)
+        rh_out, slope_out, gate_out, made_out = (refs.pop(0) for _ in range(4))
         outs = [refs.pop(0) for _ in range(owners)]
-        win, woe, sems, more_sems = refs
-        targets = expert_targets(width, hidden, shard, whole, win, woe)
-        left = fetch(w_refs, weights, me_ref[0], targets, 0, sems)
-        right = fetch(w_refs, weights, me_ref[0], targets, 1, more_sems)
-        start(left + right)
-        rows = join(seat_refs)
-        rows_out[...] = rows
-        wait(left)
+        win, woe, sems = refs
+        chunks = Chunks(w_refs, weights, width, hidden, shard, whole, win, woe, sems)
+        blocks = [ref[...].astype(F32) for ref in seat_refs]
+        rows = jnp.concatenate(blocks, 0).astype(BF)
+        rh_out[:, 0:width] = rows
+        rh_out.send(ALL, pl.ds(0, width))
+        columns = [as_column(note_of(block, used), cap) for block in blocks]
+        gate_out[...] = jnp.broadcast_to(jnp.concatenate(columns, 0), gate_out.shape)
         total_out = None
         for at in range(0, hidden, step):
+            chunks.take(at // step)
             pre = dot(rows, win[:, at : at + step]) + bin_ref[:, at : at + step]
             square = pre * pre
             bend = jnp.tanh(0.7978845608028654 * (pre + 0.044715 * square * pre))
@@ -604,52 +759,53 @@
             slope = 0.5 * (1.0 + bend) + 0.5 * pre * (1.0 - bend * bend) * (
                 0.7978845608028654 * (1.0 + 0.134145 * square)
             )
-            h_out[:, at : at + step] = h
+            rh_out[:, width + at : width + at + step] = h
             slope_out[:, at : at + step] = slope.astype(BF)
-            if at == 0:
-                wait(right)
+            rh_out.send(ALL, pl.ds(width + at, step))
+            slope_out.send(ALL, pl.ds(at, step))
             piece = dot(h, woe[at : at + step, :])
             total_out = piece if total_out is None else total_out + piece
-        part(total_out + boe_ref[...], outs)
+        total_out = total_out + boe_ref[...]
+        made_out[...] = total_out.astype(BF)
+        part(total_out, outs)
 
     shapes = [
+        sds((seats, width + hidden), BF),
+        sds((seats, hidden), BF),
+        sds((seats, LANES), F32),
         sds((seats, width), BF),
-        sds((seats, hidden), BF),
-        sds((seats, hidden), BF),
     ] + [sds((cap, width), BF)] * owners
     result = call(
         kernel,
         "expert_fwd",
         [me, *seat_blocks, *weights.arrays, bias_in, bias_oe],
-        [SM] + [VM] * owners + [ANY] * count + [VM] * 2,
+        [SM] + [LOAD] * owners + [ANY] * count + [LOAD] * 2,
         shapes,
-        [VM] * len(shapes),
+        [STORE] * (4 + owners),
         [
             pltpu.VMEM((width, hidden), BF),
             pltpu.VMEM((hidden, width), BF),
-            pltpu.SemaphoreType.DMA((copies_in(weights),)),
-            pltpu.SemaphoreType.DMA((copies_in(weights),)),
+            pltpu.SemaphoreType.DMA((2 * copies_in(weights),)),
         ],
     )
-    return result[:3], result[3:]
-
-
-def top_seats(cotangent, gates, cols, rows, cap, experts):
+    return result[:4], result[4:]
+
+
+def top_seats(cotangent, rows, cap, experts):
     tokens, width = cotangent.shape
-    padded = cols.shape[0]
-
-    def kernel(cot_ref, gates_ref, cols_ref, rows_ref, *refs):
-        grad_out, *outs = refs
+    padded = rows.shape[1]
+
+    def kernel(cot_ref, rows_ref, grad_out, *outs):
         grad_out[...] = jnp.zeros_like(grad_out)
         grad_out[0:tokens, :] = cot_ref[...].astype(F32)
-        part(seat_grads(grad_out[...], gates_ref[...], cols_ref, rows_ref, cap * experts), outs)
+        part(rows_to_seats(rows_ref, cap * experts, grad_out[...].astype(BF)), outs)
 
     shapes = [sds((padded, width), F32)] + [sds((cap, width), BF)] * experts
     result = call(
         kernel,
         "top_seats",
-        [cotangent, gates, cols, rows],
-        [VM] * 4,
+        [cotangent, rows],
+        [VM] * 2,
         shapes,
         [VM] * len(shapes),
         [],
@@ -657,51 +813,25 @@
     return result[0], result[1:]
 
 
-def gate_back(grad, x1, gates, cols, router, returned, tokens, last):
-    padded, width = grad.shape
-    owners = len(returned)
-
-    def kernel(*refs):
-        refs = list(refs)
-        grad_ref = refs.pop(0)
-        x1_ref = refs.pop(0) if last else None
-        gates_ref, cols_ref, router_ref = (refs.pop(0) for _ in range(3))
-        blocks = [refs.pop(0) for _ in range(owners)]
-        dz_out, moe_out = refs.pop(0), refs.pop(0)
-        back = join(blocks)
-        grad_here = grad_ref[...]
-        gates_here = gates_ref[...]
-        lanes = lax.broadcasted_iota(jnp.int32, gates_here.shape, 1)
-        d_gates = jnp.zeros_like(gates_here)
-        mixed = x1_ref[...] if last else None
-        for pair in range(2):
-            piece = dot(one(seat_mask(cols_ref, pair, back.shape[0])), back)
-            if last:
-                mixed = mixed + pair_gate(gates_here, cols_ref, pair) * piece
-            d_pair = jnp.sum(grad_here * piece, -1, keepdims=True)
-            d_gates = d_gates + jnp.where(lanes == cols_ref[:, 2 + pair : 3 + pair], d_pair, 0.0)
-        dz = gates_here * (d_gates - jnp.sum(d_gates * gates_here, -1, keepdims=True))
-        dz_out[...] = dz
-        high, low = split(dz)
-        moe_out[...] = dot_nt(high, router_ref[...]) + dot_nt(low, router_ref[...])
-        if last:
-            refs.pop(0)[...] = mixed[0:tokens, :]
-
-    shapes = [sds((padded, LANES), F32), sds((padded, width), F32)]
-    if last:
-        shapes.append(sds((tokens, width), F32))
+def mix(x1, gates, cols, returned, tokens):
+    width = x1.shape[1]
+
+    def kernel(x1_ref, gates_ref, cols_ref, *refs):
+        total = combine(x1_ref[...], gates_ref[...], cols_ref, join(refs[:-1]))
+        refs[-1][...] = total[0:tokens, :]
+
     return call(
         kernel,
-        "gate_back",
-        [grad] + ([x1] if last else []) + [gates, cols, router, *returned],
-        [VM] * (4 + owners + int(last)),
-        shapes,
-        [VM] * len(shapes),
+        "mix",
+        [x1, gates, cols, *returned],
+        [VM] * (3 + len(returned)),
+        sds((tokens, width), F32),
+        VM,
         [],
     )
 
 
-def expert_back(me, grad_blocks, slope, weights):
+def expert_back(me, grad_blocks, slope, gate, made, weights, used):
     owners = len(grad_blocks)
     cap, width = grad_blocks[0].shape
     seats, hidden = slope.shape
@@ -714,134 +844,226 @@
         refs = list(refs)
         me_ref = refs.pop(0)
         seat_refs = [refs.pop(0) for _ in range(owners)]
-        slope_ref = refs.pop(0)
+        slope_ref, gate_ref, made_ref = (refs.pop(0) for _ in range(3))
         w_refs = [refs.pop(0) for _ in range(count)]
-        grad_out, pre_out = refs.pop(0), refs.pop(0)
+        gd_out = refs.pop(0)
         outs = [refs.pop(0) for _ in range(owners)]
-        win, woe, sems, more_sems = refs
-        targets = expert_targets(width, hidden, shard, whole, win, woe)
-        right = fetch(w_refs, weights, me_ref[0], targets, 1, sems)
-        left = fetch(w_refs, weights, me_ref[0], targets, 0, more_sems)
-        start(right + left)
-        grad = join(seat_refs)
-        grad_out[...] = grad
-        wait(right)
+        win, woe, slopes, sems, slope_sems = refs
+        more = [
+            pltpu.make_async_copy(
+                slope_ref.at[:, pl.ds(at, step)],
+                slopes.at[:, pl.ds(at, step)],
+                slope_sems.at[at // step],
+            )
+            for at in range(0, hidden, step)
+        ]
+        chunks = Chunks(w_refs, weights, width, hidden, shard, whole, win, woe, sems, more)
+        given = jnp.concatenate([ref[...].astype(F32) for ref in seat_refs], 0)
+        grad = (given * gate_ref[:, 0:1]).astype(BF)
+        notes = given * made_ref[...].astype(F32)
+        notes = [lane_sums(notes[k * cap : (k + 1) * cap]) for k in range(owners)]
+        gd_out[:, 0:width] = grad
+        gd_out.send(ALL, pl.ds(0, width))
         total_out = None
         for at in range(0, hidden, step):
+            chunks.take(at // step)
             d_hidden = dot_nt(grad, woe[at : at + step, :])
-            d_pre = (d_hidden * slope_ref[:, at : at + step].astype(F32)).astype(BF)
-            pre_out[:, at : at + step] = d_pre
-            if at == 0:
-                wait(left)
+            d_pre = (d_hidden * slopes[:, at : at + step].astype(F32)).astype(BF)
+            gd_out[:, width + at : width + at + step] = d_pre
+            gd_out.send(ALL, pl.ds(width + at, step))
             piece = dot_nt(d_pre, win[:, at : at + step])
             total_out = piece if total_out is None else total_out + piece
-        part(total_out, outs)
-
-    shapes = [sds((seats, width), BF), sds((seats, hidden), BF)]
+        for k, ref in enumerate(outs):
+            ref[...] = with_note(total_out[k * cap : (k + 1) * cap], used, notes[k]).astype(BF)
+
+    shapes = [sds((seats, width + hidden), BF)]
     shapes += [sds((cap, width), BF)] * owners
     result = call(
         kernel,
         "expert_back",
-        [me, *grad_blocks, slope, *weights.arrays],
-        [SM] + [VM] * (owners + 1) + [ANY] * count,
+        [me, *grad_blocks, slope, gate, made, *weights.arrays],
+        [SM] + [LOAD] * owners + [ANY] + [LOAD] * 2 + [ANY] * count,
         shapes,
-        [VM] * len(shapes),
+        [STORE] * (1 + owners),
         [
             pltpu.VMEM((width, hidden), BF),
             pltpu.VMEM((hidden, width), BF),
-            pltpu.SemaphoreType.DMA((copies_in(weights),)),
-            pltpu.SemaphoreType.DMA((copies_in(weights),)),
+            pltpu.VMEM((seats, hidden), BF),
+            pltpu.SemaphoreType.DMA((2 * copies_in(weights),)),
+            pltpu.SemaphoreType.DMA((hidden // step,)),
         ],
     )
-    return result[0], result[1], result[2:]
-
-
-def spread(wide, index, outs, orders, rows, pieces, sems):
-    copies = []
-    for out, order in zip(outs, orders):
-        for k, off in enumerate(order):
-            for times, plus, first, size, into in pieces:
-                place = pl.multiple_of((index ^ off) * times + plus, 16)
-                copies.append(
-                    pltpu.make_async_copy(
-                        wide.at[pl.ds(place, rows), pl.ds(first, size)],
-                        out.at[(k, *into)],
-                        sems.at[len(copies)],
-                    )
-                )
-    return copies
+    return result[0], result[1:]
 
 
 def column_sums(value):
     return dot(jnp.ones((8, value.shape[0]), BF), value)[0:1, :]
 
 
-def expert_grads(rows_in, h, d_out, d_pre, shards, blocks):
-    seats, width = rows_in.shape
-    hidden = h.shape[1]
+def own_columns(width, shards, core):
+    shard = width // shards
+    half = width // 2
+    row = lax.broadcasted_iota(jnp.int32, (width, half), 0)
+    column = lax.broadcasted_iota(jnp.int32, (width, half), 1)
+    place = column + core * shard
+    for k in range(1, shards // 2):
+        place = place + jnp.where(column >= k * shard, shard, 0)
+    return one(row == place)
+
+
+def expert_grads(me, own, other, shards):
+    seats, both = own[0].shape
+    width = HEADS * HEAD_DIM
+    hidden = both - width
     per, shard = hidden // width, width // shards
-    total = shards * (1 + per) if blocks else 2
-
-    def kernel(rows_ref, h_ref, out_ref, pre_ref, *refs):
+    part_hidden = hidden // shards
+    sides = 2 if other else 1
+    tall = width // 2 if other else width
+    deep = hidden // 2 if other else hidden
+    total = shards * per if other else 2
+
+    blocks = shards // 2 if other else per
+    size = part_hidden if other else width
+
+    def kernel(me_ref, *refs):
         refs = list(refs)
-        outs = [refs.pop(0) for _ in range(1 if blocks else 2)]
-        bias_ref, win, woe, sems = refs
+        rh = [refs.pop(0) for _ in range(sides)]
+        gd = [refs.pop(0) for _ in range(sides)]
+        outs = [refs.pop(0) for _ in range(1 if other else 2)]
+        bias_ref, win, woe, h_held, row_held, gd_held, sems, load_sems = refs
+        core = me_ref[0] & 1
         copies = []
+        loads = {}
+
+        def fetch_in(key, source, target):
+            copy = pltpu.make_async_copy(source, target, load_sems.at[len(loads)])
+            copy.start()
+            loads[key] = copy
+
+        for i in range(sides):
+            fetch_in(("d", i), gd[i].at[:, pl.ds(0, width)], gd_held.at[i, :, pl.ds(0, width)])
+        for k in range(blocks):
+            first = width + k * size
+            if other:
+                first = pl.multiple_of(width + (2 * k + core) * size, LANES)
+            for i in range(sides):
+                here = pl.ds(k * size, size)
+                fetch_in(("h", k, i), rh[i].at[:, pl.ds(first, size)], h_held.at[i, :, here])
+        for i in range(sides):
+            fetch_in(("r", i), rh[i].at[:, pl.ds(0, width)], row_held.at[i])
+        for k in range(per):
+            here = pl.ds(width + k * width, width)
+            for i in range(sides):
+                fetch_in(("p", k, i), gd[i].at[:, here], gd_held.at[i, :, here])
 
         def send(source, target):
             copy = pltpu.make_async_copy(source, target, sems.at[len(copies)])
             copy.start()
             copies.append(copy)
 
+        def summed(pieces):
+            total = pieces[0]
+            for piece in pieces[1:]:
+                total = total + piece
+            return total
+
+        for i in range(sides):
+            loads["d", i].wait()
+        d_outs = [gd_held[i, :, 0:width] for i in range(sides)]
+        for k in range(blocks):
+            here = slice(k * size, (k + 1) * size)
+            for i in range(sides):
+                loads["h", k, i].wait()
+            total = summed([dot_tn(h_held[i, :, here], d_outs[i]) for i in range(sides)])
+            woe[here, :] = total.astype(BF)
+            if other:
+                for q in range(per):
+                    send(
+                        woe.at[pl.ds(k * size + q * shard, shard)],
+                        outs[0].at[k, 1, :, pl.ds(q * width, width)],
+                    )
+        for i in range(sides):
+            loads["r", i].wait()
+        lefts = [row_held[i] for i in range(sides)]
+        if other:
+            pick = own_columns(width, shards, core)
+            lefts = [dot(left, pick).astype(BF) for left in lefts]
         for k in range(per):
-            here = slice(k * width, (k + 1) * width)
-            woe[here, :] = dot_tn(h_ref[:, here], out_ref[...]).astype(BF)
-            if blocks:
-                for d in range(k * shards // per, (k + 1) * shards // per):
-                    for q in range(per):
-                        send(
-                            woe.at[pl.ds((d * per + q) * shard, shard)],
-                            outs[0].at[d, 1, :, pl.ds(q * width, width)],
-                        )
-        for k in range(per):
-            here = slice(k * width, (k + 1) * width)
-            win[:, here] = dot_tn(rows_ref[...], pre_ref[:, here]).astype(BF)
-        if blocks:
-            for d in range(shards):
-                send(win.at[pl.ds(d * shard, shard)], outs[0].at[d, 0])
-        else:
+            here = slice(width + k * width, width + (k + 1) * width)
+            for i in range(sides):
+                loads["p", k, i].wait()
+            total = summed([dot_tn(lefts[i], gd_held[i, :, here]) for i in range(sides)])
+            win[:, k * width : (k + 1) * width] = total.astype(BF)
+            if other:
+                for n in range(shards // 2):
+                    here = pl.ds(k * width, width)
+                    send(
+                        win.at[pl.ds(n * shard, shard), here], outs[0].at[n, 0, :, here]
+                    )
+        if not other:
             send(win, outs[0])
             send(woe, outs[1])
         bias_ref[...] = jnp.zeros_like(bias_ref)
-        sums = column_sums(pre_ref[...])
+        sums = summed([column_sums(gd_held[i]) for i in range(sides)])
         for d in range(shards):
             for q in range(per):
-                first = (d * per + q) * shard
+                first = width + (d * per + q) * shard
                 bias_ref[q : q + 1, d * shard : (d + 1) * shard] = sums[:, first : first + shard]
-        bias_ref[per : per + 1, :] = column_sums(out_ref[...])
+        bias_ref[per : per + 1, :] = sums[:, 0:width]
         wait(copies)
 
-    if blocks:
-        shapes = [sds((shards, 2, shard, hidden), BF)]
+    if other:
+        shapes = [sds((shards // 2, 2, shard, hidden), BF)]
+        args = [own[0], other[0], own[1], other[1]]
     else:
         shapes = [sds((width, hidden), BF), sds((hidden, width), BF)]
+        args = list(own)
     result = call(
         kernel,
         "expert_grads",
-        [rows_in, h, d_out, d_pre],
-        [VM] * 4,
+        [me, *args],
+        [SM] + [ANY] * len(args),
         shapes + [sds((8, width), F32)],
         [ANY] * len(shapes) + [VM],
         [
-            pltpu.VMEM((width, hidden), BF),
-            pltpu.VMEM((hidden, width), BF),
+            pltpu.VMEM((tall, hidden), BF),
+            pltpu.VMEM((deep, width), BF),
+            pltpu.VMEM((sides, seats, blocks * size), BF),
+            pltpu.VMEM((sides, seats, width), BF),
+            pltpu.VMEM((sides, seats, width + hidden), BF),
             pltpu.SemaphoreType.DMA((total,)),
+            pltpu.SemaphoreType.DMA((sides * (2 + blocks + per),)),
         ],
     )
     return result[:-1], result[-1]
 
 
-def attn_back(me, back_blocks, moe_part, grad, x, x1, qkv, cols, vecs, weights, below, tokens):
+def pick_columns(me, value, shards):
+    rows, wide = value.shape
+    width = wide // 3
+
+    def kernel(me_ref, ref, own, other):
+        core = me_ref[0] & 1
+        for out, side in ((own, core), (other, 1 - core)):
+            pick = own_columns(width, shards, side)
+            for k in range(3):
+                piece = dot(ref[:, k * width : (k + 1) * width], pick)
+                out[:, k * width // 2 : (k + 1) * width // 2] = piece.astype(BF)
+
+    return call(
+        kernel,
+        "pick_columns",
+        [me, value],
+        [SM, VM],
+        [sds((rows, wide // 2), BF)] * 2,
+        [VM] * 2,
+        [],
+    )
+
+
+def attn_back(
+    me, back_blocks, gates, router, grad, x, x1, qkv, cols, vecs, weights, below, tokens, used
+):
     padded, width = grad.shape
     owners = len(back_blocks)
     cap = back_blocks[0].shape[0]
@@ -853,30 +1075,46 @@
         refs = list(refs)
         me_ref = refs.pop(0)
         back_refs = [refs.pop(0) for _ in range(owners)]
-        part_ref, grad_ref, x_ref, x1_ref, qkv_ref, cols_ref, vec_ref = (
-            refs.pop(0) for _ in range(7)
+        gates_ref, router_ref, grad_ref, x_ref, x1_ref, qkv_ref, cols_ref, vec_ref = (
+            refs.pop(0) for _ in range(8)
         )
         w_refs = [refs.pop(0) for _ in range(count)]
         if below is not None:
-            gates_ref, below_cols, below_rows = (refs.pop(0) for _ in range(3))
-        dx_out, dy_out, dqkv_out, small_out = (refs.pop(0) for _ in range(4))
+            below_rows = refs.pop(0)
+        dx_out, back_out = refs.pop(0), refs.pop(0)
         seat_outs = [refs.pop(0) for _ in range(owners)] if below is not None else None
-        wqkv, wout, sems, more_sems = refs
+        wqkv, wout, small_out, sems, more_sems = refs
         targets = attn_targets(width, shard, wqkv, wout)
         right = fetch(w_refs, weights, me_ref[0], targets, 1, sems)
         left = fetch(w_refs, weights, me_ref[0], targets, 0, more_sems)
         start(right + left)
         vec = lambda k: vec_ref[k : k + 1, :]
+        blocks = [ref[...].astype(F32) for ref in back_refs]
+        gates = gates_ref[...]
+        lanes = lax.broadcasted_iota(jnp.int32, gates.shape, 1)
+        d_gates = jnp.zeros_like(gates)
+        for pair in range(2):
+            d_pair = jnp.zeros_like(gates)
+            for block in range(owners):
+                here = near_lanes(cols_ref, pair, block, cap)
+                d_pair = d_pair + jnp.where(here, note_of(blocks[block], used), 0.0)
+            d_pair = jnp.sum(d_pair, -1, keepdims=True)
+            d_gates = d_gates + jnp.where(lanes == cols_ref[:, 2 + pair : 3 + pair], d_pair, 0.0)
+        dz = gates * (d_gates - jnp.sum(d_gates * gates, -1, keepdims=True))
+        high, low = split(dz)
+        moe_part = dot_nt(high, router_ref[...]) + dot_nt(low, router_ref[...])
+        back_out[0:padded, 4 * width : 4 * width + LANES] = high
+        back_out[0:padded, 4 * width + LANES : 4 * width + 2 * LANES] = low
         chosen = jnp.logical_or(seat_mask(cols_ref, 0, seats), seat_mask(cols_ref, 1, seats))
-        d_moe = dot(one(chosen), join(back_refs)) + part_ref[...]
+        d_moe = dot(one(chosen), jnp.concatenate(blocks, 0).astype(BF)) + moe_part
         normed2, rstd2 = norm_rows(x1_ref[...])
         small_out[...] = jnp.zeros_like(small_out)
         small_out[1:2, :] = jnp.sum(d_moe * normed2, 0, keepdims=True)
         small_out[3:4, :] = jnp.sum(d_moe, 0, keepdims=True)
         d_x1 = grad_ref[...] + norm_back(d_moe * vec(1), normed2, rstd2)
         dy = d_x1.astype(BF)
-        dy_out[...] = dy
-        small_out[6:7, :] = jnp.sum(dy.astype(F32), 0, keepdims=True)
+        back_out[0:padded, 3 * width : 4 * width] = dy
+        small_out[6:7, :] = column_sums(dy)
         wait(right)
         d_mixed = dot_nt(dy, wout[...]).astype(BF)
         masks = head_masks()
@@ -899,16 +1137,16 @@
                 d_keys = dot_tn(d_scores, jnp.where(mask, query, 0).astype(BF))
                 here = (d_query, d_keys, d_values)
                 sums = here if sums is None else tuple(s + h for s, h in zip(sums, here))
-            dqkv_out[:, at : at + 2 * HEAD_DIM] = (sums[0] * scale).astype(BF)
-            dqkv_out[:, width + at : width + at + 2 * HEAD_DIM] = (sums[1] * scale).astype(BF)
-            dqkv_out[:, 2 * width + at : 2 * width + at + 2 * HEAD_DIM] = sums[2].astype(BF)
+            for k, value in enumerate((sums[0] * scale, sums[1] * scale, sums[2])):
+                first = k * width + at
+                back_out[0:padded, first : first + 2 * HEAD_DIM] = value.astype(BF)
         wait(left)
         d_normed = None
         for k in range(3):
-            here = dqkv_out[:, k * width : (k + 1) * width]
+            here = back_out[0:padded, k * width : (k + 1) * width]
             if k != 1:
                 row = 4 if k == 0 else 5
-                small_out[row : row + 1, :] = jnp.sum(here.astype(F32), 0, keepdims=True)
+                small_out[row : row + 1, :] = column_sums(here)
             piece = dot_nt(here, wqkv[:, k * width : (k + 1) * width])
             d_normed = piece if d_normed is None else d_normed + piece
         normed1, rstd1 = norm_rows(x_ref[...])
@@ -917,20 +1155,22 @@
         d_x = d_x1 + norm_back(d_normed * vec(0), normed1, rstd1)
         dx_out[...] = d_x[0 : dx_out.shape[0], :]
         if below is not None:
-            part(seat_grads(d_x, gates_ref[...], below_cols, below_rows, seats), seat_outs)
+            part(rows_to_seats(below_rows, seats, d_x.astype(BF)), seat_outs)
+        high, low = split(small_out[...])
+        back_out[padded : padded + 16, 0:width] = high
+        back_out[padded : padded + 16, width : 2 * width] = low
+        back_out[padded : padded + 16, 2 * width :] = jnp.zeros((16, 2 * width + 2 * LANES), BF)
 
     shapes = [
         sds((padded if below is not None else tokens, width), F32),
-        sds((padded, width), BF),
-        sds((padded, 3 * width), BF),
-        sds((16, width), F32),
+        sds((padded + 16, 4 * width + 2 * LANES), BF),
     ]
-    args = [me, *back_blocks, moe_part, grad, x, x1, qkv, cols, vecs, *weights.arrays]
-    specs = [SM] + [VM] * (owners + 7) + [ANY] * count
+    args = [me, *back_blocks, gates, router, grad, x, x1, qkv, cols, vecs, *weights.arrays]
+    specs = [SM] + [VM] * (owners + 8) + [ANY] * count
     if below is not None:
         shapes += [sds((cap, width), BF)] * owners
-        args += list(below)
-        specs += [VM] * 3
+        args += [below]
+        specs += [VM]
     result = call(
         kernel,
         "attn_back",
@@ -941,63 +1181,123 @@
         [
             pltpu.VMEM((width, 3 * width), BF),
             pltpu.VMEM((width, width), BF),
+            pltpu.VMEM((16, width), F32),
             pltpu.SemaphoreType.DMA((copies_in(weights),)),
             pltpu.SemaphoreType.DMA((copies_in(weights),)),
         ],
     )
-    return result[:4], result[4:]
-
-
-def attn_grads(me, z, a_low, o_low, moe_low, dqkv, dy, dz, small, biases, rows, order):
-    padded, width = a_low.shape
+    return result[:2], result[2:]
+
+
+def attn_grads(me, z, own, other, biases, shards, ordered):
+    padded, wide_ao = own[0].shape
+    width = HEADS * HEAD_DIM
     half = 2 * width + LANES
-    total = 4 * len(order) if order else 2
-
-    def kernel(
-        me_ref, z_ref, a_ref, o_ref, moe_ref, dqkv_ref, dy_ref, dz_ref, small_ref, bias_ref, *refs
-    ):
+    tall = width // 2 if other else width
+    shard = width // shards
+    places = [(6, 0, 0), (6, 1, 1), (2, 0, 2), (2, 1, 2), (4, 0, 3), (4, 1, 3), (0, 0, 4), (0, 1, 4)]
+    count = 2
+    if other:
+        count = 1 if ordered else 5
+
+    def kernel(me_ref, z_ref, *refs):
         refs = list(refs)
-        outs = [refs.pop(0) for _ in range(2)]
-        wide, tall, sems = refs
-        for k in range(3):
-            at = k * width + (LANES if k == 2 else 0)
-            wide[:, at : at + width] = dot_tn(
-                a_ref[...], dqkv_ref[:, k * width : (k + 1) * width]
-            ).astype(BF)
-        wide[:, 2 * width : half] = jnp.zeros((width, LANES), BF)
-        wide[:, half + width : half + 2 * width] = dot_tn(o_ref[...], dy_ref[...]).astype(BF)
-        high, low = split(dz_ref[...])
-        d_router = dot_tn(moe_ref[...], high) + dot_tn(moe_ref[...], low)
-        tall[...] = jnp.zeros_like(tall)
-        tall[16:32, :] = small_ref[...]
-        tall[pl.ds(pl.multiple_of(32 + 8 * z_ref[0], 8), 8), :] = bias_ref[...]
-        wide[:, half + 2 * width : 2 * half] = (d_router + tall[...].T).astype(BF)
-        if order:
-            pieces = [(rows, 0, p * half, half, (p, ALL, ALL)) for p in range(2)]
-            copies = spread(wide, me_ref[0], outs, (order, [o ^ 1 for o in order]), rows, pieces, sems)
+        ao = [refs.pop(0), refs.pop(0)] if other else [refs.pop(0)]
+        back = [refs.pop(0), refs.pop(0)] if other else [refs.pop(0)]
+        bias_ref = refs.pop(0)
+        outs = [refs.pop(0) for _ in range(count)]
+        wide, rows, turned, sems = refs
+        copies = []
+
+        def send(p):
+            first = p * half
+            if not other:
+                copies.append(
+                    pltpu.make_async_copy(wide.at[:, pl.ds(first, half)], outs[p], sems.at[p])
+                )
+                copies[-1].start()
+                return
+            if ordered:
+                for k in range(shards // 2):
+                    source = wide.at[pl.ds(k * shard, shard), pl.ds(first, half)]
+                    copy = pltpu.make_async_copy(source, outs[0].at[k, p], sems.at[2 * k + p])
+                    copies.append(copy)
+                    copy.start()
+                return
+            for n, (off, where, o) in enumerate(places):
+                if where != p:
+                    continue
+                at = pl.multiple_of(((me_ref[0] ^ off) >> 1) * shard, 16)
+                into = outs[o] if o < 2 else outs[o].at[p]
+                copies.append(
+                    pltpu.make_async_copy(
+                        wide.at[pl.ds(at, shard), pl.ds(first, half)], into, sems.at[n]
+                    )
+                )
+                copies[-1].start()
+
+        def product(which, first):
+            total = None
+            for left, right in zip(ao, back):
+                here = left[:, which * tall : (which + 1) * tall]
+                piece = dot_tn(here, right[0:padded, first : first + width])
+                total = piece if total is None else total + piece
+            return total.astype(BF)
+
+        wide[:, 0:width] = product(0, 0)
+        wide[:, width : 2 * width] = product(0, width)
+        wide[:, 2 * width : half] = jnp.zeros((tall, LANES), BF)
+        send(0)
+        wide[:, half : half + width] = product(0, 2 * width)
+        wide[:, half + width : half + 2 * width] = product(1, 3 * width)
+        rows[...] = jnp.zeros_like(rows)
+        small = None
+        d_router = None
+        for left, right in zip(ao, back):
+            for k in range(2):
+                piece = right[padded : padded + 16, k * width : (k + 1) * width].astype(F32)
+                small = piece if small is None else small + piece
+                first = 4 * width + k * LANES
+                piece = dot_tn(
+                    left[:, 2 * tall : 3 * tall], right[0:padded, first : first + LANES]
+                )
+                d_router = piece if d_router is None else d_router + piece
+        rows[16:32, :] = small
+        rows[pl.ds(pl.multiple_of(32 + 8 * z_ref[0], 8), 8), :] = bias_ref[...]
+        turned[...] = rows[...].T
+        if other:
+            core = me_ref[0] & 1
+            for k in range(shards // 2):
+                at = pl.multiple_of((2 * k + core) * shard, 8)
+                here = slice(k * shard, (k + 1) * shard)
+                piece = d_router[here, :] + turned[pl.ds(at, shard), :]
+                wide[here, half + 2 * width : 2 * half] = piece.astype(BF)
         else:
-            copies = [
-                pltpu.make_async_copy(wide.at[:, pl.ds(p * half, half)], outs[p], sems.at[p])
-                for p in range(2)
-            ]
-        start(copies)
+            wide[:, half + 2 * width : 2 * half] = (d_router + turned[...]).astype(BF)
+        send(1)
         wait(copies)
 
-    if order:
-        shapes = [sds((len(order), 2, rows, half), BF)] * 2
+    if other:
+        if ordered:
+            shapes = [sds((shards // 2, 2, shard, half), BF)]
+        else:
+            shapes = [sds((shard, half), BF)] * 2 + [sds((2, shard, half), BF)] * 3
+        args = [own[0], other[0], own[1], other[1]]
     else:
         shapes = [sds((width, half), BF)] * 2
+        args = list(own)
     return call(
         kernel,
         "attn_grads",
-        [me, z, a_low, o_low, moe_low, dqkv, dy, dz, small, biases],
-        [SM, SM] + [VM] * 8,
+        [me, z, *args, biases],
+        [SM, SM] + [VM] * (len(args) + 1),
         shapes,
-        [ANY] * 2,
+        [ANY] * len(shapes),
         [
-            pltpu.VMEM((width, 2 * half), BF),
+            pltpu.VMEM((tall, 2 * half), BF),
             pltpu.VMEM((LANES, width), F32),
-            pltpu.SemaphoreType.DMA((total,)),
+            pltpu.VMEM((width, LANES), F32),
+            pltpu.SemaphoreType.DMA((max(len(places), shards),)),
         ],
     )
 
@@ -1074,7 +1374,14 @@
     return lax.psum_scatter(whole, "dp", scatter_dimension=0, tiled=True)
 
 
-ORDER = [0, 2, 4, 6]
+def scatter_chips(blocks):
+    size = lax.axis_size("dp")
+    return lax.psum_scatter(
+        blocks,
+        "dp",
+        scatter_dimension=0,
+        axis_index_groups=[list(range(core, size, 2)) for core in range(2)],
+    )
 
 
 class Gather:
@@ -1129,33 +1436,37 @@
 
 
 class AttnSum:
-    def __init__(self, grads, after=()):
-        self.mine, theirs = grads
+    def __init__(self, grads):
+        self.bits = axis_bits("expert", 1)
+        self.done = 0
+        if len(grads) == 1:
+            self.total = scatter_chips(grads[0])
+            return
+        self.across, (self.x, self.y, self.own) = list(grads[:2]), grads[2:]
+        self.rows, self.width = self.across[0].shape
+
+    def cut(self):
+        self.rows, self.width = self.total.shape[1:]
+        shape = (self.rows, self.width)
+        self.parts = move(
+            "parts",
+            [self.total],
+            [(0, (p,), p, full(self.rows), shape) for p in range(2)],
+            [sds(shape, BF)] * 2,
+        )
+        self.send()
+
+    def send_across(self, after=()):
         if after:
-            theirs = hold([theirs], after)[0]
-        self.came = swap(theirs, "dp", 1)
-        self.rows, self.width = self.mine.shape[2:]
-
-    def fold0(self):
-        shape = (self.rows, self.width)
-        flat = full(self.rows)
-        places = [(3, 0, 0, flat), (3, 1, 1, flat)]
-        places += [(k, p, o, (p,)) for k, o in ((1, 2), (2, 3), (0, 4)) for p in range(2)]
-        out = fold(
-            "fold0",
-            [self.mine, self.came],
-            shape,
-            [([(0, (k, p)), (1, (k, p))], BF, [(o, into, flat)]) for k, p, o, into in places],
-            [sds(shape, BF)] * 2 + [sds((2, *shape), BF)] * 3,
-        )
-        self.across = out[:2]
-        self.x, self.y, self.own = out[2:]
-
-    def send_across(self):
+            self.across = hold(self.across, after)
         self.across = swap(self.across[0], "dp", 4), swap(self.across[1], "dp", 2)
 
     def fold1(self):
         self.x, self.y = fold1(self.x, self.y, self.across)
+
+    def send_on(self, after=()):
+        if after:
+            self.x, self.y = hold([self.x, self.y], after)
         self.came = swap(self.x, "dp", 2), swap(self.y, "dp", 4)
 
     def fold2(self):
@@ -1168,14 +1479,10 @@
             [([(i, (p,)) for i in range(3)], BF, [(p, flat, flat)]) for p in range(2)],
             [sds(shape, BF)] * 2,
         )
-        self.bits = axis_bits("expert", 1)
         self.send()
 
     def send(self):
-        n = len(self.bits)
-        up_bit = self.bits[self.done] if hasattr(self, "done") else self.bits[0]
-        self.done = getattr(self, "done", 0)
-        down_bit = self.bits[n - 1 - self.done]
+        up_bit, down_bit = self.bits[self.done], self.bits[-1 - self.done]
         self.came = swap(self.parts[0], "expert", up_bit), swap(self.parts[1], "expert", down_bit)
 
     def fold3(self, layer, layers, given):
@@ -1277,7 +1584,8 @@
     assert width == HEADS * HEAD_DIM
     padded = up(tokens, 16)
     cap = 2 * tokens // experts
-    cap_pad = up(cap, 8)
+    cap_pad = up(cap + 2, 8)
+    assert cap_pad <= LANES
     shard = w_qkv.shape[1]
     hidden_shard = w_outexp.shape[2]
     hidden = w_in.shape[3]
@@ -1287,7 +1595,6 @@
     z = lax.axis_index("expert").astype(jnp.int32).reshape(1)
     bits = axis_bits("dp", 2)
     four = bits == [2, 4] and shard % 16 == 0 and axis_bits("expert", 1) == [1, 2]
-    order = ORDER if four else None
 
     Order.token = None
 
@@ -1327,7 +1634,6 @@
             [sds((2, shard, hidden), BF)],
         )[0]
 
-    aligned = shard % 16 == 0
     whole = [(None, (0,)), (None, (1,))]
 
     def fetch_attn(layer):
@@ -1338,7 +1644,7 @@
         return Weights(attn, whole)
 
     def fetch_expert(layer):
-        if aligned:
+        if four:
             both = lax.all_gather(pack_expert(layer), "dp", axis=0)
             return Weights([both], [(OWNERS, (0, 1))])
         both = [gather_rows(w_in[layer, 0])[None], gather_rows(w_outexp[layer, 0])[None]]
@@ -1354,6 +1660,7 @@
         routes, seat_order.reshape(layers, tokens, 2), padded, cap, cap_pad, z
     )
     small = pack_small(norm_gains, biases, w_router, b_in, b_expout)
+    grad, grad_seats = top_seats(cotangent, rows[last], cap_pad, experts)
     if four:
         attn_w[0].turn()
         attn_w[0].send()
@@ -1380,8 +1687,14 @@
             cols[layer],
             rows[layer],
             cap_pad,
+            cap,
         )
+        x, x1, qkv, gates, ao = kept
         sent = exchange(sent)
+        other_ao = None
+        if four:
+            ao, other_ao = pick_columns(me, ao, shards)
+            other_ao = swap(other_ao, "dp", 1)
         if layer < last:
             if four:
                 attn_w[layer + 1].turn()
@@ -1389,58 +1702,41 @@
             if layer + 1 < last:
                 attn_w.append(fetch_attn(layer + 2))
         else:
-            grad, grad_seats = top_seats(
-                cotangent, kept[5], cols[last], rows[last], cap_pad, experts
-            )
             grad_seats = exchange(hold(grad_seats, sent[1:]))
-        held, made = expert_fwd(me, sent, expert_w[layer], bias_in, bias_oe)
+        (rh, slope, gate, out), made = expert_fwd(
+            me, sent, expert_w[layer], bias_in, bias_oe, cap
+        )
         if four and layer < last:
             attn_w[layer + 1].cross(made[:1])
-        returned = exchange(made)
-        saved.append((kept, held, returned))
-        x_args = (kept[1], kept[5], cols[layer], returned)
-
-    mixed = None
+        returned = exchange(made) if layer < last else made
+        other_rh = swap(rh, "dp", 1) if four else None
+        saved.append((x, x1, qkv, gates, ao, other_ao, rh, other_rh, slope, gate, out))
+        x_args = (x1, gates, cols[layer], returned)
+
     attn_sums, expert_sums = [None] * layers, [None] * layers
     for layer in reversed(range(layers)):
-        (x, x1, a_low, qkv, o_low, gates, moe_low), (seat_rows, h, slope), returned = saved[layer]
+        x, x1, qkv, gates, ao, other_ao, rh, other_rh, slope, gate, out = saved[layer]
         vecs, router = params[layer][:2]
-
-        def gate_part():
-            return gate_back(
-                grad, x1, gates, cols[layer], router, returned, tokens, layer == last
-            )
-
-        if layer < last:
-            dz, moe_part = gate_part()
-            if four:
-                attn_sums[layer + 1] = AttnSum(g_attn, grad_seats[1:])
-        d_out, d_pre, d_rows = expert_back(me, grad_seats, slope, expert_w[layer])
+        if four and layer < last:
+            g_attn = attn_grads(me, z, *attn_operands, g_bias, shards, True)
+            attn_sums[layer + 1] = AttnSum(hold(g_attn, grad_seats[1:]))
+        gd, d_rows = expert_back(me, grad_seats, slope, gate, out, expert_w[layer], cap)
         d_back = exchange(d_rows)
-        if layer == last:
-            dz, moe_part, mixed = gate_part()
-        g_expert, g_bias = expert_grads(seat_rows, h, d_out, d_pre, shards, aligned)
-        held = list(g_expert)
-        above = attn_sums[layer + 1] if four and layer < last else None
-        if above:
-            above.fold0()
-            held += above.across
-        held = hold(held, d_back[1:])
-        g_expert = held[: len(g_expert)]
-        if above:
-            above.across = held[len(g_expert) :]
-            above.send_across()
-        if aligned:
-            expert_sums[layer] = lax.psum_scatter(g_expert[0], "dp", scatter_dimension=0)
+        other = (other_rh, swap(gd, "dp", 1)) if four else None
+        g_expert, g_bias = expert_grads(me, (rh, gd), other, shards)
+        if four:
+            (g_expert,) = hold(g_expert, d_back[1:])
+            expert_sums[layer] = scatter_chips(g_expert)
         else:
             expert_sums[layer] = [scatter_rows(v) for v in g_expert]
         below = None
         if layer > 0:
-            below = (saved[layer - 1][0][5], cols[layer - 1], rows[layer - 1])
-        (grad, dy, dqkv, small_grads), grad_seats = attn_back(
+            below = rows[layer - 1]
+        (grad, back), grad_seats = attn_back(
             me,
             d_back,
-            moe_part,
+            gates,
+            router,
             grad,
             x,
             x1,
@@ -1450,36 +1746,37 @@
             attn_w[layer],
             below,
             tokens,
+            cap,
         )
         grad_seats = exchange(grad_seats) if layer > 0 else None
-        if above:
-            above.fold1()
-        g_attn = attn_grads(
-            me, z, a_low, o_low, moe_low, dqkv, dy, dz, small_grads, g_bias, shard, order
-        )
-        if not four:
+        if four:
+            attn_operands = (ao, back), (other_ao, swap(back, "dp", 1))
+        else:
+            g_attn = attn_grads(me, z, (ao, back), None, g_bias, shards, False)
             attn_sums[layer] = [sum_experts(scatter_rows(v)) for v in g_attn]
 
     if four:
-        done_attn, smalls = (), [None] * layers
+        done_attn, smalls, done_expert = (), [None] * layers, ()
+        for layer in reversed(range(1, layers)):
+            done_expert = expert_out(expert_sums[layer], layer, layers, done_expert, width)
+        g_attn = attn_grads(me, z, *attn_operands, g_bias, shards, False)
         attn_sums[0] = AttnSum(g_attn)
-        attn_sums[0].fold0()
         attn_sums[0].send_across()
+        attn_sums[0].fold1()
+        attn_sums[0].send_on()
         for layer in reversed(range(1, layers)):
-            attn_sums[layer].fold2()
-        attn_sums[0].fold1()
+            attn_sums[layer].cut()
+    returned = exchange(hold(made, g_attn[:1]))
+    mixed = mix(x_args[0], x_args[1], x_args[2], returned, tokens)
+    if four:
+        attn_sums[0].fold2()
         for layer in reversed(range(1, layers)):
             attn_sums[layer].fold3(layer, layers, done_attn)
-        attn_sums[0].fold2()
+        attn_sums[0].fold3(0, layers, done_attn)
         for layer in reversed(range(1, layers)):
             out = attn_sums[layer].fold3(layer, layers, done_attn)
             done_attn, smalls[layer] = out[:2], out[2]
-    if aligned:
-        done_expert = ()
-        for layer in reversed(range(layers)):
-            done_expert = expert_out(expert_sums[layer], layer, layers, done_expert, width)
-            if four and layer == 1:
-                attn_sums[0].fold3(0, layers, done_attn)
+        done_expert = expert_out(expert_sums[0], 0, layers, done_expert, width)
         grad_in, grad_oe = done_expert
     else:
         grad_in = jnp.stack([item[0] for item in expert_sums])[:, None].astype(F32)

time: 427 us -> 415 us (0.972)
  Pallas kernels: 198 us -> 185 us
  waiting for transfers between devices: 96.6 us -> 101 us
    pallas_call x43 -> x42, Pallas kernels: 198 us -> 185 us  [call(): pl.pallas_call(body, name=name, in_specs=[ANY if spec is LOAD else spec f...]
    ppermute x56 -> x58, waiting for transfers between devices: 95.3 us -> 101 us  [swap(): return lax.ppermute(value, axis, [(i, i ^ bit) for i in range(size)])]
    ppermute x56 -> x58, starting transfers between devices: 72.9 us -> 69 us  [swap(): return lax.ppermute(value, axis, [(i, i ^ bit) for i in range(size)])]
    unnamed x128 -> x132, local copies, waits for them, and re-layouts: 22.9 us -> 22.6 us
  transfers between devices with their start and end apart: 60 -> 63, of which waited for: 23 -> 22; matrix products, arithmetic and copies ran while one was open for 1% -> 1% of each run, Pallas kernels for 45% -> 43%
where the time goes in v3:
time: 415 us; the launch traced here: 411 us
  Pallas kernels  185 us (45%)
  waiting for transfers between devices  101 us (24%)
  starting transfers between devices  69.6 us (17%)
  local copies, waits for them, and re-layouts  23.4 us (6%)
  blocking collectives  16.9 us (4%)
  between operations  14.9 us (4%)
    pallas_call x42, Pallas kernels, call(): pl.pallas_call(body, name=name, in_specs=[ANY if spec is LOAD else spec f...  185 us
    ppermute x58, waiting for transfers between devices, swap(): return lax.ppermute(value, axis, [(i, i ^ bit) for i in range(size)])  101 us
    ppermute x58, starting transfers between devices, swap(): return lax.ppermute(value, axis, [(i, i ^ bit) for i in range(size)])  69 us
    unnamed x132, local copies, waits for them, and re-layouts  22.6 us
    all_gather x1, blocking collectives, per_device(): small = lax.all_gather(small, 'dp', axis=0)  16.9 us
  transfers between devices with their start and end apart: 63, of which 22 were waited for; matrix products, arithmetic and copies ran while one was open for 1% of the time, Pallas kernels for 43%

profile of v3, /device:TPU:0, one launch (start us, length us, event | category | flops | bytes accessed | tf_op | source)
XLA Modules:
  0.0 411.4 jit_solution(4985449893616844041)
XLA Ops:
  21.4 3.4 place_pairs.1
  28.7 8.5 %collective-permute-done.refs_0_.refs_3_.refs_14_ = bf16[2,96,1536]{2,1,0:T(8,128)(2,1)S(1)} collective-permute-done((bf16[2,96,1536]{2,1,0:T(8,128)(2,1)S(1)}, bf16[2,96,1536]{2,1,0:T(8,128)(2,1)S(1)}, u32[]{:S(2)}, u32[]{:S(2)}) %collective-permute-start) | collective-permute-done | bytes 589856 | tf_op jit(solution)/shard_map/ppermute | solution.py:1345
  46.0 16.9 %all-gather = f32[256,128]{1,0:T(8,128)} all-gather(f32[32,128]{1,0:T(8,128)S(1)} %copy-done.53), channel_id=2, replica_groups=mesh['dp'=8,'expert'=4] {'dp'}, dimensions={0}, use_global_device_ids=true | all-gather | bytes 147456 | tf_op jit(solution)/shard_map/all_gather | solution.py:1667
  72.4 8.6 %attn_fwd.2 = (f32[208,768]{1,0:T(8,128)}, f32[208,768]{1,0:T(8,128)}, bf16[208,2304]{1,0:T(8,128)(2,1)}, f32[208,128]{1,0:T(8,128)}, bf16[208,2304]{1,0:T(8,128...) custom-call(s32[1]{0:T(128)} %bitcast.refs_0_, ...), custom_call_target="tpu_custom_call" | custom-call | tf_op jit(solution)/shard_map/attn_fwd/pallas_call | solution.py:243
  82.6 3.2 collective-permute-start.8
  85.8 3.2 pick_columns.2
  88.9 4.8 %collective-permute-done.10.refs_0_.refs_9_.refs_14_ = bf16[2,96,1536]{2,1,0:T(8,128)(2,1)S(1)} collective-permute-done((bf16[2,96,1536]{2,1,0:T(8,128)(2,1)}, bf16[2,96,1536]{2,1,0:T(8,128)(2,1)S(1)}, u32[]{:S(2)}, u32[]{:S(2)}) %collective-permute-start.10) | collective-permute-done | bytes 589856 | tf_op jit(solution)/shard_map/ppermute | solution.py:1345
  100.9 13.2 %expert_fwd.2 = (bf16[416,3840]{1,0:T(8,128)(2,1)}, bf16[416,3072]{1,0:T(8,128)(2,1)}, f32[416,128]{1,0:T(8,128)}, bf16[416,768]{1,0:T(8,128)(2,1)}, bf16[104,76...) custom-call(s32[1]{0:T(128)} %bitcast.refs_0_, ...), custom_call_target="tpu_custom_call" | custom-call | tf_op jit(solution)/shard_map/expert_fwd/pallas_call | solution.py:243
  116.8 4.0 collective-permute-start.12
  123.4 4.4 %collective-permute-done.12.refs_5_ = bf16[104,768]{1,0:T(8,128)(2,1)S(1)} collective-permute-done((bf16[104,768]{1,0:T(8,128)(2,1)S(1)}, bf16[104,768]{1,0:T(8,128)(2,1)S(1)}, u32[]{:S(2)}, u32[]{:S(2)}) %collective-permute-start.12) | collective-permute-done | bytes 159776 | tf_op jit(solution)/shard_map/ppermute | solution.py:1345
  127.8 7.8 %collective-permute-done.13.refs_6_ = bf16[104,768]{1,0:T(8,128)(2,1)S(1)} collective-permute-done((bf16[104,768]{1,0:T(8,128)(2,1)S(1)}, bf16[104,768]{1,0:T(8,128)(2,1)S(1)}, u32[]{:S(2)}, u32[]{:S(2)}) %collective-permute-start.13) | collective-permute-done | bytes 159776 | tf_op jit(solution)/shard_map/ppermute | solution.py:1345
  136.5 8.9 %attn_fwd.3 = (f32[208,768]{1,0:T(8,128)}, f32[208,768]{1,0:T(8,128)}, bf16[208,2304]{1,0:T(8,128)(2,1)}, f32[208,128]{1,0:T(8,128)}, bf16[208,2304]{1,0:T(8,128...) custom-call(s32[1]{0:T(128)} %bitcast.refs_0_, ...), custom_call_target="tpu_custom_call" | custom-call | tf_op jit(solution)/shard_map/attn_fwd/pallas_call | solution.py:243
  150.9 3.1 pick_columns.3
  154.1 8.9 %collective-permute-done.21.refs_5_.refs_3_ = bf16[104,768]{1,0:T(8,128)(2,1)S(1)} collective-permute-done((bf16[104,768]{1,0:T(8,128)(2,1)}, bf16[104,768]{1,0:T(8,128)(2,1)S(1)}, u32[]{:S(2)}, u32[]{:S(2)}) %collective-permute-start.21) | collective-permute-done | bytes 159776 | tf_op jit(solution)/shard_map/ppermute | solution.py:1345
  168.5 12.8 %expert_fwd.3 = (bf16[416,3840]{1,0:T(8,128)(2,1)}, bf16[416,3072]{1,0:T(8,128)(2,1)}, f32[416,128]{1,0:T(8,128)}, bf16[416,768]{1,0:T(8,128)(2,1)}, bf16[104,76...) custom-call(s32[1]{0:T(128)} %bitcast.refs_0_, ...), custom_call_target="tpu_custom_call" | custom-call | tf_op jit(solution)/shard_map/expert_fwd/pallas_call | solution.py:243
  182.2 12.4 %expert_back.2 = (bf16[416,3840]{1,0:T(8,128)(2,1)}, bf16[104,768]{1,0:T(8,128)(2,1)}, bf16[104,768]{1,0:T(8,128)(2,1)}, bf16[104,768]{1,0:T(8,128)(2,1)}, bf16[104,768]{1,0:T(8,128)(2,1)}) custom-call(s32[1]{0:T(128)} %bitcast.refs_0_, bf16[104,768]{1,0:T(8,128)(2,1)} %get-tuple-element.188.refs_8_.refs_1_, bf16[104,768]{1,0:T(8,128)(2,1)} %copy-done.44, ...), custom_call_target="tpu_custom_call" | custom-call | tf_op jit(solution)/shard_map/expert_back/pallas_call | solution.py:243
  201.2 12.4 %expert_grads.2 = (bf16[4,2,96,3072]{3,2,1,0:T(8,128)(2,1)}, f32[8,768]{1,0:T(8,128)}) custom-call(s32[1]{0:T(128)} %bitcast.refs_0_, bf16[416,3840]{1,0:T(8,128)(2,1)} %get-tuple-element.200.refs_9_.refs_1_, bf16[416,3840]{1,0:T(8,128)(2,1)} %copy-done.8, bf16[416,3840]{1,0:T(8,128)(2,1)} %get-tuple-element.206.refs_3_, ...), custom_call_target="tpu_custom_call" | custom-call | tf_op jit(solution)/shard_map/expert_grads/pallas_call | solution.py:243
  214.5 13.6 %attn_back.2 = (f32[208,768]{1,0:T(8,128)}, bf16[224,3328]{1,0:T(8,128)(2,1)}, bf16[104,768]{1,0:T(8,128)(2,1)}, bf16[104,768]{1,0:T(8,128)(2,1)}, bf16[104,768]{1,0:T(8,128)(2,1)}, /*index=5*/bf16[104,768]{1,0:T(8,128)(2,1)}) custom-call(s32[1]{0:T(128)} %bitcast.refs_0_, bf16[104,768]{1,0:T(8,128)(2,1)} %get-tuple-element.201.refs_1_, ...), custom_call_target="tpu_custom_call" | custom-call | tf_op jit(solution)/shard_map/attn_back/pallas_call | solution.py:243
  234.4 5.0 %attn_grads.2.refs_0_ = bf16[4,2,96,1664]{3,2,1,0:T(8,128)(2,1)} custom-call(s32[1]{0:T(128)} %bitcast.refs_0_, s32[1]{0:T(128)} %bitcast.1.refs_0_.refs_1_, bf16[208,1152]{1,0:T(8,128)(2,1)} %get-tuple-element.187.refs_7_.refs_2_, bf16[208,1152]{1,0:T(8,128)(2,1)} %copy-done.33, bf16[224,3328]{1,0:T(8,128)(2,1)} %get-tuple-element.216.refs_4_, ...), custom_call_target="tpu_custom_call" | custom-call | tf_op jit(solution)/shard_map/attn_grads/pallas_call | solution.py:243
  239.5 5.0 %collective-permute-done.33.refs_2_.refs_3_ = bf16[104,768]{1,0:T(8,128)(2,1)S(1)} collective-permute-done((bf16[104,768]{1,0:T(8,128)(2,1)}, bf16[104,768]{1,0:T(8,128)(2,1)S(1)}, u32[]{:S(2)}, u32[]{:S(2)}) %collective-permute-start.33) | collective-permute-done | bytes 159776 | tf_op jit(solution)/shard_map/ppermute | solution.py:1345
  247.1 12.7 %expert_back.3 = (bf16[416,3840]{1,0:T(8,128)(2,1)}, bf16[104,768]{1,0:T(8,128)(2,1)}, bf16[104,768]{1,0:T(8,128)(2,1)}, bf16[104,768]{1,0:T(8,128)(2,1)}, bf16[104,768]{1,0:T(8,128)(2,1)}) custom-call(s32[1]{0:T(128)} %bitcast.refs_0_, bf16[104,768]{1,0:T(8,128)(2,1)} %get-tuple-element.208.refs_1_, bf16[104,768]{1,0:T(8,128)(2,1)} %copy-done.30, ...), custom_call_target="tpu_custom_call" | custom-call | tf_op jit(solution)/shard_map/expert_back/pallas_call | solution.py:243
  266.0 12.3 %expert_grads.3 = (bf16[4,2,96,3072]{3,2,1,0:T(8,128)(2,1)}, f32[8,768]{1,0:T(8,128)}) custom-call(s32[1]{0:T(128)} %bitcast.refs_0_, bf16[416,3840]{1,0:T(8,128)(2,1)} %get-tuple-element.166.refs_3_.refs_1_, bf16[416,3840]{1,0:T(8,128)(2,1)} %collective-permute-done.40.refs_2_, bf16[416,3840]{1,0:T(8,128)(2,1)} %get-tuple-element.224.refs_3_, ...), custom_call_target="tpu_custom_call" | custom-call | tf_op jit(solution)/shard_map/expert_grads/pallas_call | solution.py:243
  279.2 13.7 %attn_back.3 = (f32[197,768]{1,0:T(8,128)}, bf16[224,3328]{1,0:T(8,128)(2,1)}) custom-call(s32[1]{0:T(128)} %bitcast.refs_0_, bf16[104,768]{1,0:T(8,128)(2,1)} %get-tuple-element.219.refs_1_, bf16[104,768]{1,0:T(8,128)(2,1)} %copy-done.22, bf16[104,768]{1,0:T(8,128)(2,1)} %copy-done.23, bf16[104,768]{1,0:T(8,128)(2,1)} %copy-done.24, ...), custom_call_target="tpu_custom_call" | custom-call | tf_op jit(solution)/shard_map/attn_back/pallas_call | solution.py:243
  298.3 5.0 %attn_grads.3 = (bf16[96,1664]{1,0:T(8,128)(2,1)}, bf16[96,1664]{1,0:T(8,128)(2,1)}, bf16[2,96,1664]{2,1,0:T(8,128)(2,1)}, bf16[2,96,1664]{2,1,0:T(8,128)(2,1)}, bf16[2,96,1664]{2,1,0:T(8,128)(2,1)}) custom-call(s32[1]{0:T(128)} %bitcast.refs_0_, s32[1]{0:T(128)} %bitcast.1.refs_0_.refs_1_, bf16[208,1152]{1,0:T(8,128)(2,1)} %get-tuple-element.156.refs_3_.refs_2_, ...), custom_call_target="tpu_custom_call" | custom-call | tf_op jit(solution)/shard_map/attn_grads/pallas_call | solution.py:243
  305.7 12.5 %collective-permute-done.43.refs_2_ = bf16[96,1664]{1,0:T(8,128)(2,1)S(1)} collective-permute-done((bf16[96,1664]{1,0:T(8,128)(2,1)}, bf16[96,1664]{1,0:T(8,128)(2,1)S(1)}, u32[]{:S(2)}, u32[]{:S(2)}) %collective-permute-start.43) | collective-permute-done | bytes 319520 | tf_op jit(solution)/shard_map/ppermute | solution.py:1345
  329.6 4.0 collective-permute-done.45.refs_4_
  333.6 7.9 %collective-permute-done.46.refs_5_ = bf16[104,768]{1,0:T(8,128)(2,1)S(1)} collective-permute-done((bf16[104,768]{1,0:T(8,128)(2,1)}, bf16[104,768]{1,0:T(8,128)(2,1)S(1)}, u32[]{:S(2)}, u32[]{:S(2)}) %collective-permute-start.46) | collective-permute-done | bytes 159776 | tf_op jit(solution)/shard_map/ppermute | solution.py:1345
  354.2 8.3 %collective-permute-done.53.refs_3_ = bf16[96,1664]{1,0:T(8,128)(2,1)S(1)} collective-permute-done((bf16[96,1664]{1,0:T(8,128)(2,1)}, bf16[96,1664]{1,0:T(8,128)(2,1)S(1)}, u32[]{:S(2)}, u32[]{:S(2)}) %collective-permute-start.53) | collective-permute-done | bytes 319520 | tf_op jit(solution)/shard_map/ppermute | solution.py:1345
  365.4 3.2 collective-permute-start.57
  368.6 11.1 %collective-permute-done.51.refs_3_ = bf16[96,1664]{1,0:T(8,128)(2,1)S(1)} collective-permute-done((bf16[96,1664]{1,0:T(8,128)(2,1)}, bf16[96,1664]{1,0:T(8,128)(2,1)S(1)}, u32[]{:S(2)}, u32[]{:S(2)}) %collective-permute-start.51) | collective-permute-done | bytes 319520 | tf_op jit(solution)/shard_map/ppermute | solution.py:1345
  382.7 3.9 collective-permute-start.55
  386.6 7.0 %collective-permute-done.56.refs_2_ = bf16[96,1664]{1,0:T(8,128)(2,1)S(1)} collective-permute-done((bf16[96,1664]{1,0:T(8,128)(2,1)}, bf16[96,1664]{1,0:T(8,128)(2,1)S(1)}, u32[]{:S(2)}, u32[]{:S(2)}) %collective-permute-start.56) | collective-permute-done | bytes 319520 | tf_op jit(solution)/shard_map/ppermute | solution.py:1345
  (276 shorter events, 134.6 us)
Async XLA Ops:
  7.2 93.7 %all-gather.6.cloned.1.call-start = ((), (), s32[]{:S(2)}) async-start(), calls=%async_computation.3 | async-start | bytes 10616832 | tf_op jit(solution)/shard_map/all_gather | solution.py:1648
  11.3 157.1 %all-gather.8.cloned.1.call-start = ((), (), s32[]{:S(2)}) async-start(), calls=%async_computation.4 | async-start | bytes 10616832 | tf_op jit(solution)/shard_map/all_gather | solution.py:1648
  13.8 279.7 %reduce-scatter.10.cloned.1.call-start = ((), (), s32[]{:S(2)}) async-start(), calls=%async_computation.5 | async-start | bytes 5898240
  13.8 23.4 %collective-permute-start = (bf16[2,96,1536]{2,1,0:T(8,128)(2,1)S(1)}, bf16[2,96,1536]{2,1,0:T(8,128)(2,1)S(1)}, u32[]{:S(2)}, u32[]{:S(2)}) collective-permute-start(bf16[2,96,1536]{2,1,0:T(8,128)(2,1)S(1)} %copy-done), channel_id=1, source_target_pairs={{0,8},{4,12},{8,0},{12,4},{16,24},{20,28},{24,16},{28,20},{1,9},{5... | collective-permute-start | bytes 1769480 | tf_op jit(solution)/shard_map/ppermute | solution.py:1345
  16.8 22.7 %collective-permute-start.1 = (bf16[2,96,1536]{2,1,0:T(8,128)(2,1)S(1)}, bf16[2,96,1536]{2,1,0:T(8,128)(2,1)S(1)}, u32[]{:S(2)}, u32[]{:S(2)}) collective-permute-start(bf16[2,96,1536]{2,1,0:T(8,128)(2,1)S(1)} %copy-done), channel_id=1, source_target_pairs={{0,16},{4,20},{8,24},{12,28},{16,0},{20,4},{24,8},{28,12},{1,17},{... | collective-permute-start | bytes 1769480 | tf_op jit(solution)/shard_map/ppermute | solution.py:1345
  43.4 27.8 %collective-permute-start.6 = (bf16[3,2,96,1536]{3,2,1,0:T(8,128)(2,1)}, bf16[3,2,96,1536]{3,2,1,0:T(8,128)(2,1)S(1)}, u32[]{:S(2)}, u32[]{:S(2)}) collective-permute-start(bf16[3,2,96,1536]{3,2,1,0:T(8,128)(2,1)} %get-tuple-element.142), channel_id=1, source_target_pairs={{0,4},{4,0},{8,12},{12,8},{16,20},{20,16},{24,28},{28,24},{1,5},{5... | collective-permute-start | bytes 5308424 | tf_op jit(solution)/shard_map/ppermute | solution.py:1345
  43.5 25.3 %collective-permute-start.2 = (bf16[1,96,1536]{2,1,0:T(8,128)(2,1)}, bf16[1,96,1536]{2,1,0:T(8,128)(2,1)S(1)}, u32[]{:S(2)}, u32[]{:S(2)}) collective-permute-start(bf16[1,96,1536]{2,1,0:T(8,128)(2,1)} %get-tuple-element.140.refs_1_), channel_id=1, source_target_pairs={{0,16},{4,20},{8,24},{12,28},{16,0},{20,4},{24,8},{28,12},{1,17},{... | collective-permute-start | bytes 884744 | tf_op jit(solution)/shard_map/ppermute | solution.py:1345
  46.0 22.9 %collective-permute-start.3 = (bf16[1,96,1536]{2,1,0:T(8,128)(2,1)}, bf16[1,96,1536]{2,1,0:T(8,128)(2,1)}, u32[]{:S(2)}, u32[]{:S(2)}) collective-permute-start(bf16[1,96,1536]{2,1,0:T(8,128)(2,1)} %get-tuple-element.141), channel_id=1, source_target_pairs={{0,8},{4,12},{8,0},{12,4},{16,24},{20,28},{24,16},{28,20},{1,9},{5... | collective-permute-start | bytes 884744 | tf_op jit(solution)/shard_map/ppermute | solution.py:1345
  66.7 27.0 %collective-permute-start.10 = (bf16[2,96,1536]{2,1,0:T(8,128)(2,1)}, bf16[2,96,1536]{2,1,0:T(8,128)(2,1)S(1)}, u32[]{:S(2)}, u32[]{:S(2)}) collective-permute-start(bf16[2,96,1536]{2,1,0:T(8,128)(2,1)} %pack_attn.3.refs_15_.refs_2_.refs_8_.refs_13_), channel_id=1, source_target_pairs={{0,8},{4,12},{8,0},{12,4},{16,24},{20,28},{24,16},{28,20},{1,9},{5... | collective-permute-start | bytes 1769480 | tf_op jit(solution)/shard_map/ppermute | solution.py:1345
  68.8 25.0 %collective-permute-start.11 = (bf16[2,96,1536]{2,1,0:T(8,128)(2,1)}, bf16[2,96,1536]{2,1,0:T(8,128)(2,1)S(1)}, u32[]{:S(2)}, u32[]{:S(2)}) collective-permute-start(bf16[2,96,1536]{2,1,0:T(8,128)(2,1)} %pack_attn.3.refs_15_.refs_2_.refs_8_.refs_13_), channel_id=1, source_target_pairs={{0,16},{4,20},{8,24},{12,28},{16,0},{20,4},{24,8},{28,12},{1,17},{... | collective-permute-start | bytes 1769480 | tf_op jit(solution)/shard_map/ppermute | solution.py:1345
  81.0 16.7 %collective-permute-start.7 = (bf16[104,768]{1,0:T(8,128)(2,1)}, bf16[104,768]{1,0:T(8,128)(2,1)S(1)}, u32[]{:S(2)}, u32[]{:S(2)}) collective-permute-start(bf16[104,768]{1,0:T(8,128)(2,1)} %get-tuple-element.149), channel_id=1, source_target_pairs={{0,1},{1,0},{2,3},{3,2},{4,5},{5,4},{6,7},{7,6},{8,9},{9,8},{10,11... | collective-permute-start | bytes 479240 | tf_op jit(solution)/shard_map/ppermute | solution.py:1345
  98.6 23.3 %collective-permute-start.19 = (bf16[3,2,96,1536]{3,2,1,0:T(8,128)(2,1)}, bf16[3,2,96,1536]{3,2,1,0:T(8,128)(2,1)S(1)}, u32[]{:S(2)}, u32[]{:S(2)}) collective-permute-start(bf16[3,2,96,1536]{3,2,1,0:T(8,128)(2,1)} %get-tuple-element.169), channel_id=1, source_target_pairs={{0,4},{4,0},{8,12},{12,8},{16,20},{20,16},{24,28},{28,24},{1,5},{5... | collective-permute-start | bytes 5308424 | tf_op jit(solution)/shard_map/ppermute | solution.py:1345
  116.2 19.4 %collective-permute-start.17 = (bf16[1,96,1536]{2,1,0:T(8,128)(2,1)}, bf16[1,96,1536]{2,1,0:T(8,128)(2,1)S(1)}, u32[]{:S(2)}, u32[]{:S(2)}) collective-permute-start(bf16[1,96,1536]{2,1,0:T(8,128)(2,1)} %get-tuple-element.167.refs_11_.refs_16_), channel_id=1, source_target_pairs={{0,4},{4,0},{8,12},{12,8},{16,20},{20,16},{24,28},{28,24},{1,5},{5... | collective-permute-start | bytes 884744 | tf_op jit(solution)/shard_map/ppermute | solution.py:1345
  116.3 19.3 %collective-permute-start.18 = (bf16[1,96,1536]{2,1,0:T(8,128)(2,1)}, bf16[1,96,1536]{2,1,0:T(8,128)(2,1)S(1)}, u32[]{:S(2)}, u32[]{:S(2)}) collective-permute-start(bf16[1,96,1536]{2,1,0:T(8,128)(2,1)} %get-tuple-element.168.refs_12_.refs_17_), channel_id=1, source_target_pairs={{0,4},{4,0},{8,12},{12,8},{16,20},{20,16},{24,28},{28,24},{1,5},{5... | collective-permute-start | bytes 884744 | tf_op jit(solution)/shard_map/ppermute | solution.py:1345
  163.8 17.6 %collective-permute-start.24 = (bf16[104,768]{1,0:T(8,128)(2,1)}, bf16[104,768]{1,0:T(8,128)(2,1)S(1)}, u32[]{:S(2)}, u32[]{:S(2)}) collective-permute-start(bf16[104,768]{1,0:T(8,128)(2,1)} %get-tuple-element.194), channel_id=1, source_target_pairs={{0,1},{1,0},{2,3},{3,2},{4,5},{5,4},{6,7},{7,6},{8,9},{9,8},{10,11... | collective-permute-start | bytes 479240 | tf_op jit(solution)/shard_map/ppermute | solution.py:1345
  181.3 18.3 %collective-permute-start.30 = (bf16[416,3840]{1,0:T(8,128)(2,1)}, bf16[416,3840]{1,0:T(8,128)(2,1)S(1)}, u32[]{:S(2)}, u32[]{:S(2)}) collective-permute-start(bf16[416,3840]{1,0:T(8,128)(2,1)} %get-tuple-element.200.refs_9_.refs_1_), channel_id=1, source_target_pairs={{0,4},{4,0},{8,12},{12,8},{16,20},{20,16},{24,28},{28,24},{1,5},{5... | collective-permute-start | bytes 9584648 | tf_op jit(solution)/shard_map/ppermute | solution.py:1345
  195.2 18.5 %collective-permute-start.27 = (bf16[104,768]{1,0:T(8,128)(2,1)}, bf16[104,768]{1,0:T(8,128)(2,1)S(1)}, u32[]{:S(2)}, u32[]{:S(2)}) collective-permute-start(bf16[104,768]{1,0:T(8,128)(2,1)} %get-tuple-element.202), channel_id=1, source_target_pairs={{0,1},{1,0},{2,3},{3,2},{4,5},{5,4},{6,7},{7,6},{8,9},{9,8},{10,11... | collective-permute-start | bytes 479240 | tf_op jit(solution)/shard_map/ppermute | solution.py:1345
  196.2 17.4 %collective-permute-start.28 = (bf16[104,768]{1,0:T(8,128)(2,1)}, bf16[104,768]{1,0:T(8,128)(2,1)S(1)}, u32[]{:S(2)}, u32[]{:S(2)}) collective-permute-start(bf16[104,768]{1,0:T(8,128)(2,1)} %get-tuple-element.203), channel_id=1, source_target_pairs={{0,2},{1,3},{2,0},{3,1},{4,6},{5,7},{6,4},{7,5},{8,10},{9,11},{10,... | collective-permute-start | bytes 479240 | tf_op jit(solution)/shard_map/ppermute | solution.py:1345
  214.5 108.8 %reduce-scatter.12.cloned.1.call-start = ((), (), s32[]{:S(2)}) async-start(), calls=%async_computation.6 | async-start | bytes 3194880
  245.1 152.2 %reduce-scatter.14.cloned.1.call-start = ((), (), s32[]{:S(2)}) async-start(), calls=%async_computation.7 | async-start | bytes 5898240
  247.1 18.3 %collective-permute-start.40 = (bf16[416,3840]{1,0:T(8,128)(2,1)S(1)}, bf16[416,3840]{1,0:T(8,128)(2,1)}, u32[]{:S(2)}, u32[]{:S(2)}) collective-permute-start(bf16[416,3840]{1,0:T(8,128)(2,1)S(1)} %copy-done.1), channel_id=1, source_target_pairs={{0,4},{4,0},{8,12},{12,8},{16,20},{20,16},{24,28},{28,24},{1,5},{5... | collective-permute-start | bytes 9584648 | tf_op jit(solution)/shard_map/ppermute | solution.py:1345
  260.3 18.0 %collective-permute-start.37 = (bf16[104,768]{1,0:T(8,128)(2,1)}, bf16[104,768]{1,0:T(8,128)(2,1)S(1)}, u32[]{:S(2)}, u32[]{:S(2)}) collective-permute-start(bf16[104,768]{1,0:T(8,128)(2,1)} %get-tuple-element.220), channel_id=1, source_target_pairs={{0,1},{1,0},{2,3},{3,2},{4,5},{5,4},{6,7},{7,6},{8,9},{9,8},{10,11... | collective-permute-start | bytes 479240 | tf_op jit(solution)/shard_map/ppermute | solution.py:1345
  321.2 24.7 %collective-permute-start.48 = (bf16[2,96,1664]{2,1,0:T(8,128)(2,1)}, bf16[2,96,1664]{2,1,0:T(8,128)(2,1)S(1)}, u32[]{:S(2)}, u32[]{:S(2)}) collective-permute-start(bf16[2,96,1664]{2,1,0:T(8,128)(2,1)} %get-tuple-element.234.refs_1_), channel_id=1, source_target_pairs={{0,8},{4,12},{8,0},{12,4},{16,24},{20,28},{24,16},{28,20},{1,9},{5... | collective-permute-start | bytes 1916936 | tf_op jit(solution)/shard_map/ppermute | solution.py:1345
  322.7 25.6 %collective-permute-start.49 = (bf16[2,96,1664]{2,1,0:T(8,128)(2,1)}, bf16[2,96,1664]{2,1,0:T(8,128)(2,1)S(1)}, u32[]{:S(2)}, u32[]{:S(2)}) collective-permute-start(bf16[2,96,1664]{2,1,0:T(8,128)(2,1)} %get-tuple-element.241), channel_id=1, source_target_pairs={{0,16},{4,20},{8,24},{12,28},{16,0},{20,4},{24,8},{28,12},{1,17},{... | collective-permute-start | bytes 1916936 | tf_op jit(solution)/shard_map/ppermute | solution.py:1345
  333.6 20.6 %collective-permute-start.52 = (bf16[96,1664]{1,0:T(8,128)(2,1)}, bf16[96,1664]{1,0:T(8,128)(2,1)S(1)}, u32[]{:S(2)}, u32[]{:S(2)}) collective-permute-start(bf16[96,1664]{1,0:T(8,128)(2,1)} %get-tuple-element.235.refs_5_.refs_0_), channel_id=1, source_target_pairs={{0,1},{1,0},{2,3},{3,2},{4,5},{5,4},{6,7},{7,6},{8,9},{9,8},{10,11... | collective-permute-start | bytes 958472 | tf_op jit(solution)/shard_map/ppermute | solution.py:1345
  341.5 21.0 %collective-permute-start.53 = (bf16[96,1664]{1,0:T(8,128)(2,1)}, bf16[96,1664]{1,0:T(8,128)(2,1)S(1)}, u32[]{:S(2)}, u32[]{:S(2)}) collective-permute-start(bf16[96,1664]{1,0:T(8,128)(2,1)} %get-tuple-element.244.refs_1_), channel_id=1, source_target_pairs={{0,2},{1,3},{2,0},{3,1},{4,6},{5,7},{6,4},{7,5},{8,10},{9,11},{10,... | collective-permute-start | bytes 958472 | tf_op jit(solution)/shard_map/ppermute | solution.py:1345
  351.8 16.9 %collective-permute-start.50 = (bf16[96,1664]{1,0:T(8,128)(2,1)}, bf16[96,1664]{1,0:T(8,128)(2,1)S(1)}, u32[]{:S(2)}, u32[]{:S(2)}) collective-permute-start(bf16[96,1664]{1,0:T(8,128)(2,1)} %get-tuple-element.242.refs_4_.refs_0_), channel_id=1, source_target_pairs={{0,1},{1,0},{2,3},{3,2},{4,5},{5,4},{6,7},{7,6},{8,9},{9,8},{10,11... | collective-permute-start | bytes 958472 | tf_op jit(solution)/shard_map/ppermute | solution.py:1345
  353.2 26.5 %collective-permute-start.51 = (bf16[96,1664]{1,0:T(8,128)(2,1)}, bf16[96,1664]{1,0:T(8,128)(2,1)S(1)}, u32[]{:S(2)}, u32[]{:S(2)}) collective-permute-start(bf16[96,1664]{1,0:T(8,128)(2,1)} %get-tuple-element.243.refs_1_), channel_id=1, source_target_pairs={{0,2},{1,3},{2,0},{3,1},{4,6},{5,7},{6,4},{7,5},{8,10},{9,11},{10,... | collective-permute-start | bytes 958472 | tf_op jit(solution)/shard_map/ppermute | solution.py:1345
  365.3 28.3 %collective-permute-start.56 = (bf16[96,1664]{1,0:T(8,128)(2,1)}, bf16[96,1664]{1,0:T(8,128)(2,1)S(1)}, u32[]{:S(2)}, u32[]{:S(2)}) collective-permute-start(bf16[96,1664]{1,0:T(8,128)(2,1)} %get-tuple-element.245.refs_4_.refs_0_), channel_id=1, source_target_pairs={{0,2},{1,3},{2,0},{3,1},{4,6},{5,7},{6,4},{7,5},{8,10},{9,11},{10,... | collective-permute-start | bytes 958472 | tf_op jit(solution)/shard_map/ppermute | solution.py:1345
  365.4 28.2 %collective-permute-start.57 = (bf16[96,1664]{1,0:T(8,128)(2,1)}, bf16[96,1664]{1,0:T(8,128)(2,1)S(1)}, u32[]{:S(2)}, u32[]{:S(2)}) collective-permute-start(bf16[96,1664]{1,0:T(8,128)(2,1)} %get-tuple-element.248.refs_1_), channel_id=1, source_target_pairs={{0,1},{1,0},{2,3},{3,2},{4,5},{5,4},{6,7},{7,6},{8,9},{9,8},{10,11... | collective-permute-start | bytes 958472 | tf_op jit(solution)/shard_map/ppermute | solution.py:1345
  382.6 17.3 %collective-permute-start.54 = (bf16[96,1664]{1,0:T(8,128)(2,1)}, bf16[96,1664]{1,0:T(8,128)(2,1)S(1)}, u32[]{:S(2)}, u32[]{:S(2)}) collective-permute-start(bf16[96,1664]{1,0:T(8,128)(2,1)} %get-tuple-element.246.refs_4_.refs_0_), channel_id=1, source_target_pairs={{0,2},{1,3},{2,0},{3,1},{4,6},{5,7},{6,4},{7,5},{8,10},{9,11},{10,... | collective-permute-start | bytes 958472 | tf_op jit(solution)/shard_map/ppermute | solution.py:1345
  382.7 17.3 %collective-permute-start.55 = (bf16[96,1664]{1,0:T(8,128)(2,1)}, bf16[96,1664]{1,0:T(8,128)(2,1)S(1)}, u32[]{:S(2)}, u32[]{:S(2)}) collective-permute-start(bf16[96,1664]{1,0:T(8,128)(2,1)} %get-tuple-element.247.refs_1_), channel_id=1, source_target_pairs={{0,1},{1,0},{2,3},{3,2},{4,5},{5,4},{6,7},{7,6},{8,9},{9,8},{10,11... | collective-permute-start | bytes 958472 | tf_op jit(solution)/shard_map/ppermute | solution.py:1345
  (95 other events, 581.4 us)
Sparse Core Ops, SparseCore 0:
  11.4 82.1 all-gather.5
  95.5 62.7 all-gather.7
  214.6 56.0 reduce-scatter.9
  273.7 43.8 reduce-scatter.11
  320.4 66.6 reduce-scatter.13

commit v4 on v3

--- a/solution.py
+++ b/solution.py
@@ -509,12 +509,13 @@
     )
 
 
-def unpack_small(gathered, layers, shard, per, experts):
+def unpack_small(gathered, layers, shard, per, experts, after):
     shards = gathered.shape[0]
     width = shards * shard
     height = small_rows(per, experts)
 
     def kernel(ref, *refs):
+        refs = refs[len(after) :]
         tall = refs[-1]
         for layer in range(layers):
             vec, router, bias_in, bias_oe = refs[4 * layer : 4 * layer + 4]
@@ -543,8 +544,8 @@
     outs = call(
         kernel,
         "unpack_small",
-        [gathered],
-        [VM],
+        [gathered, *after],
+        [VM] + [ANY] * len(after),
         shapes,
         [VM] * len(shapes),
         [pltpu.VMEM((LANES, width), F32)],
@@ -723,7 +724,7 @@
     return result[:5], result[5:]
 
 
-def expert_fwd(me, seat_blocks, weights, bias_in, bias_oe, used):
+def expert_fwd(me, z, seat_blocks, weights, bias_in, bias_oe, used, ordered):
     owners = len(seat_blocks)
     cap, width = seat_blocks[0].shape
     seats = owners * cap
@@ -735,12 +736,12 @@
 
     def kernel(*refs):
         refs = list(refs)
-        me_ref = refs.pop(0)
+        me_ref, z_ref = refs.pop(0), refs.pop(0)
         seat_refs = [refs.pop(0) for _ in range(owners)]
         w_refs = [refs.pop(0) for _ in range(count)]
         bin_ref, boe_ref = refs.pop(0), refs.pop(0)
         rh_out, slope_out, gate_out, made_out = (refs.pop(0) for _ in range(4))
-        outs = [refs.pop(0) for _ in range(owners)]
+        outs = [refs.pop(0) for _ in range(1 if ordered else owners)]
         win, woe, sems = refs
         chunks = Chunks(w_refs, weights, width, hidden, shard, whole, win, woe, sems)
         blocks = [ref[...].astype(F32) for ref in seat_refs]
@@ -767,6 +768,8 @@
             total_out = piece if total_out is None else total_out + piece
         total_out = total_out + boe_ref[...]
         made_out[...] = total_out.astype(BF)
+        if ordered:
+            outs = [outs[0].held.at[z_ref[0] ^ k] for k in range(owners)]
         part(total_out, outs)
 
     shapes = [
@@ -774,14 +777,14 @@
         sds((seats, hidden), BF),
         sds((seats, LANES), F32),
         sds((seats, width), BF),
-    ] + [sds((cap, width), BF)] * owners
+    ] + ([sds((owners, cap, width), BF)] if ordered else [sds((cap, width), BF)] * owners)
     result = call(
         kernel,
         "expert_fwd",
-        [me, *seat_blocks, *weights.arrays, bias_in, bias_oe],
-        [SM] + [LOAD] * owners + [ANY] * count + [LOAD] * 2,
+        [me, z, *seat_blocks, *weights.arrays, bias_in, bias_oe],
+        [SM, SM] + [LOAD] * owners + [ANY] * count + [LOAD] * 2,
         shapes,
-        [STORE] * (4 + owners),
+        [STORE] * len(shapes),
         [
             pltpu.VMEM((width, hidden), BF),
             pltpu.VMEM((hidden, width), BF),
@@ -791,49 +794,51 @@
     return result[:4], result[4:]
 
 
-def top_seats(cotangent, rows, cap, experts):
+def top_seats(z, cotangent, rows, cap, experts):
     tokens, width = cotangent.shape
     padded = rows.shape[1]
 
-    def kernel(cot_ref, rows_ref, grad_out, *outs):
+    def kernel(z_ref, cot_ref, rows_ref, grad_out, out):
         grad_out[...] = jnp.zeros_like(grad_out)
         grad_out[0:tokens, :] = cot_ref[...].astype(F32)
-        part(rows_to_seats(rows_ref, cap * experts, grad_out[...].astype(BF)), outs)
-
-    shapes = [sds((padded, width), F32)] + [sds((cap, width), BF)] * experts
-    result = call(
+        sent = rows_to_seats(rows_ref, cap * experts, grad_out[...].astype(BF))
+        part(sent, [out.at[z_ref[0] ^ k] for k in range(experts)])
+
+    return call(
         kernel,
         "top_seats",
-        [cotangent, rows],
+        [z, cotangent, rows],
+        [SM, VM, VM],
+        [sds((padded, width), F32), sds((experts, cap, width), BF)],
         [VM] * 2,
-        shapes,
-        [VM] * len(shapes),
         [],
     )
-    return result[0], result[1:]
-
-
-def mix(x1, gates, cols, returned, tokens):
+
+
+def mix(z, x1, gates, cols, returned, tokens):
     width = x1.shape[1]
 
-    def kernel(x1_ref, gates_ref, cols_ref, *refs):
-        total = combine(x1_ref[...], gates_ref[...], cols_ref, join(refs[:-1]))
-        refs[-1][...] = total[0:tokens, :]
+    def kernel(z_ref, x1_ref, gates_ref, cols_ref, ref, out):
+        blocks = join([ref.at[z_ref[0] ^ k] for k in range(ref.shape[0])])
+        total = combine(x1_ref[...], gates_ref[...], cols_ref, blocks)
+        out[...] = total[0:tokens, :]
 
     return call(
         kernel,
         "mix",
-        [x1, gates, cols, *returned],
-        [VM] * (3 + len(returned)),
+        [z, x1, gates, cols, returned],
+        [SM] + [VM] * 4,
         sds((tokens, width), F32),
         VM,
         [],
     )
 
 
-def expert_back(me, grad_blocks, slope, gate, made, weights, used):
-    owners = len(grad_blocks)
-    cap, width = grad_blocks[0].shape
+def expert_back(me, z, grad_blocks, slope, gate, made, weights, used):
+    ordered = grad_blocks[0].ndim == 3
+    cap, width = grad_blocks[0].shape[-2:]
+    owners = slope.shape[0] // cap
+    count_in = len(grad_blocks)
     seats, hidden = slope.shape
     count = len(weights.arrays)
     shard = weights.arrays[0].shape[-2]
@@ -842,8 +847,8 @@
 
     def kernel(*refs):
         refs = list(refs)
-        me_ref = refs.pop(0)
-        seat_refs = [refs.pop(0) for _ in range(owners)]
+        me_ref, z_ref = refs.pop(0), refs.pop(0)
+        seat_refs = [refs.pop(0) for _ in range(count_in)]
         slope_ref, gate_ref, made_ref = (refs.pop(0) for _ in range(3))
         w_refs = [refs.pop(0) for _ in range(count)]
         gd_out = refs.pop(0)
@@ -858,7 +863,11 @@
             for at in range(0, hidden, step)
         ]
         chunks = Chunks(w_refs, weights, width, hidden, shard, whole, win, woe, sems, more)
-        given = jnp.concatenate([ref[...].astype(F32) for ref in seat_refs], 0)
+        if ordered:
+            given = [seat_refs[0][z_ref[0] ^ k].astype(F32) for k in range(owners)]
+        else:
+            given = [ref[...].astype(F32) for ref in seat_refs]
+        given = jnp.concatenate(given, 0)
         grad = (given * gate_ref[:, 0:1]).astype(BF)
         notes = given * made_ref[...].astype(F32)
         notes = [lane_sums(notes[k * cap : (k + 1) * cap]) for k in range(owners)]
@@ -881,8 +890,8 @@
     result = call(
         kernel,
         "expert_back",
-        [me, *grad_blocks, slope, gate, made, *weights.arrays],
-        [SM] + [LOAD] * owners + [ANY] + [LOAD] * 2 + [ANY] * count,
+        [me, z, *grad_blocks, slope, gate, made, *weights.arrays],
+        [SM, SM] + [LOAD] * count_in + [ANY] + [LOAD] * 2 + [ANY] * count,
         shapes,
         [STORE] * (1 + owners),
         [
@@ -1390,27 +1399,20 @@
         self.x, self.y = swap(shard, "dp", 2), swap(shard, "dp", 4)
 
     def turn(self):
-        two, rows, width = self.shard.shape
-        block = (two, rows, width)
+        _, rows, width = self.shard.shape
         half = (1, rows, width)
         self.cut = move(
             "cut",
-            [self.x, self.y, self.shard],
-            [
-                (0, (pl.ds(0, 1),), 0, (ALL,), half),
-                (1, (pl.ds(1, 1),), 1, (ALL,), half),
-                (0, (ALL,), 2, (1,), block),
-                (1, (ALL,), 2, (2,), block),
-                (2, (ALL,), 2, (0,), block),
-            ],
-            [sds(half, BF)] * 2 + [sds((3, *block), BF)],
+            [self.x, self.y],
+            [(0, (pl.ds(0, 1),), 0, (ALL,), half), (1, (pl.ds(1, 1),), 1, (ALL,), half)],
+            [sds(half, BF)] * 2,
         )
 
     def send(self, after=()):
         if after:
             self.cut = hold(self.cut, after)
         self.xy = swap(self.cut[0], "dp", 4), swap(self.cut[1], "dp", 2)
-        self.other = swap(self.cut[2], "dp", 1)
+        self.other = [swap(value, "dp", 1) for value in (self.shard, self.x, self.y)]
 
     def cross(self, after=()):
         if after:
@@ -1426,7 +1428,9 @@
             (self.xy[1], 6, (1,)),
             (self.across[0], 7, (0,)),
             (self.across[1], 7, (1,)),
-            (self.other, (1, 3, 5), (0, 1)),
+            (self.other[0], 1, (0, 1)),
+            (self.other[1], 3, (0, 1)),
+            (self.other[2], 5, (0, 1)),
         ]
         return Weights([p[0] for p in pieces], [p[1:] for p in pieces])
 
@@ -1445,16 +1449,102 @@
         self.across, (self.x, self.y, self.own) = list(grads[:2]), grads[2:]
         self.rows, self.width = self.across[0].shape
 
-    def cut(self):
+    def cut(self, z):
         self.rows, self.width = self.total.shape[1:]
         shape = (self.rows, self.width)
-        self.parts = move(
+
+        def kernel(z_ref, total, keep, give, held, in_sems, out_sems):
+            here = z_ref[0] & 1
+            loads = [
+                pltpu.make_async_copy(total.at[k], held.at[k], in_sems.at[k]) for k in range(2)
+            ]
+            start(loads)
+            wait(loads)
+            stores = [
+                pltpu.make_async_copy(held.at[here], keep, out_sems.at[0]),
+                pltpu.make_async_copy(held.at[1 - here], give, out_sems.at[1]),
+            ]
+            start(stores)
+            wait(stores)
+
+        self.keep, give = call(
+            kernel,
             "parts",
-            [self.total],
-            [(0, (p,), p, full(self.rows), shape) for p in range(2)],
+            [z, self.total],
+            [SM, ANY],
             [sds(shape, BF)] * 2,
+            [ANY] * 2,
+            [
+                pltpu.VMEM((2, *shape), BF),
+                pltpu.SemaphoreType.DMA((2,)),
+                pltpu.SemaphoreType.DMA((2,)),
+            ],
         )
-        self.send()
+        self.come = swap(give, "expert", 1)
+
+    def halves(self):
+        shape = (self.rows, self.width)
+        flat = full(self.rows)
+        (self.keep,) = fold(
+            "fold3",
+            [self.keep, self.come],
+            shape,
+            [([(0, flat), (1, flat)], BF, [(0, flat, flat)])],
+            [sds(shape, BF)],
+        )
+        if self.done == 0:
+            self.come = swap(self.keep, "expert", 2)
+        else:
+            self.come = swap(self.keep, "expert", 1)
+        self.done += 1
+
+    def put(self, z, layer, layers, given):
+        shape = (self.rows, self.width)
+        wide = (self.width - LANES) // 2
+        count = len(given)
+
+        def kernel(z_ref, keep, come, *refs):
+            refs = refs[count:]
+            qkv, out, small, low, high, in_sems, out_sems = refs
+            here = z_ref[0] & 1
+            loads = [
+                pltpu.make_async_copy(keep, low.at[here], in_sems.at[0]),
+                pltpu.make_async_copy(come, low.at[1 - here], in_sems.at[1]),
+            ]
+            start(loads)
+            wait(loads)
+            high[...] = low[...].astype(F32)
+            stores = [
+                (high.at[0, :, pl.ds(0, 2 * wide)], qkv.at[layer, :, pl.ds(0, 2 * wide)]),
+                (high.at[1, :, pl.ds(0, wide)], qkv.at[layer, :, pl.ds(2 * wide, wide)]),
+                (high.at[1, :, pl.ds(wide, wide)], out.at[layer]),
+                (high.at[1, :, pl.ds(2 * wide, LANES)], small),
+            ]
+            stores = [
+                pltpu.make_async_copy(a, b, out_sems.at[n]) for n, (a, b) in enumerate(stores)
+            ]
+            start(stores)
+            wait(stores)
+
+        return call(
+            kernel,
+            "attn_out",
+            [z, self.keep, self.come, *given],
+            [SM] + [ANY] * (2 + count),
+            [
+                sds((layers, self.rows, 3 * wide), F32),
+                sds((layers, self.rows, wide), F32),
+                sds((self.rows, LANES), F32),
+            ],
+            [ANY] * 3,
+            [
+                pltpu.VMEM((2, *shape), BF),
+                pltpu.VMEM((2, *shape), F32),
+                pltpu.SemaphoreType.DMA((2,)),
+                pltpu.SemaphoreType.DMA((4,)),
+            ],
+            {3: 0, 4: 1} if given else None,
+        )
 
     def send_across(self, after=()):
         if after:
@@ -1660,12 +1750,13 @@
         routes, seat_order.reshape(layers, tokens, 2), padded, cap, cap_pad, z
     )
     small = pack_small(norm_gains, biases, w_router, b_in, b_expout)
-    grad, grad_seats = top_seats(cotangent, rows[last], cap_pad, experts)
+    grad, grad_seats = top_seats(z, cotangent, rows[last], cap_pad, experts)
+    grad_seats = [lax.all_to_all(grad_seats, "expert", 0, 0, tiled=True)]
     if four:
         attn_w[0].turn()
         attn_w[0].send()
     small = lax.all_gather(small, "dp", axis=0)
-    params = unpack_small(small, layers, shard, per, experts)
+    params = unpack_small(small, layers, shard, per, experts, grad_seats)
     if last > 0:
         attn_w.append(fetch_attn(1))
 
@@ -1701,10 +1792,8 @@
                 attn_w[layer + 1].send(sent[1:])
             if layer + 1 < last:
                 attn_w.append(fetch_attn(layer + 2))
-        else:
-            grad_seats = exchange(hold(grad_seats, sent[1:]))
         (rh, slope, gate, out), made = expert_fwd(
-            me, sent, expert_w[layer], bias_in, bias_oe, cap
+            me, z, sent, expert_w[layer], bias_in, bias_oe, cap, layer == last
         )
         if four and layer < last:
             attn_w[layer + 1].cross(made[:1])
@@ -1720,7 +1809,7 @@
         if four and layer < last:
             g_attn = attn_grads(me, z, *attn_operands, g_bias, shards, True)
             attn_sums[layer + 1] = AttnSum(hold(g_attn, grad_seats[1:]))
-        gd, d_rows = expert_back(me, grad_seats, slope, gate, out, expert_w[layer], cap)
+        gd, d_rows = expert_back(me, z, grad_seats, slope, gate, out, expert_w[layer], cap)
         d_back = exchange(d_rows)
         other = (other_rh, swap(gd, "dp", 1)) if four else None
         g_expert, g_bias = expert_grads(me, (rh, gd), other, shards)
@@ -1759,22 +1848,25 @@
         done_attn, smalls, done_expert = (), [None] * layers, ()
         for layer in reversed(range(1, layers)):
             done_expert = expert_out(expert_sums[layer], layer, layers, done_expert, width)
+        made = hold(made, [back])
         g_attn = attn_grads(me, z, *attn_operands, g_bias, shards, False)
         attn_sums[0] = AttnSum(g_attn)
         attn_sums[0].send_across()
         attn_sums[0].fold1()
         attn_sums[0].send_on()
         for layer in reversed(range(1, layers)):
-            attn_sums[layer].cut()
-    returned = exchange(hold(made, g_attn[:1]))
-    mixed = mix(x_args[0], x_args[1], x_args[2], returned, tokens)
+            attn_sums[layer].cut(z)
+        for layer in reversed(range(1, layers)):
+            attn_sums[layer].halves()
+    returned = lax.all_to_all(made[0], "expert", 0, 0, tiled=True)
+    mixed = mix(z, x_args[0], x_args[1], x_args[2], returned, tokens)
     if four:
         attn_sums[0].fold2()
         for layer in reversed(range(1, layers)):
-            attn_sums[layer].fold3(layer, layers, done_attn)
+            attn_sums[layer].halves()
         attn_sums[0].fold3(0, layers, done_attn)
         for layer in reversed(range(1, layers)):
-            out = attn_sums[layer].fold3(layer, layers, done_attn)
+            out = attn_sums[layer].put(z, layer, layers, done_attn)
             done_attn, smalls[layer] = out[:2], out[2]
         done_expert = expert_out(expert_sums[0], 0, layers, done_expert, width)
         grad_in, grad_oe = done_expert

time: 415 us -> 397 us (0.957)
  waiting for transfers between devices: 101 us -> 88.1 us
  blocking collectives: 16.9 us -> 10.8 us
    ppermute x58 -> x55, waiting for transfers between devices: 101 us -> 74.2 us  [swap(): return lax.ppermute(value, axis, [(i, i ^ bit) for i in range(size)])]
    all_to_all x0 -> x2, starting transfers between devices: none -> 9.68 us  [the longest x1 4.89 us: per_device(): grad_seats = [lax.all_to_all(grad_seats, 'expert', 0, 0, tiled=True)]]
    unnamed x8, waiting for transfers between devices: 0.11 us -> 8.33 us
    ppermute x58 -> x55, starting transfers between devices: 69 us -> 60.8 us  [swap(): return lax.ppermute(value, axis, [(i, i ^ bit) for i in range(size)])]
    all_gather x1, blocking collectives: 16.9 us -> 10.8 us  [per_device(): small = lax.all_gather(small, 'dp', axis=0)]
    all_gather x2, waiting for transfers between devices: 0.01 us -> 5.54 us  [fetch_expert(): both = lax.all_gather(pack_expert(layer), 'dp', axis=0)]
    unnamed x132 -> x128, local copies, waits for them, and re-layouts: 22.6 us -> 22.2 us
  transfers between devices with their start and end apart: 63 -> 62, of which waited for: 22 -> 22; matrix products, arithmetic and copies ran while one was open for 1% -> 1% of each run, Pallas kernels for 43% -> 42%
where the time goes in v4:
time: 397 us; the launch traced here: 393 us
  Pallas kernels  185 us (47%)
  waiting for transfers between devices  88.1 us (22%)
  starting transfers between devices  70.8 us (18%)
  local copies, waits for them, and re-layouts  23 us (6%)
  between operations  14.9 us (4%)
  blocking collectives  10.8 us (3%)
    pallas_call x42, Pallas kernels, call(): pl.pallas_call(body, name=name, in_specs=[ANY if spec is LOAD else spec f...  185 us
    ppermute x55, waiting for transfers between devices, swap(): return lax.ppermute(value, axis, [(i, i ^ bit) for i in range(size)])  74.2 us
    ppermute x55, starting transfers between devices, swap(): return lax.ppermute(value, axis, [(i, i ^ bit) for i in range(size)])  60.8 us
    unnamed x128, local copies, waits for them, and re-layouts  22.2 us
    all_gather x1, blocking collectives, per_device(): small = lax.all_gather(small, 'dp', axis=0)  10.8 us
    unnamed x8, waiting for transfers between devices  8.33 us
  transfers between devices with their start and end apart: 62, of which 22 were waited for; matrix products, arithmetic and copies ran while one was open for 1% of the time, Pallas kernels for 42%

profile of v4, /device:TPU:0, one launch (start us, length us, event | category | flops | bytes accessed | tf_op | source)
XLA Modules:
  0.0 392.8 jit_solution(14354357570333871196)
XLA Ops:
  21.2 3.4 place_pairs.1
  28.6 4.9 %all-to-all-start = ((bf16[4,104,768]{2,1,0:T(8,128)(2,1)}), bf16[4,104,768]{2,1,0:T(8,128)(2,1)S(1)}, u32[]{:S(2)}, u32[]{:S(2)}) async-start(bf16[4,104,768]{2,1,0:T(8,128)(2,1)} %get-tuple-element.123), calls=%async_computation | async-start | bytes 1277952 | tf_op jit(solution)/shard_map/all_to_all | solution.py:1754
  33.5 3.4 collective-permute-done.refs_0_.refs_3_.refs_14_
  44.4 6.0 %collective-permute-done.2.refs_5_.refs_16_ = bf16[1,96,1536]{2,1,0:T(8,128)(2,1)S(1)} collective-permute-done((bf16[1,96,1536]{2,1,0:T(8,128)(2,1)}, bf16[1,96,1536]{2,1,0:T(8,128)(2,1)S(1)}, u32[]{:S(2)}, u32[]{:S(2)}) %collective-permute-start.2) | collective-permute-done | bytes 294944 | tf_op jit(solution)/shard_map/ppermute | solution.py:1354
  50.9 10.8 %all-gather = f32[256,128]{1,0:T(8,128)} all-gather(f32[32,128]{1,0:T(8,128)S(1)} %copy-done.51), channel_id=2, replica_groups=mesh['dp'=8,'expert'=4] {'dp'}, dimensions={0}, use_global_device_ids=true | all-gather | bytes 147456 | tf_op jit(solution)/shard_map/all_gather | solution.py:1758
  71.2 8.9 %attn_fwd.2 = (f32[208,768]{1,0:T(8,128)}, f32[208,768]{1,0:T(8,128)}, bf16[208,2304]{1,0:T(8,128)(2,1)}, f32[208,128]{1,0:T(8,128)}, bf16[208,2304]{1,0:T(8,128...) custom-call(s32[1]{0:T(128)} %bitcast.1.refs_0_, ...), custom_call_target="tpu_custom_call" | custom-call | tf_op jit(solution)/shard_map/attn_fwd/pallas_call | solution.py:243
  84.5 4.7 %collective-permute-done.9.refs_2_.refs_3_ = bf16[104,768]{1,0:T(8,128)(2,1)S(1)} collective-permute-done((bf16[104,768]{1,0:T(8,128)(2,1)}, bf16[104,768]{1,0:T(8,128)(2,1)S(1)}, u32[]{:S(2)}, u32[]{:S(2)}) %collective-permute-start.9) | collective-permute-done | bytes 159776 | tf_op jit(solution)/shard_map/ppermute | solution.py:1354
  92.3 3.2 pick_columns.2
  100.2 13.4 %expert_fwd.2 = (bf16[416,3840]{1,0:T(8,128)(2,1)}, bf16[416,3072]{1,0:T(8,128)(2,1)}, f32[416,128]{1,0:T(8,128)}, bf16[416,768]{1,0:T(8,128)(2,1)}, bf16[104,76...) custom-call(s32[1]{0:T(128)} %bitcast.1.refs_0_, ...), custom_call_target="tpu_custom_call" | custom-call | tf_op jit(solution)/shard_map/expert_fwd/pallas_call | solution.py:243
  120.1 4.4 %collective-permute-done.14.refs_5_ = bf16[104,768]{1,0:T(8,128)(2,1)S(1)} collective-permute-done((bf16[104,768]{1,0:T(8,128)(2,1)S(1)}, bf16[104,768]{1,0:T(8,128)(2,1)S(1)}, u32[]{:S(2)}, u32[]{:S(2)}) %collective-permute-start.14) | collective-permute-done | bytes 159776 | tf_op jit(solution)/shard_map/ppermute | solution.py:1354
  124.5 7.4 %collective-permute-done.15.refs_6_ = bf16[104,768]{1,0:T(8,128)(2,1)S(1)} collective-permute-done((bf16[104,768]{1,0:T(8,128)(2,1)S(1)}, bf16[104,768]{1,0:T(8,128)(2,1)S(1)}, u32[]{:S(2)}, u32[]{:S(2)}) %collective-permute-start.15) | collective-permute-done | bytes 159776 | tf_op jit(solution)/shard_map/ppermute | solution.py:1354
  132.9 9.3 %attn_fwd.3 = (f32[208,768]{1,0:T(8,128)}, f32[208,768]{1,0:T(8,128)}, bf16[208,2304]{1,0:T(8,128)(2,1)}, f32[208,128]{1,0:T(8,128)}, bf16[208,2304]{1,0:T(8,128...) custom-call(s32[1]{0:T(128)} %bitcast.1.refs_0_, ...), custom_call_target="tpu_custom_call" | custom-call | tf_op jit(solution)/shard_map/attn_fwd/pallas_call | solution.py:243
  147.4 3.2 pick_columns.3
  150.6 5.5 %all-gather.8.cloned.1.call-done = bf16[16,96,3072]{2,1,0:T(8,128)(2,1)} async-done(((bf16[2,96,3072]{2,1,0:T(8,128)(2,1)}), bf16[16,96,3072]{2,1,0:T(8,128)(2,1)}) %all-gather.8.cloned.1.call-update) | async-done | bytes 9437200 | tf_op jit(solution)/shard_map/all_gather | solution.py:1738
  156.2 3.4 collective-permute-done.25.refs_4_
  160.3 12.3 %expert_fwd.3 = (bf16[416,3840]{1,0:T(8,128)(2,1)}, bf16[416,3072]{1,0:T(8,128)(2,1)}, f32[416,128]{1,0:T(8,128)}, bf16[416,768]{1,0:T(8,128)(2,1)}, bf16[4,104,768]{2,1,0:T(8,128)(2,1)}) custom-call(s32[1]{0:T(128)} %bitcast.1.refs_0_, s32[1]{0:T(128)} %bitcast.refs_0_.refs_1_, bf16[104,768]{1,0:T(8,128)(2,1)} %get-tuple-element.154.refs_2_, ...), custom_call_target="tpu_custom_call" | custom-call | tf_op jit(solution)/shard_map/expert_fwd/pallas_call | solution.py:243
  172.7 12.4 %expert_back.2 = (bf16[416,3840]{1,0:T(8,128)(2,1)}, bf16[104,768]{1,0:T(8,128)(2,1)}, bf16[104,768]{1,0:T(8,128)(2,1)}, bf16[104,768]{1,0:T(8,128)(2,1)}, bf16[104,768]{1,0:T(8,128)(2,1)}) custom-call(s32[1]{0:T(128)} %bitcast.1.refs_0_, s32[1]{0:T(128)} %bitcast.refs_0_.refs_1_, bf16[4,104,768]{2,1,0:T(8,128)(2,1)} %copy-done.3, ...), custom_call_target="tpu_custom_call" | custom-call | tf_op jit(solution)/shard_map/expert_back/pallas_call | solution.py:243
  192.0 12.6 %expert_grads.2 = (bf16[4,2,96,3072]{3,2,1,0:T(8,128)(2,1)}, f32[8,768]{1,0:T(8,128)}) custom-call(s32[1]{0:T(128)} %bitcast.1.refs_0_, bf16[416,3840]{1,0:T(8,128)(2,1)} %get-tuple-element.167.refs_7_.refs_1_, bf16[416,3840]{1,0:T(8,128)(2,1)} %copy-done.8, bf16[416,3840]{1,0:T(8,128)(2,1)} %get-tuple-element.173.refs_3_, ...), custom_call_target="tpu_custom_call" | custom-call | tf_op jit(solution)/shard_map/expert_grads/pallas_call | solution.py:243
  205.5 13.8 %attn_back.2 = (f32[208,768]{1,0:T(8,128)}, bf16[224,3328]{1,0:T(8,128)(2,1)}, bf16[104,768]{1,0:T(8,128)(2,1)}, bf16[104,768]{1,0:T(8,128)(2,1)}, bf16[104,768]{1,0:T(8,128)(2,1)}, /*index=5*/bf16[104,768]{1,0:T(8,128)(2,1)}) custom-call(s32[1]{0:T(128)} %bitcast.1.refs_0_, bf16[104,768]{1,0:T(8,128)(2,1)} %get-tuple-element.168.refs_1_, ...), custom_call_target="tpu_custom_call" | custom-call | tf_op jit(solution)/shard_map/attn_back/pallas_call | solution.py:243
  225.6 5.0 %attn_grads.2.refs_0_ = bf16[4,2,96,1664]{3,2,1,0:T(8,128)(2,1)} custom-call(s32[1]{0:T(128)} %bitcast.1.refs_0_, s32[1]{0:T(128)} %bitcast.refs_0_.refs_1_, bf16[208,1152]{1,0:T(8,128)(2,1)} %get-tuple-element.162.refs_9_.refs_2_, bf16[208,1152]{1,0:T(8,128)(2,1)} %copy-done.35, bf16[224,3328]{1,0:T(8,128)(2,1)} %get-tuple-element.183.refs_4_, ...), custom_call_target="tpu_custom_call" | custom-call | tf_op jit(solution)/shard_map/attn_grads/pallas_call | solution.py:243
  230.7 5.9 %collective-permute-done.33.refs_2_.refs_4_ = bf16[104,768]{1,0:T(8,128)(2,1)S(1)} collective-permute-done((bf16[104,768]{1,0:T(8,128)(2,1)}, bf16[104,768]{1,0:T(8,128)(2,1)S(1)}, u32[]{:S(2)}, u32[]{:S(2)}) %collective-permute-start.33) | collective-permute-done | bytes 159776 | tf_op jit(solution)/shard_map/ppermute | solution.py:1354
  239.1 12.7 %expert_back.3 = (bf16[416,3840]{1,0:T(8,128)(2,1)}, bf16[104,768]{1,0:T(8,128)(2,1)}, bf16[104,768]{1,0:T(8,128)(2,1)}, bf16[104,768]{1,0:T(8,128)(2,1)}, bf16[104,768]{1,0:T(8,128)(2,1)}) custom-call(s32[1]{0:T(128)} %bitcast.1.refs_0_, s32[1]{0:T(128)} %bitcast.refs_0_.refs_1_, bf16[104,768]{1,0:T(8,128)(2,1)} %get-tuple-element.175.refs_2_, ...), custom_call_target="tpu_custom_call" | custom-call | tf_op jit(solution)/shard_map/expert_back/pallas_call | solution.py:243
  258.2 12.3 %expert_grads.3 = (bf16[4,2,96,3072]{3,2,1,0:T(8,128)(2,1)}, f32[8,768]{1,0:T(8,128)}) custom-call(s32[1]{0:T(128)} %bitcast.1.refs_0_, bf16[416,3840]{1,0:T(8,128)(2,1)} %get-tuple-element.146.refs_3_.refs_1_, bf16[416,3840]{1,0:T(8,128)(2,1)} %collective-permute-done.40.refs_2_, bf16[416,3840]{1,0:T(8,128)(2,1)} %get-tuple-element.191.refs_3_, ...), custom_call_target="tpu_custom_call" | custom-call | tf_op jit(solution)/shard_map/expert_grads/pallas_call | solution.py:243
  271.3 13.6 %attn_back.3 = (f32[197,768]{1,0:T(8,128)}, bf16[224,3328]{1,0:T(8,128)(2,1)}) custom-call(s32[1]{0:T(128)} %bitcast.1.refs_0_, bf16[104,768]{1,0:T(8,128)(2,1)} %get-tuple-element.186.refs_1_, bf16[104,768]{1,0:T(8,128)(2,1)} %copy-done.29, bf16[104,768]{1,0:T(8,128)(2,1)} %copy-done.30, bf16[104,768]{1,0:T(8,128)(2,1)} %copy-done.31, ...), custom_call_target="tpu_custom_call" | custom-call | tf_op jit(solution)/shard_map/attn_back/pallas_call | solution.py:243
  290.3 5.0 %attn_grads.3 = (bf16[96,1664]{1,0:T(8,128)(2,1)}, bf16[96,1664]{1,0:T(8,128)(2,1)}, bf16[2,96,1664]{2,1,0:T(8,128)(2,1)}, bf16[2,96,1664]{2,1,0:T(8,128)(2,1)}, bf16[2,96,1664]{2,1,0:T(8,128)(2,1)}) custom-call(s32[1]{0:T(128)} %bitcast.1.refs_0_, s32[1]{0:T(128)} %bitcast.refs_0_.refs_1_, bf16[208,1152]{1,0:T(8,128)(2,1)} %get-tuple-element.137.refs_2_, ...), custom_call_target="tpu_custom_call" | custom-call | tf_op jit(solution)/shard_map/attn_grads/pallas_call | solution.py:243
  298.1 4.8 %all-to-all-start.1 = ((bf16[4,104,768]{2,1,0:T(8,128)(2,1)}), bf16[4,104,768]{2,1,0:T(8,128)(2,1)S(1)}, u32[]{:S(2)}, u32[]{:S(2)}) async-start(bf16[4,104,768]{2,1,0:T(8,128)(2,1)} %hold.11.refs_7_), calls=%async_computation.1 | async-start | bytes 1277952 | tf_op jit(solution)/shard_map/all_to_all | solution.py:1861
  302.9 7.0 %collective-permute-done.44.refs_2_ = bf16[96,1664]{1,0:T(8,128)(2,1)S(1)} collective-permute-done((bf16[96,1664]{1,0:T(8,128)(2,1)}, bf16[96,1664]{1,0:T(8,128)(2,1)S(1)}, u32[]{:S(2)}, u32[]{:S(2)}) %collective-permute-start.44) | collective-permute-done | bytes 319520 | tf_op jit(solution)/shard_map/ppermute | solution.py:1354
  318.4 8.2 %collective-permute-done.46.refs_1_ = bf16[96,1664]{1,0:T(8,128)(2,1)S(1)} collective-permute-done((bf16[96,1664]{1,0:T(8,128)(2,1)}, bf16[96,1664]{1,0:T(8,128)(2,1)S(1)}, u32[]{:S(2)}, u32[]{:S(2)}) %collective-permute-start.46) | collective-permute-done | bytes 319520 | tf_op jit(solution)/shard_map/ppermute | solution.py:1354
  334.6 4.3 %collective-permute-done.47.refs_1_ = bf16[2,96,1664]{2,1,0:T(8,128)(2,1)S(1)} collective-permute-done((bf16[2,96,1664]{2,1,0:T(8,128)(2,1)}, bf16[2,96,1664]{2,1,0:T(8,128)(2,1)S(1)}, u32[]{:S(2)}, u32[]{:S(2)}) %collective-permute-start.47) | collective-permute-done | bytes 639008 | tf_op jit(solution)/shard_map/ppermute | solution.py:1354
  351.8 7.6 %collective-permute-done.49.refs_2_ = bf16[96,1664]{1,0:T(8,128)(2,1)S(1)} collective-permute-done((bf16[96,1664]{1,0:T(8,128)(2,1)}, bf16[96,1664]{1,0:T(8,128)(2,1)S(1)}, u32[]{:S(2)}, u32[]{:S(2)}) %collective-permute-start.49) | collective-permute-done | bytes 319520 | tf_op jit(solution)/shard_map/ppermute | solution.py:1354
  362.9 3.1 collective-permute-start.52
  370.4 8.2 %reduce-scatter.14.cloned.1.call-done = bf16[1,2,96,3072]{3,2,1,0:T(8,128)(2,1)} async-done(((bf16[4,2,96,3072]{3,2,1,0:T(8,128)(2,1)}), bf16[1,2,96,3072]{3,2,1,0:T(8,128)(2,1)}) %reduce-scatter.14.cloned.1.call-update) | async-done | bytes 1179664
  (270 shorter events, 137.0 us)
Async XLA Ops:
  7.2 93.1 %all-gather.6.cloned.1.call-start = ((), (), s32[]{:S(2)}) async-start(), calls=%async_computation.5 | async-start | bytes 10616832 | tf_op jit(solution)/shard_map/all_gather | solution.py:1738
  11.3 144.8 %all-gather.8.cloned.1.call-start = ((), (), s32[]{:S(2)}) async-start(), calls=%async_computation.6 | async-start | bytes 10616832 | tf_op jit(solution)/shard_map/all_gather | solution.py:1738
  13.7 23.2 %collective-permute-start = (bf16[2,96,1536]{2,1,0:T(8,128)(2,1)S(1)}, bf16[2,96,1536]{2,1,0:T(8,128)(2,1)S(1)}, u32[]{:S(2)}, u32[]{:S(2)}) collective-permute-start(bf16[2,96,1536]{2,1,0:T(8,128)(2,1)S(1)} %copy-done.2), channel_id=1, source_target_pairs={{0,8},{4,12},{8,0},{12,4},{16,24},{20,28},{24,16},{28,20},{1,9},{5... | collective-permute-start | bytes 1769480 | tf_op jit(solution)/shard_map/ppermute | solution.py:1354
  16.7 22.5 %collective-permute-start.1 = (bf16[2,96,1536]{2,1,0:T(8,128)(2,1)S(1)}, bf16[2,96,1536]{2,1,0:T(8,128)(2,1)S(1)}, u32[]{:S(2)}, u32[]{:S(2)}) collective-permute-start(bf16[2,96,1536]{2,1,0:T(8,128)(2,1)S(1)} %copy-done.2), channel_id=1, source_target_pairs={{0,16},{4,20},{8,24},{12,28},{16,0},{20,4},{24,8},{28,12},{1,17},{... | collective-permute-start | bytes 1769480 | tf_op jit(solution)/shard_map/ppermute | solution.py:1354
  28.6 33.1 %all-to-all-start = ((bf16[4,104,768]{2,1,0:T(8,128)(2,1)}), bf16[4,104,768]{2,1,0:T(8,128)(2,1)S(1)}, u32[]{:S(2)}, u32[]{:S(2)}) async-start(bf16[4,104,768]{2,1,0:T(8,128)(2,1)} %get-tuple-element.123), calls=%async_computation | async-start | bytes 1277952 | tf_op jit(solution)/shard_map/all_to_all | solution.py:1754
  33.5 252.0 %reduce-scatter.10.cloned.1.call-start = ((), (), s32[]{:S(2)}) async-start(), calls=%async_computation.7 | async-start | bytes 5898240
  33.5 32.9 %collective-permute-start.6 = (bf16[2,96,1536]{2,1,0:T(8,128)(2,1)S(1)}, bf16[2,96,1536]{2,1,0:T(8,128)(2,1)S(1)}, u32[]{:S(2)}, u32[]{:S(2)}) collective-permute-start(bf16[2,96,1536]{2,1,0:T(8,128)(2,1)S(1)} %copy-done.2), channel_id=1, source_target_pairs={{0,4},{4,0},{8,12},{12,8},{16,20},{20,16},{24,28},{28,24},{1,5},{5... | collective-permute-start | bytes 1769480 | tf_op jit(solution)/shard_map/ppermute | solution.py:1354
  44.4 22.7 %collective-permute-start.3 = (bf16[1,96,1536]{2,1,0:T(8,128)(2,1)}, bf16[1,96,1536]{2,1,0:T(8,128)(2,1)}, u32[]{:S(2)}, u32[]{:S(2)}) collective-permute-start(bf16[1,96,1536]{2,1,0:T(8,128)(2,1)} %get-tuple-element.122), channel_id=1, source_target_pairs={{0,8},{4,12},{8,0},{12,4},{16,24},{20,28},{24,16},{28,20},{1,9},{5... | collective-permute-start | bytes 884744 | tf_op jit(solution)/shard_map/ppermute | solution.py:1354
  50.4 18.1 %collective-permute-start.4 = (bf16[1,96,1536]{2,1,0:T(8,128)(2,1)S(1)}, bf16[1,96,1536]{2,1,0:T(8,128)(2,1)}, u32[]{:S(2)}, u32[]{:S(2)}) collective-permute-start(bf16[1,96,1536]{2,1,0:T(8,128)(2,1)S(1)} %collective-permute-done.2.refs_5_.refs_16_), channel_id=1, source_target_pairs={{0,4},{4,0},{8,12},{12,8},{16,20},{20,16},{24,28},{28,24},{1,5},{5... | collective-permute-start | bytes 884744 | tf_op jit(solution)/shard_map/ppermute | solution.py:1354
  50.4 19.9 %collective-permute-start.7 = (bf16[2,96,1536]{2,1,0:T(8,128)(2,1)}, bf16[2,96,1536]{2,1,0:T(8,128)(2,1)S(1)}, u32[]{:S(2)}, u32[]{:S(2)}) collective-permute-start(bf16[2,96,1536]{2,1,0:T(8,128)(2,1)} %copy-done.6), channel_id=1, source_target_pairs={{0,4},{4,0},{8,12},{12,8},{16,20},{20,16},{24,28},{28,24},{1,5},{5... | collective-permute-start | bytes 1769480 | tf_op jit(solution)/shard_map/ppermute | solution.py:1354
  50.9 19.4 %collective-permute-start.8 = (bf16[2,96,1536]{2,1,0:T(8,128)(2,1)}, bf16[2,96,1536]{2,1,0:T(8,128)(2,1)}, u32[]{:S(2)}, u32[]{:S(2)}) collective-permute-start(bf16[2,96,1536]{2,1,0:T(8,128)(2,1)} %copy-done.7), channel_id=1, source_target_pairs={{0,4},{4,0},{8,12},{12,8},{16,20},{20,16},{24,28},{28,24},{1,5},{5... | collective-permute-start | bytes 1769480 | tf_op jit(solution)/shard_map/ppermute | solution.py:1354
  66.4 25.5 %collective-permute-start.12 = (bf16[2,96,1536]{2,1,0:T(8,128)(2,1)}, bf16[2,96,1536]{2,1,0:T(8,128)(2,1)S(1)}, u32[]{:S(2)}, u32[]{:S(2)}) collective-permute-start(bf16[2,96,1536]{2,1,0:T(8,128)(2,1)} %pack_attn.3.refs_17_.refs_8_.refs_13_), channel_id=1, source_target_pairs={{0,8},{4,12},{8,0},{12,4},{16,24},{20,28},{24,16},{28,20},{1,9},{5... | collective-permute-start | bytes 1769480 | tf_op jit(solution)/shard_map/ppermute | solution.py:1354
  67.0 24.8 %collective-permute-start.13 = (bf16[2,96,1536]{2,1,0:T(8,128)(2,1)}, bf16[2,96,1536]{2,1,0:T(8,128)(2,1)S(1)}, u32[]{:S(2)}, u32[]{:S(2)}) collective-permute-start(bf16[2,96,1536]{2,1,0:T(8,128)(2,1)} %pack_attn.3.refs_17_.refs_8_.refs_13_), channel_id=1, source_target_pairs={{0,16},{4,20},{8,24},{12,28},{16,0},{20,4},{24,8},{28,12},{1,17},{... | collective-permute-start | bytes 1769480 | tf_op jit(solution)/shard_map/ppermute | solution.py:1354
  89.3 26.4 %collective-permute-start.21 = (bf16[2,96,1536]{2,1,0:T(8,128)(2,1)S(1)}, bf16[2,96,1536]{2,1,0:T(8,128)(2,1)S(1)}, u32[]{:S(2)}, u32[]{:S(2)}) collective-permute-start(bf16[2,96,1536]{2,1,0:T(8,128)(2,1)S(1)} %copy-done.1), channel_id=1, source_target_pairs={{0,4},{4,0},{8,12},{12,8},{16,20},{20,16},{24,28},{28,24},{1,5},{5... | collective-permute-start | bytes 1769480 | tf_op jit(solution)/shard_map/ppermute | solution.py:1354
  91.8 25.4 %collective-permute-start.22 = (bf16[2,96,1536]{2,1,0:T(8,128)(2,1)S(1)}, bf16[2,96,1536]{2,1,0:T(8,128)(2,1)}, u32[]{:S(2)}, u32[]{:S(2)}) collective-permute-start(bf16[2,96,1536]{2,1,0:T(8,128)(2,1)S(1)} %collective-permute-done.12.refs_0_.refs_9_.refs_14_), channel_id=1, source_target_pairs={{0,4},{4,0},{8,12},{12,8},{16,20},{20,16},{24,28},{28,24},{1,5},{5... | collective-permute-start | bytes 1769480 | tf_op jit(solution)/shard_map/ppermute | solution.py:1354
  91.8 27.8 %collective-permute-start.23 = (bf16[2,96,1536]{2,1,0:T(8,128)(2,1)S(1)}, bf16[2,96,1536]{2,1,0:T(8,128)(2,1)}, u32[]{:S(2)}, u32[]{:S(2)}) collective-permute-start(bf16[2,96,1536]{2,1,0:T(8,128)(2,1)S(1)} %collective-permute-done.13.refs_1_.refs_10_.refs_15_), channel_id=1, source_target_pairs={{0,4},{4,0},{8,12},{12,8},{16,20},{20,16},{24,28},{28,24},{1,5},{5... | collective-permute-start | bytes 1769480 | tf_op jit(solution)/shard_map/ppermute | solution.py:1354
  115.1 16.9 %collective-permute-start.19 = (bf16[1,96,1536]{2,1,0:T(8,128)(2,1)}, bf16[1,96,1536]{2,1,0:T(8,128)(2,1)S(1)}, u32[]{:S(2)}, u32[]{:S(2)}) collective-permute-start(bf16[1,96,1536]{2,1,0:T(8,128)(2,1)} %get-tuple-element.147.refs_11_.refs_16_), channel_id=1, source_target_pairs={{0,4},{4,0},{8,12},{12,8},{16,20},{20,16},{24,28},{28,24},{1,5},{5... | collective-permute-start | bytes 884744 | tf_op jit(solution)/shard_map/ppermute | solution.py:1354
  115.2 16.8 %collective-permute-start.20 = (bf16[1,96,1536]{2,1,0:T(8,128)(2,1)}, bf16[1,96,1536]{2,1,0:T(8,128)(2,1)S(1)}, u32[]{:S(2)}, u32[]{:S(2)}) collective-permute-start(bf16[1,96,1536]{2,1,0:T(8,128)(2,1)} %get-tuple-element.148.refs_12_.refs_17_), channel_id=1, source_target_pairs={{0,4},{4,0},{8,12},{12,8},{16,20},{20,16},{24,28},{28,24},{1,5},{5... | collective-permute-start | bytes 884744 | tf_op jit(solution)/shard_map/ppermute | solution.py:1354
  172.7 17.7 %collective-permute-start.30 = (bf16[416,3840]{1,0:T(8,128)(2,1)}, bf16[416,3840]{1,0:T(8,128)(2,1)S(1)}, u32[]{:S(2)}, u32[]{:S(2)}) collective-permute-start(bf16[416,3840]{1,0:T(8,128)(2,1)} %get-tuple-element.167.refs_7_.refs_1_), channel_id=1, source_target_pairs={{0,4},{4,0},{8,12},{12,8},{16,20},{20,16},{24,28},{28,24},{1,5},{5... | collective-permute-start | bytes 9584648 | tf_op jit(solution)/shard_map/ppermute | solution.py:1354
  185.7 18.9 %collective-permute-start.27 = (bf16[104,768]{1,0:T(8,128)(2,1)}, bf16[104,768]{1,0:T(8,128)(2,1)S(1)}, u32[]{:S(2)}, u32[]{:S(2)}) collective-permute-start(bf16[104,768]{1,0:T(8,128)(2,1)} %get-tuple-element.169), channel_id=1, source_target_pairs={{0,1},{1,0},{2,3},{3,2},{4,5},{5,4},{6,7},{7,6},{8,9},{9,8},{10,11... | collective-permute-start | bytes 479240 | tf_op jit(solution)/shard_map/ppermute | solution.py:1354
  187.9 16.7 %collective-permute-start.28 = (bf16[104,768]{1,0:T(8,128)(2,1)}, bf16[104,768]{1,0:T(8,128)(2,1)S(1)}, u32[]{:S(2)}, u32[]{:S(2)}) collective-permute-start(bf16[104,768]{1,0:T(8,128)(2,1)} %get-tuple-element.170), channel_id=1, source_target_pairs={{0,2},{1,3},{2,0},{3,1},{4,6},{5,7},{6,4},{7,5},{8,10},{9,11},{10,... | collective-permute-start | bytes 479240 | tf_op jit(solution)/shard_map/ppermute | solution.py:1354
  188.9 15.8 %collective-permute-start.29 = (bf16[104,768]{1,0:T(8,128)(2,1)}, bf16[104,768]{1,0:T(8,128)(2,1)S(1)}, u32[]{:S(2)}, u32[]{:S(2)}) collective-permute-start(bf16[104,768]{1,0:T(8,128)(2,1)} %get-tuple-element.171), channel_id=1, source_target_pairs={{0,3},{1,2},{2,1},{3,0},{4,7},{5,6},{6,5},{7,4},{8,11},{9,10},{10,... | collective-permute-start | bytes 479240 | tf_op jit(solution)/shard_map/ppermute | solution.py:1354
  205.4 109.4 %reduce-scatter.12.cloned.1.call-start = ((), (), s32[]{:S(2)}) async-start(), calls=%async_computation.8 | async-start | bytes 3194880
  237.2 141.4 %reduce-scatter.14.cloned.1.call-start = ((), (), s32[]{:S(2)}) async-start(), calls=%async_computation.9 | async-start | bytes 5898240
  239.1 18.5 %collective-permute-start.40 = (bf16[416,3840]{1,0:T(8,128)(2,1)S(1)}, bf16[416,3840]{1,0:T(8,128)(2,1)}, u32[]{:S(2)}, u32[]{:S(2)}) collective-permute-start(bf16[416,3840]{1,0:T(8,128)(2,1)S(1)} %copy-done), channel_id=1, source_target_pairs={{0,4},{4,0},{8,12},{12,8},{16,20},{20,16},{24,28},{28,24},{1,5},{5... | collective-permute-start | bytes 9584648 | tf_op jit(solution)/shard_map/ppermute | solution.py:1354
  252.5 18.0 %collective-permute-start.37 = (bf16[104,768]{1,0:T(8,128)(2,1)}, bf16[104,768]{1,0:T(8,128)(2,1)S(1)}, u32[]{:S(2)}, u32[]{:S(2)}) collective-permute-start(bf16[104,768]{1,0:T(8,128)(2,1)} %get-tuple-element.187), channel_id=1, source_target_pairs={{0,1},{1,0},{2,3},{3,2},{4,5},{5,4},{6,7},{7,6},{8,9},{9,8},{10,11... | collective-permute-start | bytes 479240 | tf_op jit(solution)/shard_map/ppermute | solution.py:1354
  298.1 32.9 %all-to-all-start.1 = ((bf16[4,104,768]{2,1,0:T(8,128)(2,1)}), bf16[4,104,768]{2,1,0:T(8,128)(2,1)S(1)}, u32[]{:S(2)}, u32[]{:S(2)}) async-start(bf16[4,104,768]{2,1,0:T(8,128)(2,1)} %hold.11.refs_7_), calls=%async_computation.1 | async-start | bytes 1277952 | tf_op jit(solution)/shard_map/all_to_all | solution.py:1861
  312.8 26.2 %collective-permute-start.47 = (bf16[2,96,1664]{2,1,0:T(8,128)(2,1)}, bf16[2,96,1664]{2,1,0:T(8,128)(2,1)S(1)}, u32[]{:S(2)}, u32[]{:S(2)}) collective-permute-start(bf16[2,96,1664]{2,1,0:T(8,128)(2,1)} %get-tuple-element.202.refs_2_), channel_id=1, source_target_pairs={{0,8},{4,12},{8,0},{12,4},{16,24},{20,28},{24,16},{28,20},{1,9},{5... | collective-permute-start | bytes 1916936 | tf_op jit(solution)/shard_map/ppermute | solution.py:1354
  314.3 27.1 %collective-permute-start.48 = (bf16[2,96,1664]{2,1,0:T(8,128)(2,1)}, bf16[2,96,1664]{2,1,0:T(8,128)(2,1)S(1)}, u32[]{:S(2)}, u32[]{:S(2)}) collective-permute-start(bf16[2,96,1664]{2,1,0:T(8,128)(2,1)} %get-tuple-element.206), channel_id=1, source_target_pairs={{0,16},{4,20},{8,24},{12,28},{16,0},{20,4},{24,8},{28,12},{1,17},{... | collective-permute-start | bytes 1916936 | tf_op jit(solution)/shard_map/ppermute | solution.py:1354
  329.2 19.3 %collective-permute-start.51 = (bf16[96,1664]{1,0:T(8,128)(2,1)}, bf16[96,1664]{1,0:T(8,128)(2,1)S(1)}, u32[]{:S(2)}, u32[]{:S(2)}) collective-permute-start(bf16[96,1664]{1,0:T(8,128)(2,1)} %fold3.3.refs_5_.refs_0_), channel_id=1, source_target_pairs={{0,2},{1,3},{2,0},{3,1},{4,6},{5,7},{6,4},{7,5},{8,10},{9,11},{10,... | collective-permute-start | bytes 958472 | tf_op jit(solution)/shard_map/ppermute | solution.py:1354
  351.1 16.3 %collective-permute-start.54 = (bf16[96,1664]{1,0:T(8,128)(2,1)}, bf16[96,1664]{1,0:T(8,128)(2,1)S(1)}, u32[]{:S(2)}, u32[]{:S(2)}) collective-permute-start(bf16[96,1664]{1,0:T(8,128)(2,1)} %fold3.4.refs_4_.refs_1_), channel_id=1, source_target_pairs={{0,1},{1,0},{2,3},{3,2},{4,5},{5,4},{6,7},{7,6},{8,9},{9,8},{10,11... | collective-permute-start | bytes 958472 | tf_op jit(solution)/shard_map/ppermute | solution.py:1354
  362.9 18.3 %collective-permute-start.52 = (bf16[96,1664]{1,0:T(8,128)(2,1)}, bf16[96,1664]{1,0:T(8,128)(2,1)S(1)}, u32[]{:S(2)}, u32[]{:S(2)}) collective-permute-start(bf16[96,1664]{1,0:T(8,128)(2,1)} %get-tuple-element.209.refs_3_.refs_0_), channel_id=1, source_target_pairs={{0,2},{1,3},{2,0},{3,1},{4,6},{5,7},{6,4},{7,5},{8,10},{9,11},{10,... | collective-permute-start | bytes 958472 | tf_op jit(solution)/shard_map/ppermute | solution.py:1354
  (92 other events, 599.3 us)
Sparse Core Ops, SparseCore 0:
  11.4 79.2 all-gather.5
  93.2 62.9 all-gather.7
  205.6 56.6 reduce-scatter.9
  265.2 43.5 reduce-scatter.11
  311.6 67.0 reduce-scatter.13

commit v5 on v4

--- a/solution.py
+++ b/solution.py
@@ -16,6 +16,8 @@
 LANES = 128
 NEG = -1e30
 VMEM_LIMIT = 60 * 1024 * 1024
+LIMITS = {name: 16 * 1024 * 1024 for name in ("fold1", "fold2", "fold3", "mix")}
+LIMITS["attn_grads"] = 24 * 1024 * 1024
 
 
 def up(value, step):
@@ -250,7 +252,9 @@
         out_shape=outs,
         scratch_shapes=list(scratch) + extra,
         input_output_aliases=aliases or {},
-        compiler_params=pltpu.CompilerParams(vmem_limit_bytes=VMEM_LIMIT),
+        compiler_params=pltpu.CompilerParams(
+            vmem_limit_bytes=LIMITS.get(name, VMEM_LIMIT)
+        ),
     )(*args, *after)
     Order.token = result[0] if isinstance(result, (tuple, list)) else result
     return result
@@ -272,7 +276,7 @@
     )
 
 
-def move(name, args, copies, outs):
+def move(name, args, copies, outs, aliases=None):
     total = len(copies)
 
     def kernel(*refs):
@@ -302,6 +306,7 @@
         [ANY] * len(outs),
         [pltpu.VMEM(shape, BF) for *_, shape in copies]
         + [pltpu.SemaphoreType.DMA((total,)), pltpu.SemaphoreType.DMA((total,))],
+        aliases,
     )
 
 
@@ -724,7 +729,7 @@
     return result[:5], result[5:]
 
 
-def expert_fwd(me, z, seat_blocks, weights, bias_in, bias_oe, used, ordered):
+def expert_fwd(me, seat_blocks, weights, bias_in, bias_oe, used):
     owners = len(seat_blocks)
     cap, width = seat_blocks[0].shape
     seats = owners * cap
@@ -736,12 +741,12 @@
 
     def kernel(*refs):
         refs = list(refs)
-        me_ref, z_ref = refs.pop(0), refs.pop(0)
+        me_ref = refs.pop(0)
         seat_refs = [refs.pop(0) for _ in range(owners)]
         w_refs = [refs.pop(0) for _ in range(count)]
         bin_ref, boe_ref = refs.pop(0), refs.pop(0)
         rh_out, slope_out, gate_out, made_out = (refs.pop(0) for _ in range(4))
-        outs = [refs.pop(0) for _ in range(1 if ordered else owners)]
+        outs = [refs.pop(0) for _ in range(owners)]
         win, woe, sems = refs
         chunks = Chunks(w_refs, weights, width, hidden, shard, whole, win, woe, sems)
         blocks = [ref[...].astype(F32) for ref in seat_refs]
@@ -768,8 +773,6 @@
             total_out = piece if total_out is None else total_out + piece
         total_out = total_out + boe_ref[...]
         made_out[...] = total_out.astype(BF)
-        if ordered:
-            outs = [outs[0].held.at[z_ref[0] ^ k] for k in range(owners)]
         part(total_out, outs)
 
     shapes = [
@@ -777,12 +780,12 @@
         sds((seats, hidden), BF),
         sds((seats, LANES), F32),
         sds((seats, width), BF),
-    ] + ([sds((owners, cap, width), BF)] if ordered else [sds((cap, width), BF)] * owners)
+    ] + [sds((cap, width), BF)] * owners
     result = call(
         kernel,
         "expert_fwd",
-        [me, z, *seat_blocks, *weights.arrays, bias_in, bias_oe],
-        [SM, SM] + [LOAD] * owners + [ANY] * count + [LOAD] * 2,
+        [me, *seat_blocks, *weights.arrays, bias_in, bias_oe],
+        [SM] + [LOAD] * owners + [ANY] * count + [LOAD] * 2,
         shapes,
         [STORE] * len(shapes),
         [
@@ -794,6 +797,99 @@
     return result[:4], result[4:]
 
 
+def expert_both(me, z, seat_blocks, grads, weights, bias_in, bias_oe, used, shards):
+    size = bias_in.shape[1] // shards
+    owners = len(seat_blocks)
+    cap, width = seat_blocks[0].shape
+    seats = owners * cap
+    hidden = bias_in.shape[1]
+    count = len(weights.arrays)
+    shard = weights.arrays[0].shape[-2]
+    whole = weights.places[0][0] is None
+    step = width
+
+    def kernel(*refs):
+        refs = list(refs)
+        me_ref, z_ref = refs.pop(0), refs.pop(0)
+        seat_refs = [refs.pop(0) for _ in range(owners)]
+        grad_ref = refs.pop(0)
+        w_refs = [refs.pop(0) for _ in range(count)]
+        bin_ref, boe_ref = refs.pop(0), refs.pop(0)
+        rp_out, hd_out, give_out, made_out = (refs.pop(0) for _ in range(4))
+        outs = [refs.pop(0) for _ in range(owners)]
+        win, woe, slopes, sems = refs
+        chunks = Chunks(w_refs, weights, width, hidden, shard, whole, win, woe, sems)
+        blocks = [ref[...].astype(F32) for ref in seat_refs]
+        rows = jnp.concatenate(blocks, 0).astype(BF)
+        rp_out[:, 0:width] = rows
+        other = 1 - (me_ref[0] & 1)
+        gate = jnp.concatenate([as_column(note_of(block, used), cap) for block in blocks], 0)
+        total_out = None
+        for at in range(0, hidden, step):
+            chunks.take(at // step)
+            pre = dot(rows, win[:, at : at + step]) + bin_ref[:, at : at + step]
+            square = pre * pre
+            bend = jnp.tanh(0.7978845608028654 * (pre + 0.044715 * square * pre))
+            h = (0.5 * pre * (1.0 + bend)).astype(BF)
+            slope = 0.5 * (1.0 + bend) + 0.5 * pre * (1.0 - bend * bend) * (
+                0.7978845608028654 * (1.0 + 0.134145 * square)
+            )
+            hd_out[:, at : at + step] = h
+            slopes[:, at : at + step] = slope.astype(BF)
+            piece = dot(h, woe[at : at + step, :])
+            total_out = piece if total_out is None else total_out + piece
+        made = (total_out + boe_ref[...]).astype(BF).astype(F32)
+        for k in range(owners):
+            made_out.held[z_ref[0] ^ k] = made[k * cap : (k + 1) * cap].astype(BF)
+        given = [grad_ref[z_ref[0] ^ k].astype(F32) for k in range(owners)]
+        given = jnp.concatenate(given, 0)
+        grad = (given * gate).astype(BF)
+        hd_out[:, hidden : hidden + width] = grad
+        for k in range(shards // 2):
+            first = pl.multiple_of((2 * k + other) * size, LANES)
+            give_out[:, k * size : (k + 1) * size] = hd_out.held[:, pl.ds(first, size)]
+        give_out[:, hidden // 2 : hidden // 2 + width] = grad
+        hd_out.send(ALL, ALL)
+        give_out.send(ALL, ALL)
+        made_out.send(ALL)
+        notes = given * made
+        notes = [lane_sums(notes[k * cap : (k + 1) * cap]) for k in range(owners)]
+        total_out = None
+        for at in range(0, hidden, step):
+            d_hidden = dot_nt(grad, woe[at : at + step, :])
+            d_pre = (d_hidden * slopes[:, at : at + step].astype(F32)).astype(BF)
+            rp_out[:, width + at : width + at + step] = d_pre
+            piece = dot_nt(d_pre, win[:, at : at + step])
+            total_out = piece if total_out is None else total_out + piece
+            if at == hidden // 2 - step:
+                rp_out.send(ALL, pl.ds(0, width + hidden // 2))
+        rp_out.send(ALL, pl.ds(width + hidden // 2, hidden // 2))
+        for k, ref in enumerate(outs):
+            ref[...] = with_note(total_out[k * cap : (k + 1) * cap], used, notes[k]).astype(BF)
+
+    shapes = [
+        sds((seats, width + hidden), BF),
+        sds((seats, hidden + width), BF),
+        sds((seats, hidden // 2 + width), BF),
+        sds((owners, cap, width), BF),
+    ] + [sds((cap, width), BF)] * owners
+    result = call(
+        kernel,
+        "expert_both",
+        [me, z, *seat_blocks, grads, *weights.arrays, bias_in, bias_oe],
+        [SM, SM] + [LOAD] * (owners + 1) + [ANY] * count + [LOAD] * 2,
+        shapes,
+        [STORE] * len(shapes),
+        [
+            pltpu.VMEM((width, hidden), BF),
+            pltpu.VMEM((hidden, width), BF),
+            pltpu.VMEM((seats, hidden), BF),
+            pltpu.SemaphoreType.DMA((2 * copies_in(weights),)),
+        ],
+    )
+    return result[:4], result[4:]
+
+
 def top_seats(z, cotangent, rows, cap, experts):
     tokens, width = cotangent.shape
     padded = rows.shape[1]
@@ -802,7 +898,8 @@
         grad_out[...] = jnp.zeros_like(grad_out)
         grad_out[0:tokens, :] = cot_ref[...].astype(F32)
         sent = rows_to_seats(rows_ref, cap * experts, grad_out[...].astype(BF))
-        part(sent, [out.at[z_ref[0] ^ k] for k in range(experts)])
+        for k in range(experts):
+            out[z_ref[0] ^ k] = sent[k * cap : (k + 1) * cap].astype(BF)
 
     return call(
         kernel,
@@ -834,11 +931,9 @@
     )
 
 
-def expert_back(me, z, grad_blocks, slope, gate, made, weights, used):
-    ordered = grad_blocks[0].ndim == 3
-    cap, width = grad_blocks[0].shape[-2:]
-    owners = slope.shape[0] // cap
-    count_in = len(grad_blocks)
+def expert_back(me, grad_blocks, slope, gate, made, weights, used):
+    owners = len(grad_blocks)
+    cap, width = grad_blocks[0].shape
     seats, hidden = slope.shape
     count = len(weights.arrays)
     shard = weights.arrays[0].shape[-2]
@@ -847,8 +942,8 @@
 
     def kernel(*refs):
         refs = list(refs)
-        me_ref, z_ref = refs.pop(0), refs.pop(0)
-        seat_refs = [refs.pop(0) for _ in range(count_in)]
+        me_ref = refs.pop(0)
+        seat_refs = [refs.pop(0) for _ in range(owners)]
         slope_ref, gate_ref, made_ref = (refs.pop(0) for _ in range(3))
         w_refs = [refs.pop(0) for _ in range(count)]
         gd_out = refs.pop(0)
@@ -863,11 +958,7 @@
             for at in range(0, hidden, step)
         ]
         chunks = Chunks(w_refs, weights, width, hidden, shard, whole, win, woe, sems, more)
-        if ordered:
-            given = [seat_refs[0][z_ref[0] ^ k].astype(F32) for k in range(owners)]
-        else:
-            given = [ref[...].astype(F32) for ref in seat_refs]
-        given = jnp.concatenate(given, 0)
+        given = jnp.concatenate([ref[...].astype(F32) for ref in seat_refs], 0)
         grad = (given * gate_ref[:, 0:1]).astype(BF)
         notes = given * made_ref[...].astype(F32)
         notes = [lane_sums(notes[k * cap : (k + 1) * cap]) for k in range(owners)]
@@ -890,8 +981,8 @@
     result = call(
         kernel,
         "expert_back",
-        [me, z, *grad_blocks, slope, gate, made, *weights.arrays],
-        [SM, SM] + [LOAD] * count_in + [ANY] + [LOAD] * 2 + [ANY] * count,
+        [me, *grad_blocks, slope, gate, made, *weights.arrays],
+        [SM] + [LOAD] * owners + [ANY] + [LOAD] * 2 + [ANY] * count,
         shapes,
         [STORE] * (1 + owners),
         [
@@ -920,55 +1011,42 @@
     return one(row == place)
 
 
-def expert_grads(me, own, other, shards):
-    seats, both = own[0].shape
+def expert_grads(me, rows_in, h, d_out, d_pre, sizes, paired, shards, given=()):
     width = HEADS * HEAD_DIM
-    hidden = both - width
+    seats, hidden = sizes
+    sides = 2 if paired else 1
     per, shard = hidden // width, width // shards
     part_hidden = hidden // shards
-    sides = 2 if other else 1
-    tall = width // 2 if other else width
-    deep = hidden // 2 if other else hidden
-    total = shards * per if other else 2
-
-    blocks = shards // 2 if other else per
-    size = part_hidden if other else width
+    tall = width // 2 if paired else width
+    deep = hidden // 2 if paired else hidden
+    total = shards * per if paired else 2
+    blocks = shards // 2 if paired else per
+    size = part_hidden if paired else width
+    arrays = []
+    for operand in (*rows_in, *h, *d_out, *d_pre):
+        if not any(operand[0] is known for known in arrays):
+            arrays.append(operand[0])
+    place = lambda operand: [operand[0] is known for known in arrays].index(True)
 
     def kernel(me_ref, *refs):
         refs = list(refs)
-        rh = [refs.pop(0) for _ in range(sides)]
-        gd = [refs.pop(0) for _ in range(sides)]
-        outs = [refs.pop(0) for _ in range(1 if other else 2)]
-        bias_ref, win, woe, h_held, row_held, gd_held, sems, load_sems = refs
+        ins = [refs.pop(0) for _ in arrays]
+        bias_given = [refs.pop(0) for _ in given][-1:]
+        outs = [refs.pop(0) for _ in range(1 if paired else 2)]
+        bias_ref, win, woe, h_held, row_held, out_held, pre_held, sems, load_sems = refs
         core = me_ref[0] & 1
         copies = []
         loads = {}
+
+        def send(source, target):
+            copy = pltpu.make_async_copy(source, target, sems.at[len(copies)])
+            copy.start()
+            copies.append(copy)
 
         def fetch_in(key, source, target):
             copy = pltpu.make_async_copy(source, target, load_sems.at[len(loads)])
             copy.start()
             loads[key] = copy
-
-        for i in range(sides):
-            fetch_in(("d", i), gd[i].at[:, pl.ds(0, width)], gd_held.at[i, :, pl.ds(0, width)])
-        for k in range(blocks):
-            first = width + k * size
-            if other:
-                first = pl.multiple_of(width + (2 * k + core) * size, LANES)
-            for i in range(sides):
-                here = pl.ds(k * size, size)
-                fetch_in(("h", k, i), rh[i].at[:, pl.ds(first, size)], h_held.at[i, :, here])
-        for i in range(sides):
-            fetch_in(("r", i), rh[i].at[:, pl.ds(0, width)], row_held.at[i])
-        for k in range(per):
-            here = pl.ds(width + k * width, width)
-            for i in range(sides):
-                fetch_in(("p", k, i), gd[i].at[:, here], gd_held.at[i, :, here])
-
-        def send(source, target):
-            copy = pltpu.make_async_copy(source, target, sems.at[len(copies)])
-            copy.start()
-            copies.append(copy)
 
         def summed(pieces):
             total = pieces[0]
@@ -976,62 +1054,79 @@
                 total = total + piece
             return total
 
-        for i in range(sides):
-            loads["d", i].wait()
-        d_outs = [gd_held[i, :, 0:width] for i in range(sides)]
+        for i, operand in enumerate(d_out):
+            source = ins[place(operand)].at[:, pl.ds(operand[1], width)]
+            fetch_in(("d", i), source, out_held.at[i])
         for k in range(blocks):
-            here = slice(k * size, (k + 1) * size)
+            for i, operand in enumerate(h):
+                first = operand[1] + k * size
+                if paired and operand[2]:
+                    first = pl.multiple_of(operand[1] + (2 * k + core) * size, LANES)
+                source = ins[place(operand)].at[:, pl.ds(first, size)]
+                fetch_in(("h", k, i), source, h_held.at[i, :, pl.ds(k * size, size)])
+        for i, operand in enumerate(rows_in):
+            source = ins[place(operand)].at[:, pl.ds(operand[1], width)]
+            fetch_in(("r", i), source, row_held.at[i])
+        for k in range(per):
+            for i, operand in enumerate(d_pre):
+                source = ins[place(operand)].at[:, pl.ds(operand[1] + k * width, width)]
+                fetch_in(("p", k, i), source, pre_held.at[i, :, pl.ds(k * width, width)])
+        if bias_given:
+            bias_ref[...] = bias_given[0][...]
+        else:
+            bias_ref[...] = jnp.zeros_like(bias_ref)
+        if h:
             for i in range(sides):
-                loads["h", k, i].wait()
-            total = summed([dot_tn(h_held[i, :, here], d_outs[i]) for i in range(sides)])
-            woe[here, :] = total.astype(BF)
-            if other:
+                loads["d", i].wait()
+            for k in range(blocks):
+                here = slice(k * size, (k + 1) * size)
+                for i in range(sides):
+                    loads["h", k, i].wait()
+                total = summed([dot_tn(h_held[i, :, here], out_held[i]) for i in range(sides)])
+                woe[here, :] = total.astype(BF)
+                if paired:
+                    for q in range(per):
+                        send(
+                            woe.at[pl.ds(k * size + q * shard, shard)],
+                            outs[0].at[k, 1, :, pl.ds(q * width, width)],
+                        )
+            bias_ref[per : per + 1, :] = summed([column_sums(out_held[i]) for i in range(sides)])
+        if rows_in:
+            for i in range(sides):
+                loads["r", i].wait()
+            lefts = [row_held[i] for i in range(sides)]
+            if paired:
+                pick = own_columns(width, shards, core)
+                lefts = [dot(value, pick).astype(BF) for value in lefts]
+            for k in range(per):
+                here = slice(k * width, (k + 1) * width)
+                for i in range(sides):
+                    loads["p", k, i].wait()
+                total = summed([dot_tn(lefts[i], pre_held[i, :, here]) for i in range(sides)])
+                win[:, here] = total.astype(BF)
+                if paired:
+                    for n in range(shards // 2):
+                        into = pl.ds(k * width, width)
+                        send(win.at[pl.ds(n * shard, shard), into], outs[0].at[n, 0, :, into])
+            sums = summed([column_sums(pre_held[i]) for i in range(sides)])
+            for d in range(shards):
                 for q in range(per):
-                    send(
-                        woe.at[pl.ds(k * size + q * shard, shard)],
-                        outs[0].at[k, 1, :, pl.ds(q * width, width)],
-                    )
-        for i in range(sides):
-            loads["r", i].wait()
-        lefts = [row_held[i] for i in range(sides)]
-        if other:
-            pick = own_columns(width, shards, core)
-            lefts = [dot(left, pick).astype(BF) for left in lefts]
-        for k in range(per):
-            here = slice(width + k * width, width + (k + 1) * width)
-            for i in range(sides):
-                loads["p", k, i].wait()
-            total = summed([dot_tn(lefts[i], gd_held[i, :, here]) for i in range(sides)])
-            win[:, k * width : (k + 1) * width] = total.astype(BF)
-            if other:
-                for n in range(shards // 2):
-                    here = pl.ds(k * width, width)
-                    send(
-                        win.at[pl.ds(n * shard, shard), here], outs[0].at[n, 0, :, here]
-                    )
-        if not other:
+                    first = (d * per + q) * shard
+                    bias_ref[q : q + 1, d * shard : (d + 1) * shard] = sums[:, first : first + shard]
+        if not paired:
             send(win, outs[0])
             send(woe, outs[1])
-        bias_ref[...] = jnp.zeros_like(bias_ref)
-        sums = summed([column_sums(gd_held[i]) for i in range(sides)])
-        for d in range(shards):
-            for q in range(per):
-                first = width + (d * per + q) * shard
-                bias_ref[q : q + 1, d * shard : (d + 1) * shard] = sums[:, first : first + shard]
-        bias_ref[per : per + 1, :] = sums[:, 0:width]
         wait(copies)
 
-    if other:
+    if paired:
         shapes = [sds((shards // 2, 2, shard, hidden), BF)]
-        args = [own[0], other[0], own[1], other[1]]
     else:
         shapes = [sds((width, hidden), BF), sds((hidden, width), BF)]
-        args = list(own)
     result = call(
         kernel,
         "expert_grads",
-        [me, *args],
-        [SM] + [ANY] * len(args),
+        [me, *arrays, *given],
+        [SM] + [ANY] * (len(arrays) + max(len(given) - 1, 0)) + [VM] * min(len(given), 1),
         shapes + [sds((8, width), F32)],
         [ANY] * len(shapes) + [VM],
         [
@@ -1039,10 +1134,12 @@
             pltpu.VMEM((deep, width), BF),
             pltpu.VMEM((sides, seats, blocks * size), BF),
             pltpu.VMEM((sides, seats, width), BF),
-            pltpu.VMEM((sides, seats, width + hidden), BF),
+            pltpu.VMEM((sides, seats, width), BF),
+            pltpu.VMEM((sides, seats, hidden), BF),
             pltpu.SemaphoreType.DMA((total,)),
             pltpu.SemaphoreType.DMA((sides * (2 + blocks + per),)),
         ],
+        {1 + len(arrays): 0} if given else None,
     )
     return result[:-1], result[-1]
 
@@ -1401,11 +1498,12 @@
     def turn(self):
         _, rows, width = self.shard.shape
         half = (1, rows, width)
-        self.cut = move(
+        *self.cut, self.x, self.y = move(
             "cut",
             [self.x, self.y],
             [(0, (pl.ds(0, 1),), 0, (ALL,), half), (1, (pl.ds(1, 1),), 1, (ALL,), half)],
-            [sds(half, BF)] * 2,
+            [sds(half, BF)] * 2 + [sds(self.x.shape, BF)] * 2,
+            {0: 2, 1: 3},
         )
 
     def send(self, after=()):
@@ -1792,27 +1890,60 @@
                 attn_w[layer + 1].send(sent[1:])
             if layer + 1 < last:
                 attn_w.append(fetch_attn(layer + 2))
-        (rh, slope, gate, out), made = expert_fwd(
-            me, z, sent, expert_w[layer], bias_in, bias_oe, cap, layer == last
-        )
-        if four and layer < last:
-            attn_w[layer + 1].cross(made[:1])
-        returned = exchange(made) if layer < last else made
-        other_rh = swap(rh, "dp", 1) if four else None
-        saved.append((x, x1, qkv, gates, ao, other_ao, rh, other_rh, slope, gate, out))
-        x_args = (x1, gates, cols[layer], returned)
+        common = (x, x1, qkv, gates, ao, other_ao)
+        if layer < last:
+            (rh, slope, gate, out), made = expert_fwd(
+                me, sent, expert_w[layer], bias_in, bias_oe, cap
+            )
+            if four:
+                attn_w[layer + 1].cross(made[:1])
+            returned = exchange(made)
+            other_rh = swap(rh, "dp", 1) if four else None
+            saved.append((*common, rh, other_rh, slope, gate, out))
+            x_args = (x1, gates, cols[layer], returned)
+        else:
+            (rp, hd, give, made), d_rows = expert_both(
+                me, z, sent, grad_seats[0], expert_w[layer], bias_in, bias_oe, cap, shards
+            )
+            saved.append(common)
 
     attn_sums, expert_sums = [None] * layers, [None] * layers
     for layer in reversed(range(layers)):
-        x, x1, qkv, gates, ao, other_ao, rh, other_rh, slope, gate, out = saved[layer]
+        x, x1, qkv, gates, ao, other_ao = saved[layer][:6]
         vecs, router = params[layer][:2]
-        if four and layer < last:
-            g_attn = attn_grads(me, z, *attn_operands, g_bias, shards, True)
-            attn_sums[layer + 1] = AttnSum(hold(g_attn, grad_seats[1:]))
-        gd, d_rows = expert_back(me, z, grad_seats, slope, gate, out, expert_w[layer], cap)
-        d_back = exchange(d_rows)
-        other = (other_rh, swap(gd, "dp", 1)) if four else None
-        g_expert, g_bias = expert_grads(me, (rh, gd), other, shards)
+        sizes = (experts * cap_pad, w_in.shape[3])
+        if layer == last:
+            rows_at, pre_at = [(rp, 0)], [(rp, width)]
+            h_at, out_at = [(hd, 0, True)], [(hd, sizes[1])]
+            if four:
+                other = swap(give, "dp", 1)
+                h_at, out_at = h_at + [(other, 0, False)], out_at + [(other, sizes[1] // 2)]
+                other = swap(rp, "dp", 1)
+                rows_at, pre_at = rows_at + [(other, 0)], pre_at + [(other, width)]
+            d_back = exchange(d_rows)
+            g_expert, g_bias = expert_grads(
+                me, rows_at, h_at, out_at, pre_at, sizes, four, shards
+            )
+        else:
+            rh, other_rh, slope, gate, out = saved[layer][6:]
+            if four:
+                g_attn = attn_grads(me, z, *attn_operands, g_bias, shards, True)
+                attn_sums[layer + 1] = AttnSum(hold(g_attn, grad_seats[1:]))
+            gd, d_rows = expert_back(me, grad_seats, slope, gate, out, expert_w[layer], cap)
+            d_back = exchange(d_rows)
+            lefts, backs = [rh], [gd]
+            if four:
+                lefts, backs = [rh, other_rh], [gd, swap(gd, "dp", 1)]
+            g_expert, g_bias = expert_grads(
+                me,
+                [(v, 0) for v in lefts],
+                [(v, width, True) for v in lefts],
+                [(v, 0) for v in backs],
+                [(v, width) for v in backs],
+                sizes,
+                four,
+                shards,
+            )
         if four:
             (g_expert,) = hold(g_expert, d_back[1:])
             expert_sums[layer] = scatter_chips(g_expert)
@@ -1848,7 +1979,7 @@
         done_attn, smalls, done_expert = (), [None] * layers, ()
         for layer in reversed(range(1, layers)):
             done_expert = expert_out(expert_sums[layer], layer, layers, done_expert, width)
-        made = hold(made, [back])
+        (made,) = hold([made], [back])
         g_attn = attn_grads(me, z, *attn_operands, g_bias, shards, False)
         attn_sums[0] = AttnSum(g_attn)
         attn_sums[0].send_across()
@@ -1858,8 +1989,8 @@
             attn_sums[layer].cut(z)
         for layer in reversed(range(1, layers)):
             attn_sums[layer].halves()
-    returned = lax.all_to_all(made[0], "expert", 0, 0, tiled=True)
-    mixed = mix(z, x_args[0], x_args[1], x_args[2], returned, tokens)
+    returned = lax.all_to_all(made, "expert", 0, 0, tiled=True)
+    mixed = mix(z, saved[last][1], saved[last][3], cols[last], returned, tokens)
     if four:
         attn_sums[0].fold2()
         for layer in reversed(range(1, layers)):

time: 397 us -> 394 us (level)
  Pallas kernels: 185 us -> 167 us
  waiting for transfers between devices: 88.1 us -> 101 us
  local copies, waits for them, and re-layouts: 23 us -> 27.4 us
    ppermute x55, waiting for transfers between devices: 74.2 us -> 95.4 us  [swap(): return lax.ppermute(value, axis, [(i, i ^ bit) for i in range(size)])]
    pallas_call x42 -> x41, Pallas kernels: 185 us -> 167 us  [call(): pl.pallas_call(body, name=name, in_specs=[ANY if spec is LOAD else spec f...]
    unnamed x8, waiting for transfers between devices: 8.33 us -> 1.64 us
    unnamed x128 -> x142, local copies, waits for them, and re-layouts: 22.2 us -> 26.6 us
  transfers between devices with their start and end apart: 62 -> 62, of which waited for: 22 -> 23; matrix products, arithmetic and copies ran while one was open for 1% -> 1% of each run, Pallas kernels for 42% -> 36%
where the time goes in v5:
time: 394 us; the launch traced here: 389 us
  Pallas kernels  167 us (42%)
  waiting for transfers between devices  101 us (26%)
  starting transfers between devices  68.3 us (17%)
  local copies, waits for them, and re-layouts  27.4 us (7%)
  between operations  14.9 us (4%)
  blocking collectives  10.6 us (3%)
    pallas_call x41, Pallas kernels, call(): pl.pallas_call(body, name=name, in_specs=[ANY if spec is LOAD else spec f...  167 us
    ppermute x55, waiting for transfers between devices, swap(): return lax.ppermute(value, axis, [(i, i ^ bit) for i in range(size)])  95.4 us
    ppermute x55, starting transfers between devices, swap(): return lax.ppermute(value, axis, [(i, i ^ bit) for i in range(size)])  58.7 us
    unnamed x142, local copies, waits for them, and re-layouts  26.6 us
    all_gather x1, blocking collectives, per_device(): small = lax.all_gather(small, 'dp', axis=0)  10.6 us
  transfers between devices with their start and end apart: 62, of which 23 were waited for; matrix products, arithmetic and copies ran while one was open for 1% of the time, Pallas kernels for 36%

profile of v5, /device:TPU:0, one launch (start us, length us, event | category | flops | bytes accessed | tf_op | source)
XLA Modules:
  0.0 389.0 jit_solution(5978438810498495887)
XLA Ops:
  13.7 3.0 collective-permute-start.1
  21.2 3.4 place_pairs.1
  28.6 4.9 %all-to-all-start = ((bf16[4,104,768]{2,1,0:T(8,128)(2,1)}), bf16[4,104,768]{2,1,0:T(8,128)(2,1)S(1)}, u32[]{:S(2)}, u32[]{:S(2)}) async-start(bf16[4,104,768]{2,1,0:T(8,128)(2,1)} %get-tuple-element.127), calls=%async_computation | async-start | bytes 1277952 | tf_op jit(solution)/shard_map/all_to_all | solution.py:1852
  33.5 3.0 collective-permute-done.1.refs_1_
  36.4 3.3 collective-permute-done.refs_0_
  44.9 5.5 %collective-permute-done.3.refs_6_.refs_17_ = bf16[1,96,1536]{2,1,0:T(8,128)(2,1)S(1)} collective-permute-done((bf16[1,96,1536]{2,1,0:T(8,128)(2,1)}, bf16[1,96,1536]{2,1,0:T(8,128)(2,1)S(1)}, u32[]{:S(2)}, u32[]{:S(2)}) %collective-permute-start.3) | collective-permute-done | bytes 294944 | tf_op jit(solution)/shard_map/ppermute | solution.py:1451
  51.0 10.6 %all-gather = f32[256,128]{1,0:T(8,128)} all-gather(f32[32,128]{1,0:T(8,128)S(1)} %copy-done.59), channel_id=2, replica_groups=mesh['dp'=8,'expert'=4] {'dp'}, dimensions={0}, use_global_device_ids=true | all-gather | bytes 147456 | tf_op jit(solution)/shard_map/all_gather | solution.py:1856
  70.9 8.9 %attn_fwd.2 = (f32[208,768]{1,0:T(8,128)}, f32[208,768]{1,0:T(8,128)}, bf16[208,2304]{1,0:T(8,128)(2,1)}, f32[208,128]{1,0:T(8,128)}, bf16[208,2304]{1,0:T(8,128...) custom-call(s32[1]{0:T(128)} %bitcast.1.refs_0_, ...), custom_call_target="tpu_custom_call" | custom-call | tf_op jit(solution)/shard_map/attn_fwd/pallas_call | solution.py:245
  84.2 3.2 pick_columns.2
  87.4 4.6 %collective-permute-done.13.refs_1_ = bf16[2,96,1536]{2,1,0:T(8,128)(2,1)S(1)} collective-permute-done((bf16[2,96,1536]{2,1,0:T(8,128)(2,1)}, bf16[2,96,1536]{2,1,0:T(8,128)(2,1)S(1)}, u32[]{:S(2)}, u32[]{:S(2)}) %collective-permute-start.13) | collective-permute-done | bytes 589856 | tf_op jit(solution)/shard_map/ppermute | solution.py:1451
  99.2 13.0 %expert_fwd.1 = (bf16[416,3840]{1,0:T(8,128)(2,1)}, bf16[416,3072]{1,0:T(8,128)(2,1)}, f32[416,128]{1,0:T(8,128)}, bf16[416,768]{1,0:T(8,128)(2,1)}, bf16[104,76...) custom-call(s32[1]{0:T(128)} %bitcast.1.refs_0_, ...), custom_call_target="tpu_custom_call" | custom-call | tf_op jit(solution)/shard_map/expert_fwd/pallas_call | solution.py:245
  113.7 3.2 collective-permute-start.14
  119.5 4.3 %collective-permute-done.14.refs_5_ = bf16[104,768]{1,0:T(8,128)(2,1)S(1)} collective-permute-done((bf16[104,768]{1,0:T(8,128)(2,1)S(1)}, bf16[104,768]{1,0:T(8,128)(2,1)S(1)}, u32[]{:S(2)}, u32[]{:S(2)}) %collective-permute-start.14) | collective-permute-done | bytes 159776 | tf_op jit(solution)/shard_map/ppermute | solution.py:1451
  123.8 7.9 %collective-permute-done.15.refs_6_ = bf16[104,768]{1,0:T(8,128)(2,1)S(1)} collective-permute-done((bf16[104,768]{1,0:T(8,128)(2,1)S(1)}, bf16[104,768]{1,0:T(8,128)(2,1)S(1)}, u32[]{:S(2)}, u32[]{:S(2)}) %collective-permute-start.15) | collective-permute-done | bytes 159776 | tf_op jit(solution)/shard_map/ppermute | solution.py:1451
  132.6 9.2 %attn_fwd.3 = (f32[208,768]{1,0:T(8,128)}, f32[208,768]{1,0:T(8,128)}, bf16[208,2304]{1,0:T(8,128)(2,1)}, f32[208,128]{1,0:T(8,128)}, bf16[208,2304]{1,0:T(8,128...) custom-call(s32[1]{0:T(128)} %bitcast.1.refs_0_, ...), custom_call_target="tpu_custom_call" | custom-call | tf_op jit(solution)/shard_map/attn_fwd/pallas_call | solution.py:245
  147.2 3.2 pick_columns.3
  150.4 3.8 all-gather.8.cloned.1.call-done
  154.2 5.1 %collective-permute-done.25.refs_4_ = bf16[104,768]{1,0:T(8,128)(2,1)S(1)} collective-permute-done((bf16[104,768]{1,0:T(8,128)(2,1)}, bf16[104,768]{1,0:T(8,128)(2,1)S(1)}, u32[]{:S(2)}, u32[]{:S(2)}) %collective-permute-start.25) | collective-permute-done | bytes 159776 | tf_op jit(solution)/shard_map/ppermute | solution.py:1451
  160.0 17.6 %expert_both.1 = (bf16[416,3840]{1,0:T(8,128)(2,1)}, bf16[416,3840]{1,0:T(8,128)(2,1)}, bf16[416,2304]{1,0:T(8,128)(2,1)}, bf16[4,104,768]{2,1,0:T(8,128)(2,1)},...) custom-call(s32[1]{0:T(128)} %bitcast.1.refs_0_, ...), custom_call_target="tpu_custom_call" | custom-call | tf_op jit(solution)/shard_map/expert_both/pallas_call | solution.py:245
  182.9 3.5 collective-permute-done.31.refs_4_
  189.3 12.6 %expert_grads.2 = (bf16[4,2,96,3072]{3,2,1,0:T(8,128)(2,1)}, f32[8,768]{1,0:T(8,128)}) custom-call(s32[1]{0:T(128)} %bitcast.1.refs_0_, bf16[416,3840]{1,0:T(8,128)(2,1)} %get-tuple-element.175.refs_1_, bf16[416,3840]{1,0:T(8,128)(2,1)} %copy-done.27, bf16[416,3840]{1,0:T(8,128)(2,1)} %get-tuple-element.176.refs_3_, bf16[416,2304]{1,0:T(8,128)(2,1)} %copy-done.34), custom_call_target="tpu_custom_call" | custom-call | tf_op jit(solution)/shard_map/expert_grads/pallas_call | solution.py:245
  202.8 13.9 %attn_back.2 = (f32[208,768]{1,0:T(8,128)}, bf16[224,3328]{1,0:T(8,128)(2,1)}, bf16[104,768]{1,0:T(8,128)(2,1)}, bf16[104,768]{1,0:T(8,128)(2,1)}, bf16[104,768]{1,0:T(8,128)(2,1)}, /*index=5*/bf16[104,768]{1,0:T(8,128)(2,1)}) custom-call(s32[1]{0:T(128)} %bitcast.1.refs_0_, bf16[104,768]{1,0:T(8,128)(2,1)} %get-tuple-element.170.refs_1_, ...), custom_call_target="tpu_custom_call" | custom-call | tf_op jit(solution)/shard_map/attn_back/pallas_call | solution.py:245
  228.4 6.1 %collective-permute-done.33.refs_2_.refs_3_ = bf16[104,768]{1,0:T(8,128)(2,1)S(1)} collective-permute-done((bf16[104,768]{1,0:T(8,128)(2,1)}, bf16[104,768]{1,0:T(8,128)(2,1)S(1)}, u32[]{:S(2)}, u32[]{:S(2)}) %collective-permute-start.33) | collective-permute-done | bytes 159776 | tf_op jit(solution)/shard_map/ppermute | solution.py:1451
  237.0 13.2 %expert_back.1 = (bf16[416,3840]{1,0:T(8,128)(2,1)}, bf16[104,768]{1,0:T(8,128)(2,1)}, bf16[104,768]{1,0:T(8,128)(2,1)}, bf16[104,768]{1,0:T(8,128)(2,1)}, bf16[104,768]{1,0:T(8,128)(2,1)}) custom-call(s32[1]{0:T(128)} %bitcast.1.refs_0_, bf16[104,768]{1,0:T(8,128)(2,1)} %get-tuple-element.179.refs_1_, bf16[104,768]{1,0:T(8,128)(2,1)} %copy-done.48, ...), custom_call_target="tpu_custom_call" | custom-call | tf_op jit(solution)/shard_map/expert_back/pallas_call | solution.py:245
  256.4 12.4 %expert_grads.3 = (bf16[4,2,96,3072]{3,2,1,0:T(8,128)(2,1)}, f32[8,768]{1,0:T(8,128)}) custom-call(s32[1]{0:T(128)} %bitcast.1.refs_0_, bf16[416,3840]{1,0:T(8,128)(2,1)} %get-tuple-element.152.refs_3_.refs_1_, bf16[416,3840]{1,0:T(8,128)(2,1)} %collective-permute-done.40.refs_2_, bf16[416,3840]{1,0:T(8,128)(2,1)} %get-tuple-element.195.refs_3_, ...), custom_call_target="tpu_custom_call" | custom-call | tf_op jit(solution)/shard_map/expert_grads/pallas_call | solution.py:245
  269.6 13.5 %attn_back.3 = (f32[197,768]{1,0:T(8,128)}, bf16[224,3328]{1,0:T(8,128)(2,1)}) custom-call(s32[1]{0:T(128)} %bitcast.1.refs_0_, bf16[104,768]{1,0:T(8,128)(2,1)} %get-tuple-element.190.refs_1_, bf16[104,768]{1,0:T(8,128)(2,1)} %copy-done.45, bf16[104,768]{1,0:T(8,128)(2,1)} %copy-done.46, bf16[104,768]{1,0:T(8,128)(2,1)} %copy-done.47, ...), custom_call_target="tpu_custom_call" | custom-call | tf_op jit(solution)/shard_map/attn_back/pallas_call | solution.py:245
  295.0 4.3 %all-to-all-start.1 = ((bf16[4,104,768]{2,1,0:T(8,128)(2,1)}), bf16[4,104,768]{2,1,0:T(8,128)(2,1)S(1)}, u32[]{:S(2)}, u32[]{:S(2)}) async-start(bf16[4,104,768]{2,1,0:T(8,128)(2,1)} %hold.11.refs_7_), calls=%async_computation.1 | async-start | bytes 1277952 | tf_op jit(solution)/shard_map/all_to_all | solution.py:1992
  299.3 7.8 %collective-permute-done.45.refs_3_ = bf16[96,1664]{1,0:T(8,128)(2,1)S(1)} collective-permute-done((bf16[96,1664]{1,0:T(8,128)(2,1)}, bf16[96,1664]{1,0:T(8,128)(2,1)S(1)}, u32[]{:S(2)}, u32[]{:S(2)}) %collective-permute-start.45) | collective-permute-done | bytes 319520 | tf_op jit(solution)/shard_map/ppermute | solution.py:1451
  314.8 8.2 %collective-permute-done.46.refs_1_ = bf16[96,1664]{1,0:T(8,128)(2,1)S(1)} collective-permute-done((bf16[96,1664]{1,0:T(8,128)(2,1)}, bf16[96,1664]{1,0:T(8,128)(2,1)S(1)}, u32[]{:S(2)}, u32[]{:S(2)}) %collective-permute-start.46) | collective-permute-done | bytes 319520 | tf_op jit(solution)/shard_map/ppermute | solution.py:1451
  327.7 6.1 %collective-permute-done.48.refs_2_ = bf16[2,96,1664]{2,1,0:T(8,128)(2,1)} collective-permute-done((bf16[2,96,1664]{2,1,0:T(8,128)(2,1)}, bf16[2,96,1664]{2,1,0:T(8,128)(2,1)}, u32[]{:S(2)}, u32[]{:S(2)}) %collective-permute-start.48) | collective-permute-done | bytes 639008 | tf_op jit(solution)/shard_map/ppermute | solution.py:1451
  344.6 9.7 %collective-permute-done.50.refs_3_ = bf16[96,1664]{1,0:T(8,128)(2,1)S(1)} collective-permute-done((bf16[96,1664]{1,0:T(8,128)(2,1)S(1)}, bf16[96,1664]{1,0:T(8,128)(2,1)S(1)}, u32[]{:S(2)}, u32[]{:S(2)}) %collective-permute-start.50) | collective-permute-done | bytes 319520 | tf_op jit(solution)/shard_map/ppermute | solution.py:1451
  360.0 10.4 %collective-permute-done.54.refs_2_ = bf16[96,1664]{1,0:T(8,128)(2,1)S(1)} collective-permute-done((bf16[96,1664]{1,0:T(8,128)(2,1)S(1)}, bf16[96,1664]{1,0:T(8,128)(2,1)S(1)}, u32[]{:S(2)}, u32[]{:S(2)}) %collective-permute-start.54) | collective-permute-done | bytes 319520 | tf_op jit(solution)/shard_map/ppermute | solution.py:1451
  (283 shorter events, 135.0 us)
Async XLA Ops:
  7.2 92.0 %all-gather.6.cloned.1.call-start = ((), (), s32[]{:S(2)}) async-start(), calls=%async_computation.5 | async-start | bytes 10616832 | tf_op jit(solution)/shard_map/all_gather | solution.py:1836
  11.3 142.8 %all-gather.8.cloned.1.call-start = ((), (), s32[]{:S(2)}) async-start(), calls=%async_computation.6 | async-start | bytes 10616832 | tf_op jit(solution)/shard_map/all_gather | solution.py:1836
  13.7 22.8 %collective-permute-start.1 = (bf16[2,96,1536]{2,1,0:T(8,128)(2,1)S(1)}, bf16[2,96,1536]{2,1,0:T(8,128)(2,1)S(1)}, u32[]{:S(2)}, u32[]{:S(2)}) collective-permute-start(bf16[2,96,1536]{2,1,0:T(8,128)(2,1)S(1)} %copy-done.21), channel_id=1, source_target_pairs={{0,16},{4,20},{8,24},{12,28},{16,0},{20,4},{24,8},{28,12},{1,17},{... | collective-permute-start | bytes 1769480 | tf_op jit(solution)/shard_map/ppermute | solution.py:1451
  16.7 23.0 %collective-permute-start = (bf16[2,96,1536]{2,1,0:T(8,128)(2,1)S(1)}, bf16[2,96,1536]{2,1,0:T(8,128)(2,1)S(1)}, u32[]{:S(2)}, u32[]{:S(2)}) collective-permute-start(bf16[2,96,1536]{2,1,0:T(8,128)(2,1)S(1)} %copy-done.21), channel_id=1, source_target_pairs={{0,8},{4,12},{8,0},{12,4},{16,24},{20,28},{24,16},{28,20},{1,9},{5... | collective-permute-start | bytes 1769480 | tf_op jit(solution)/shard_map/ppermute | solution.py:1451
  28.6 33.0 %all-to-all-start = ((bf16[4,104,768]{2,1,0:T(8,128)(2,1)}), bf16[4,104,768]{2,1,0:T(8,128)(2,1)S(1)}, u32[]{:S(2)}, u32[]{:S(2)}) async-start(bf16[4,104,768]{2,1,0:T(8,128)(2,1)} %get-tuple-element.127), calls=%async_computation | async-start | bytes 1277952 | tf_op jit(solution)/shard_map/all_to_all | solution.py:1852
  33.4 250.2 %reduce-scatter.10.cloned.1.call-start = ((), (), s32[]{:S(2)}) async-start(), calls=%async_computation.7 | async-start | bytes 5898240
  33.4 32.8 %collective-permute-start.6 = (bf16[2,96,1536]{2,1,0:T(8,128)(2,1)S(1)}, bf16[2,96,1536]{2,1,0:T(8,128)(2,1)S(1)}, u32[]{:S(2)}, u32[]{:S(2)}) collective-permute-start(bf16[2,96,1536]{2,1,0:T(8,128)(2,1)S(1)} %copy-done.21), channel_id=1, source_target_pairs={{0,4},{4,0},{8,12},{12,8},{16,20},{20,16},{24,28},{28,24},{1,5},{5... | collective-permute-start | bytes 1769480 | tf_op jit(solution)/shard_map/ppermute | solution.py:1451
  44.9 22.0 %collective-permute-start.2 = (bf16[1,96,1536]{2,1,0:T(8,128)(2,1)}, bf16[1,96,1536]{2,1,0:T(8,128)(2,1)}, u32[]{:S(2)}, u32[]{:S(2)}) collective-permute-start(bf16[1,96,1536]{2,1,0:T(8,128)(2,1)} %get-tuple-element.125.refs_2_), channel_id=1, source_target_pairs={{0,16},{4,20},{8,24},{12,28},{16,0},{20,4},{24,8},{28,12},{1,17},{... | collective-permute-start | bytes 884744 | tf_op jit(solution)/shard_map/ppermute | solution.py:1451
  50.4 17.9 %collective-permute-start.5 = (bf16[1,96,1536]{2,1,0:T(8,128)(2,1)S(1)}, bf16[1,96,1536]{2,1,0:T(8,128)(2,1)}, u32[]{:S(2)}, u32[]{:S(2)}) collective-permute-start(bf16[1,96,1536]{2,1,0:T(8,128)(2,1)S(1)} %collective-permute-done.3.refs_6_.refs_17_), channel_id=1, source_target_pairs={{0,4},{4,0},{8,12},{12,8},{16,20},{20,16},{24,28},{28,24},{1,5},{5... | collective-permute-start | bytes 884744 | tf_op jit(solution)/shard_map/ppermute | solution.py:1451
  50.4 19.7 %collective-permute-start.7 = (bf16[2,96,1536]{2,1,0:T(8,128)(2,1)}, bf16[2,96,1536]{2,1,0:T(8,128)(2,1)}, u32[]{:S(2)}, u32[]{:S(2)}) collective-permute-start(bf16[2,96,1536]{2,1,0:T(8,128)(2,1)} %get-tuple-element.123.refs_3_.refs_14_), channel_id=1, source_target_pairs={{0,4},{4,0},{8,12},{12,8},{16,20},{20,16},{24,28},{28,24},{1,5},{5... | collective-permute-start | bytes 1769480 | tf_op jit(solution)/shard_map/ppermute | solution.py:1451
  50.9 19.2 %collective-permute-start.8 = (bf16[2,96,1536]{2,1,0:T(8,128)(2,1)}, bf16[2,96,1536]{2,1,0:T(8,128)(2,1)}, u32[]{:S(2)}, u32[]{:S(2)}) collective-permute-start(bf16[2,96,1536]{2,1,0:T(8,128)(2,1)} %get-tuple-element.124.refs_4_.refs_15_), channel_id=1, source_target_pairs={{0,4},{4,0},{8,12},{12,8},{16,20},{20,16},{24,28},{28,24},{1,5},{5... | collective-permute-start | bytes 1769480 | tf_op jit(solution)/shard_map/ppermute | solution.py:1451
  66.3 25.7 %collective-permute-start.13 = (bf16[2,96,1536]{2,1,0:T(8,128)(2,1)}, bf16[2,96,1536]{2,1,0:T(8,128)(2,1)S(1)}, u32[]{:S(2)}, u32[]{:S(2)}) collective-permute-start(bf16[2,96,1536]{2,1,0:T(8,128)(2,1)} %pack_attn.3.refs_17_.refs_8_.refs_13_), channel_id=1, source_target_pairs={{0,16},{4,20},{8,24},{12,28},{16,0},{20,4},{24,8},{28,12},{1,17},{... | collective-permute-start | bytes 1769480 | tf_op jit(solution)/shard_map/ppermute | solution.py:1451
  66.9 25.1 %collective-permute-start.12 = (bf16[2,96,1536]{2,1,0:T(8,128)(2,1)}, bf16[2,96,1536]{2,1,0:T(8,128)(2,1)S(1)}, u32[]{:S(2)}, u32[]{:S(2)}) collective-permute-start(bf16[2,96,1536]{2,1,0:T(8,128)(2,1)} %pack_attn.3.refs_17_.refs_8_.refs_13_), channel_id=1, source_target_pairs={{0,8},{4,12},{8,0},{12,4},{16,24},{20,28},{24,16},{28,20},{1,9},{5... | collective-permute-start | bytes 1769480 | tf_op jit(solution)/shard_map/ppermute | solution.py:1451
  92.0 21.7 %collective-permute-start.21 = (bf16[2,96,1536]{2,1,0:T(8,128)(2,1)S(1)}, bf16[2,96,1536]{2,1,0:T(8,128)(2,1)S(1)}, u32[]{:S(2)}, u32[]{:S(2)}) collective-permute-start(bf16[2,96,1536]{2,1,0:T(8,128)(2,1)S(1)} %copy-done.20), channel_id=1, source_target_pairs={{0,4},{4,0},{8,12},{12,8},{16,20},{20,16},{24,28},{28,24},{1,5},{5... | collective-permute-start | bytes 1769480 | tf_op jit(solution)/shard_map/ppermute | solution.py:1451
  94.9 22.0 %collective-permute-start.22 = (bf16[2,96,1536]{2,1,0:T(8,128)(2,1)}, bf16[2,96,1536]{2,1,0:T(8,128)(2,1)S(1)}, u32[]{:S(2)}, u32[]{:S(2)}) collective-permute-start(bf16[2,96,1536]{2,1,0:T(8,128)(2,1)} %get-tuple-element.149.refs_9_.refs_14_), channel_id=1, source_target_pairs={{0,4},{4,0},{8,12},{12,8},{16,20},{20,16},{24,28},{28,24},{1,5},{5... | collective-permute-start | bytes 1769480 | tf_op jit(solution)/shard_map/ppermute | solution.py:1451
  95.3 22.7 %collective-permute-start.23 = (bf16[2,96,1536]{2,1,0:T(8,128)(2,1)}, bf16[2,96,1536]{2,1,0:T(8,128)(2,1)S(1)}, u32[]{:S(2)}, u32[]{:S(2)}) collective-permute-start(bf16[2,96,1536]{2,1,0:T(8,128)(2,1)} %get-tuple-element.150.refs_10_.refs_15_), channel_id=1, source_target_pairs={{0,4},{4,0},{8,12},{12,8},{16,20},{20,16},{24,28},{28,24},{1,5},{5... | collective-permute-start | bytes 1769480 | tf_op jit(solution)/shard_map/ppermute | solution.py:1451
  113.1 18.6 %collective-permute-start.19 = (bf16[1,96,1536]{2,1,0:T(8,128)(2,1)}, bf16[1,96,1536]{2,1,0:T(8,128)(2,1)S(1)}, u32[]{:S(2)}, u32[]{:S(2)}) collective-permute-start(bf16[1,96,1536]{2,1,0:T(8,128)(2,1)} %get-tuple-element.153.refs_11_.refs_16_), channel_id=1, source_target_pairs={{0,4},{4,0},{8,12},{12,8},{16,20},{20,16},{24,28},{28,24},{1,5},{5... | collective-permute-start | bytes 884744 | tf_op jit(solution)/shard_map/ppermute | solution.py:1451
  113.2 18.5 %collective-permute-start.20 = (bf16[1,96,1536]{2,1,0:T(8,128)(2,1)}, bf16[1,96,1536]{2,1,0:T(8,128)(2,1)S(1)}, u32[]{:S(2)}, u32[]{:S(2)}) collective-permute-start(bf16[1,96,1536]{2,1,0:T(8,128)(2,1)} %get-tuple-element.154.refs_12_.refs_17_), channel_id=1, source_target_pairs={{0,4},{4,0},{8,12},{12,8},{16,20},{20,16},{24,28},{28,24},{1,5},{5... | collective-permute-start | bytes 884744 | tf_op jit(solution)/shard_map/ppermute | solution.py:1451
  178.2 23.7 %collective-permute-start.27 = (bf16[104,768]{1,0:T(8,128)(2,1)}, bf16[104,768]{1,0:T(8,128)(2,1)S(1)}, u32[]{:S(2)}, u32[]{:S(2)}) collective-permute-start(bf16[104,768]{1,0:T(8,128)(2,1)} %get-tuple-element.171), channel_id=1, source_target_pairs={{0,1},{1,0},{2,3},{3,2},{4,5},{5,4},{6,7},{7,6},{8,9},{9,8},{10,11... | collective-permute-start | bytes 479240 | tf_op jit(solution)/shard_map/ppermute | solution.py:1451
  180.5 21.5 %collective-permute-start.28 = (bf16[104,768]{1,0:T(8,128)(2,1)}, bf16[104,768]{1,0:T(8,128)(2,1)S(1)}, u32[]{:S(2)}, u32[]{:S(2)}) collective-permute-start(bf16[104,768]{1,0:T(8,128)(2,1)} %get-tuple-element.172), channel_id=1, source_target_pairs={{0,2},{1,3},{2,0},{3,1},{4,6},{5,7},{6,4},{7,5},{8,10},{9,11},{10,... | collective-permute-start | bytes 479240 | tf_op jit(solution)/shard_map/ppermute | solution.py:1451
  181.5 20.5 %collective-permute-start.29 = (bf16[104,768]{1,0:T(8,128)(2,1)}, bf16[104,768]{1,0:T(8,128)(2,1)S(1)}, u32[]{:S(2)}, u32[]{:S(2)}) collective-permute-start(bf16[104,768]{1,0:T(8,128)(2,1)} %get-tuple-element.173), channel_id=1, source_target_pairs={{0,3},{1,2},{2,1},{3,0},{4,7},{5,6},{6,5},{7,4},{8,11},{9,10},{10,... | collective-permute-start | bytes 479240 | tf_op jit(solution)/shard_map/ppermute | solution.py:1451
  202.8 108.6 %reduce-scatter.12.cloned.1.call-start = ((), (), s32[]{:S(2)}) async-start(), calls=%async_computation.8 | async-start | bytes 3194880
  235.2 139.8 %reduce-scatter.14.cloned.1.call-start = ((), (), s32[]{:S(2)}) async-start(), calls=%async_computation.9 | async-start | bytes 5898240
  237.0 18.3 %collective-permute-start.40 = (bf16[416,3840]{1,0:T(8,128)(2,1)S(1)}, bf16[416,3840]{1,0:T(8,128)(2,1)}, u32[]{:S(2)}, u32[]{:S(2)}) collective-permute-start(bf16[416,3840]{1,0:T(8,128)(2,1)S(1)} %copy-done.19), channel_id=1, source_target_pairs={{0,4},{4,0},{8,12},{12,8},{16,20},{20,16},{24,28},{28,24},{1,5},{5... | collective-permute-start | bytes 9584648 | tf_op jit(solution)/shard_map/ppermute | solution.py:1451
  250.7 18.1 %collective-permute-start.37 = (bf16[104,768]{1,0:T(8,128)(2,1)}, bf16[104,768]{1,0:T(8,128)(2,1)S(1)}, u32[]{:S(2)}, u32[]{:S(2)}) collective-permute-start(bf16[104,768]{1,0:T(8,128)(2,1)} %get-tuple-element.191), channel_id=1, source_target_pairs={{0,1},{1,0},{2,3},{3,2},{4,5},{5,4},{6,7},{7,6},{8,9},{9,8},{10,11... | collective-permute-start | bytes 479240 | tf_op jit(solution)/shard_map/ppermute | solution.py:1451
  295.0 31.3 %all-to-all-start.1 = ((bf16[4,104,768]{2,1,0:T(8,128)(2,1)}), bf16[4,104,768]{2,1,0:T(8,128)(2,1)S(1)}, u32[]{:S(2)}, u32[]{:S(2)}) async-start(bf16[4,104,768]{2,1,0:T(8,128)(2,1)} %hold.11.refs_7_), calls=%async_computation.1 | async-start | bytes 1277952 | tf_op jit(solution)/shard_map/all_to_all | solution.py:1992
  309.2 24.6 %collective-permute-start.48 = (bf16[2,96,1664]{2,1,0:T(8,128)(2,1)}, bf16[2,96,1664]{2,1,0:T(8,128)(2,1)}, u32[]{:S(2)}, u32[]{:S(2)}) collective-permute-start(bf16[2,96,1664]{2,1,0:T(8,128)(2,1)} %get-tuple-element.210), channel_id=1, source_target_pairs={{0,16},{4,20},{8,24},{12,28},{16,0},{20,4},{24,8},{28,12},{1,17},{... | collective-permute-start | bytes 1916936 | tf_op jit(solution)/shard_map/ppermute | solution.py:1451
  310.8 25.2 %collective-permute-start.47 = (bf16[2,96,1664]{2,1,0:T(8,128)(2,1)S(1)}, bf16[2,96,1664]{2,1,0:T(8,128)(2,1)}, u32[]{:S(2)}, u32[]{:S(2)}) collective-permute-start(bf16[2,96,1664]{2,1,0:T(8,128)(2,1)S(1)} %get-tuple-element.206.refs_2_), channel_id=1, source_target_pairs={{0,8},{4,12},{8,0},{12,4},{16,24},{20,28},{24,16},{28,20},{1,9},{5... | collective-permute-start | bytes 1916936 | tf_op jit(solution)/shard_map/ppermute | solution.py:1451
  324.4 19.6 %collective-permute-start.51 = (bf16[96,1664]{1,0:T(8,128)(2,1)S(1)}, bf16[96,1664]{1,0:T(8,128)(2,1)S(1)}, u32[]{:S(2)}, u32[]{:S(2)}) collective-permute-start(bf16[96,1664]{1,0:T(8,128)(2,1)S(1)} %fold3.3.refs_5_.refs_0_), channel_id=1, source_target_pairs={{0,2},{1,3},{2,0},{3,1},{4,6},{5,7},{6,4},{7,5},{8,10},{9,11},{10,... | collective-permute-start | bytes 958472 | tf_op jit(solution)/shard_map/ppermute | solution.py:1451
  344.5 25.9 %collective-permute-start.54 = (bf16[96,1664]{1,0:T(8,128)(2,1)S(1)}, bf16[96,1664]{1,0:T(8,128)(2,1)S(1)}, u32[]{:S(2)}, u32[]{:S(2)}) collective-permute-start(bf16[96,1664]{1,0:T(8,128)(2,1)S(1)} %fold3.4.refs_4_.refs_1_), channel_id=1, source_target_pairs={{0,1},{1,0},{2,3},{3,2},{4,5},{5,4},{6,7},{7,6},{8,9},{9,8},{10,11... | collective-permute-start | bytes 958472 | tf_op jit(solution)/shard_map/ppermute | solution.py:1451
  357.6 20.1 %collective-permute-start.53 = (bf16[96,1664]{1,0:T(8,128)(2,1)S(1)}, bf16[96,1664]{1,0:T(8,128)(2,1)S(1)}, u32[]{:S(2)}, u32[]{:S(2)}) collective-permute-start(bf16[96,1664]{1,0:T(8,128)(2,1)S(1)} %get-tuple-element.214.refs_1_), channel_id=1, source_target_pairs={{0,1},{1,0},{2,3},{3,2},{4,5},{5,4},{6,7},{7,6},{8,9},{9,8},{10,11... | collective-permute-start | bytes 958472 | tf_op jit(solution)/shard_map/ppermute | solution.py:1451
  357.8 19.8 %collective-permute-start.52 = (bf16[96,1664]{1,0:T(8,128)(2,1)S(1)}, bf16[96,1664]{1,0:T(8,128)(2,1)S(1)}, u32[]{:S(2)}, u32[]{:S(2)}) collective-permute-start(bf16[96,1664]{1,0:T(8,128)(2,1)S(1)} %get-tuple-element.213.refs_3_.refs_0_), channel_id=1, source_target_pairs={{0,2},{1,3},{2,0},{3,1},{4,6},{5,7},{6,4},{7,5},{8,10},{9,11},{10,... | collective-permute-start | bytes 958472 | tf_op jit(solution)/shard_map/ppermute | solution.py:1451
  (99 other events, 789.8 us)
Sparse Core Ops, SparseCore 0:
  11.4 79.9 all-gather.5
  93.8 60.2 all-gather.7
  202.9 56.6 reduce-scatter.9
  262.5 43.1 reduce-scatter.11
  308.6 66.3 reduce-scatter.13

commit v6 on v5

--- a/solution.py
+++ b/solution.py
@@ -16,8 +16,9 @@
 LANES = 128
 NEG = -1e30
 VMEM_LIMIT = 60 * 1024 * 1024
-LIMITS = {name: 16 * 1024 * 1024 for name in ("fold1", "fold2", "fold3", "mix")}
+LIMITS = {name: 16 * 1024 * 1024 for name in ("fold1", "fold2", "fold3", "mix", "attn_last")}
 LIMITS["attn_grads"] = 24 * 1024 * 1024
+LIMITS["pick_columns"] = 62 * 1024 * 1024
 
 
 def up(value, step):
@@ -138,8 +139,17 @@
     return (lanes < HEAD_DIM, lanes >= HEAD_DIM)
 
 
-def head_probs(query, keys, mask, tokens):
-    query = jnp.where(mask, query, 0).astype(F32) * HEAD_DIM ** (-0.5)
+def stacked(value, masks):
+    return jnp.concatenate([jnp.where(mask, value, 0).astype(value.dtype) for mask in masks], 0)
+
+
+def unstacked(value, masks):
+    rows = value.shape[0] // 2
+    return jnp.where(masks[0], value[:rows], value[rows:])
+
+
+def pair_probs(query, keys, masks, tokens):
+    query = stacked(query, masks).astype(F32) * HEAD_DIM ** (-0.5)
     scores = dot_nt(query.astype(BF), keys)
     lanes = lax.broadcasted_iota(jnp.int32, scores.shape, 1)
     scores = jnp.where(lanes < tokens, scores, NEG)
@@ -149,6 +159,7 @@
 
 VM = pl.BlockSpec(memory_space=pltpu.VMEM)
 ANY = pl.BlockSpec(memory_space=pl.ANY)
+HBM = pl.BlockSpec(memory_space=pltpu.HBM)
 SM = pl.BlockSpec(memory_space=pltpu.SMEM)
 
 
@@ -245,7 +256,7 @@
     result = pl.pallas_call(
         body,
         name=name,
-        in_specs=[ANY if spec is LOAD else spec for spec in specs] + [ANY] * len(after),
+        in_specs=[HBM if spec is LOAD else spec for spec in specs] + [ANY] * len(after),
         out_specs=ANY if single and out_specs is STORE else (
             out_specs if single else [ANY if spec is STORE else spec for spec in out_kinds]
         ),
@@ -256,7 +267,7 @@
             vmem_limit_bytes=LIMITS.get(name, VMEM_LIMIT)
         ),
     )(*args, *after)
-    Order.token = result[0] if isinstance(result, (tuple, list)) else result
+    Order.token = result if single else min(result, key=lambda value: value.size)
     return result
 
 
@@ -316,10 +327,15 @@
     wide = [t for t, task in enumerate(tasks) if task[1] == F32]
     slim = [t for t, task in enumerate(tasks) if task[1] != F32]
 
+    last = name.endswith("_out")
+    mark = [sds((8, LANES), F32)] if last else []
+
     def kernel(*refs):
         ins, rest = refs[: len(args)], refs[len(args) :]
         results = rest[: len(outs)]
-        loaded, wide_ref, slim_ref, in_sems, out_sems = rest[len(outs) :]
+        loaded, wide_ref, slim_ref, in_sems, out_sems = rest[len(outs) + len(mark) :]
+        for ref in rest[len(outs) : len(outs) + len(mark)]:
+            ref[...] = jnp.zeros_like(ref)
         loads = [
             pltpu.make_async_copy(ins[i].at[where], loaded.at[n], in_sems.at[n])
             for n, (_, (i, where)) in enumerate(terms)
@@ -346,13 +362,13 @@
         for copy in stores:
             copy.wait()
 
-    return call(
+    result = call(
         kernel,
         name,
         args,
         [ANY] * len(args),
-        outs,
-        [ANY] * len(outs),
+        list(outs) + mark,
+        [HBM if last else ANY] * len(outs) + [VM] * len(mark),
         [
             pltpu.VMEM((len(terms), *block), BF),
             pltpu.VMEM((max(len(wide), 1), *(block if wide else (16, LANES))), F32),
@@ -362,6 +378,7 @@
         ],
         aliases=aliases,
     )
+    return result[: len(outs)]
 
 
 ALL = slice(None)
@@ -667,11 +684,8 @@
             query = qkv_out[:, at : at + 2 * HEAD_DIM]
             keys = qkv_out[:, width + at : width + at + 2 * HEAD_DIM]
             values = qkv_out[:, 2 * width + at : 2 * width + at + 2 * HEAD_DIM]
-            mixed = None
-            for mask in masks:
-                probs = head_probs(query, keys, mask, tokens).astype(BF)
-                piece = dot(probs, jnp.where(mask, values, 0).astype(BF))
-                mixed = piece if mixed is None else mixed + piece
+            probs = pair_probs(query, keys, masks, tokens).astype(BF)
+            mixed = unstacked(dot(probs, values), masks)
             ao_out[:, width + at : width + at + 2 * HEAD_DIM] = mixed.astype(BF)
         x1 = x + dot(ao_out[:, width : 2 * width], wout[...]) + vec(6)
         x1_out[...] = x1
@@ -1231,18 +1245,15 @@
             keys = qkv_ref[:, width + at : width + at + 2 * HEAD_DIM]
             values = qkv_ref[:, 2 * width + at : 2 * width + at + 2 * HEAD_DIM]
             d_o = d_mixed[:, at : at + 2 * HEAD_DIM]
-            sums = None
-            for mask in masks:
-                probs = head_probs(query, keys, mask, tokens)
-                d_here = jnp.where(mask, d_o, 0).astype(BF)
-                d_probs = dot_nt(d_here, values)
-                d_values = dot_tn(probs.astype(BF), d_here)
-                d_scores = probs * (d_probs - jnp.sum(d_probs * probs, -1, keepdims=True))
-                d_scores = d_scores.astype(BF)
-                d_query = dot(d_scores, jnp.where(mask, keys, 0).astype(BF))
-                d_keys = dot_tn(d_scores, jnp.where(mask, query, 0).astype(BF))
-                here = (d_query, d_keys, d_values)
-                sums = here if sums is None else tuple(s + h for s, h in zip(sums, here))
+            probs = pair_probs(query, keys, masks, tokens)
+            d_here = stacked(d_o, masks)
+            d_probs = dot_nt(d_here, values)
+            d_values = dot_tn(probs.astype(BF), d_here)
+            d_scores = probs * (d_probs - jnp.sum(d_probs * probs, -1, keepdims=True))
+            d_scores = d_scores.astype(BF)
+            d_query = unstacked(dot(d_scores, keys), masks)
+            d_keys = dot_tn(d_scores, stacked(query, masks))
+            sums = (d_query, d_keys, d_values)
             for k, value in enumerate((sums[0] * scale, sums[1] * scale, sums[2])):
                 first = k * width + at
                 back_out[0:padded, first : first + 2 * HEAD_DIM] = value.astype(BF)
@@ -1596,6 +1607,67 @@
             self.come = swap(self.keep, "expert", 1)
         self.done += 1
 
+    def finish(self, z, layer, layers, given, smalls, experts, per):
+        rows, half = self.rows, self.width
+        wide = (half - LANES) // 2
+        others = sorted(smalls)
+        count = len(given)
+
+        def kernel(z_ref, *refs):
+            refs = list(refs)
+            terms = [refs.pop(0) for _ in range(4)]
+            ins = {n: refs.pop(0) for n in others}
+            del refs[:count]
+            qkv, out, gains, biases, router, bias_in, bias_oe, high, square, sems = refs
+            for p in range(2):
+                high[p] = terms[p][...].astype(F32) + terms[2 + p][...].astype(F32)
+            copies = [
+                (high.at[0, :, pl.ds(0, 2 * wide)], qkv.at[layer, :, pl.ds(0, 2 * wide)]),
+                (high.at[1, :, pl.ds(0, wide)], qkv.at[layer, :, pl.ds(2 * wide, wide)]),
+                (high.at[1, :, pl.ds(wide, wide)], out.at[layer]),
+            ]
+            copies = [pltpu.make_async_copy(a, b, sems.at[n]) for n, (a, b) in enumerate(copies)]
+            start(copies)
+            for n in range(layers):
+                square[...] = jnp.zeros_like(square)
+                if n == layer:
+                    square[0:rows, :] = high[1, :, 2 * wide : 2 * wide + LANES]
+                else:
+                    square[0:rows, :] = ins[n][...]
+                square[...] = square[...].T
+                router[n] = square[0:experts, 0:rows]
+                gains[n] = square[16:18, 0:rows]
+                for k in range(5):
+                    biases[k, n : n + 1, :] = square[18 + k : 19 + k, 0:rows]
+                own = square[pl.ds(pl.multiple_of(32 + 8 * z_ref[0], 8), 8), :]
+                for q in range(per):
+                    bias_in[n, :, q * rows : (q + 1) * rows] = own[q : q + 1, 0:rows]
+                bias_oe[n] = own[per : per + 1, 0:rows]
+            wait(copies)
+
+        return call(
+            kernel,
+            "attn_last",
+            [z, *self.parts, *self.came, *[smalls[n] for n in others], *given],
+            [SM] + [VM] * (4 + len(others)) + [HBM] * count,
+            [
+                sds((layers, rows, 3 * wide), F32),
+                sds((layers, rows, wide), F32),
+                sds((layers, 2, rows), F32),
+                sds((5, layers, rows), F32),
+                sds((layers, experts, rows), F32),
+                sds((layers, 1, per * rows), F32),
+                sds((layers, 1, rows), F32),
+            ],
+            [HBM] * 2 + [VM] * 5,
+            [
+                pltpu.VMEM((2, rows, half), F32),
+                pltpu.VMEM((LANES, LANES), F32),
+                pltpu.SemaphoreType.DMA((3,)),
+            ],
+            {5 + len(others): 0, 6 + len(others): 1} if given else None,
+        )
+
     def put(self, z, layer, layers, given):
         shape = (self.rows, self.width)
         wide = (self.width - LANES) // 2
@@ -1634,7 +1706,7 @@
                 sds((layers, self.rows, wide), F32),
                 sds((self.rows, LANES), F32),
             ],
-            [ANY] * 3,
+            [HBM] * 3,
             [
                 pltpu.VMEM((2, *shape), BF),
                 pltpu.VMEM((2, *shape), F32),
@@ -1881,7 +1953,7 @@
         x, x1, qkv, gates, ao = kept
         sent = exchange(sent)
         other_ao = None
-        if four:
+        if four and layer < last:
             ao, other_ao = pick_columns(me, ao, shards)
             other_ao = swap(other_ao, "dp", 1)
         if layer < last:
@@ -1905,7 +1977,10 @@
             (rp, hd, give, made), d_rows = expert_both(
                 me, z, sent, grad_seats[0], expert_w[layer], bias_in, bias_oe, cap, shards
             )
-            saved.append(common)
+            if four:
+                ao, other_ao = pick_columns(me, ao, shards)
+                other_ao = swap(other_ao, "dp", 1)
+            saved.append((x, x1, qkv, gates, ao, other_ao))
 
     attn_sums, expert_sums = [None] * layers, [None] * layers
     for layer in reversed(range(layers)):
@@ -2005,15 +2080,17 @@
         grad_in = jnp.stack([item[0] for item in expert_sums])[:, None].astype(F32)
         grad_oe = jnp.stack([item[1] for item in expert_sums])[:, None].astype(F32)
     if four:
-        out = attn_sums[0].fold3(0, layers, done_attn)
-        (grad_qkv, grad_out), smalls[0] = out[:2], out[2]
+        smalls = {n: smalls[n] for n in range(1, layers)}
+        out = attn_sums[0].finish(z, 0, layers, done_attn, smalls, experts, per)
+        grad_qkv, grad_out, gains, shifts, grad_router, grad_bin, grad_boe = out
     else:
         left = jnp.stack([item[0] for item in attn_sums])
         right = jnp.stack([item[1] for item in attn_sums])
         grad_qkv = jnp.concatenate([left[:, :, : 2 * width], right[:, :, :width]], 2)
         grad_out = right[:, :, width : 2 * width]
         smalls = [right[layer, :, 2 * width :] for layer in range(layers)]
-    gains, shifts, grad_router, grad_bin, grad_boe = small_out(smalls, z, experts, per)
+        small = small_out(smalls, z, experts, per)
+        gains, shifts, grad_router, grad_bin, grad_boe = small
     return (
         mixed,
         grad,

time: 394 us -> 389 us (0.987)
  local copies, waits for them, and re-layouts: 27.4 us -> 23.4 us
    ppermute x55, waiting for transfers between devices: 95.4 us -> 89.6 us  [swap(): return lax.ppermute(value, axis, [(i, i ^ bit) for i in range(size)])]
    unnamed x142 -> x126, local copies, waits for them, and re-layouts: 26.6 us -> 22.6 us
    pallas_call x41 -> x40, Pallas kernels: 167 us -> 167 us  [call(): pl.pallas_call(body, name=name, in_specs=[HBM if spec is LOAD else spec f...]
  transfers between devices with their start and end apart: 62 -> 62, of which waited for: 23 -> 24; matrix products, arithmetic and copies ran while one was open for 1% -> 1% of each run, Pallas kernels for 36% -> 37%
where the time goes in v6:
time: 389 us; the launch traced here: 385 us
  Pallas kernels  167 us (43%)
  waiting for transfers between devices  99.5 us (26%)
  starting transfers between devices  69.4 us (18%)
  local copies, waits for them, and re-layouts  23.4 us (6%)
  between operations  14.9 us (4%)
  blocking collectives  10.6 us (3%)
    pallas_call x40, Pallas kernels, call(): pl.pallas_call(body, name=name, in_specs=[HBM if spec is LOAD else spec f...  167 us
    ppermute x55, waiting for transfers between devices, swap(): return lax.ppermute(value, axis, [(i, i ^ bit) for i in range(size)])  89.6 us
    ppermute x55, starting transfers between devices, swap(): return lax.ppermute(value, axis, [(i, i ^ bit) for i in range(size)])  59.8 us
    unnamed x126, local copies, waits for them, and re-layouts  22.6 us
    all_gather x1, blocking collectives, per_device(): small = lax.all_gather(small, 'dp', axis=0)  10.6 us
  transfers between devices with their start and end apart: 62, of which 24 were waited for; matrix products, arithmetic and copies ran while one was open for 1% of the time, Pallas kernels for 37%

profile of v6, /device:TPU:0, one launch (start us, length us, event | category | flops | bytes accessed | tf_op | source)
XLA Modules:
  0.0 384.9 jit_solution(4603618268395215178)
XLA Ops:
  21.2 3.4 place_pairs.1
  28.6 4.9 %all-to-all-start = ((bf16[4,104,768]{2,1,0:T(8,128)(2,1)}), bf16[4,104,768]{2,1,0:T(8,128)(2,1)S(1)}, u32[]{:S(2)}, u32[]{:S(2)}) async-start(bf16[4,104,768]{2,1,0:T(8,128)(2,1)} %get-tuple-element.128), calls=%async_computation | async-start | bytes 1277952 | tf_op jit(solution)/shard_map/all_to_all | solution.py:1924
  36.4 3.3 collective-permute-done.refs_0_
  44.9 5.6 %collective-permute-done.3.refs_6_.refs_17_ = bf16[1,96,1536]{2,1,0:T(8,128)(2,1)} collective-permute-done((bf16[1,96,1536]{2,1,0:T(8,128)(2,1)}, bf16[1,96,1536]{2,1,0:T(8,128)(2,1)}, u32[]{:S(2)}, u32[]{:S(2)}) %collective-permute-start.3) | collective-permute-done | bytes 294944 | tf_op jit(solution)/shard_map/ppermute | solution.py:1462
  51.1 10.6 %all-gather = f32[256,128]{1,0:T(8,128)} all-gather(f32[32,128]{1,0:T(8,128)S(1)} %copy-done.53), channel_id=2, replica_groups=mesh['dp'=8,'expert'=4] {'dp'}, dimensions={0}, use_global_device_ids=true | all-gather | bytes 147456 | tf_op jit(solution)/shard_map/all_gather | solution.py:1928
  71.4 8.8 %attn_fwd.2 = (f32[208,768]{1,0:T(8,128)}, f32[208,768]{1,0:T(8,128)}, bf16[208,2304]{1,0:T(8,128)(2,1)}, f32[208,128]{1,0:T(8,128)}, bf16[208,2304]{1,0:T(8,128...) custom-call(s32[1]{0:T(128)} %bitcast.1.refs_0_, ...), custom_call_target="tpu_custom_call" | custom-call | tf_op jit(solution)/shard_map/attn_fwd/pallas_call | solution.py:256
  84.6 3.2 pick_columns.2
  87.8 4.2 %collective-permute-done.13.refs_1_ = bf16[2,96,1536]{2,1,0:T(8,128)(2,1)S(1)} collective-permute-done((bf16[2,96,1536]{2,1,0:T(8,128)(2,1)}, bf16[2,96,1536]{2,1,0:T(8,128)(2,1)S(1)}, u32[]{:S(2)}, u32[]{:S(2)}) %collective-permute-start.13) | collective-permute-done | bytes 589856 | tf_op jit(solution)/shard_map/ppermute | solution.py:1462
  99.0 13.0 %expert_fwd.1 = (bf16[416,3840]{1,0:T(8,128)(2,1)}, bf16[416,3072]{1,0:T(8,128)(2,1)}, f32[416,128]{1,0:T(8,128)}, bf16[416,768]{1,0:T(8,128)(2,1)}, bf16[104,76...) custom-call(s32[1]{0:T(128)} %bitcast.1.refs_0_, ...), custom_call_target="tpu_custom_call" | custom-call | tf_op jit(solution)/shard_map/expert_fwd/pallas_call | solution.py:256
  113.5 3.2 collective-permute-start.14
  119.2 4.6 %collective-permute-done.14.refs_5_ = bf16[104,768]{1,0:T(8,128)(2,1)S(1)} collective-permute-done((bf16[104,768]{1,0:T(8,128)(2,1)}, bf16[104,768]{1,0:T(8,128)(2,1)S(1)}, u32[]{:S(2)}, u32[]{:S(2)}) %collective-permute-start.14) | collective-permute-done | bytes 159776 | tf_op jit(solution)/shard_map/ppermute | solution.py:1462
  123.8 7.8 %collective-permute-done.15.refs_6_ = bf16[104,768]{1,0:T(8,128)(2,1)S(1)} collective-permute-done((bf16[104,768]{1,0:T(8,128)(2,1)}, bf16[104,768]{1,0:T(8,128)(2,1)S(1)}, u32[]{:S(2)}, u32[]{:S(2)}) %collective-permute-start.15) | collective-permute-done | bytes 159776 | tf_op jit(solution)/shard_map/ppermute | solution.py:1462
  132.6 9.1 %attn_fwd.3 = (f32[208,768]{1,0:T(8,128)}, f32[208,768]{1,0:T(8,128)}, bf16[208,2304]{1,0:T(8,128)(2,1)}, f32[208,128]{1,0:T(8,128)}, bf16[208,2304]{1,0:T(8,128...) custom-call(s32[1]{0:T(128)} %bitcast.1.refs_0_, ...), custom_call_target="tpu_custom_call" | custom-call | tf_op jit(solution)/shard_map/attn_fwd/pallas_call | solution.py:256
  147.1 6.9 %all-gather.8.cloned.1.call-done = bf16[16,96,3072]{2,1,0:T(8,128)(2,1)} async-done(((bf16[2,96,3072]{2,1,0:T(8,128)(2,1)}), bf16[16,96,3072]{2,1,0:T(8,128)(2,1)}) %all-gather.8.cloned.1.call-update) | async-done | bytes 9437200 | tf_op jit(solution)/shard_map/all_gather | solution.py:1908
  154.0 5.2 %collective-permute-done.25.refs_4_ = bf16[104,768]{1,0:T(8,128)(2,1)S(1)} collective-permute-done((bf16[104,768]{1,0:T(8,128)(2,1)}, bf16[104,768]{1,0:T(8,128)(2,1)S(1)}, u32[]{:S(2)}, u32[]{:S(2)}) %collective-permute-start.25) | collective-permute-done | bytes 159776 | tf_op jit(solution)/shard_map/ppermute | solution.py:1462
  159.9 17.6 %expert_both.1 = (bf16[416,3840]{1,0:T(8,128)(2,1)}, bf16[416,3840]{1,0:T(8,128)(2,1)}, bf16[416,2304]{1,0:T(8,128)(2,1)}, bf16[4,104,768]{2,1,0:T(8,128)(2,1)},...) custom-call(s32[1]{0:T(128)} %bitcast.1.refs_0_, ...), custom_call_target="tpu_custom_call" | custom-call | tf_op jit(solution)/shard_map/expert_both/pallas_call | solution.py:256
  187.2 12.5 %expert_grads.2 = (bf16[4,2,96,3072]{3,2,1,0:T(8,128)(2,1)}, f32[8,768]{1,0:T(8,128)}) custom-call(s32[1]{0:T(128)} %bitcast.1.refs_0_, bf16[416,3840]{1,0:T(8,128)(2,1)} %get-tuple-element.173.refs_1_, bf16[416,3840]{1,0:T(8,128)(2,1)} %collective-permute-done.30.refs_2_, bf16[416,3840]{1,0:T(8,128)(2,1)} %get-tuple-element.174.refs_3_, ...), custom_call_target="tpu_custom_call" | custom-call | tf_op jit(solution)/shard_map/expert_grads/pallas_call | solution.py:256
  200.0 13.4 %attn_back.2 = (f32[208,768]{1,0:T(8,128)}, bf16[224,3328]{1,0:T(8,128)(2,1)}, bf16[104,768]{1,0:T(8,128)(2,1)}, bf16[104,768]{1,0:T(8,128)(2,1)}, bf16[104,768]{1,0:T(8,128)(2,1)}, /*index=5*/bf16[104,768]{1,0:T(8,128)(2,1)}) custom-call(s32[1]{0:T(128)} %bitcast.1.refs_0_, bf16[104,768]{1,0:T(8,128)(2,1)} %get-tuple-element.167.refs_2_.refs_1_, ...), custom_call_target="tpu_custom_call" | custom-call | tf_op jit(solution)/shard_map/attn_back/pallas_call | solution.py:256
  225.0 6.1 %collective-permute-done.33.refs_2_.refs_3_ = bf16[104,768]{1,0:T(8,128)(2,1)S(1)} collective-permute-done((bf16[104,768]{1,0:T(8,128)(2,1)}, bf16[104,768]{1,0:T(8,128)(2,1)S(1)}, u32[]{:S(2)}, u32[]{:S(2)}) %collective-permute-start.33) | collective-permute-done | bytes 159776 | tf_op jit(solution)/shard_map/ppermute | solution.py:1462
  233.6 12.7 %expert_back.1 = (bf16[416,3840]{1,0:T(8,128)(2,1)}, bf16[104,768]{1,0:T(8,128)(2,1)}, bf16[104,768]{1,0:T(8,128)(2,1)}, bf16[104,768]{1,0:T(8,128)(2,1)}, bf16[104,768]{1,0:T(8,128)(2,1)}) custom-call(s32[1]{0:T(128)} %bitcast.1.refs_0_, bf16[104,768]{1,0:T(8,128)(2,1)} %get-tuple-element.180.refs_7_.refs_1_, bf16[104,768]{1,0:T(8,128)(2,1)} %copy-done.44, ...), custom_call_target="tpu_custom_call" | custom-call | tf_op jit(solution)/shard_map/expert_back/pallas_call | solution.py:256
  252.7 12.5 %expert_grads.3 = (bf16[4,2,96,3072]{3,2,1,0:T(8,128)(2,1)}, f32[8,768]{1,0:T(8,128)}) custom-call(s32[1]{0:T(128)} %bitcast.1.refs_0_, bf16[416,3840]{1,0:T(8,128)(2,1)} %get-tuple-element.195.refs_1_, bf16[416,3840]{1,0:T(8,128)(2,1)} %collective-permute-done.40.refs_2_, bf16[416,3840]{1,0:T(8,128)(2,1)} %get-tuple-element.196.refs_3_, ...), custom_call_target="tpu_custom_call" | custom-call | tf_op jit(solution)/shard_map/expert_grads/pallas_call | solution.py:256
  266.1 13.2 %attn_back.3 = (f32[197,768]{1,0:T(8,128)}, bf16[224,3328]{1,0:T(8,128)(2,1)}) custom-call(s32[1]{0:T(128)} %bitcast.1.refs_0_, bf16[104,768]{1,0:T(8,128)(2,1)} %get-tuple-element.188.refs_5_.refs_1_, bf16[104,768]{1,0:T(8,128)(2,1)} %copy-done.41, bf16[104,768]{1,0:T(8,128)(2,1)} %copy-done.42, bf16[104,768]{1,0:T(8,128)(2,1)} %copy-done.43, ...), custom_call_target="tpu_custom_call" | custom-call | tf_op jit(solution)/shard_map/attn_back/pallas_call | solution.py:256
  279.8 3.3 expert_out.2
  285.1 4.3 %attn_grads.3 = (bf16[96,1664]{1,0:T(8,128)(2,1)}, bf16[96,1664]{1,0:T(8,128)(2,1)}, bf16[2,96,1664]{2,1,0:T(8,128)(2,1)S(1)}, bf16[2,96,1664]{2,1,0:T(8,128)(2,1)}, bf16[2,96,1664]{2,1,0:T(8,128)(2,1)S(1)}) custom-call(s32[1]{0:T(128)} %bitcast.1.refs_0_, s32[1]{0:T(128)} %bitcast.refs_0_.refs_1_, bf16[208,1152]{1,0:T(8,128)(2,1)S(1)} %copy-done.6, ...), custom_call_target="tpu_custom_call" | custom-call | tf_op jit(solution)/shard_map/attn_grads/pallas_call | solution.py:256
  291.9 4.3 %all-to-all-start.1 = ((bf16[4,104,768]{2,1,0:T(8,128)(2,1)}), bf16[4,104,768]{2,1,0:T(8,128)(2,1)S(1)}, u32[]{:S(2)}, u32[]{:S(2)}) async-start(bf16[4,104,768]{2,1,0:T(8,128)(2,1)} %hold.11.refs_7_), calls=%async_computation.1 | async-start | bytes 1277952 | tf_op jit(solution)/shard_map/all_to_all | solution.py:2067
  296.3 8.0 %collective-permute-done.45.refs_3_ = bf16[96,1664]{1,0:T(8,128)(2,1)S(1)} collective-permute-done((bf16[96,1664]{1,0:T(8,128)(2,1)}, bf16[96,1664]{1,0:T(8,128)(2,1)S(1)}, u32[]{:S(2)}, u32[]{:S(2)}) %collective-permute-start.45) | collective-permute-done | bytes 319520 | tf_op jit(solution)/shard_map/ppermute | solution.py:1462
  312.1 7.8 %collective-permute-done.46.refs_1_ = bf16[96,1664]{1,0:T(8,128)(2,1)S(1)} collective-permute-done((bf16[96,1664]{1,0:T(8,128)(2,1)}, bf16[96,1664]{1,0:T(8,128)(2,1)S(1)}, u32[]{:S(2)}, u32[]{:S(2)}) %collective-permute-start.46) | collective-permute-done | bytes 319520 | tf_op jit(solution)/shard_map/ppermute | solution.py:1462
  325.0 5.2 %collective-permute-done.48.refs_2_ = bf16[2,96,1664]{2,1,0:T(8,128)(2,1)} collective-permute-done((bf16[2,96,1664]{2,1,0:T(8,128)(2,1)}, bf16[2,96,1664]{2,1,0:T(8,128)(2,1)}, u32[]{:S(2)}, u32[]{:S(2)}) %collective-permute-start.48) | collective-permute-done | bytes 639008 | tf_op jit(solution)/shard_map/ppermute | solution.py:1462
  338.7 3.6 collective-permute-done.51.refs_1_
  343.7 7.6 %collective-permute-done.50.refs_3_ = bf16[96,1664]{1,0:T(8,128)(2,1)S(1)} collective-permute-done((bf16[96,1664]{1,0:T(8,128)(2,1)S(1)}, bf16[96,1664]{1,0:T(8,128)(2,1)S(1)}, u32[]{:S(2)}, u32[]{:S(2)}) %collective-permute-start.50) | collective-permute-done | bytes 319520 | tf_op jit(solution)/shard_map/ppermute | solution.py:1462
  355.8 10.6 %collective-permute-done.54.refs_2_ = bf16[96,1664]{1,0:T(8,128)(2,1)S(1)} collective-permute-done((bf16[96,1664]{1,0:T(8,128)(2,1)S(1)}, bf16[96,1664]{1,0:T(8,128)(2,1)S(1)}, u32[]{:S(2)}, u32[]{:S(2)}) %collective-permute-start.54) | collective-permute-done | bytes 319520 | tf_op jit(solution)/shard_map/ppermute | solution.py:1462
  372.3 3.2 expert_out.3
  (266 shorter events, 130.5 us)
Async XLA Ops:
  7.2 91.8 %all-gather.6.cloned.1.call-start = ((), (), s32[]{:S(2)}) async-start(), calls=%async_computation.5 | async-start | bytes 10616832 | tf_op jit(solution)/shard_map/all_gather | solution.py:1908
  11.3 142.7 %all-gather.8.cloned.1.call-start = ((), (), s32[]{:S(2)}) async-start(), calls=%async_computation.6 | async-start | bytes 10616832 | tf_op jit(solution)/shard_map/all_gather | solution.py:1908
  13.7 22.8 %collective-permute-start.1 = (bf16[2,96,1536]{2,1,0:T(8,128)(2,1)S(1)}, bf16[2,96,1536]{2,1,0:T(8,128)(2,1)S(1)}, u32[]{:S(2)}, u32[]{:S(2)}) collective-permute-start(bf16[2,96,1536]{2,1,0:T(8,128)(2,1)S(1)} %copy-done.22), channel_id=1, source_target_pairs={{0,16},{4,20},{8,24},{12,28},{16,0},{20,4},{24,8},{28,12},{1,17},{... | collective-permute-start | bytes 1769480 | tf_op jit(solution)/shard_map/ppermute | solution.py:1462
  16.7 23.0 %collective-permute-start = (bf16[2,96,1536]{2,1,0:T(8,128)(2,1)S(1)}, bf16[2,96,1536]{2,1,0:T(8,128)(2,1)S(1)}, u32[]{:S(2)}, u32[]{:S(2)}) collective-permute-start(bf16[2,96,1536]{2,1,0:T(8,128)(2,1)S(1)} %copy-done.22), channel_id=1, source_target_pairs={{0,8},{4,12},{8,0},{12,4},{16,24},{20,28},{24,16},{28,20},{1,9},{5... | collective-permute-start | bytes 1769480 | tf_op jit(solution)/shard_map/ppermute | solution.py:1462
  28.6 33.1 %all-to-all-start = ((bf16[4,104,768]{2,1,0:T(8,128)(2,1)}), bf16[4,104,768]{2,1,0:T(8,128)(2,1)S(1)}, u32[]{:S(2)}, u32[]{:S(2)}) async-start(bf16[4,104,768]{2,1,0:T(8,128)(2,1)} %get-tuple-element.128), calls=%async_computation | async-start | bytes 1277952 | tf_op jit(solution)/shard_map/all_to_all | solution.py:1924
  33.5 246.4 %reduce-scatter.10.cloned.1.call-start = ((), (), s32[]{:S(2)}) async-start(), calls=%async_computation.7 | async-start | bytes 5898240
  33.5 32.9 %collective-permute-start.6 = (bf16[2,96,1536]{2,1,0:T(8,128)(2,1)S(1)}, bf16[2,96,1536]{2,1,0:T(8,128)(2,1)}, u32[]{:S(2)}, u32[]{:S(2)}) collective-permute-start(bf16[2,96,1536]{2,1,0:T(8,128)(2,1)S(1)} %copy-done.22), channel_id=1, source_target_pairs={{0,4},{4,0},{8,12},{12,8},{16,20},{20,16},{24,28},{28,24},{1,5},{5... | collective-permute-start | bytes 1769480 | tf_op jit(solution)/shard_map/ppermute | solution.py:1462
  44.9 22.1 %collective-permute-start.2 = (bf16[1,96,1536]{2,1,0:T(8,128)(2,1)}, bf16[1,96,1536]{2,1,0:T(8,128)(2,1)}, u32[]{:S(2)}, u32[]{:S(2)}) collective-permute-start(bf16[1,96,1536]{2,1,0:T(8,128)(2,1)} %get-tuple-element.126.refs_2_), channel_id=1, source_target_pairs={{0,16},{4,20},{8,24},{12,28},{16,0},{20,4},{24,8},{28,12},{1,17},{... | collective-permute-start | bytes 884744 | tf_op jit(solution)/shard_map/ppermute | solution.py:1462
  50.5 17.9 %collective-permute-start.5 = (bf16[1,96,1536]{2,1,0:T(8,128)(2,1)}, bf16[1,96,1536]{2,1,0:T(8,128)(2,1)}, u32[]{:S(2)}, u32[]{:S(2)}) collective-permute-start(bf16[1,96,1536]{2,1,0:T(8,128)(2,1)} %collective-permute-done.3.refs_6_.refs_17_), channel_id=1, source_target_pairs={{0,4},{4,0},{8,12},{12,8},{16,20},{20,16},{24,28},{28,24},{1,5},{5... | collective-permute-start | bytes 884744 | tf_op jit(solution)/shard_map/ppermute | solution.py:1462
  50.5 19.7 %collective-permute-start.7 = (bf16[2,96,1536]{2,1,0:T(8,128)(2,1)}, bf16[2,96,1536]{2,1,0:T(8,128)(2,1)S(1)}, u32[]{:S(2)}, u32[]{:S(2)}) collective-permute-start(bf16[2,96,1536]{2,1,0:T(8,128)(2,1)} %get-tuple-element.124.refs_3_.refs_14_), channel_id=1, source_target_pairs={{0,4},{4,0},{8,12},{12,8},{16,20},{20,16},{24,28},{28,24},{1,5},{5... | collective-permute-start | bytes 1769480 | tf_op jit(solution)/shard_map/ppermute | solution.py:1462
  51.1 19.2 %collective-permute-start.8 = (bf16[2,96,1536]{2,1,0:T(8,128)(2,1)}, bf16[2,96,1536]{2,1,0:T(8,128)(2,1)S(1)}, u32[]{:S(2)}, u32[]{:S(2)}) collective-permute-start(bf16[2,96,1536]{2,1,0:T(8,128)(2,1)} %get-tuple-element.125.refs_4_.refs_15_), channel_id=1, source_target_pairs={{0,4},{4,0},{8,12},{12,8},{16,20},{20,16},{24,28},{28,24},{1,5},{5... | collective-permute-start | bytes 1769480 | tf_op jit(solution)/shard_map/ppermute | solution.py:1462
  66.3 25.7 %collective-permute-start.13 = (bf16[2,96,1536]{2,1,0:T(8,128)(2,1)}, bf16[2,96,1536]{2,1,0:T(8,128)(2,1)S(1)}, u32[]{:S(2)}, u32[]{:S(2)}) collective-permute-start(bf16[2,96,1536]{2,1,0:T(8,128)(2,1)} %pack_attn.3.refs_17_.refs_8_.refs_13_), channel_id=1, source_target_pairs={{0,16},{4,20},{8,24},{12,28},{16,0},{20,4},{24,8},{28,12},{1,17},{... | collective-permute-start | bytes 1769480 | tf_op jit(solution)/shard_map/ppermute | solution.py:1462
  67.0 25.0 %collective-permute-start.12 = (bf16[2,96,1536]{2,1,0:T(8,128)(2,1)}, bf16[2,96,1536]{2,1,0:T(8,128)(2,1)S(1)}, u32[]{:S(2)}, u32[]{:S(2)}) collective-permute-start(bf16[2,96,1536]{2,1,0:T(8,128)(2,1)} %pack_attn.3.refs_17_.refs_8_.refs_13_), channel_id=1, source_target_pairs={{0,8},{4,12},{8,0},{12,4},{16,24},{20,28},{24,16},{28,20},{1,9},{5... | collective-permute-start | bytes 1769480 | tf_op jit(solution)/shard_map/ppermute | solution.py:1462
  92.0 21.5 %collective-permute-start.21 = (bf16[2,96,1536]{2,1,0:T(8,128)(2,1)S(1)}, bf16[2,96,1536]{2,1,0:T(8,128)(2,1)S(1)}, u32[]{:S(2)}, u32[]{:S(2)}) collective-permute-start(bf16[2,96,1536]{2,1,0:T(8,128)(2,1)S(1)} %copy-done.21), channel_id=1, source_target_pairs={{0,4},{4,0},{8,12},{12,8},{16,20},{20,16},{24,28},{28,24},{1,5},{5... | collective-permute-start | bytes 1769480 | tf_op jit(solution)/shard_map/ppermute | solution.py:1462
  95.0 21.6 %collective-permute-start.22 = (bf16[2,96,1536]{2,1,0:T(8,128)(2,1)}, bf16[2,96,1536]{2,1,0:T(8,128)(2,1)S(1)}, u32[]{:S(2)}, u32[]{:S(2)}) collective-permute-start(bf16[2,96,1536]{2,1,0:T(8,128)(2,1)} %get-tuple-element.149.refs_9_.refs_14_), channel_id=1, source_target_pairs={{0,4},{4,0},{8,12},{12,8},{16,20},{20,16},{24,28},{28,24},{1,5},{5... | collective-permute-start | bytes 1769480 | tf_op jit(solution)/shard_map/ppermute | solution.py:1462
  95.3 22.5 %collective-permute-start.23 = (bf16[2,96,1536]{2,1,0:T(8,128)(2,1)}, bf16[2,96,1536]{2,1,0:T(8,128)(2,1)S(1)}, u32[]{:S(2)}, u32[]{:S(2)}) collective-permute-start(bf16[2,96,1536]{2,1,0:T(8,128)(2,1)} %get-tuple-element.150.refs_10_.refs_15_), channel_id=1, source_target_pairs={{0,4},{4,0},{8,12},{12,8},{16,20},{20,16},{24,28},{28,24},{1,5},{5... | collective-permute-start | bytes 1769480 | tf_op jit(solution)/shard_map/ppermute | solution.py:1462
  112.9 18.7 %collective-permute-start.19 = (bf16[1,96,1536]{2,1,0:T(8,128)(2,1)}, bf16[1,96,1536]{2,1,0:T(8,128)(2,1)S(1)}, u32[]{:S(2)}, u32[]{:S(2)}) collective-permute-start(bf16[1,96,1536]{2,1,0:T(8,128)(2,1)} %get-tuple-element.153.refs_11_.refs_16_), channel_id=1, source_target_pairs={{0,4},{4,0},{8,12},{12,8},{16,20},{20,16},{24,28},{28,24},{1,5},{5... | collective-permute-start | bytes 884744 | tf_op jit(solution)/shard_map/ppermute | solution.py:1462
  112.9 18.7 %collective-permute-start.20 = (bf16[1,96,1536]{2,1,0:T(8,128)(2,1)}, bf16[1,96,1536]{2,1,0:T(8,128)(2,1)S(1)}, u32[]{:S(2)}, u32[]{:S(2)}) collective-permute-start(bf16[1,96,1536]{2,1,0:T(8,128)(2,1)} %get-tuple-element.154.refs_12_.refs_17_), channel_id=1, source_target_pairs={{0,4},{4,0},{8,12},{12,8},{16,20},{20,16},{24,28},{28,24},{1,5},{5... | collective-permute-start | bytes 884744 | tf_op jit(solution)/shard_map/ppermute | solution.py:1462
  178.1 21.7 %collective-permute-start.27 = (bf16[104,768]{1,0:T(8,128)(2,1)}, bf16[104,768]{1,0:T(8,128)(2,1)}, u32[]{:S(2)}, u32[]{:S(2)}) collective-permute-start(bf16[104,768]{1,0:T(8,128)(2,1)} %get-tuple-element.168), channel_id=1, source_target_pairs={{0,1},{1,0},{2,3},{3,2},{4,5},{5,4},{6,7},{7,6},{8,9},{9,8},{10,11... | collective-permute-start | bytes 479240 | tf_op jit(solution)/shard_map/ppermute | solution.py:1462
  180.3 19.5 %collective-permute-start.28 = (bf16[104,768]{1,0:T(8,128)(2,1)}, bf16[104,768]{1,0:T(8,128)(2,1)}, u32[]{:S(2)}, u32[]{:S(2)}) collective-permute-start(bf16[104,768]{1,0:T(8,128)(2,1)} %get-tuple-element.169), channel_id=1, source_target_pairs={{0,2},{1,3},{2,0},{3,1},{4,6},{5,7},{6,4},{7,5},{8,10},{9,11},{10,... | collective-permute-start | bytes 479240 | tf_op jit(solution)/shard_map/ppermute | solution.py:1462
  181.4 18.5 %collective-permute-start.29 = (bf16[104,768]{1,0:T(8,128)(2,1)}, bf16[104,768]{1,0:T(8,128)(2,1)}, u32[]{:S(2)}, u32[]{:S(2)}) collective-permute-start(bf16[104,768]{1,0:T(8,128)(2,1)} %get-tuple-element.170), channel_id=1, source_target_pairs={{0,3},{1,2},{2,1},{3,0},{4,7},{5,6},{6,5},{7,4},{8,11},{9,10},{10,... | collective-permute-start | bytes 479240 | tf_op jit(solution)/shard_map/ppermute | solution.py:1462
  199.9 108.7 %reduce-scatter.12.cloned.1.call-start = ((), (), s32[]{:S(2)}) async-start(), calls=%async_computation.8 | async-start | bytes 3194880
  231.8 140.5 %reduce-scatter.14.cloned.1.call-start = ((), (), s32[]{:S(2)}) async-start(), calls=%async_computation.9 | async-start | bytes 5898240
  233.6 18.5 %collective-permute-start.40 = (bf16[416,3840]{1,0:T(8,128)(2,1)S(1)}, bf16[416,3840]{1,0:T(8,128)(2,1)}, u32[]{:S(2)}, u32[]{:S(2)}) collective-permute-start(bf16[416,3840]{1,0:T(8,128)(2,1)S(1)} %copy-done.28), channel_id=1, source_target_pairs={{0,4},{4,0},{8,12},{12,8},{16,20},{20,16},{24,28},{28,24},{1,5},{5... | collective-permute-start | bytes 9584648 | tf_op jit(solution)/shard_map/ppermute | solution.py:1462
  247.0 18.2 %collective-permute-start.37 = (bf16[104,768]{1,0:T(8,128)(2,1)}, bf16[104,768]{1,0:T(8,128)(2,1)S(1)}, u32[]{:S(2)}, u32[]{:S(2)}) collective-permute-start(bf16[104,768]{1,0:T(8,128)(2,1)} %get-tuple-element.189), channel_id=1, source_target_pairs={{0,1},{1,0},{2,3},{3,2},{4,5},{5,4},{6,7},{7,6},{8,9},{9,8},{10,11... | collective-permute-start | bytes 479240 | tf_op jit(solution)/shard_map/ppermute | solution.py:1462
  291.9 31.5 %all-to-all-start.1 = ((bf16[4,104,768]{2,1,0:T(8,128)(2,1)}), bf16[4,104,768]{2,1,0:T(8,128)(2,1)S(1)}, u32[]{:S(2)}, u32[]{:S(2)}) async-start(bf16[4,104,768]{2,1,0:T(8,128)(2,1)} %hold.11.refs_7_), calls=%async_computation.1 | async-start | bytes 1277952 | tf_op jit(solution)/shard_map/all_to_all | solution.py:2067
  306.5 23.6 %collective-permute-start.48 = (bf16[2,96,1664]{2,1,0:T(8,128)(2,1)}, bf16[2,96,1664]{2,1,0:T(8,128)(2,1)}, u32[]{:S(2)}, u32[]{:S(2)}) collective-permute-start(bf16[2,96,1664]{2,1,0:T(8,128)(2,1)} %get-tuple-element.211), channel_id=1, source_target_pairs={{0,16},{4,20},{8,24},{12,28},{16,0},{20,4},{24,8},{28,12},{1,17},{... | collective-permute-start | bytes 1916936 | tf_op jit(solution)/shard_map/ppermute | solution.py:1462
  307.9 24.2 %collective-permute-start.47 = (bf16[2,96,1664]{2,1,0:T(8,128)(2,1)S(1)}, bf16[2,96,1664]{2,1,0:T(8,128)(2,1)}, u32[]{:S(2)}, u32[]{:S(2)}) collective-permute-start(bf16[2,96,1664]{2,1,0:T(8,128)(2,1)S(1)} %get-tuple-element.207.refs_2_), channel_id=1, source_target_pairs={{0,8},{4,12},{8,0},{12,4},{16,24},{20,28},{24,16},{28,20},{1,9},{5... | collective-permute-start | bytes 1916936 | tf_op jit(solution)/shard_map/ppermute | solution.py:1462
  321.3 21.0 %collective-permute-start.51 = (bf16[96,1664]{1,0:T(8,128)(2,1)S(1)}, bf16[96,1664]{1,0:T(8,128)(2,1)}, u32[]{:S(2)}, u32[]{:S(2)}) collective-permute-start(bf16[96,1664]{1,0:T(8,128)(2,1)S(1)} %fold3.3.refs_5_.refs_0_), channel_id=1, source_target_pairs={{0,2},{1,3},{2,0},{3,1},{4,6},{5,7},{6,4},{7,5},{8,10},{9,11},{10,... | collective-permute-start | bytes 958472 | tf_op jit(solution)/shard_map/ppermute | solution.py:1462
  343.6 22.9 %collective-permute-start.54 = (bf16[96,1664]{1,0:T(8,128)(2,1)S(1)}, bf16[96,1664]{1,0:T(8,128)(2,1)S(1)}, u32[]{:S(2)}, u32[]{:S(2)}) collective-permute-start(bf16[96,1664]{1,0:T(8,128)(2,1)S(1)} %fold3.4.refs_4_.refs_1_), channel_id=1, source_target_pairs={{0,1},{1,0},{2,3},{3,2},{4,5},{5,4},{6,7},{7,6},{8,9},{9,8},{10,11... | collective-permute-start | bytes 958472 | tf_op jit(solution)/shard_map/ppermute | solution.py:1462
  353.6 22.0 %collective-permute-start.53 = (bf16[96,1664]{1,0:T(8,128)(2,1)S(1)}, bf16[96,1664]{1,0:T(8,128)(2,1)S(1)}, u32[]{:S(2)}, u32[]{:S(2)}) collective-permute-start(bf16[96,1664]{1,0:T(8,128)(2,1)S(1)} %get-tuple-element.215.refs_2_), channel_id=1, source_target_pairs={{0,1},{1,0},{2,3},{3,2},{4,5},{5,4},{6,7},{7,6},{8,9},{9,8},{10,11... | collective-permute-start | bytes 958472 | tf_op jit(solution)/shard_map/ppermute | solution.py:1462
  353.9 21.6 %collective-permute-start.52 = (bf16[96,1664]{1,0:T(8,128)(2,1)S(1)}, bf16[96,1664]{1,0:T(8,128)(2,1)S(1)}, u32[]{:S(2)}, u32[]{:S(2)}) collective-permute-start(bf16[96,1664]{1,0:T(8,128)(2,1)S(1)} %get-tuple-element.214.refs_3_.refs_1_), channel_id=1, source_target_pairs={{0,2},{1,3},{2,0},{3,1},{4,6},{5,7},{6,4},{7,5},{8,10},{9,11},{10,... | collective-permute-start | bytes 958472 | tf_op jit(solution)/shard_map/ppermute | solution.py:1462
  (91 other events, 755.4 us)
Sparse Core Ops, SparseCore 0:
  11.4 79.8 all-gather.5
  93.7 60.2 all-gather.7
  200.0 56.6 reduce-scatter.9
  259.7 43.8 reduce-scatter.11
  306.4 65.7 reduce-scatter.13

commit v7 on v6

--- a/solution.py
+++ b/solution.py
@@ -18,7 +18,7 @@
 VMEM_LIMIT = 60 * 1024 * 1024
 LIMITS = {name: 16 * 1024 * 1024 for name in ("fold1", "fold2", "fold3", "mix", "attn_last")}
 LIMITS["attn_grads"] = 24 * 1024 * 1024
-LIMITS["pick_columns"] = 62 * 1024 * 1024
+LIMITS["pick_columns"] = 63 * 1024 * 1024
 
 
 def up(value, step):

time: 389 us -> 389 us (level)
    unnamed x126 -> x132, local copies, waits for them, and re-layouts: 22.6 us -> 22 us
where the time goes in v7:
time: 389 us; the launch traced here: 385 us
  Pallas kernels  167 us (43%)
  waiting for transfers between devices  101 us (26%)
  starting transfers between devices  68.6 us (18%)
  local copies, waits for them, and re-layouts  22.8 us (6%)
  between operations  14.9 us (4%)
  blocking collectives  10.7 us (3%)
    pallas_call x40, Pallas kernels, call(): pl.pallas_call(body, name=name, in_specs=[HBM if spec is LOAD else spec f...  167 us
    ppermute x55, waiting for transfers between devices, swap(): return lax.ppermute(value, axis, [(i, i ^ bit) for i in range(size)])  91 us
    ppermute x55, starting transfers between devices, swap(): return lax.ppermute(value, axis, [(i, i ^ bit) for i in range(size)])  59.1 us
    unnamed x132, local copies, waits for them, and re-layouts  22 us
    all_gather x1, blocking collectives, per_device(): small = lax.all_gather(small, 'dp', axis=0)  10.7 us
  transfers between devices with their start and end apart: 62, of which 24 were waited for; matrix products, arithmetic and copies ran while one was open for 1% of the time, Pallas kernels for 37%

profile of v7, /device:TPU:0, one launch (start us, length us, event | category | flops | bytes accessed | tf_op | source)
XLA Modules:
  0.0 384.8 jit_solution(18432119364359724515)
XLA Ops:
  21.2 3.4 place_pairs.1
  28.6 4.9 %all-to-all-start = ((bf16[4,104,768]{2,1,0:T(8,128)(2,1)}), bf16[4,104,768]{2,1,0:T(8,128)(2,1)S(1)}, u32[]{:S(2)}, u32[]{:S(2)}) async-start(bf16[4,104,768]{2,1,0:T(8,128)(2,1)} %get-tuple-element.128), calls=%async_computation | async-start | bytes 1277952 | tf_op jit(solution)/shard_map/all_to_all | solution.py:1924
  36.4 3.3 collective-permute-done.refs_0_
  44.9 5.5 %collective-permute-done.3.refs_6_.refs_17_ = bf16[1,96,1536]{2,1,0:T(8,128)(2,1)S(1)} collective-permute-done((bf16[1,96,1536]{2,1,0:T(8,128)(2,1)}, bf16[1,96,1536]{2,1,0:T(8,128)(2,1)S(1)}, u32[]{:S(2)}, u32[]{:S(2)}) %collective-permute-start.3) | collective-permute-done | bytes 294944 | tf_op jit(solution)/shard_map/ppermute | solution.py:1462
  51.0 10.7 %all-gather = f32[256,128]{1,0:T(8,128)} all-gather(f32[32,128]{1,0:T(8,128)S(1)} %copy-done.56), channel_id=2, replica_groups=mesh['dp'=8,'expert'=4] {'dp'}, dimensions={0}, use_global_device_ids=true | all-gather | bytes 147456 | tf_op jit(solution)/shard_map/all_gather | solution.py:1928
  71.3 8.8 %attn_fwd.2 = (f32[208,768]{1,0:T(8,128)}, f32[208,768]{1,0:T(8,128)}, bf16[208,2304]{1,0:T(8,128)(2,1)}, f32[208,128]{1,0:T(8,128)}, bf16[208,2304]{1,0:T(8,128...) custom-call(s32[1]{0:T(128)} %bitcast.1.refs_0_, ...), custom_call_target="tpu_custom_call" | custom-call | tf_op jit(solution)/shard_map/attn_fwd/pallas_call | solution.py:256
  84.6 3.2 pick_columns.2
  87.8 4.3 %collective-permute-done.13.refs_1_ = bf16[2,96,1536]{2,1,0:T(8,128)(2,1)} collective-permute-done((bf16[2,96,1536]{2,1,0:T(8,128)(2,1)}, bf16[2,96,1536]{2,1,0:T(8,128)(2,1)}, u32[]{:S(2)}, u32[]{:S(2)}) %collective-permute-start.13) | collective-permute-done | bytes 589856 | tf_op jit(solution)/shard_map/ppermute | solution.py:1462
  99.5 13.0 %expert_fwd.1 = (bf16[416,3840]{1,0:T(8,128)(2,1)}, bf16[416,3072]{1,0:T(8,128)(2,1)}, f32[416,128]{1,0:T(8,128)}, bf16[416,768]{1,0:T(8,128)(2,1)}, bf16[104,76...) custom-call(s32[1]{0:T(128)} %bitcast.1.refs_0_, ...), custom_call_target="tpu_custom_call" | custom-call | tf_op jit(solution)/shard_map/expert_fwd/pallas_call | solution.py:256
  119.2 4.6 %collective-permute-done.14.refs_5_ = bf16[104,768]{1,0:T(8,128)(2,1)S(1)} collective-permute-done((bf16[104,768]{1,0:T(8,128)(2,1)}, bf16[104,768]{1,0:T(8,128)(2,1)S(1)}, u32[]{:S(2)}, u32[]{:S(2)}) %collective-permute-start.14) | collective-permute-done | bytes 159776 | tf_op jit(solution)/shard_map/ppermute | solution.py:1462
  123.8 7.8 %collective-permute-done.15.refs_6_ = bf16[104,768]{1,0:T(8,128)(2,1)S(1)} collective-permute-done((bf16[104,768]{1,0:T(8,128)(2,1)}, bf16[104,768]{1,0:T(8,128)(2,1)S(1)}, u32[]{:S(2)}, u32[]{:S(2)}) %collective-permute-start.15) | collective-permute-done | bytes 159776 | tf_op jit(solution)/shard_map/ppermute | solution.py:1462
  132.5 9.1 %attn_fwd.3 = (f32[208,768]{1,0:T(8,128)}, f32[208,768]{1,0:T(8,128)}, bf16[208,2304]{1,0:T(8,128)(2,1)}, f32[208,128]{1,0:T(8,128)}, bf16[208,2304]{1,0:T(8,128...) custom-call(s32[1]{0:T(128)} %bitcast.1.refs_0_, ...), custom_call_target="tpu_custom_call" | custom-call | tf_op jit(solution)/shard_map/attn_fwd/pallas_call | solution.py:256
  147.0 6.7 %all-gather.8.cloned.1.call-done = bf16[16,96,3072]{2,1,0:T(8,128)(2,1)} async-done(((bf16[2,96,3072]{2,1,0:T(8,128)(2,1)}), bf16[16,96,3072]{2,1,0:T(8,128)(2,1)}) %all-gather.8.cloned.1.call-update) | async-done | bytes 9437200 | tf_op jit(solution)/shard_map/all_gather | solution.py:1908
  153.6 5.4 %collective-permute-done.25.refs_4_ = bf16[104,768]{1,0:T(8,128)(2,1)S(1)} collective-permute-done((bf16[104,768]{1,0:T(8,128)(2,1)}, bf16[104,768]{1,0:T(8,128)(2,1)S(1)}, u32[]{:S(2)}, u32[]{:S(2)}) %collective-permute-start.25) | collective-permute-done | bytes 159776 | tf_op jit(solution)/shard_map/ppermute | solution.py:1462
  159.7 17.6 %expert_both.1 = (bf16[416,3840]{1,0:T(8,128)(2,1)}, bf16[416,3840]{1,0:T(8,128)(2,1)}, bf16[416,2304]{1,0:T(8,128)(2,1)}, bf16[4,104,768]{2,1,0:T(8,128)(2,1)},...) custom-call(s32[1]{0:T(128)} %bitcast.1.refs_0_, ...), custom_call_target="tpu_custom_call" | custom-call | tf_op jit(solution)/shard_map/expert_both/pallas_call | solution.py:256
  182.6 3.2 pick_columns.3
  186.3 12.6 %expert_grads.2 = (bf16[4,2,96,3072]{3,2,1,0:T(8,128)(2,1)}, f32[8,768]{1,0:T(8,128)}) custom-call(s32[1]{0:T(128)} %bitcast.1.refs_0_, bf16[416,3840]{1,0:T(8,128)(2,1)} %get-tuple-element.173.refs_1_, bf16[416,3840]{1,0:T(8,128)(2,1)} %collective-permute-done.30.refs_2_, bf16[416,3840]{1,0:T(8,128)(2,1)} %get-tuple-element.174.refs_3_, ...), custom_call_target="tpu_custom_call" | custom-call | tf_op jit(solution)/shard_map/expert_grads/pallas_call | solution.py:256
  199.8 13.4 %attn_back.2 = (f32[208,768]{1,0:T(8,128)}, bf16[224,3328]{1,0:T(8,128)(2,1)}, bf16[104,768]{1,0:T(8,128)(2,1)}, bf16[104,768]{1,0:T(8,128)(2,1)}, bf16[104,768]{1,0:T(8,128)(2,1)}, /*index=5*/bf16[104,768]{1,0:T(8,128)(2,1)}) custom-call(s32[1]{0:T(128)} %bitcast.1.refs_0_, bf16[104,768]{1,0:T(8,128)(2,1)} %get-tuple-element.167.refs_2_.refs_1_, ...), custom_call_target="tpu_custom_call" | custom-call | tf_op jit(solution)/shard_map/attn_back/pallas_call | solution.py:256
  224.7 6.2 %collective-permute-done.33.refs_2_.refs_3_ = bf16[104,768]{1,0:T(8,128)(2,1)S(1)} collective-permute-done((bf16[104,768]{1,0:T(8,128)(2,1)}, bf16[104,768]{1,0:T(8,128)(2,1)S(1)}, u32[]{:S(2)}, u32[]{:S(2)}) %collective-permute-start.33) | collective-permute-done | bytes 159776 | tf_op jit(solution)/shard_map/ppermute | solution.py:1462
  233.5 12.7 %expert_back.1 = (bf16[416,3840]{1,0:T(8,128)(2,1)}, bf16[104,768]{1,0:T(8,128)(2,1)}, bf16[104,768]{1,0:T(8,128)(2,1)}, bf16[104,768]{1,0:T(8,128)(2,1)}, bf16[104,768]{1,0:T(8,128)(2,1)}) custom-call(s32[1]{0:T(128)} %bitcast.1.refs_0_, bf16[104,768]{1,0:T(8,128)(2,1)} %get-tuple-element.180.refs_7_.refs_1_, bf16[104,768]{1,0:T(8,128)(2,1)} %copy-done.47, ...), custom_call_target="tpu_custom_call" | custom-call | tf_op jit(solution)/shard_map/expert_back/pallas_call | solution.py:256
  252.6 12.5 %expert_grads.3 = (bf16[4,2,96,3072]{3,2,1,0:T(8,128)(2,1)}, f32[8,768]{1,0:T(8,128)}) custom-call(s32[1]{0:T(128)} %bitcast.1.refs_0_, bf16[416,3840]{1,0:T(8,128)(2,1)} %get-tuple-element.195.refs_1_, bf16[416,3840]{1,0:T(8,128)(2,1)} %collective-permute-done.40.refs_2_, bf16[416,3840]{1,0:T(8,128)(2,1)} %get-tuple-element.196.refs_3_, ...), custom_call_target="tpu_custom_call" | custom-call | tf_op jit(solution)/shard_map/expert_grads/pallas_call | solution.py:256
  265.9 13.2 %attn_back.3 = (f32[197,768]{1,0:T(8,128)}, bf16[224,3328]{1,0:T(8,128)(2,1)}) custom-call(s32[1]{0:T(128)} %bitcast.1.refs_0_, bf16[104,768]{1,0:T(8,128)(2,1)} %get-tuple-element.188.refs_5_.refs_1_, bf16[104,768]{1,0:T(8,128)(2,1)} %copy-done.44, bf16[104,768]{1,0:T(8,128)(2,1)} %copy-done.45, bf16[104,768]{1,0:T(8,128)(2,1)} %copy-done.46, ...), custom_call_target="tpu_custom_call" | custom-call | tf_op jit(solution)/shard_map/attn_back/pallas_call | solution.py:256
  279.7 3.3 expert_out.2
  285.0 4.3 %attn_grads.3 = (bf16[96,1664]{1,0:T(8,128)(2,1)}, bf16[96,1664]{1,0:T(8,128)(2,1)}, bf16[2,96,1664]{2,1,0:T(8,128)(2,1)S(1)}, bf16[2,96,1664]{2,1,0:T(8,128)(2,1)}, bf16[2,96,1664]{2,1,0:T(8,128)(2,1)S(1)}) custom-call(s32[1]{0:T(128)} %bitcast.1.refs_0_, s32[1]{0:T(128)} %bitcast.refs_0_.refs_1_, bf16[208,1152]{1,0:T(8,128)(2,1)S(1)} %copy-done.6, ...), custom_call_target="tpu_custom_call" | custom-call | tf_op jit(solution)/shard_map/attn_grads/pallas_call | solution.py:256
  291.9 4.2 %all-to-all-start.1 = ((bf16[4,104,768]{2,1,0:T(8,128)(2,1)}), bf16[4,104,768]{2,1,0:T(8,128)(2,1)S(1)}, u32[]{:S(2)}, u32[]{:S(2)}) async-start(bf16[4,104,768]{2,1,0:T(8,128)(2,1)} %hold.11.refs_7_), calls=%async_computation.1 | async-start | bytes 1277952 | tf_op jit(solution)/shard_map/all_to_all | solution.py:2067
  296.1 8.0 %collective-permute-done.45.refs_3_ = bf16[96,1664]{1,0:T(8,128)(2,1)S(1)} collective-permute-done((bf16[96,1664]{1,0:T(8,128)(2,1)}, bf16[96,1664]{1,0:T(8,128)(2,1)S(1)}, u32[]{:S(2)}, u32[]{:S(2)}) %collective-permute-start.45) | collective-permute-done | bytes 319520 | tf_op jit(solution)/shard_map/ppermute | solution.py:1462
  312.0 7.8 %collective-permute-done.46.refs_1_ = bf16[96,1664]{1,0:T(8,128)(2,1)S(1)} collective-permute-done((bf16[96,1664]{1,0:T(8,128)(2,1)}, bf16[96,1664]{1,0:T(8,128)(2,1)S(1)}, u32[]{:S(2)}, u32[]{:S(2)}) %collective-permute-start.46) | collective-permute-done | bytes 319520 | tf_op jit(solution)/shard_map/ppermute | solution.py:1462
  324.9 5.2 %collective-permute-done.48.refs_2_ = bf16[2,96,1664]{2,1,0:T(8,128)(2,1)} collective-permute-done((bf16[2,96,1664]{2,1,0:T(8,128)(2,1)}, bf16[2,96,1664]{2,1,0:T(8,128)(2,1)}, u32[]{:S(2)}, u32[]{:S(2)}) %collective-permute-start.48) | collective-permute-done | bytes 639008 | tf_op jit(solution)/shard_map/ppermute | solution.py:1462
  338.5 3.7 collective-permute-done.51.refs_1_
  343.5 7.6 %collective-permute-done.50.refs_3_ = bf16[96,1664]{1,0:T(8,128)(2,1)S(1)} collective-permute-done((bf16[96,1664]{1,0:T(8,128)(2,1)S(1)}, bf16[96,1664]{1,0:T(8,128)(2,1)S(1)}, u32[]{:S(2)}, u32[]{:S(2)}) %collective-permute-start.50) | collective-permute-done | bytes 319520 | tf_op jit(solution)/shard_map/ppermute | solution.py:1462
  355.7 10.6 %collective-permute-done.54.refs_2_ = bf16[96,1664]{1,0:T(8,128)(2,1)S(1)} collective-permute-done((bf16[96,1664]{1,0:T(8,128)(2,1)S(1)}, bf16[96,1664]{1,0:T(8,128)(2,1)S(1)}, u32[]{:S(2)}, u32[]{:S(2)}) %collective-permute-start.54) | collective-permute-done | bytes 319520 | tf_op jit(solution)/shard_map/ppermute | solution.py:1462
  372.1 3.2 expert_out.3
  (272 shorter events, 130.1 us)
Async XLA Ops:
  7.2 92.3 %all-gather.6.cloned.1.call-start = ((), (), s32[]{:S(2)}) async-start(), calls=%async_computation.5 | async-start | bytes 10616832 | tf_op jit(solution)/shard_map/all_gather | solution.py:1908
  11.3 142.3 %all-gather.8.cloned.1.call-start = ((), (), s32[]{:S(2)}) async-start(), calls=%async_computation.6 | async-start | bytes 10616832 | tf_op jit(solution)/shard_map/all_gather | solution.py:1908
  13.7 22.8 %collective-permute-start.1 = (bf16[2,96,1536]{2,1,0:T(8,128)(2,1)S(1)}, bf16[2,96,1536]{2,1,0:T(8,128)(2,1)S(1)}, u32[]{:S(2)}, u32[]{:S(2)}) collective-permute-start(bf16[2,96,1536]{2,1,0:T(8,128)(2,1)S(1)} %copy-done.22), channel_id=1, source_target_pairs={{0,16},{4,20},{8,24},{12,28},{16,0},{20,4},{24,8},{28,12},{1,17},{... | collective-permute-start | bytes 1769480 | tf_op jit(solution)/shard_map/ppermute | solution.py:1462
  16.7 23.0 %collective-permute-start = (bf16[2,96,1536]{2,1,0:T(8,128)(2,1)S(1)}, bf16[2,96,1536]{2,1,0:T(8,128)(2,1)S(1)}, u32[]{:S(2)}, u32[]{:S(2)}) collective-permute-start(bf16[2,96,1536]{2,1,0:T(8,128)(2,1)S(1)} %copy-done.22), channel_id=1, source_target_pairs={{0,8},{4,12},{8,0},{12,4},{16,24},{20,28},{24,16},{28,20},{1,9},{5... | collective-permute-start | bytes 1769480 | tf_op jit(solution)/shard_map/ppermute | solution.py:1462
  28.6 33.0 %all-to-all-start = ((bf16[4,104,768]{2,1,0:T(8,128)(2,1)}), bf16[4,104,768]{2,1,0:T(8,128)(2,1)S(1)}, u32[]{:S(2)}, u32[]{:S(2)}) async-start(bf16[4,104,768]{2,1,0:T(8,128)(2,1)} %get-tuple-element.128), calls=%async_computation | async-start | bytes 1277952 | tf_op jit(solution)/shard_map/all_to_all | solution.py:1924
  33.5 246.2 %reduce-scatter.10.cloned.1.call-start = ((), (), s32[]{:S(2)}) async-start(), calls=%async_computation.7 | async-start | bytes 5898240
  33.5 32.8 %collective-permute-start.6 = (bf16[2,96,1536]{2,1,0:T(8,128)(2,1)S(1)}, bf16[2,96,1536]{2,1,0:T(8,128)(2,1)S(1)}, u32[]{:S(2)}, u32[]{:S(2)}) collective-permute-start(bf16[2,96,1536]{2,1,0:T(8,128)(2,1)S(1)} %copy-done.22), channel_id=1, source_target_pairs={{0,4},{4,0},{8,12},{12,8},{16,20},{20,16},{24,28},{28,24},{1,5},{5... | collective-permute-start | bytes 1769480 | tf_op jit(solution)/shard_map/ppermute | solution.py:1462
  44.9 22.0 %collective-permute-start.2 = (bf16[1,96,1536]{2,1,0:T(8,128)(2,1)}, bf16[1,96,1536]{2,1,0:T(8,128)(2,1)}, u32[]{:S(2)}, u32[]{:S(2)}) collective-permute-start(bf16[1,96,1536]{2,1,0:T(8,128)(2,1)} %get-tuple-element.126.refs_2_), channel_id=1, source_target_pairs={{0,16},{4,20},{8,24},{12,28},{16,0},{20,4},{24,8},{28,12},{1,17},{... | collective-permute-start | bytes 884744 | tf_op jit(solution)/shard_map/ppermute | solution.py:1462
  50.4 17.9 %collective-permute-start.5 = (bf16[1,96,1536]{2,1,0:T(8,128)(2,1)S(1)}, bf16[1,96,1536]{2,1,0:T(8,128)(2,1)}, u32[]{:S(2)}, u32[]{:S(2)}) collective-permute-start(bf16[1,96,1536]{2,1,0:T(8,128)(2,1)S(1)} %collective-permute-done.3.refs_6_.refs_17_), channel_id=1, source_target_pairs={{0,4},{4,0},{8,12},{12,8},{16,20},{20,16},{24,28},{28,24},{1,5},{5... | collective-permute-start | bytes 884744 | tf_op jit(solution)/shard_map/ppermute | solution.py:1462
  50.4 19.7 %collective-permute-start.7 = (bf16[2,96,1536]{2,1,0:T(8,128)(2,1)}, bf16[2,96,1536]{2,1,0:T(8,128)(2,1)S(1)}, u32[]{:S(2)}, u32[]{:S(2)}) collective-permute-start(bf16[2,96,1536]{2,1,0:T(8,128)(2,1)} %get-tuple-element.124.refs_3_.refs_14_), channel_id=1, source_target_pairs={{0,4},{4,0},{8,12},{12,8},{16,20},{20,16},{24,28},{28,24},{1,5},{5... | collective-permute-start | bytes 1769480 | tf_op jit(solution)/shard_map/ppermute | solution.py:1462
  50.9 19.2 %collective-permute-start.8 = (bf16[2,96,1536]{2,1,0:T(8,128)(2,1)}, bf16[2,96,1536]{2,1,0:T(8,128)(2,1)S(1)}, u32[]{:S(2)}, u32[]{:S(2)}) collective-permute-start(bf16[2,96,1536]{2,1,0:T(8,128)(2,1)} %get-tuple-element.125.refs_4_.refs_15_), channel_id=1, source_target_pairs={{0,4},{4,0},{8,12},{12,8},{16,20},{20,16},{24,28},{28,24},{1,5},{5... | collective-permute-start | bytes 1769480 | tf_op jit(solution)/shard_map/ppermute | solution.py:1462
  66.3 25.8 %collective-permute-start.13 = (bf16[2,96,1536]{2,1,0:T(8,128)(2,1)}, bf16[2,96,1536]{2,1,0:T(8,128)(2,1)}, u32[]{:S(2)}, u32[]{:S(2)}) collective-permute-start(bf16[2,96,1536]{2,1,0:T(8,128)(2,1)} %pack_attn.3.refs_17_.refs_8_.refs_13_), channel_id=1, source_target_pairs={{0,16},{4,20},{8,24},{12,28},{16,0},{20,4},{24,8},{28,12},{1,17},{... | collective-permute-start | bytes 1769480 | tf_op jit(solution)/shard_map/ppermute | solution.py:1462
  66.9 25.2 %collective-permute-start.12 = (bf16[2,96,1536]{2,1,0:T(8,128)(2,1)}, bf16[2,96,1536]{2,1,0:T(8,128)(2,1)}, u32[]{:S(2)}, u32[]{:S(2)}) collective-permute-start(bf16[2,96,1536]{2,1,0:T(8,128)(2,1)} %pack_attn.3.refs_17_.refs_8_.refs_13_), channel_id=1, source_target_pairs={{0,8},{4,12},{8,0},{12,4},{16,24},{20,28},{24,16},{28,20},{1,9},{5... | collective-permute-start | bytes 1769480 | tf_op jit(solution)/shard_map/ppermute | solution.py:1462
  92.1 21.9 %collective-permute-start.21 = (bf16[2,96,1536]{2,1,0:T(8,128)(2,1)S(1)}, bf16[2,96,1536]{2,1,0:T(8,128)(2,1)S(1)}, u32[]{:S(2)}, u32[]{:S(2)}) collective-permute-start(bf16[2,96,1536]{2,1,0:T(8,128)(2,1)S(1)} %copy-done.21), channel_id=1, source_target_pairs={{0,4},{4,0},{8,12},{12,8},{16,20},{20,16},{24,28},{28,24},{1,5},{5... | collective-permute-start | bytes 1769480 | tf_op jit(solution)/shard_map/ppermute | solution.py:1462
  94.0 22.6 %collective-permute-start.22 = (bf16[2,96,1536]{2,1,0:T(8,128)(2,1)}, bf16[2,96,1536]{2,1,0:T(8,128)(2,1)S(1)}, u32[]{:S(2)}, u32[]{:S(2)}) collective-permute-start(bf16[2,96,1536]{2,1,0:T(8,128)(2,1)} %get-tuple-element.149.refs_9_.refs_14_), channel_id=1, source_target_pairs={{0,4},{4,0},{8,12},{12,8},{16,20},{20,16},{24,28},{28,24},{1,5},{5... | collective-permute-start | bytes 1769480 | tf_op jit(solution)/shard_map/ppermute | solution.py:1462
  94.5 23.2 %collective-permute-start.23 = (bf16[2,96,1536]{2,1,0:T(8,128)(2,1)}, bf16[2,96,1536]{2,1,0:T(8,128)(2,1)S(1)}, u32[]{:S(2)}, u32[]{:S(2)}) collective-permute-start(bf16[2,96,1536]{2,1,0:T(8,128)(2,1)} %get-tuple-element.150.refs_10_.refs_15_), channel_id=1, source_target_pairs={{0,4},{4,0},{8,12},{12,8},{16,20},{20,16},{24,28},{28,24},{1,5},{5... | collective-permute-start | bytes 1769480 | tf_op jit(solution)/shard_map/ppermute | solution.py:1462
  113.4 18.1 %collective-permute-start.19 = (bf16[1,96,1536]{2,1,0:T(8,128)(2,1)}, bf16[1,96,1536]{2,1,0:T(8,128)(2,1)S(1)}, u32[]{:S(2)}, u32[]{:S(2)}) collective-permute-start(bf16[1,96,1536]{2,1,0:T(8,128)(2,1)} %get-tuple-element.153.refs_11_.refs_16_), channel_id=1, source_target_pairs={{0,4},{4,0},{8,12},{12,8},{16,20},{20,16},{24,28},{28,24},{1,5},{5... | collective-permute-start | bytes 884744 | tf_op jit(solution)/shard_map/ppermute | solution.py:1462
  113.5 18.1 %collective-permute-start.20 = (bf16[1,96,1536]{2,1,0:T(8,128)(2,1)}, bf16[1,96,1536]{2,1,0:T(8,128)(2,1)S(1)}, u32[]{:S(2)}, u32[]{:S(2)}) collective-permute-start(bf16[1,96,1536]{2,1,0:T(8,128)(2,1)} %get-tuple-element.154.refs_12_.refs_17_), channel_id=1, source_target_pairs={{0,4},{4,0},{8,12},{12,8},{16,20},{20,16},{24,28},{28,24},{1,5},{5... | collective-permute-start | bytes 884744 | tf_op jit(solution)/shard_map/ppermute | solution.py:1462
  178.0 20.9 %collective-permute-start.27 = (bf16[104,768]{1,0:T(8,128)(2,1)}, bf16[104,768]{1,0:T(8,128)(2,1)S(1)}, u32[]{:S(2)}, u32[]{:S(2)}) collective-permute-start(bf16[104,768]{1,0:T(8,128)(2,1)} %get-tuple-element.168), channel_id=1, source_target_pairs={{0,1},{1,0},{2,3},{3,2},{4,5},{5,4},{6,7},{7,6},{8,9},{9,8},{10,11... | collective-permute-start | bytes 479240 | tf_op jit(solution)/shard_map/ppermute | solution.py:1462
  180.2 18.7 %collective-permute-start.28 = (bf16[104,768]{1,0:T(8,128)(2,1)}, bf16[104,768]{1,0:T(8,128)(2,1)S(1)}, u32[]{:S(2)}, u32[]{:S(2)}) collective-permute-start(bf16[104,768]{1,0:T(8,128)(2,1)} %get-tuple-element.169), channel_id=1, source_target_pairs={{0,2},{1,3},{2,0},{3,1},{4,6},{5,7},{6,4},{7,5},{8,10},{9,11},{10,... | collective-permute-start | bytes 479240 | tf_op jit(solution)/shard_map/ppermute | solution.py:1462
  181.1 17.7 %collective-permute-start.29 = (bf16[104,768]{1,0:T(8,128)(2,1)}, bf16[104,768]{1,0:T(8,128)(2,1)S(1)}, u32[]{:S(2)}, u32[]{:S(2)}) collective-permute-start(bf16[104,768]{1,0:T(8,128)(2,1)} %get-tuple-element.170), channel_id=1, source_target_pairs={{0,3},{1,2},{2,1},{3,0},{4,7},{5,6},{6,5},{7,4},{8,11},{9,10},{10,... | collective-permute-start | bytes 479240 | tf_op jit(solution)/shard_map/ppermute | solution.py:1462
  199.7 108.8 %reduce-scatter.12.cloned.1.call-start = ((), (), s32[]{:S(2)}) async-start(), calls=%async_computation.8 | async-start | bytes 3194880
  231.6 140.5 %reduce-scatter.14.cloned.1.call-start = ((), (), s32[]{:S(2)}) async-start(), calls=%async_computation.9 | async-start | bytes 5898240
  233.5 18.4 %collective-permute-start.40 = (bf16[416,3840]{1,0:T(8,128)(2,1)S(1)}, bf16[416,3840]{1,0:T(8,128)(2,1)}, u32[]{:S(2)}, u32[]{:S(2)}) collective-permute-start(bf16[416,3840]{1,0:T(8,128)(2,1)S(1)} %copy-done.26), channel_id=1, source_target_pairs={{0,4},{4,0},{8,12},{12,8},{16,20},{20,16},{24,28},{28,24},{1,5},{5... | collective-permute-start | bytes 9584648 | tf_op jit(solution)/shard_map/ppermute | solution.py:1462
  246.9 18.2 %collective-permute-start.37 = (bf16[104,768]{1,0:T(8,128)(2,1)}, bf16[104,768]{1,0:T(8,128)(2,1)S(1)}, u32[]{:S(2)}, u32[]{:S(2)}) collective-permute-start(bf16[104,768]{1,0:T(8,128)(2,1)} %get-tuple-element.189), channel_id=1, source_target_pairs={{0,1},{1,0},{2,3},{3,2},{4,5},{5,4},{6,7},{7,6},{8,9},{9,8},{10,11... | collective-permute-start | bytes 479240 | tf_op jit(solution)/shard_map/ppermute | solution.py:1462
  291.9 31.5 %all-to-all-start.1 = ((bf16[4,104,768]{2,1,0:T(8,128)(2,1)}), bf16[4,104,768]{2,1,0:T(8,128)(2,1)S(1)}, u32[]{:S(2)}, u32[]{:S(2)}) async-start(bf16[4,104,768]{2,1,0:T(8,128)(2,1)} %hold.11.refs_7_), calls=%async_computation.1 | async-start | bytes 1277952 | tf_op jit(solution)/shard_map/all_to_all | solution.py:2067
  306.4 23.6 %collective-permute-start.48 = (bf16[2,96,1664]{2,1,0:T(8,128)(2,1)}, bf16[2,96,1664]{2,1,0:T(8,128)(2,1)}, u32[]{:S(2)}, u32[]{:S(2)}) collective-permute-start(bf16[2,96,1664]{2,1,0:T(8,128)(2,1)} %get-tuple-element.211), channel_id=1, source_target_pairs={{0,16},{4,20},{8,24},{12,28},{16,0},{20,4},{24,8},{28,12},{1,17},{... | collective-permute-start | bytes 1916936 | tf_op jit(solution)/shard_map/ppermute | solution.py:1462
  307.8 24.2 %collective-permute-start.47 = (bf16[2,96,1664]{2,1,0:T(8,128)(2,1)S(1)}, bf16[2,96,1664]{2,1,0:T(8,128)(2,1)}, u32[]{:S(2)}, u32[]{:S(2)}) collective-permute-start(bf16[2,96,1664]{2,1,0:T(8,128)(2,1)S(1)} %get-tuple-element.207.refs_2_), channel_id=1, source_target_pairs={{0,8},{4,12},{8,0},{12,4},{16,24},{20,28},{24,16},{28,20},{1,9},{5... | collective-permute-start | bytes 1916936 | tf_op jit(solution)/shard_map/ppermute | solution.py:1462
  321.2 21.0 %collective-permute-start.51 = (bf16[96,1664]{1,0:T(8,128)(2,1)S(1)}, bf16[96,1664]{1,0:T(8,128)(2,1)}, u32[]{:S(2)}, u32[]{:S(2)}) collective-permute-start(bf16[96,1664]{1,0:T(8,128)(2,1)S(1)} %fold3.3.refs_5_.refs_0_), channel_id=1, source_target_pairs={{0,2},{1,3},{2,0},{3,1},{4,6},{5,7},{6,4},{7,5},{8,10},{9,11},{10,... | collective-permute-start | bytes 958472 | tf_op jit(solution)/shard_map/ppermute | solution.py:1462
  343.4 22.8 %collective-permute-start.54 = (bf16[96,1664]{1,0:T(8,128)(2,1)S(1)}, bf16[96,1664]{1,0:T(8,128)(2,1)S(1)}, u32[]{:S(2)}, u32[]{:S(2)}) collective-permute-start(bf16[96,1664]{1,0:T(8,128)(2,1)S(1)} %fold3.4.refs_4_.refs_1_), channel_id=1, source_target_pairs={{0,1},{1,0},{2,3},{3,2},{4,5},{5,4},{6,7},{7,6},{8,9},{9,8},{10,11... | collective-permute-start | bytes 958472 | tf_op jit(solution)/shard_map/ppermute | solution.py:1462
  353.4 22.0 %collective-permute-start.53 = (bf16[96,1664]{1,0:T(8,128)(2,1)S(1)}, bf16[96,1664]{1,0:T(8,128)(2,1)S(1)}, u32[]{:S(2)}, u32[]{:S(2)}) collective-permute-start(bf16[96,1664]{1,0:T(8,128)(2,1)S(1)} %get-tuple-element.215.refs_2_), channel_id=1, source_target_pairs={{0,1},{1,0},{2,3},{3,2},{4,5},{5,4},{6,7},{7,6},{8,9},{9,8},{10,11... | collective-permute-start | bytes 958472 | tf_op jit(solution)/shard_map/ppermute | solution.py:1462
  353.8 21.6 %collective-permute-start.52 = (bf16[96,1664]{1,0:T(8,128)(2,1)S(1)}, bf16[96,1664]{1,0:T(8,128)(2,1)S(1)}, u32[]{:S(2)}, u32[]{:S(2)}) collective-permute-start(bf16[96,1664]{1,0:T(8,128)(2,1)S(1)} %get-tuple-element.214.refs_3_.refs_1_), channel_id=1, source_target_pairs={{0,2},{1,3},{2,0},{3,1},{4,6},{5,7},{6,4},{7,5},{8,10},{9,11},{10,... | collective-permute-start | bytes 958472 | tf_op jit(solution)/shard_map/ppermute | solution.py:1462
  (94 other events, 777.7 us)
Sparse Core Ops, SparseCore 0:
  11.4 79.9 all-gather.5
  93.8 59.7 all-gather.7
  199.8 56.7 reduce-scatter.9
  259.6 43.8 reduce-scatter.11
  306.3 65.7 reduce-scatter.13
